TPU v7x, 32 devices: a whole 2x2x4 slice. The times are simulated.
32 devices in a mesh: dp: 8 (over z, y), tensor: 4 (over x, core).
Axes of the slice: x: 2, y: 2, z: 4, core: 2. Of those that a mesh axis runs over, the one named last changes fastest.
Arguments:
- hidden_in: bfloat16 [8192, 1536], P('dp'), may hold values from -6 to 6
- pre_gain: float32 [1536], replicated, may hold values from 0.1 to 1.9
- w_gate: bfloat16 [1536, 3072], P(None, 'tensor'), may hold values from -0.15625 to 0.15625
- w_value: bfloat16 [1536, 3072], P(None, 'tensor'), may hold values from -0.15625 to 0.15625
- w_bc: bfloat16 [1536, 256], replicated, may hold values from -0.15625 to 0.15625
- w_dt: bfloat16 [1536, 48], P(None, 'tensor'), may hold values from -0.15625 to 0.15625
- conv_x: float32 [4, 3072], P(None, 'tensor'), may hold values from -3 to 3
- conv_x_bias: float32 [3072], P('tensor'), may hold values from -2 to 2
- conv_bc: float32 [4, 256], replicated, may hold values from -3 to 3
- conv_bc_bias: float32 [256], replicated, may hold values from -2 to 2
- dt_bias: float32 [48], P('tensor'), may hold values from -7 to -3
- a_log: float32 [48], P('tensor'), may hold values from 0 to 2.77
- d_skip: float32 [48], P('tensor'), may hold values from 0.5 to 1.5
- gate_gain: float32 [3072], P('tensor'), may hold values from 0.1 to 1.9
- w_out: bfloat16 [3072, 1536], P('tensor'), may hold values from -0.109375 to 0.109375
- cotangent: bfloat16 [8192, 1536], P('dp'), may hold values from -6 to 6
- segments: int32 [8, 1024], P('dp'), may hold values from 0 to 31, never falling along the last dimension, each value on 1 to 512 neighbouring positions
Outputs:
- block_out: bfloat16 [8192, 1536], P(('dp', 'tensor'))
- hidden_grad: float32 [8192, 1536], P(('dp', 'tensor'))
- pre_gain_grad: float32 [1536], replicated
- w_gate_grad: float32 [1536, 3072], P(None, 'tensor')
- w_value_grad: float32 [1536, 3072], P(None, 'tensor')
- w_bc_grad: float32 [1536, 256], P(None, 'tensor')
- w_dt_grad: float32 [1536, 48], P(None, 'tensor')
- conv_x_grad: float32 [4, 3072], P(None, 'tensor')
- conv_x_bias_grad: float32 [3072], P('tensor')
- conv_bc_grad: float32 [4, 256], replicated
- conv_bc_bias_grad: float32 [256], replicated
- dt_bias_grad: float32 [48], P('tensor')
- a_log_grad: float32 [48], P('tensor')
- d_skip_grad: float32 [48], P('tensor')
- gate_gain_grad: float32 [3072], P('tensor')
- w_out_grad: float32 [3072, 1536], P('tensor')
Inputs may be any that keep to these rules, and one draw needn't show every extreme that they name: `segments`: within a sequence document numbers never fall; a document has at most 512 tokens.
All inputs are finite; a program needn't handle non-finite values.
Results may differ from a plain program's by a relative error of at most 0.02.
Values may be sent and summed in bfloat16 or wider, within the bound.
No kernel may reach another device: no remote copies, remote signals or barrier semaphores. Data moves between devices by JAX's collectives and lax.ppermute only.
A program may use at most 192 MiB of HBM per device.

v0:
```python
import jax
import jax.numpy as jnp
from jax import lax
from jax.sharding import PartitionSpec as P

D = 1536
STATE = 128
CONV = 4
SPAN = 256
SEQ_LEN = 1024
INNER = 3072


EPS = 1e-05
HIGH = lax.Precision.HIGHEST


def causal_conv(inputs, segments, weight, conv_bias):
    result = conv_bias + weight[CONV - 1] * inputs
    for offset in range(1, CONV):
        shifted = jnp.pad(inputs, ((0, 0), (offset, 0), (0, 0)))[:, :-offset]
        earlier = jnp.pad(segments, ((0, 0), (offset, 0)), constant_values=-1)[:, :-offset]
        same_doc = (earlier == segments).astype(jnp.float32)[..., None]
        result = result + weight[CONV - 1 - offset] * shifted * same_doc
    return jax.nn.silu(result)


def scan_sequence(values, step_sizes, log_rates, bmat, cmat, segments):
    span_count = SEQ_LEN // SPAN
    head_count = log_rates.shape[1]
    values = values.reshape(span_count, SPAN, head_count, -1)
    step_sizes = step_sizes.reshape(span_count, SPAN, head_count)
    log_rates = log_rates.reshape(span_count, SPAN, head_count)
    bmat = bmat.reshape(span_count, SPAN, -1)
    cmat = cmat.reshape(span_count, SPAN, -1)
    blocks = segments.reshape(span_count, SPAN)
    before = jnp.concatenate([jnp.full((1,), -1, jnp.int32), blocks[:-1, -1]])
    cumulative = jnp.cumsum(log_rates, axis=1)
    row_index = lax.broadcasted_iota(jnp.int32, (SPAN, SPAN), 0)
    col_index = lax.broadcasted_iota(jnp.int32, (SPAN, SPAN), 1)
    inside = (blocks[:, :, None] == blocks[:, None, :]) & (row_index >= col_index)[None]
    gaps = cumulative[:, :, None, :] - cumulative[:, None, :, :]
    decays = (
        jnp.exp(jnp.where(inside[..., None], gaps, 0.0)) * inside.astype(jnp.float32)[..., None]
    )
    scores = jnp.einsum("cin,cjn->cij", cmat, bmat, precision=HIGH)
    weights = scores[..., None] * decays * step_sizes[:, None, :, :]
    inside_part = jnp.einsum("cijh,cjhp->cihp", weights, values, precision=HIGH)
    same_last = (blocks == blocks[:, -1:]).astype(jnp.float32)[..., None]
    tail_weight = same_last * jnp.exp(cumulative[:, -1:, :] - cumulative) * step_sizes
    span_states = jnp.einsum(
        "cjhp,cjn->chpn", tail_weight[..., None] * values, bmat, precision=HIGH
    )
    kept_mask = (blocks == before[:, None]).astype(jnp.float32)
    carry_rate = jnp.exp(cumulative[:, -1, :]) * kept_mask[:, -1:]
    carried_state = jnp.zeros(span_states.shape[1:], jnp.float32)
    entering = []
    for position in range(span_count):
        entering.append(carried_state)
        carried_state = carry_rate[position][:, None, None] * carried_state + span_states[position]
    entering = jnp.stack(entering)
    reach_gain = jnp.exp(cumulative) * kept_mask[..., None]
    carried = jnp.einsum("cin,chpn->cihp", cmat, entering, precision=HIGH) * reach_gain[..., None]
    return (inside_part + carried).reshape(SEQ_LEN, head_count, -1)


def mix_heads(
    gate_pre, inner_pre, step_raw, state_io, segments, conv_x, conv_x_bias, dt_bias, a_log, d_skip
):
    values = causal_conv(inner_pre, segments, conv_x, conv_x_bias)
    step_sizes = jax.nn.softplus(step_raw + dt_bias)
    log_rates = -jnp.exp(a_log) * step_sizes
    seq_count, length, channels = values.shape
    head_count = step_sizes.shape[-1]
    head_values = values.reshape(seq_count, length, head_count, channels // head_count)

    def per_sequence(packed):
        vals, sizes, rates_in, states_in, segs_in = packed
        return scan_sequence(
            vals, sizes, rates_in, states_in[:, :STATE], states_in[:, STATE:], segs_in
        )

    scanned = lax.map(
        jax.checkpoint(per_sequence), (head_values, step_sizes, log_rates, state_io, segments)
    )
    scanned = scanned + d_skip[:, None] * head_values
    return scanned.reshape(seq_count, length, channels) * jax.nn.silu(gate_pre)


def shards(
    hidden_in,
    pre_gain,
    w_gate,
    w_value,
    w_bc,
    w_dt,
    conv_x,
    conv_x_bias,
    conv_bc,
    conv_bc_bias,
    dt_bias,
    a_log,
    d_skip,
    gate_gain,
    w_out,
    cotangent,
    segments,
):
    row_count = hidden_in.shape[0]
    seq_count = segments.shape[0]
    ranks = lax.axis_size("tensor")
    my_rank = lax.axis_index("tensor")
    own_rows = row_count // ranks
    row_start = my_rank * own_rows
    pair_width = w_bc.shape[1] // ranks
    pair_start = my_rank * pair_width
    contract_first = (((0,), (0,)), ((), ()))
    contract_last = (((1,), (1,)), ((), ()))
    hidden32 = hidden_in.astype(jnp.float32)
    inv_rms = lax.rsqrt(jnp.mean(hidden32 * hidden32, axis=-1, keepdims=True) + EPS)
    normed = (hidden32 * inv_rms * pre_gain).astype(jnp.bfloat16)
    gate_pre = jnp.dot(normed, w_gate, preferred_element_type=jnp.float32)
    inner_pre = jnp.dot(normed, w_value, preferred_element_type=jnp.float32)
    state_pre = jnp.dot(normed, w_bc, preferred_element_type=jnp.float32)
    step_raw = jnp.dot(normed, w_dt, preferred_element_type=jnp.float32)

    def conv_states(state_flat, conv_weight, conv_offset):
        return causal_conv(
            state_flat.reshape(seq_count, SEQ_LEN, -1), segments, conv_weight, conv_offset
        )

    state_io, state_back = jax.vjp(conv_states, state_pre, conv_bc, conv_bc_bias)

    def heads_part(
        gate_flat,
        inner_flat,
        step_flat,
        states_in,
        conv_weight,
        conv_offset,
        bias_step,
        log_decay,
        skip_weight,
    ):
        return mix_heads(
            gate_flat.reshape(seq_count, SEQ_LEN, -1),
            inner_flat.reshape(seq_count, SEQ_LEN, -1),
            step_flat.reshape(seq_count, SEQ_LEN, -1),
            states_in,
            segments,
            conv_weight,
            conv_offset,
            bias_step,
            log_decay,
            skip_weight,
        ).reshape(row_count, -1)

    mixed_out, heads_back = jax.vjp(
        heads_part,
        gate_pre,
        inner_pre,
        step_raw,
        state_io,
        conv_x,
        conv_x_bias,
        dt_bias,
        a_log,
        d_skip,
    )
    square_sum = lax.psum(jnp.sum(mixed_out * mixed_out, axis=-1, keepdims=True), "tensor")
    inv_gate = lax.rsqrt(square_sum / INNER + EPS)
    gated = (mixed_out * inv_gate * gate_gain).astype(jnp.bfloat16)
    own_hidden = lax.dynamic_slice_in_dim(hidden32, row_start, own_rows, 0)
    branch_sum = lax.psum(
        jnp.dot(gated, w_out, preferred_element_type=jnp.float32).astype(jnp.bfloat16), "tensor"
    ).astype(jnp.float32)
    branch_own = lax.dynamic_slice_in_dim(branch_sum, row_start, own_rows, 0)
    block_out = (own_hidden + branch_own).astype(jnp.bfloat16)
    gated_grad = lax.dot_general(
        cotangent, w_out, contract_last, preferred_element_type=jnp.float32
    )
    w_out_grad = lax.dot_general(
        gated, cotangent, contract_first, preferred_element_type=jnp.float32
    )
    gate_gain_grad = jnp.sum(gated_grad * mixed_out * inv_gate, axis=0)
    scaled_grad = gated_grad * gate_gain
    scale_dot = lax.psum(jnp.sum(scaled_grad * mixed_out, axis=-1, keepdims=True), "tensor")
    mixed_grad = (
        scaled_grad * inv_gate - mixed_out * (inv_gate * inv_gate * inv_gate) * scale_dot / INNER
    )
    (
        gate_grad,
        inner_grad,
        step_grad,
        state_part,
        conv_x_grad,
        conv_x_bias_grad,
        dt_bias_grad,
        a_log_grad,
        d_skip_grad,
    ) = heads_back(mixed_grad)
    state_total = lax.psum(state_part.astype(jnp.bfloat16), "tensor").astype(jnp.float32)
    state_grad, conv_bc_grad, conv_bc_bias_grad = state_back(state_total)
    gate_low = gate_grad.astype(jnp.bfloat16)
    inner_low = inner_grad.astype(jnp.bfloat16)
    step_low = step_grad.astype(jnp.bfloat16)
    pair_low = lax.dynamic_slice_in_dim(state_grad, pair_start, pair_width, 1).astype(jnp.bfloat16)
    pair_weight = lax.dynamic_slice_in_dim(w_bc, pair_start, pair_width, 1)
    w_gate_grad = lax.dot_general(
        normed, gate_low, contract_first, preferred_element_type=jnp.float32
    )
    w_value_grad = lax.dot_general(
        normed, inner_low, contract_first, preferred_element_type=jnp.float32
    )
    w_bc_grad = lax.dot_general(
        normed, pair_low, contract_first, preferred_element_type=jnp.float32
    )
    w_dt_grad = lax.dot_general(
        normed, step_low, contract_first, preferred_element_type=jnp.float32
    )
    total = lax.dot_general(gate_low, w_gate, contract_last, preferred_element_type=jnp.float32)
    total = total + lax.dot_general(
        inner_low, w_value, contract_last, preferred_element_type=jnp.float32
    )
    total = total + lax.dot_general(
        pair_low, pair_weight, contract_last, preferred_element_type=jnp.float32
    )
    normed_grad = lax.psum(
        (
            total
            + lax.dot_general(step_low, w_dt, contract_last, preferred_element_type=jnp.float32)
        ).astype(jnp.bfloat16),
        "tensor",
    ).astype(jnp.float32)
    normed_own = lax.dynamic_slice_in_dim(normed_grad, row_start, own_rows, 0)
    own_inv = lax.dynamic_slice_in_dim(inv_rms, row_start, own_rows, 0)
    own_cotan = lax.dynamic_slice_in_dim(cotangent, row_start, own_rows, 0).astype(jnp.float32)
    gain_scaled = normed_own * pre_gain
    own_dot = jnp.sum(gain_scaled * own_hidden, axis=-1, keepdims=True)
    hidden_grad = (
        own_cotan + own_inv * gain_scaled - own_hidden * (own_inv * own_inv * own_inv) * own_dot / D
    )
    pre_gain_grad = lax.psum(jnp.sum(normed_own * own_hidden * own_inv, axis=0), ("dp", "tensor"))
    summed = (
        lax.psum(w_gate_grad.astype(jnp.bfloat16), "dp").astype(jnp.float32),
        lax.psum(w_value_grad.astype(jnp.bfloat16), "dp").astype(jnp.float32),
        lax.psum(w_bc_grad.astype(jnp.bfloat16), "dp").astype(jnp.float32),
        lax.psum(w_dt_grad.astype(jnp.bfloat16), "dp").astype(jnp.float32),
        lax.psum(conv_x_grad.astype(jnp.bfloat16), "dp").astype(jnp.float32),
        lax.psum(conv_x_bias_grad.astype(jnp.bfloat16), "dp").astype(jnp.float32),
        lax.psum(conv_bc_grad.astype(jnp.bfloat16), "dp").astype(jnp.float32),
        lax.psum(conv_bc_bias_grad.astype(jnp.bfloat16), "dp").astype(jnp.float32),
        lax.psum(dt_bias_grad.astype(jnp.bfloat16), "dp").astype(jnp.float32),
        lax.psum(a_log_grad.astype(jnp.bfloat16), "dp").astype(jnp.float32),
        lax.psum(d_skip_grad.astype(jnp.bfloat16), "dp").astype(jnp.float32),
        lax.psum(gate_gain_grad.astype(jnp.bfloat16), "dp").astype(jnp.float32),
        lax.psum(w_out_grad.astype(jnp.bfloat16), "dp").astype(jnp.float32),
    )
    return (
        block_out,
        hidden_grad,
        pre_gain_grad,
        summed[0],
        summed[1],
        summed[2],
        summed[3],
        summed[4],
        summed[5],
        summed[6],
        summed[7],
        summed[8],
        summed[9],
        summed[10],
        summed[11],
        summed[12],
    )


def solution(mesh):
    in_specs = (
        P("dp", None),
        P(),
        P(None, "tensor"),
        P(None, "tensor"),
        P(),
        P(None, "tensor"),
        P(None, "tensor"),
        P("tensor"),
        P(),
        P(),
        P("tensor"),
        P("tensor"),
        P("tensor"),
        P("tensor"),
        P("tensor", None),
        P("dp", None),
        P("dp", None),
    )
    out_specs = (
        P(("dp", "tensor"), None),
        P(("dp", "tensor"), None),
        P(),
        P(None, "tensor"),
        P(None, "tensor"),
        P(None, "tensor"),
        P(None, "tensor"),
        P(None, "tensor"),
        P("tensor"),
        P(),
        P(),
        P("tensor"),
        P("tensor"),
        P("tensor"),
        P("tensor"),
        P("tensor", None),
    )
    return jax.shard_map(shards, mesh=mesh, in_specs=in_specs, out_specs=out_specs, check_vma=False)
```

profile of v0, /device:TPU:0, one launch (start us, length us, event | category | flops | bytes accessed | tf_op | source)
XLA Modules:
  0.0 692.7 jit_solution(5938428577417683294)
XLA Ops:
  24.4 5.2 fusion.141
  37.6 5.1 reshape.589
  53.9 15.4 %fusion.6 = f32[4,12,64,256]{3,2,1,0:T(8,128)S(1)} fusion(f32[4,256,12]{1,2,0:T(8,128)S(1)} %copy.367, f32[4,256,256]{2,1,0:T(8,128)S(1)} %get-tuple-element.171, f32[4,256,12]{1,2,0:T(8,128)S(1)} %copy-done.56, f32[4,256,256]{2,1,0:T(8,128)S(1)} %fusion.143, pred[4,256,256]{2,1,0:T(8,128)(4,1)S(1)} %get-tuple-element.170, f32[4,256,12,64]{1,0,3,2:T(4,128)S(1)} %copy-done.13), kind=kOutput, calls=%fused_computation.10 | convolution fusion | flops 2431647744 | bytes 8749056 | tf_op jit(solution)/shard_map/jvp()/while/body/eval_jaxpr/cijh,cjhp->cihp/dot_general | solution.py:48
  81.8 10.4 %multiply_reduce_fusion.8 = (f32[1024]{0:T(1024)}, f32[1024,768]{1,0:T(8,128)}, f32[1024,768]{1,0:T(8,128)}) fusion(f32[1024,768]{1,0:T(8,128)} %copy.374, f32[1,1024,768]{2,1,0:T(8,128)} %get-tuple-element.147, f32[768]{0:T(1024)S(1)} %mul.1047, bf16[1024,1536]{1,0:T(8,128)(2,1)} %copy-done.1, bf16[1536,768]{1,0:T(8,128)(2,1)S(1)} %copy-done), kind=kOutput, calls=%fused_computation.86 | convolution fusion | flops 2426141696 | bytes 18095104 | tf_op jit(solution)/shard_map/dot_general | solution.py:122
  92.2 9.0 %psum.133 = f32[1024,1]{0,1:T(1,128)} all-reduce(f32[1024,1]{0,1:T(1,128)} %bitcast.381), channel_id=1, replica_groups=mesh['dp'=8,'tensor'=4] {'tensor'}, use_global_device_ids=true, to_apply=%region_4.5 | all-reduce | flops 1024 | bytes 8192 | tf_op jit(solution)/shard_map/psum | solution.py:170
  102.5 8.6 %multiply_reduce_fusion.2 = (bf16[768]{0:T(1024)(128)(2,1)}, f32[1024]{0:T(1024)}, f32[1024,768]{1,0:T(8,128)}) fusion(f32[1024,768]{1,0:T(8,128)} %get-tuple-element.142, f32[1024]{0:T(1024)S(1)} %bitcast.358, f32[768]{0:T(1024)} %param.30, bf16[1024,1536]{1,0:T(8,128)(2,1)} %param.32, bf16[768,1536]{1,0:T(8,128)(2,1)} %param.31), kind=kOutput, calls=%fused_computation.78 | convolution fusion | flops 2420635904 | bytes 11809280 | tf_op jit(solution)/shard_map/dot_general | solution.py:179
  111.0 6.4 psum.135
  117.5 7.5 %fusion.42 = (f32[768]{0:T(1024)}, f32[1024,768]{1,0:T(8,128)}) fusion(f32[1,1024,768]{2,1,0:T(8,128)} %get-tuple-element.147, f32[1024,768]{1,0:T(8,128)} %get-tuple-element.195, f32[1024]{0:T(1024)} %psum.135, f32[1024,768]{1,0:T(8,128)} %get-tuple-element.142, f32[1024]{0:T(1024)} %bitcast.363, f32[1024]{0:T(1024)S(1)} %bitcast.359, ...), kind=kLoop, calls=%fused_computation.65 | loop fusion | flops 13368576 | bytes 15747072 | tf_op jit(solution)/shard_map/transpose(jvp())/reduce_sum | solution.py:86
  146.4 5.5 reshape.603
  169.2 5.3 fusion.86
  175.9 5.4 fusion.87
  181.3 21.5 %fusion.14 = (f32[4,256,12]{1,2,0:T(8,128)}, f32[4,256,12]{1,2,0:T(8,128)}, f32[4,256,12]{1,2,0:T(8,128)}, f32[4,256,256]{2,1,0:T(8,128)S(1)}) fusion(f32[4,256,12]{1,2,0:T(8,128)S(1)} %get-tuple-element.174, f32[4,256,256]{2,1,0:T(8,128)S(1)} %copy-done.32, f32[4,256,12]{1,2,0:T(8,128)S(1)} %bitcast.326, f32[4,256,256]{2,1,0:T(8,128)S(1)} %fusion.145, ...), kind=kOutput, calls=%fused_computation.18 | convolution fusion | flops 2462806016 | bytes 9945088 | tf_op jit(solution)/shard_map/transpose(jvp())/while/body/eval_jaxpr/checkpoint/cijh,cjhp->cihp/dot_general | solution.py:48
  209.2 8.1 %fusion.35 = bf16[1024,768]{1,0:T(8,128)(2,1)} fusion(f32[1024,768]{1,0:T(8,128)} %get-tuple-element.195, f32[1024]{0:T(1024)} %psum.135, f32[1024,768]{1,0:T(8,128)} %get-tuple-element.142, f32[1024,768]{1,0:T(8,128)} %get-tuple-element.196, f32[1024]{0:T(1024)} %bitcast.364, f32[768]{0:T(1024)} %param.30, f32[1024]{0:T(1024)} %bitcast.360, ...), kind=kLoop, calls=%fused_computation.54 | loop fusion | flops 18087936 | bytes 17319936 | tf_op jit(solution)/shard_map/convert_element_type | solution.py:204
  221.7 11.8 %bitcast_add_fusion = f32[4,256,12,64]{1,3,2,0:T(8,128)S(1)} fusion(f32[4,256,12,64]{1,3,2,0:T(8,128)S(1)} %copy-done.26, f32[4,256,12]{1,2,0:T(8,128)S(1)} %copy-done.55, f32[4,256,256]{2,1,0:T(8,128)S(1)} %copy-done.33, f32[4,256,12]{1,2,0:T(8,128)S(1)} %bitcast.327, f32[4,256,256]{2,1,0:T(8,128)S(1)} %copy-done.35, ...), kind=kOutput, calls=%fused_computation.68 | convolution fusion | flops 2433220608 | bytes 11943936 | tf_op jit(solution)/shard_map/transpose(jvp())/while/body/eval_jaxpr/checkpoint/cijh,cjhp->cihp/dot_general | solution.py:48
  241.5 12.4 %multiply_reduce_fusion.6 = (f32[768]{0:T(1024)}, f32[768]{0:T(1024)}, f32[768]{0:T(1024)}, bf16[768]{0:T(1024)(128)(2,1)}, f32[768]{0:T(1024)}, /*index=5*/f32[1,1024,768]{2,1,0:T(8,128)}) fusion(f32[1,1024,768]{2,1,0:T(8,128)} %bitcast.294, f32[1024]{0:T(1024)S(1)} %bitcast.349, f32[1024]{0:T(1024)S(1)} %bitcast.343, f32[1024]{0:T(1024)S(1)} %bitcast.337, ...), kind=kLoop, calls=%fused_computation.82 | loop fusion | flops 18084096 | bytes 18903552 | tf_op jit(solution)/shard_map/transpose(jvp())/reduce_sum | solution.py:24
  265.1 9.9 %reduce-window.26 = f32[4,12,2,128]{3,1,2,0:T(8,128)S(1)} reduce-window(f32[4,12,2,128]{3,1,2,0:T(8,128)S(1)} %copy.403, f32[]{:T(128)} %constant.101.clone.1), window={size=1x1x1x128 pad=0_0x0_0x0_0x0_127}, to_apply=%region_21.22 | reduce-window | flops 1560576 | bytes 98308 | tf_op jit(solution)/shard_map/reduce-window.4
  286.8 4.6 fusion.144
  301.9 5.6 add_convert_fusion
  307.6 6.8 convolution_convert_fusion.2
  323.9 5.5 convert_element_type.198
  332.9 38.0 %all-reduce.33 = (bf16[1536,12]{0,1:T(8,128)(2,1)S(1)}, bf16[4,768]{1,0:T(4,128)(2,1)S(1)}, bf16[768]{0:T(1024)(128)(2,1)S(1)}, bf16[4,256]{1,0:T(4,128)(2,1)S(1...) all-reduce(bf16[1536,12]{0,1:T(8,128)(2,1)S(1)} %convolution_conver, ...), channel_id=1, replica_groups=mesh['dp'=8,'tensor'=4] {'dp'}, use_global_device_ids=true, to_apply=%region_30.31 | all-reduce | flops 24356 | bytes 97424 | tf_op jit(solution)/shard_map/psum | solution.py:248
  376.1 51.8 %all-reduce.44.cloned.1.call-done = (bf16[1024,1536]{1,0:T(8,128)(2,1)}, bf16[1024,1536]{1,0:T(8,128)(2,1)}) async-done(((bf16[1024,1536]{1,0:T(8,128)(2,1)}, bf16[1024,1536]{1,0:T(8,128)(2,1)}), (bf16[1024,1536]{1,0:T(8,128)(2,1)}, bf16[1024,1536]{1,0:T(8,128)(2,1)})) %all-reduce.44.cloned.1.call-update) | async-done | bytes 6291472 | tf_op jit(solution)/shard_map/psum | solution.py:174
  430.0 44.0 %psum.138 = f32[1536]{0:T(1024)} all-reduce(f32[1536]{0:T(1024)S(1)} %get-tuple-element.92), channel_id=1, replica_groups=mesh['dp'=8,'tensor'=4] {'dp','tensor'}, use_global_device_ids=true, to_apply=%region_26.27 | all-reduce | flops 1536 | bytes 12288 | tf_op jit(solution)/shard_map/psum | solution.py:243
  478.1 197.4 %all-reduce.42.cloned.1.call-done = (bf16[1536,768]{1,0:T(8,128)(2,1)}, bf16[1536,768]{1,0:T(8,128)(2,1)}, bf16[1536,64]{0,1:T(8,128)(2,1)}, bf16[768,1536]{1,0:T(8,128)(2,1)}) async-done(((bf16[1536,768]{1,0:T(8,128)(2,1)}, bf16[1536,768]{1,0:T(8,128)(2,1)}, bf16[1536,64]{0,1:T(8,128)(2,1)}, bf16[768,1536]{1,0:T(8,128)(2,1)}), (bf16[1536,768]{1,0:T(8,128)(2,1)}, bf16[1536,768]{1,0:T(8,128)(2,1)}, ...) | async-done | bytes 7274512 | tf_op jit(solution)/shard_map/psum | solution.py:245
  (397 shorter events, 175.8 us)
Async XLA Ops:
  7.2 74.6 %copy-start = (bf16[1536,768]{1,0:T(8,128)(2,1)S(1)}, bf16[1536,768]{1,0:T(8,128)(2,1)}, u32[]{:S(2)}) copy-start(bf16[1536,768]{1,0:T(8,128)(2,1)} %param.19) | copy-start | bytes 7077892
  7.2 6.9 copy-start.110
  7.2 6.9 %copy-start.52 = (f32[1536]{0:T(1024)S(1)}, f32[1536]{0:T(1024)}, u32[]{:S(2)}) copy-start(f32[1536]{0:T(1024)} %param.18) | copy-start | bytes 18436
  7.2 288.1 %all-reduce.40.cloned.1.call-start = ((), (), s32[]{:S(2)}) async-start(), calls=%async_computation | async-start | bytes 1048576 | tf_op jit(solution)/shard_map/psum | solution.py:202
  21.5 8.1 %copy-start.36 = (f32[4,12,256]{2,0,1:T(4,128)}, f32[4,12,256]{2,0,1:T(4,128)S(1)}, u32[]{:S(2)}) copy-start(f32[4,12,256]{2,0,1:T(4,128)S(1)} %reduce_window_sum.45) | copy-start | bytes 147460
  53.7 15.6 %copy-start.70 = (f32[4]{0:T(128)}, f32[4]{0:T(128)S(1)}, u32[]{:S(2)}) copy-start(f32[4]{0:T(128)S(1)} %pad.196.clone) | copy-start | bytes 52
  81.8 10.4 %copy-start.67 = (f32[768]{0:T(1024)}, f32[768]{0:T(1024)S(1)}, u32[]{:S(2)}) copy-start(f32[768]{0:T(1024)S(1)} %mul.1047) | copy-start | bytes 9220
  102.5 15.0 %copy-start.64 = (f32[1024,1]{0,1:T(1,128)}, f32[1024,1]{0,1:T(1,128)S(1)}, u32[]{:S(2)}) copy-start(f32[1024,1]{0,1:T(1,128)S(1)} %get-tuple-element.140) | copy-start | bytes 12292
  166.2 8.4 %copy-start.45 = (f32[4,256,12]{1,2,0:T(8,128)}, f32[4,256,12]{1,2,0:T(8,128)S(1)}, u32[]{:S(2)}) copy-start(f32[4,256,12]{1,2,0:T(8,128)S(1)} %get-tuple-element.166) | copy-start | bytes 147460
  166.2 15.1 %copy-start.54 = (f32[4,256,12]{1,2,0:T(8,128)}, f32[4,256,12]{1,2,0:T(8,128)S(1)}, u32[]{:S(2)}) copy-start(f32[4,256,12]{1,2,0:T(8,128)S(1)} %get-tuple-element.174) | copy-start | bytes 147460
  175.8 27.0 %copy-start.34 = (f32[4,256,256]{2,1,0:T(8,128)}, f32[4,256,256]{2,1,0:T(8,128)S(1)}, u32[]{:S(2)}) copy-start(f32[4,256,256]{2,1,0:T(8,128)S(1)} %fusion.145) | copy-start | bytes 3145732
  206.7 221.2 %all-reduce.44.cloned.1.call-start = ((), (), s32[]{:S(2)}) async-start(), calls=%async_computation.2 | async-start | bytes 12582912 | tf_op jit(solution)/shard_map/psum | solution.py:174
  209.2 8.1 %copy-start.14 = (f32[1024,768]{1,0:T(8,128)S(1)}, f32[1024,768]{1,0:T(8,128)}, u32[]{:S(2)}) copy-start(f32[1024,768]{1,0:T(8,128)} %get-tuple-element.142) | copy-start | bytes 9437188
  209.2 8.1 %copy-start.65 = (f32[1024,1]{0,1:T(1,128)S(1)}, f32[1024,1]{0,1:T(1,128)}, u32[]{:S(2)}) copy-start(f32[1024,1]{0,1:T(1,128)} %copy-done.64) | copy-start | bytes 12292
  209.2 8.1 %copy-start.80 = (f32[768]{0:T(1024)S(1)}, f32[768]{0:T(1024)}, u32[]{:S(2)}) copy-start(f32[768]{0:T(1024)} %param.30) | copy-start | bytes 9220
  209.2 8.1 %copy-start.108 = (bf16[768,1536]{1,0:T(8,128)(2,1)S(1)}, bf16[768,1536]{1,0:T(8,128)(2,1)}, u32[]{:S(2)}) copy-start(bf16[768,1536]{1,0:T(8,128)(2,1)} %param.31) | copy-start | bytes 7077892
  241.5 12.4 %copy-start.5 = (f32[1024,768]{0,1:T(8,128)S(1)}, f32[1024,768]{0,1:T(8,128)}, u32[]{:S(2)}) copy-start(f32[1024,768]{0,1:T(8,128)} %copy.376) | copy-start | bytes 9437188
  241.5 12.4 %copy-start.9 = (f32[1024,128]{1,0:T(8,128)S(1)}, f32[1024,128]{1,0:T(8,128)}, u32[]{:S(2)}) copy-start(f32[1024,128]{1,0:T(8,128)} %get-tuple-element.160) | copy-start | bytes 1572868
  241.5 12.4 %copy-start.21 = (f32[1,12,64,128]{3,2,1,0:T(8,128)S(1)}, f32[1,12,64,128]{3,2,1,0:T(8,128)}, u32[]{:S(2)}) copy-start(f32[1,12,64,128]{3,2,1,0:T(8,128)} %copy-done.20) | copy-start | bytes 1179652
  241.5 12.4 %copy-start.23 = (f32[1,12,64,128]{3,2,1,0:T(8,128)S(1)}, f32[1,12,64,128]{3,2,1,0:T(8,128)}, u32[]{:S(2)}) copy-start(f32[1,12,64,128]{3,2,1,0:T(8,128)} %copy-done.22) | copy-start | bytes 1179652
  241.5 12.5 %copy-start.25 = (f32[1,12,64,128]{3,2,1,0:T(8,128)S(1)}, f32[1,12,64,128]{3,2,1,0:T(8,128)}, u32[]{:S(2)}) copy-start(f32[1,12,64,128]{3,2,1,0:T(8,128)} %copy-done.24) | copy-start | bytes 1179652
  241.5 12.5 %copy-start.72 = (f32[4]{0:T(128)S(1)}, f32[4]{0:T(128)}, u32[]{:S(2)}) copy-start(f32[4]{0:T(128)} %copy-done.70) | copy-start | bytes 52
  307.5 368.0 %all-reduce.42.cloned.1.call-start = ((), (), s32[]{:S(2)}) async-start(), calls=%async_computation.1 | async-start | bytes 14548992 | tf_op jit(solution)/shard_map/psum | solution.py:245
  329.4 98.5 %copy-start.53 = (f32[1536]{0:T(1024)S(1)}, f32[1536]{0:T(1024)}, u32[]{:S(2)}) copy-start(f32[1536]{0:T(1024)} %param.18) | copy-start | bytes 18436
  (93 other events, 353.0 us)
Sparse Core Ops, SparseCore 0:
  206.8 33.6 all-reduce.39
  307.6 120.2 all-reduce.43
  433.0 242.4 all-reduce.41
where the time goes:
time: 697 us; the launch traced here: 693 us
  waiting for transfers between devices  249 us (36%)
  matrix products  155 us (22%)
  other arithmetic  110 us (16%)
  blocking collectives  97.5 us (14%)
  local copies, waits for them, and re-layouts  65.7 us (9%)
  between operations  15.7 us (2%)
    psum x1, waiting for transfers between devices, shards(): lax.psum(w_gate_grad.astype(jnp.bfloat16), 'dp').astype(jnp.float32)  197 us
    psum x1, waiting for transfers between devices, shards(): lax.psum(jnp.dot(gated, w_out, preferred_element_type=jnp.float32).astype...  51.8 us
    dot_general x3, matrix products, scan_sequence(): inside_part = jnp.einsum('cijh,cjhp->cihp', weights, values, precision=HIGH)  48.7 us
    psum x1, blocking collectives, shards(): lax.psum(jnp.sum(normed_own * own_hidden * own_inv, axis=0), ('dp', 'tens...  44 us
    psum x1, blocking collectives, shards(): lax.psum(w_dt_grad.astype(jnp.bfloat16), 'dp').astype(jnp.float32)  38 us
    another operation x10, other arithmetic  18.9 us
    dot_general x4, matrix products, scan_sequence(): jnp.einsum('cjhp,cjn->chpn', tail_weight[..., None] * values, bmat, preci...  16 us
    reduce_sum x2, other arithmetic, causal_conv(): result = result + weight[CONV - 1 - offset] * shifted * same_doc  15 us
  transfers between devices with their start and end apart: 3, of which 2 were waited for; matrix products, arithmetic and copies ran while one was open for 18% of the time, Pallas kernels for 0%

commit v1 on v0

--- a/solution.py
+++ b/solution.py
@@ -85,6 +85,69 @@
     )
     scanned = scanned + d_skip[:, None] * head_values
     return scanned.reshape(seq_count, length, channels) * jax.nn.silu(gate_pre)
+
+
+def swap(array, axis, bit):
+    size = lax.axis_size(axis)
+    return lax.ppermute(array, axis, [(source, source ^ bit) for source in range(size)])
+
+
+def half_of(array, which):
+    half = array.shape[0] // 2
+    return lax.dynamic_slice_in_dim(array, which * half, half, 0)
+
+
+def axis_bits(axis):
+    size = lax.axis_size(axis)
+    return [1 << place for place in range(size.bit_length() - 1)]
+
+
+def sum_over(array, axis, order):
+    place = lax.axis_index(axis)
+    part = array
+    for bit in order:
+        mine = (place // bit) % 2
+        sent = half_of(part, 1 - mine).astype(jnp.bfloat16)
+        part = half_of(part, mine).astype(jnp.float32) + swap(sent, axis, bit).astype(jnp.float32)
+    part = part.astype(jnp.bfloat16)
+    for bit in reversed(order):
+        mine = (place // bit) % 2
+        other = swap(part, axis, bit)
+        first = jnp.where(mine == 0, part, other)
+        second = jnp.where(mine == 0, other, part)
+        part = jnp.concatenate([first, second], axis=0)
+    return part
+
+
+def sum_rows(array):
+    bits = axis_bits("dp")
+    swapped = [bits[1], bits[0]] + bits[2:]
+    cut = array.shape[0] * 3 // 4
+    first = sum_over(array[:cut], "dp", bits)
+    second = sum_over(array[cut:], "dp", swapped)
+    return jnp.concatenate([first, second], axis=0).astype(jnp.float32)
+
+
+def scatter_tensor(array, dim):
+    part = array.astype(jnp.bfloat16)
+    rank = lax.axis_index("tensor")
+    bits = axis_bits("tensor")
+    count = 1 << len(bits)
+    shape = part.shape
+    grouped = part.reshape(shape[:dim] + (2,) * len(bits) + (shape[dim] // count,) + shape[dim + 1 :])
+    for place, bit in enumerate(bits):
+        mine = (rank // bit) % 2
+        axis_at = dim + len(bits) - 1 - place
+        sent = lax.dynamic_index_in_dim(grouped, 1 - mine, axis_at, keepdims=False)
+        kept = lax.dynamic_index_in_dim(grouped, mine, axis_at, keepdims=False)
+        grouped = kept.astype(jnp.float32) + swap(sent.astype(jnp.bfloat16), "tensor", bit).astype(jnp.float32)
+    return grouped
+
+
+def sum_tensor(array):
+    for bit in axis_bits("tensor"):
+        array = array + swap(array, "tensor", bit)
+    return array
 
 
 def shards(
@@ -129,7 +192,7 @@
             state_flat.reshape(seq_count, SEQ_LEN, -1), segments, conv_weight, conv_offset
         )
 
-    state_io, state_back = jax.vjp(conv_states, state_pre, conv_bc, conv_bc_bias)
+    state_io = conv_states(state_pre, conv_bc, conv_bc_bias)
 
     def heads_part(
         gate_flat,
@@ -167,24 +230,25 @@
         a_log,
         d_skip,
     )
-    square_sum = lax.psum(jnp.sum(mixed_out * mixed_out, axis=-1, keepdims=True), "tensor")
+    gated_grad = lax.dot_general(
+        cotangent, w_out, contract_last, preferred_element_type=jnp.float32
+    )
+    scaled_grad = gated_grad * gate_gain
+    token_sums = sum_tensor(
+        jnp.stack([jnp.sum(mixed_out * mixed_out, axis=-1), jnp.sum(scaled_grad * mixed_out, axis=-1)])
+    )
+    square_sum = token_sums[0][:, None]
+    scale_dot = token_sums[1][:, None]
     inv_gate = lax.rsqrt(square_sum / INNER + EPS)
     gated = (mixed_out * inv_gate * gate_gain).astype(jnp.bfloat16)
     own_hidden = lax.dynamic_slice_in_dim(hidden32, row_start, own_rows, 0)
-    branch_sum = lax.psum(
-        jnp.dot(gated, w_out, preferred_element_type=jnp.float32).astype(jnp.bfloat16), "tensor"
-    ).astype(jnp.float32)
-    branch_own = lax.dynamic_slice_in_dim(branch_sum, row_start, own_rows, 0)
-    block_out = (own_hidden + branch_own).astype(jnp.bfloat16)
-    gated_grad = lax.dot_general(
-        cotangent, w_out, contract_last, preferred_element_type=jnp.float32
-    )
     w_out_grad = lax.dot_general(
         gated, cotangent, contract_first, preferred_element_type=jnp.float32
     )
+    w_out_sum = sum_rows(w_out_grad)
+    branch_own = scatter_tensor(jnp.dot(gated, w_out, preferred_element_type=jnp.float32), 0)
+    block_out = (own_hidden + branch_own).astype(jnp.bfloat16)
     gate_gain_grad = jnp.sum(gated_grad * mixed_out * inv_gate, axis=0)
-    scaled_grad = gated_grad * gate_gain
-    scale_dot = lax.psum(jnp.sum(scaled_grad * mixed_out, axis=-1, keepdims=True), "tensor")
     mixed_grad = (
         scaled_grad * inv_gate - mixed_out * (inv_gate * inv_gate * inv_gate) * scale_dot / INNER
     )
@@ -199,25 +263,27 @@
         a_log_grad,
         d_skip_grad,
     ) = heads_back(mixed_grad)
-    state_total = lax.psum(state_part.astype(jnp.bfloat16), "tensor").astype(jnp.float32)
-    state_grad, conv_bc_grad, conv_bc_bias_grad = state_back(state_total)
     gate_low = gate_grad.astype(jnp.bfloat16)
+    w_gate_sum = sum_rows(
+        lax.dot_general(normed, gate_low, contract_first, preferred_element_type=jnp.float32)
+    )
     inner_low = inner_grad.astype(jnp.bfloat16)
+    w_value_sum = sum_rows(
+        lax.dot_general(normed, inner_low, contract_first, preferred_element_type=jnp.float32)
+    )
+    state_own = scatter_tensor(state_part.reshape(row_count, -1), 1)
+    _, state_back = jax.vjp(
+        conv_states,
+        lax.dynamic_slice_in_dim(state_pre, pair_start, pair_width, 1),
+        lax.dynamic_slice_in_dim(conv_bc, pair_start, pair_width, 1),
+        lax.dynamic_slice_in_dim(conv_bc_bias, pair_start, pair_width, 0),
+    )
+    pair_grad, pair_conv_grad, pair_bias_grad = state_back(
+        state_own.reshape(seq_count, SEQ_LEN, -1)
+    )
+    pair_low = pair_grad.astype(jnp.bfloat16)
     step_low = step_grad.astype(jnp.bfloat16)
-    pair_low = lax.dynamic_slice_in_dim(state_grad, pair_start, pair_width, 1).astype(jnp.bfloat16)
     pair_weight = lax.dynamic_slice_in_dim(w_bc, pair_start, pair_width, 1)
-    w_gate_grad = lax.dot_general(
-        normed, gate_low, contract_first, preferred_element_type=jnp.float32
-    )
-    w_value_grad = lax.dot_general(
-        normed, inner_low, contract_first, preferred_element_type=jnp.float32
-    )
-    w_bc_grad = lax.dot_general(
-        normed, pair_low, contract_first, preferred_element_type=jnp.float32
-    )
-    w_dt_grad = lax.dot_general(
-        normed, step_low, contract_first, preferred_element_type=jnp.float32
-    )
     total = lax.dot_general(gate_low, w_gate, contract_last, preferred_element_type=jnp.float32)
     total = total + lax.dot_general(
         inner_low, w_value, contract_last, preferred_element_type=jnp.float32
@@ -225,14 +291,8 @@
     total = total + lax.dot_general(
         pair_low, pair_weight, contract_last, preferred_element_type=jnp.float32
     )
-    normed_grad = lax.psum(
-        (
-            total
-            + lax.dot_general(step_low, w_dt, contract_last, preferred_element_type=jnp.float32)
-        ).astype(jnp.bfloat16),
-        "tensor",
-    ).astype(jnp.float32)
-    normed_own = lax.dynamic_slice_in_dim(normed_grad, row_start, own_rows, 0)
+    total = total + lax.dot_general(step_low, w_dt, contract_last, preferred_element_type=jnp.float32)
+    normed_own = scatter_tensor(total, 0)
     own_inv = lax.dynamic_slice_in_dim(inv_rms, row_start, own_rows, 0)
     own_cotan = lax.dynamic_slice_in_dim(cotangent, row_start, own_rows, 0).astype(jnp.float32)
     gain_scaled = normed_own * pre_gain
@@ -240,39 +300,74 @@
     hidden_grad = (
         own_cotan + own_inv * gain_scaled - own_hidden * (own_inv * own_inv * own_inv) * own_dot / D
     )
-    pre_gain_grad = lax.psum(jnp.sum(normed_own * own_hidden * own_inv, axis=0), ("dp", "tensor"))
-    summed = (
-        lax.psum(w_gate_grad.astype(jnp.bfloat16), "dp").astype(jnp.float32),
-        lax.psum(w_value_grad.astype(jnp.bfloat16), "dp").astype(jnp.float32),
-        lax.psum(w_bc_grad.astype(jnp.bfloat16), "dp").astype(jnp.float32),
-        lax.psum(w_dt_grad.astype(jnp.bfloat16), "dp").astype(jnp.float32),
-        lax.psum(conv_x_grad.astype(jnp.bfloat16), "dp").astype(jnp.float32),
-        lax.psum(conv_x_bias_grad.astype(jnp.bfloat16), "dp").astype(jnp.float32),
-        lax.psum(conv_bc_grad.astype(jnp.bfloat16), "dp").astype(jnp.float32),
-        lax.psum(conv_bc_bias_grad.astype(jnp.bfloat16), "dp").astype(jnp.float32),
-        lax.psum(dt_bias_grad.astype(jnp.bfloat16), "dp").astype(jnp.float32),
-        lax.psum(a_log_grad.astype(jnp.bfloat16), "dp").astype(jnp.float32),
-        lax.psum(d_skip_grad.astype(jnp.bfloat16), "dp").astype(jnp.float32),
-        lax.psum(gate_gain_grad.astype(jnp.bfloat16), "dp").astype(jnp.float32),
-        lax.psum(w_out_grad.astype(jnp.bfloat16), "dp").astype(jnp.float32),
-    )
+    w_bc_rows = lax.dot_general(pair_low, normed, contract_first, preferred_element_type=jnp.float32)
+    w_dt_rows = lax.dot_general(step_low, normed, contract_first, preferred_element_type=jnp.float32)
+    spread = jnp.zeros((CONV + 1, w_bc.shape[1]), jnp.float32)
+    spread = lax.dynamic_update_slice_in_dim(
+        spread, jnp.concatenate([pair_conv_grad, pair_bias_grad[None]]), pair_start, 1
+    )
+    gain_part = jnp.sum(total * hidden32 * inv_rms, axis=0)
+    shared = sum_tensor(jnp.concatenate([gain_part, spread.reshape(-1)]))
+    small = jnp.concatenate(
+        [
+            conv_x_grad.reshape(-1),
+            conv_x_bias_grad,
+            gate_gain_grad,
+            shared,
+            dt_bias_grad,
+            a_log_grad,
+            d_skip_grad,
+        ]
+    )
+    small_rows = -(-small.shape[0] // D)
+    used_rows = w_bc_rows.shape[0] + w_dt_rows.shape[0] + small_rows
+    all_rows = -(-used_rows // 128) * 128
+    packed = jnp.concatenate(
+        [
+            w_bc_rows,
+            w_dt_rows,
+            jnp.pad(small, (0, small_rows * D - small.shape[0])).reshape(small_rows, D),
+            jnp.zeros((all_rows - used_rows, D), jnp.float32),
+        ]
+    )
+    packed = sum_over(packed, "dp", axis_bits("dp")).astype(jnp.float32)
+    channels = conv_x.shape[1]
+    heads = dt_bias.shape[0]
+    w_bc_sum = packed[:pair_width].T
+    w_dt_sum = packed[pair_width : pair_width + heads].T
+    small = packed[pair_width + heads : used_rows].reshape(-1)
+    pieces = []
+    at = 0
+    for length in (
+        CONV * channels,
+        channels,
+        channels,
+        D,
+        CONV * w_bc.shape[1],
+        w_bc.shape[1],
+        heads,
+        heads,
+        heads,
+    ):
+        pieces.append(small[at : at + length])
+        at += length
     return (
         block_out,
         hidden_grad,
-        pre_gain_grad,
-        summed[0],
-        summed[1],
-        summed[2],
-        summed[3],
-        summed[4],
-        summed[5],
-        summed[6],
-        summed[7],
-        summed[8],
-        summed[9],
-        summed[10],
-        summed[11],
-        summed[12],
+        pieces[3],
+        w_gate_sum,
+        w_value_sum,
+        w_bc_sum,
+        w_dt_sum,
+        pieces[0].reshape(CONV, channels),
+        pieces[1],
+        pieces[4].reshape(CONV, -1),
+        pieces[5],
+        pieces[6],
+        pieces[7],
+        pieces[8],
+        pieces[2],
+        w_out_sum,
     )
 
 

time: 697 us -> 639 us (0.917)
  blocking collectives: 97.5 us -> 0 us
  local copies, waits for them, and re-layouts: 65.7 us -> 116 us
  waiting for transfers between devices: 249 us -> 205 us
  starting transfers between devices: 0.12 us -> 38.1 us
  between operations: 15.7 us -> 3.34 us
    psum x3 -> x0, waiting for transfers between devices: 249 us -> none  [the longest x1 197 us: shards(): lax.psum(w_gate_grad.astype(jnp.bfloat16), 'dp').astype(jnp.float32)]
    ppermute x0 -> x52, waiting for transfers between devices: none -> 205 us  [swap(): lax.ppermute(array, axis, [(source, source ^ bit) for source in range(siz...]
    psum x4 -> x0, blocking collectives: 97.5 us -> none  [the longest x1 44 us: shards(): lax.psum(jnp.sum(normed_own * own_hidden * own_inv, axis=0), ('dp', 'tens...]
    ppermute x0 -> x52, starting transfers between devices: none -> 38.1 us  [swap(): lax.ppermute(array, axis, [(source, source ^ bit) for source in range(siz...]
    add x0 -> x21, other arithmetic: none -> 18.4 us  [the longest x14 11.3 us: sum_over(): half_of(part, mine).astype(jnp.float32)]
    convert_element_type x19 -> x13, other arithmetic: 25.2 us -> 9.22 us  [the longest x3 7.93 us: sum_rows(): return jnp.concatenate([first, second], axis=0).astype(jnp.float32)]
    convert_element_type x0 -> x24, local copies, waits for them, and re-layouts: none -> 15.8 us  [the longest x21 15.6 us: sum_over(): sent = half_of(part, 1 - mine).astype(jnp.bfloat16)]
    slice x0 -> x11, local copies, waits for them, and re-layouts: none -> 13.1 us  [the longest x3 6.1 us: sum_rows(): first = sum_over(array[:cut], 'dp', bits)]
  transfers between devices with their start and end apart: 3 -> 52, of which waited for: 2 -> 34; matrix products, arithmetic and copies ran while one was open for 18% -> 16% of each run, Pallas kernels for 0% -> 0%
where the time goes in v1:
time: 639 us; the launch traced here: 634 us
  waiting for transfers between devices  205 us (32%)
  matrix products  161 us (25%)
  local copies, waits for them, and re-layouts  116 us (18%)
  other arithmetic  111 us (17%)
  starting transfers between devices  38.1 us (6%)
    ppermute x52, waiting for transfers between devices, swap(): lax.ppermute(array, axis, [(source, source ^ bit) for source in range(siz...  205 us
    dot_general x3, matrix products, scan_sequence(): inside_part = jnp.einsum('cijh,cjhp->cihp', weights, values, precision=HIGH)  53.1 us
    ppermute x52, starting transfers between devices, swap(): lax.ppermute(array, axis, [(source, source ^ bit) for source in range(siz...  38.1 us
    unnamed x291, local copies, waits for them, and re-layouts  18.8 us
    another operation x10, other arithmetic  17.1 us
    dot_general x4, matrix products, scan_sequence(): jnp.einsum('cjhp,cjn->chpn', tail_weight[..., None] * values, bmat, preci...  16.8 us
    dot_general x4, matrix products, scan_sequence(): jnp.einsum('cin,chpn->cihp', cmat, entering, precision=HIGH)  15.8 us
    convert_element_type x21, local copies, waits for them, and re-layouts, sum_over(): sent = half_of(part, 1 - mine).astype(jnp.bfloat16)  15.6 us
  transfers between devices with their start and end apart: 52, of which 34 were waited for; matrix products, arithmetic and copies ran while one was open for 16% of the time, Pallas kernels for 0%

profile of v1, /device:TPU:0, one launch (start us, length us, event | category | flops | bytes accessed | tf_op | source)
XLA Modules:
  0.0 634.5 jit_solution(9591751644089552767)
XLA Ops:
  46.9 15.4 %fusion.6 = f32[4,12,64,256]{3,2,1,0:T(8,128)S(1)} fusion(f32[4,256,12]{1,2,0:T(8,128)S(1)} %copy.404, f32[4,256,256]{2,1,0:T(8,128)S(1)} %get-tuple-element.197, f32[4,256,12]{1,2,0:T(8,128)S(1)} %copy-done.78, f32[4,256,256]{2,1,0:T(8,128)S(1)} %fusion.162, pred[4,256,256]{2,1,0:T(8,128)(4,1)S(1)} %get-tuple-element.196, f32[4,256,12,64]{1,0,3,2:T(4,128)S(1)} %copy-done.21), kind=kOutput, calls=%fused_computation.10 | convolution fusion | flops 2431647744 | bytes 8749056 | tf_op jit(solution)/shard_map/jvp()/while/body/eval_jaxpr/cijh,cjhp->cihp/dot_general | solution.py:48
  73.3 6.9 %fusion.163 = f32[1024,768]{1,0:T(8,128)} fusion(bf16[1024,1536]{1,0:T(8,128)(2,1)} %copy-done.1, bf16[1536,768]{1,0:T(8,128)(2,1)} %param.19), kind=kOutput, calls=%fused_computation.427 | convolution fusion | flops 2415919104 | bytes 8650752 | tf_op jit(solution)/shard_map/dot_general | solution.py:185
  82.2 10.5 %multiply_reduce_fusion.9 = (f32[1024]{0:T(1024)S(1)}, f32[1024]{0:T(1024)S(1)}, f32[1024,768]{1,0:T(8,128)}, f32[1024,768]{1,0:T(8,128)}) fusion(f32[768]{0:T(1024)S(1)} %copy-done.68, f32[1024,768]{1,0:T(8,128)} %fusion.163, f32[1024,768]{1,0:T(8,128)} %copy.411, f32[1,1024,768]{2,1,0:T(8,128)} %get-tuple-element.127, f32[768]{0:T(1024)} %mul.1220, ...), kind=kOutput, calls=%fused_computation.86 | convolution fusion | flops 2428499968 | bytes 21248000 | tf_op jit(solution)/shard_map/dot_general | solution.py:233
  110.0 5.7 fusion.144
  158.5 6.1 fusion.83
  170.1 6.2 fusion.84
  185.9 24.7 %fusion.14 = (f32[4,256,12]{1,2,0:T(8,128)S(1)}, f32[4,256,12]{1,2,0:T(8,128)S(1)}, f32[4,256,12]{1,2,0:T(8,128)S(1)}, f32[4,256,256]{2,1,0:T(8,128)}) fusion(f32[4,256,12]{1,2,0:T(8,128)} %get-tuple-element.200, f32[4,256,256]{2,1,0:T(8,128)} %get-tuple-element.195, f32[4,256,12]{1,2,0:T(8,128)S(1)} %bitcast.406, f32[4,256,256]{2,1,0:T(8,128)S(1)} %fusion.165, ...), kind=kOutput, calls=%fused_computation.18 | convolution fusion | flops 2462806016 | bytes 9945088 | tf_op jit(solution)/shard_map/transpose(jvp())/while/body/eval_jaxpr/checkpoint/cijh,cjhp->cihp/dot_general | solution.py:48
  212.9 10.6 %reduce-window.26 = f32[4,12,2,128]{3,1,2,0:T(8,128)S(1)} reduce-window(f32[4,12,2,128]{3,1,2,0:T(8,128)} %copy.445, f32[]{:T(128)} %constant.394.clone.1), window={size=1x1x1x128 pad=0_0x0_0x0_0x0_127}, to_apply=%region_17.18 | reduce-window | flops 1560576 | bytes 98308 | tf_op jit(solution)/shard_map/reduce-window.4
  235.7 13.0 %bitcast_add_fusion = f32[4,256,12,64]{1,3,2,0:T(8,128)S(1)} fusion(f32[4,256,12,64]{1,3,2,0:T(8,128)S(1)} %copy-done.41, f32[4,256,12]{1,2,0:T(8,128)} %get-tuple-element.200, f32[4,256,256]{2,1,0:T(8,128)S(1)} %copy-done.57, f32[4,256,12]{1,2,0:T(8,128)S(1)} %bitcast.407, f32[4,256,256]{2,1,0:T(8,128)} %copy-done.58, ...), kind=kOutput, calls=%fused_computation.68 | convolution fusion | flops 2433220608 | bytes 11943936 | tf_op jit(solution)/shard_map/transpose(jvp())/while/body/eval_jaxpr/checkpoint/cijh,cjhp->cihp/dot_general | solution.py:48
  256.8 10.2 %multiply_reduce_fusion.7 = (f32[768]{0:T(1024)}, f32[768]{0:T(1024)}, f32[768]{0:T(1024)}, f32[768]{0:T(1024)}, f32[768]{0:T(1024)}, /*index=5*/f32[1,1024,768]{2,1,0:T(8,128)S(1)}) fusion(f32[1,1024,768]{2,1,0:T(8,128)} %bitcast.374, f32[1024]{0:T(1024)S(1)} %bitcast.435, f32[1024]{0:T(1024)S(1)} %bitcast.429, f32[1024]{0:T(1024)S(1)} %bitcast.423, ...), kind=kLoop, calls=%fused_computation.82 | loop fusion | flops 18084096 | bytes 18905088 | tf_op jit(solution)/shard_map/transpose(jvp())/reduce_sum | solution.py:24
  354.2 7.9 %multiply_reduce_fusion.1 = (f32[1536]{0:T(1024)S(1)}, bf16[1024,1536]{1,0:T(8,128)(2,1)S(1)}) fusion(bf16[1024,1536]{1,0:T(8,128)(2,1)S(1)} %copy-done.9, f32[1024]{0:T(1024)S(1)} %copy-done.86, f32[1024,1536]{1,0:T(8,128)} %fusion.124, bf16[1536,256]{1,0:T(8,128)(2,1)S(1)} %copy-done.73, s32[]{:T(128)S(6)} %select_n.571, ...), kind=kOutput, calls=%fused_computation.19 | convolution fusion | flops 213907968 | bytes 25831428 | tf_op jit(solution)/shard_map/dot_general | solution.py:291
  405.7 7.0 %collective-permute-done.49 = bf16[24,1536]{1,0:T(8,128)(2,1)S(1)} collective-permute-done((bf16[24,1536]{1,0:T(8,128)(2,1)S(1)}, bf16[24,1536]{1,0:T(8,128)(2,1)S(1)}, u32[]{:S(2)}, u32[]{:S(2)}) %collective-permute-start.49) | collective-permute-done | bytes 73760 | tf_op jit(solution)/shard_map/ppermute | solution.py:92
  424.1 5.8 collective-permute-done.10
  470.2 7.9 %collective-permute-done.14 = bf16[32,1536]{1,0:T(8,128)(2,1)S(1)} collective-permute-done((bf16[32,1536]{1,0:T(8,128)(2,1)S(1)}, bf16[32,1536]{1,0:T(8,128)(2,1)S(1)}, u32[]{:S(2)}, u32[]{:S(2)}) %collective-permute-start.14) | collective-permute-done | bytes 98336 | tf_op jit(solution)/shard_map/ppermute | solution.py:92
  482.5 5.6 collective-permute-done.27
  505.2 6.7 %collective-permute-done.29 = bf16[288,768]{1,0:T(8,128)(2,1)} collective-permute-done((bf16[288,768]{1,0:T(8,128)(2,1)}, bf16[288,768]{1,0:T(8,128)(2,1)}, u32[]{:S(2)}, u32[]{:S(2)}) %collective-permute-start.29) | collective-permute-done | bytes 442400 | tf_op jit(solution)/shard_map/ppermute | solution.py:92
  513.6 9.0 %collective-permute-done.17 = bf16[288,768]{1,0:T(8,128)(2,1)} collective-permute-done((bf16[288,768]{1,0:T(8,128)(2,1)}, bf16[288,768]{1,0:T(8,128)(2,1)}, u32[]{:S(2)}, u32[]{:S(2)}) %collective-permute-start.17) | collective-permute-done | bytes 442400 | tf_op jit(solution)/shard_map/ppermute | solution.py:92
  526.8 15.1 %collective-permute-done.30 = bf16[144,768]{1,0:T(8,128)(2,1)S(1)} collective-permute-done((bf16[144,768]{1,0:T(8,128)(2,1)S(1)}, bf16[144,768]{1,0:T(8,128)(2,1)S(1)}, u32[]{:S(2)}, u32[]{:S(2)}) %collective-permute-start.30) | collective-permute-done | bytes 221216 | tf_op jit(solution)/shard_map/ppermute | solution.py:92
  542.0 9.4 %collective-permute-done.18 = bf16[144,768]{1,0:T(8,128)(2,1)S(1)} collective-permute-done((bf16[144,768]{1,0:T(8,128)(2,1)S(1)}, bf16[144,768]{1,0:T(8,128)(2,1)S(1)}, u32[]{:S(2)}, u32[]{:S(2)}) %collective-permute-start.18) | collective-permute-done | bytes 221216 | tf_op jit(solution)/shard_map/ppermute | solution.py:92
  568.4 7.1 %collective-permute-done.44 = bf16[144,1536]{1,0:T(8,128)(2,1)S(1)} collective-permute-done((bf16[144,1536]{1,0:T(8,128)(2,1)S(1)}, bf16[144,1536]{1,0:T(8,128)(2,1)S(1)}, u32[]{:S(2)}, u32[]{:S(2)}) %collective-permute-start.44) | collective-permute-done | bytes 442400 | tf_op jit(solution)/shard_map/ppermute | solution.py:92
  576.0 9.0 %collective-permute-done.32 = bf16[288,768]{1,0:T(8,128)(2,1)S(1)} collective-permute-done((bf16[288,768]{1,0:T(8,128)(2,1)S(1)}, bf16[288,768]{1,0:T(8,128)(2,1)S(1)}, u32[]{:S(2)}, u32[]{:S(2)}) %collective-permute-start.32) | collective-permute-done | bytes 442400 | tf_op jit(solution)/shard_map/ppermute | solution.py:92
  585.5 7.0 %collective-permute-done.20 = bf16[288,768]{1,0:T(8,128)(2,1)S(1)} collective-permute-done((bf16[288,768]{1,0:T(8,128)(2,1)S(1)}, bf16[288,768]{1,0:T(8,128)(2,1)S(1)}, u32[]{:S(2)}, u32[]{:S(2)}) %collective-permute-start.20) | collective-permute-done | bytes 442400 | tf_op jit(solution)/shard_map/ppermute | solution.py:92
  598.7 18.6 %collective-permute-done.33 = bf16[576,768]{1,0:T(8,128)(2,1)S(1)} collective-permute-done((bf16[576,768]{1,0:T(8,128)(2,1)S(1)}, bf16[576,768]{1,0:T(8,128)(2,1)S(1)}, u32[]{:S(2)}, u32[]{:S(2)}) %collective-permute-start.33) | collective-permute-done | bytes 884768 | tf_op jit(solution)/shard_map/ppermute | solution.py:92
  623.1 8.2 %collective-permute-done.21 = bf16[576,768]{1,0:T(8,128)(2,1)S(1)} collective-permute-done((bf16[576,768]{1,0:T(8,128)(2,1)S(1)}, bf16[576,768]{1,0:T(8,128)(2,1)S(1)}, u32[]{:S(2)}, u32[]{:S(2)}) %collective-permute-start.21) | collective-permute-done | bytes 884768 | tf_op jit(solution)/shard_map/ppermute | solution.py:92
  (660 shorter events, 397.4 us)
Async XLA Ops:
  298.8 163.7 %collective-permute-start.40 = (bf16[288,1536]{1,0:T(8,128)(2,1)}, bf16[288,1536]{1,0:T(8,128)(2,1)}, u32[]{:S(2)}, u32[]{:S(2)}) collective-permute-start(bf16[288,1536]{1,0:T(8,128)(2,1)} %dynamic-slice_convert_fusion), channel_id=1, source_target_pairs={{0,4},{4,0},{8,12},{12,8},{16,20},{20,16},{24,28},{28,24},{1,5},{5... | collective-permute-start | bytes 2654216 | tf_op jit(solution)/shard_map/ppermute | solution.py:92
  302.2 32.3 %collective-permute-start.46 = (bf16[96,1536]{1,0:T(8,128)(2,1)}, bf16[96,1536]{1,0:T(8,128)(2,1)}, u32[]{:S(2)}, u32[]{:S(2)}) collective-permute-start(bf16[96,1536]{1,0:T(8,128)(2,1)} %dynamic-slice_convert_fusion.8), channel_id=1, source_target_pairs={{0,8},{4,12},{8,0},{12,4},{16,24},{20,28},{24,16},{28,20},{1,9},{5... | collective-permute-start | bytes 884744 | tf_op jit(solution)/shard_map/ppermute | solution.py:92
  325.7 134.5 %collective-permute-start.28 = (bf16[576,768]{1,0:T(8,128)(2,1)}, bf16[576,768]{1,0:T(8,128)(2,1)}, u32[]{:S(2)}, u32[]{:S(2)}) collective-permute-start(bf16[576,768]{1,0:T(8,128)(2,1)} %dynamic-slice_convert_fusion.1), channel_id=1, source_target_pairs={{0,4},{4,0},{8,12},{12,8},{16,20},{20,16},{24,28},{28,24},{1,5},{5... | collective-permute-start | bytes 2654216 | tf_op jit(solution)/shard_map/ppermute | solution.py:92
  331.7 135.3 %collective-permute-start.16 = (bf16[576,768]{1,0:T(8,128)(2,1)}, bf16[576,768]{1,0:T(8,128)(2,1)}, u32[]{:S(2)}, u32[]{:S(2)}) collective-permute-start(bf16[576,768]{1,0:T(8,128)(2,1)} %dynamic-slice_convert_fusion.2), channel_id=1, source_target_pairs={{0,4},{4,0},{8,12},{12,8},{16,20},{20,16},{24,28},{28,24},{1,5},{5... | collective-permute-start | bytes 2654216 | tf_op jit(solution)/shard_map/ppermute | solution.py:92
  337.9 213.6 %collective-permute-start.2 = (bf16[2,256,1536]{2,1,0:T(8,128)(2,1)}, bf16[2,256,1536]{2,1,0:T(8,128)(2,1)}, u32[]{:S(2)}, u32[]{:S(2)}) collective-permute-start(bf16[2,256,1536]{2,1,0:T(8,128)(2,1)} %dynamic-slice_bitcast_fusion.1), channel_id=1, source_target_pairs={{0,1},{1,0},{2,3},{3,2},{4,5},{5,4},{6,7},{7,6},{8,9},{9,8},{10,11... | collective-permute-start | bytes 4718600 | tf_op jit(solution)/shard_map/ppermute | solution.py:92
  460.2 105.9 %collective-permute-start.6 = (bf16[2,256,1536]{2,1,0:T(8,128)(2,1)}, bf16[2,256,1536]{2,1,0:T(8,128)(2,1)}, u32[]{:S(2)}, u32[]{:S(2)}) collective-permute-start(bf16[2,256,1536]{2,1,0:T(8,128)(2,1)} %dynamic-slice_bitcast_fusion), channel_id=1, source_target_pairs={{0,1},{1,0},{2,3},{3,2},{4,5},{5,4},{6,7},{7,6},{8,9},{9,8},{10,11... | collective-permute-start | bytes 4718600 | tf_op jit(solution)/shard_map/ppermute | solution.py:92
  460.3 18.3 %collective-permute-start.51 = (bf16[96,1536]{1,0:T(8,128)(2,1)S(1)}, bf16[96,1536]{1,0:T(8,128)(2,1)S(1)}, u32[]{:S(2)}, u32[]{:S(2)}) collective-permute-start(bf16[96,1536]{1,0:T(8,128)(2,1)S(1)} %pad_maximum_fusion.11), channel_id=1, source_target_pairs={{0,8},{4,12},{8,0},{12,4},{16,24},{20,28},{24,16},{28,20},{1,9},{5... | collective-permute-start | bytes 884744 | tf_op jit(solution)/shard_map/ppermute | solution.py:92
  462.6 18.7 %collective-permute-start.39 = (bf16[192,768]{1,0:T(8,128)(2,1)S(1)}, bf16[192,768]{1,0:T(8,128)(2,1)S(1)}, u32[]{:S(2)}, u32[]{:S(2)}) collective-permute-start(bf16[192,768]{1,0:T(8,128)(2,1)S(1)} %pad_maximum_fusion.10), channel_id=1, source_target_pairs={{0,8},{4,12},{8,0},{12,4},{16,24},{20,28},{24,16},{28,20},{1,9},{5... | collective-permute-start | bytes 884744 | tf_op jit(solution)/shard_map/ppermute | solution.py:92
  478.5 22.0 %collective-permute-start.41 = (bf16[144,1536]{1,0:T(8,128)(2,1)}, bf16[144,1536]{1,0:T(8,128)(2,1)}, u32[]{:S(2)}, u32[]{:S(2)}) collective-permute-start(bf16[144,1536]{1,0:T(8,128)(2,1)} %dynamic-slice_convert_fusion.5), channel_id=1, source_target_pairs={{0,8},{4,12},{8,0},{12,4},{16,24},{20,28},{24,16},{28,20},{1,9},{5... | collective-permute-start | bytes 1327112 | tf_op jit(solution)/shard_map/ppermute | solution.py:92
  481.3 30.6 %collective-permute-start.29 = (bf16[288,768]{1,0:T(8,128)(2,1)}, bf16[288,768]{1,0:T(8,128)(2,1)}, u32[]{:S(2)}, u32[]{:S(2)}) collective-permute-start(bf16[288,768]{1,0:T(8,128)(2,1)} %dynamic-slice_convert_fusion.6), channel_id=1, source_target_pairs={{0,8},{4,12},{8,0},{12,4},{16,24},{20,28},{24,16},{28,20},{1,9},{5... | collective-permute-start | bytes 1327112 | tf_op jit(solution)/shard_map/ppermute | solution.py:92
  493.7 28.8 %collective-permute-start.17 = (bf16[288,768]{1,0:T(8,128)(2,1)}, bf16[288,768]{1,0:T(8,128)(2,1)}, u32[]{:S(2)}, u32[]{:S(2)}) collective-permute-start(bf16[288,768]{1,0:T(8,128)(2,1)} %dynamic-slice_convert_fusion.7), channel_id=1, source_target_pairs={{0,8},{4,12},{8,0},{12,4},{16,24},{20,28},{24,16},{28,20},{1,9},{5... | collective-permute-start | bytes 1327112 | tf_op jit(solution)/shard_map/ppermute | solution.py:92
  502.4 21.8 %collective-permute-start.42 = (bf16[72,1536]{1,0:T(8,128)(2,1)S(1)}, bf16[72,1536]{1,0:T(8,128)(2,1)S(1)}, u32[]{:S(2)}, u32[]{:S(2)}) collective-permute-start(bf16[72,1536]{1,0:T(8,128)(2,1)S(1)} %dynamic-slice_convert_fusion.12), channel_id=1, source_target_pairs={{0,16},{4,20},{8,24},{12,28},{16,0},{20,4},{24,8},{28,12},{1,17},{... | collective-permute-start | bytes 663560 | tf_op jit(solution)/shard_map/ppermute | solution.py:92
  513.0 28.9 %collective-permute-start.30 = (bf16[144,768]{1,0:T(8,128)(2,1)S(1)}, bf16[144,768]{1,0:T(8,128)(2,1)S(1)}, u32[]{:S(2)}, u32[]{:S(2)}) collective-permute-start(bf16[144,768]{1,0:T(8,128)(2,1)S(1)} %dynamic-slice_convert_fusion.13), channel_id=1, source_target_pairs={{0,16},{4,20},{8,24},{12,28},{16,0},{20,4},{24,8},{28,12},{1,17},{... | collective-permute-start | bytes 663560 | tf_op jit(solution)/shard_map/ppermute | solution.py:92
  523.7 27.7 %collective-permute-start.18 = (bf16[144,768]{1,0:T(8,128)(2,1)S(1)}, bf16[144,768]{1,0:T(8,128)(2,1)S(1)}, u32[]{:S(2)}, u32[]{:S(2)}) collective-permute-start(bf16[144,768]{1,0:T(8,128)(2,1)S(1)} %dynamic-slice_convert_fusion.14), channel_id=1, source_target_pairs={{0,16},{4,20},{8,24},{12,28},{16,0},{20,4},{24,8},{28,12},{1,17},{... | collective-permute-start | bytes 663560 | tf_op jit(solution)/shard_map/ppermute | solution.py:92
  524.3 34.3 %collective-permute-start.43 = (bf16[72,1536]{1,0:T(8,128)(2,1)S(1)}, bf16[72,1536]{1,0:T(8,128)(2,1)S(1)}, u32[]{:S(2)}, u32[]{:S(2)}) collective-permute-start(bf16[72,1536]{1,0:T(8,128)(2,1)S(1)} %add_convert_fusion.1), channel_id=1, source_target_pairs={{0,16},{4,20},{8,24},{12,28},{16,0},{20,4},{24,8},{28,12},{1,17},{... | collective-permute-start | bytes 663560 | tf_op jit(solution)/shard_map/ppermute | solution.py:92
  541.9 21.4 %collective-permute-start.31 = (bf16[144,768]{1,0:T(8,128)(2,1)S(1)}, bf16[144,768]{1,0:T(8,128)(2,1)S(1)}, u32[]{:S(2)}, u32[]{:S(2)}) collective-permute-start(bf16[144,768]{1,0:T(8,128)(2,1)S(1)} %add_convert_fusion.2), channel_id=1, source_target_pairs={{0,16},{4,20},{8,24},{12,28},{16,0},{20,4},{24,8},{28,12},{1,17},{... | collective-permute-start | bytes 663560 | tf_op jit(solution)/shard_map/ppermute | solution.py:92
  553.5 39.7 %collective-permute-start.3 = (bf16[256,1536]{1,0:T(8,128)(2,1)S(1)}, bf16[256,1536]{1,0:T(8,128)(2,1)S(1)}, u32[]{:S(2)}, u32[]{:S(2)}) collective-permute-start(bf16[256,1536]{1,0:T(8,128)(2,1)S(1)} %fusion.97), channel_id=1, source_target_pairs={{0,2},{1,3},{2,0},{3,1},{4,6},{5,7},{6,4},{7,5},{8,10},{9,11},{10,... | collective-permute-start | bytes 2359304 | tf_op jit(solution)/shard_map/ppermute | solution.py:92
  558.7 16.8 %collective-permute-start.44 = (bf16[144,1536]{1,0:T(8,128)(2,1)S(1)}, bf16[144,1536]{1,0:T(8,128)(2,1)S(1)}, u32[]{:S(2)}, u32[]{:S(2)}) collective-permute-start(bf16[144,1536]{1,0:T(8,128)(2,1)S(1)} %pad_maximum_fusion.8), channel_id=1, source_target_pairs={{0,8},{4,12},{8,0},{12,4},{16,24},{20,28},{24,16},{28,20},{1,9},{5... | collective-permute-start | bytes 1327112 | tf_op jit(solution)/shard_map/ppermute | solution.py:92
  563.4 21.6 %collective-permute-start.32 = (bf16[288,768]{1,0:T(8,128)(2,1)S(1)}, bf16[288,768]{1,0:T(8,128)(2,1)S(1)}, u32[]{:S(2)}, u32[]{:S(2)}) collective-permute-start(bf16[288,768]{1,0:T(8,128)(2,1)S(1)} %pad_maximum_fusion.7), channel_id=1, source_target_pairs={{0,8},{4,12},{8,0},{12,4},{16,24},{20,28},{24,16},{28,20},{1,9},{5... | collective-permute-start | bytes 1327112 | tf_op jit(solution)/shard_map/ppermute | solution.py:92
  566.1 26.4 %collective-permute-start.20 = (bf16[288,768]{1,0:T(8,128)(2,1)S(1)}, bf16[288,768]{1,0:T(8,128)(2,1)S(1)}, u32[]{:S(2)}, u32[]{:S(2)}) collective-permute-start(bf16[288,768]{1,0:T(8,128)(2,1)S(1)} %pad_maximum_fusion.6), channel_id=1, source_target_pairs={{0,8},{4,12},{8,0},{12,4},{16,24},{20,28},{24,16},{28,20},{1,9},{5... | collective-permute-start | bytes 1327112 | tf_op jit(solution)/shard_map/ppermute | solution.py:92
  568.3 24.5 %collective-permute-start.7 = (bf16[256,1536]{1,0:T(8,128)(2,1)S(1)}, bf16[256,1536]{1,0:T(8,128)(2,1)S(1)}, u32[]{:S(2)}, u32[]{:S(2)}) collective-permute-start(bf16[256,1536]{1,0:T(8,128)(2,1)S(1)} %fusion.98), channel_id=1, source_target_pairs={{0,2},{1,3},{2,0},{3,1},{4,6},{5,7},{6,4},{7,5},{8,10},{9,11},{10,... | collective-permute-start | bytes 2359304 | tf_op jit(solution)/shard_map/ppermute | solution.py:92
  575.8 22.6 %collective-permute-start.45 = (bf16[288,1536]{1,0:T(8,128)(2,1)S(1)}, bf16[288,1536]{1,0:T(8,128)(2,1)S(1)}, u32[]{:S(2)}, u32[]{:S(2)}) collective-permute-start(bf16[288,1536]{1,0:T(8,128)(2,1)S(1)} %pad_maximum_fusion.5), channel_id=1, source_target_pairs={{0,4},{4,0},{8,12},{12,8},{16,20},{20,16},{24,28},{28,24},{1,5},{5... | collective-permute-start | bytes 2654216 | tf_op jit(solution)/shard_map/ppermute | solution.py:92
  585.2 32.1 %collective-permute-start.33 = (bf16[576,768]{1,0:T(8,128)(2,1)S(1)}, bf16[576,768]{1,0:T(8,128)(2,1)S(1)}, u32[]{:S(2)}, u32[]{:S(2)}) collective-permute-start(bf16[576,768]{1,0:T(8,128)(2,1)S(1)} %pad_maximum_fusion.4), channel_id=1, source_target_pairs={{0,4},{4,0},{8,12},{12,8},{16,20},{20,16},{24,28},{28,24},{1,5},{5... | collective-permute-start | bytes 2654216 | tf_op jit(solution)/shard_map/ppermute | solution.py:92
  592.7 38.7 %collective-permute-start.21 = (bf16[576,768]{1,0:T(8,128)(2,1)S(1)}, bf16[576,768]{1,0:T(8,128)(2,1)S(1)}, u32[]{:S(2)}, u32[]{:S(2)}) collective-permute-start(bf16[576,768]{1,0:T(8,128)(2,1)S(1)} %pad_maximum_fusion.3), channel_id=1, source_target_pairs={{0,4},{4,0},{8,12},{12,8},{16,20},{20,16},{24,28},{28,24},{1,5},{5... | collective-permute-start | bytes 2654216 | tf_op jit(solution)/shard_map/ppermute | solution.py:92
  (169 other events, 1588.1 us)

commit v2 on v1

v2 whole, which is shorter than its diff:
```python
import functools
import math

import jax
import jax.numpy as jnp
from jax import lax
from jax.experimental import pallas as pl
from jax.experimental.pallas import tpu as pltpu
from jax.sharding import PartitionSpec as P

STATE = 128
CONV = 4
BLOCK = 256
PIECE = 128
LANES = 128
EPS = 1e-05
HIGH = lax.Precision.HIGHEST
LOG2E = math.log2(math.e)
BF16 = jnp.bfloat16
F32 = jnp.float32


def dot(left, right):
    return jnp.dot(left, right, preferred_element_type=F32)


def dot_last(left, right):
    return lax.dot_general(left, right, (((1,), (1,)), ((), ())), preferred_element_type=F32)


def dot_first(left, right):
    return lax.dot_general(left, right, (((0,), (0,)), ((), ())), preferred_element_type=F32)


def two_terms(array):
    upper = array.astype(BF16)
    return upper, (array - upper.astype(F32)).astype(BF16)


def sigmoid(array):
    return 0.5 * jnp.tanh(0.5 * array) + 0.5


def spread_heads(array, heads_twice):
    upper, rest = two_terms(array)
    return dot(jnp.concatenate([upper, rest], axis=1), heads_twice)


def sum_heads(array, heads):
    upper, rest = two_terms(array)
    return dot_last(upper, heads) + dot_last(rest, heads)


def triangle(rows, columns):
    return rows >= columns


def forward_kernel(
    hidden_ref,
    cotan_ref,
    gain_ref,
    w_gate_ref,
    w_value_ref,
    w_bc_ref,
    w_dt_ref,
    w_out_ref,
    channel_ref,
    conv_bc_ref,
    head_ref,
    side_ref,
    seg_row_ref,
    heads_ref,
    normed_ref,
    gate_ref,
    scan_ref,
    value_ref,
    slope_ref,
    inner_ref,
    grad_ref,
    step_ref,
    cum_ref,
    bc_ref,
    state_ref,
    enter_ref,
    sums_ref,
    tail_x,
    tail_bc,
    carried,
):
    block = pl.program_id(0)

    @pl.when(block == 0)
    def _():
        tail_x[0:8, :] = jnp.zeros((8, tail_x.shape[1]), F32)
        tail_bc[0:8, :] = jnp.zeros((8, tail_bc.shape[1]), F32)
        carried[...] = jnp.zeros(carried.shape, F32)

    hidden = hidden_ref[...].astype(F32)
    inv_rms = lax.rsqrt(jnp.mean(hidden * hidden, axis=-1, keepdims=True) + EPS)
    normed = (hidden * inv_rms * gain_ref[0:1, :]).astype(BF16)
    normed_ref[...] = normed
    tail_x[8:, :] = dot(normed, w_value_ref[...])
    tail_bc[8:, :] = dot(normed, w_bc_ref[...])
    step_in = dot(normed, w_dt_ref[...]) + head_ref[0:1, :]
    step_ref[...] = step_in
    step = jnp.maximum(step_in, 0.0) + jnp.log1p(jnp.exp(-jnp.abs(step_in)))
    rate = head_ref[1:2, :] * step * LOG2E
    gate_ref[...] = dot(normed, w_gate_ref[...])
    grad_ref[...] = dot_last(cotan_ref[...], w_out_ref[...])
    masks = [None] + [side_ref[:, k : k + 1] for k in range(1, CONV)]

    def conv(tail, taps_ref, lanes):
        result = taps_ref[CONV : CONV + 1, lanes] + taps_ref[CONV - 1 : CONV, lanes] * tail[8:, lanes]
        for k in range(1, CONV):
            shifted = tail[8 - k : 8 - k + BLOCK, lanes]
            result = result + taps_ref[CONV - 1 - k : CONV - k, lanes] * shifted * masks[k]
        return result

    channels = tail_x.shape[1]
    for at in range(0, channels, LANES):
        lanes = slice(at, at + LANES)
        before = conv(tail_x, channel_ref, lanes)
        half = sigmoid(before)
        value_ref[:, lanes] = before * half
        slope_ref[:, lanes] = half * (1.0 + before * (1.0 - half))
        inner_ref[:, lanes] = tail_x[8:, lanes]
    for at in range(0, 2 * STATE, LANES):
        lanes = slice(at, at + LANES)
        before = conv(tail_bc, conv_bc_ref, lanes)
        bc_ref[:, lanes] = (before * sigmoid(before)).astype(BF16)
        state_ref[:, lanes] = tail_bc[8:, lanes]
    tail_x[0:8, :] = tail_x[BLOCK:, :]
    tail_bc[0:8, :] = tail_bc[BLOCK:, :]

    row_at = lax.broadcasted_iota(jnp.int32, (PIECE, PIECE), 0)
    col_at = lax.broadcasted_iota(jnp.int32, (PIECE, PIECE), 1)
    lower = (row_at >= col_at).astype(F32)
    first_half = lax.broadcasted_iota(jnp.int32, (PIECE, LANES), 1) < LANES // 2
    heads = heads_ref[...]
    heads_twice = jnp.concatenate([heads, heads], axis=0)
    for piece in range(BLOCK // PIECE):
        rows = slice(piece * PIECE, (piece + 1) * PIECE)
        cum = jnp.dot(lower, rate[rows], precision=HIGH, preferred_element_type=F32)
        cum_ref[rows, :] = cum
        cum_t = cum.T
        same = (side_ref[rows, 0:1] == seg_row_ref[0:1, rows]) & (row_at >= col_at)
        bias = jnp.where(same, 0.0, -1e30)
        reach = jnp.exp2(cum) * side_ref[rows, 4:5]
        tail = jnp.exp2(cum[PIECE - 1 : PIECE, :] - cum) * side_ref[rows, 5:6]
        wide = spread_heads(jnp.concatenate([step[rows], reach, tail], axis=0), heads_twice)
        b_low = bc_ref[rows, 0:STATE]
        c_low = bc_ref[rows, STATE : 2 * STATE]
        scores = dot_last(c_low, b_low)
        enter = carried[...].astype(BF16)
        enter_ref[piece] = enter
        for pair in range(channels // LANES):
            lanes = slice(pair * LANES, (pair + 1) * LANES)
            values = value_ref[rows, lanes]
            scaled = wide[0:PIECE, lanes] * values
            low = scaled.astype(BF16)
            weights = []
            for head in (2 * pair, 2 * pair + 1):
                gaps = (cum[:, head : head + 1] - cum_t[head : head + 1, :]) + bias
                weights.append((scores * jnp.exp2(gaps)).astype(BF16))
            zero = jnp.zeros_like(low)
            both = jnp.concatenate(
                [jnp.where(first_half, low, zero), jnp.where(first_half, zero, low)], axis=0
            )
            out = dot(jnp.concatenate(weights, axis=1), both)
            out = out + dot(c_low, enter[:, lanes]) * wide[PIECE : 2 * PIECE, lanes]
            scan_ref[rows, lanes] = out + channel_ref[5:6, lanes] * values
            tailed = (wide[2 * PIECE :, lanes] * scaled).astype(BF16)
            kept = wide[2 * PIECE - 1 : 2 * PIECE, lanes]
            carried[:, lanes] = kept * carried[:, lanes] + dot_first(b_low, tailed)

    squares = jnp.zeros((8, BLOCK), F32)
    crosses = jnp.zeros((8, BLOCK), F32)
    ones = jnp.ones((8, LANES), BF16)
    square_part = jnp.zeros((BLOCK, LANES), F32)
    cross_part = jnp.zeros((BLOCK, LANES), F32)
    for at in range(0, channels, LANES):
        lanes = slice(at, at + LANES)
        gate = gate_ref[:, lanes]
        mixed = scan_ref[:, lanes] * (gate * sigmoid(gate))
        square_part = square_part + mixed * mixed
        cross_part = cross_part + mixed * (grad_ref[:, lanes] * channel_ref[6:7, lanes])
    upper, rest = two_terms(square_part)
    squares = dot_last(ones, upper) + dot_last(ones, rest)
    upper, rest = two_terms(cross_part)
    crosses = dot_last(ones, upper) + dot_last(ones, rest)
    is_first = lax.broadcasted_iota(jnp.int32, (8, BLOCK), 0) == 0
    sums_ref[...] = jnp.where(is_first, squares, crosses)


def gate_kernel(
    gate_ref,
    scan_ref,
    grad_ref,
    sums_ref,
    channel_ref,
    gated_ref,
    gate_low_ref,
    dscan_ref,
    gain_ref,
):
    @pl.when(pl.program_id(0) == 0)
    def _():
        gain_ref[...] = jnp.zeros(gain_ref.shape, F32)

    row_at = lax.broadcasted_iota(jnp.int32, (8, LANES), 0)

    def column(which):
        pick = (row_at == which).astype(F32)
        return lax.dot_general(
            sums_ref[...], pick, (((0,), (0,)), ((), ())), precision=HIGH, preferred_element_type=F32
        )

    channels = gate_ref.shape[1]
    inv_gate = lax.rsqrt(column(0) + EPS)
    pull = inv_gate * inv_gate * column(1)
    for at in range(0, channels, LANES):
        lanes = slice(at, at + LANES)
        gate = gate_ref[:, lanes]
        scan = scan_ref[:, lanes]
        half = sigmoid(gate)
        act = gate * half
        mixed = scan * act
        gain = channel_ref[6:7, lanes]
        normal = mixed * inv_gate
        gated_ref[:, lanes] = (normal * gain).astype(BF16)
        grad = grad_ref[:, lanes]
        gain_ref[:, lanes] += jnp.sum((grad * normal).reshape(-1, 8, LANES), axis=0)
        mixed_grad = inv_gate * (grad * gain - mixed * pull)
        gate_low_ref[:, lanes] = (mixed_grad * scan * (half * (1.0 + gate * (1.0 - half)))).astype(BF16)
        dscan_ref[:, lanes] = (mixed_grad * act).astype(BF16)


def backward_kernel(
    dscan_ref,
    scan_ref,
    value_ref,
    slope_ref,
    inner_ref,
    step_ref,
    cum_ref,
    bc_ref,
    enter_ref,
    channel_ref,
    head_ref,
    side_ref,
    seg_row_ref,
    heads_ref,
    inner_low_ref,
    step_low_ref,
    state_part_ref,
    channel_grad_ref,
    head_grad_ref,
    later,
    leaving,
):
    @pl.when(pl.program_id(0) == 0)
    def _():
        later[PIECE:, :] = jnp.zeros((8, later.shape[1]), F32)
        leaving[...] = jnp.zeros(leaving.shape, F32)
        channel_grad_ref[...] = jnp.zeros(channel_grad_ref.shape, F32)
        head_grad_ref[...] = jnp.zeros(head_grad_ref.shape, F32)

    channels = inner_ref.shape[1]
    row_at = lax.broadcasted_iota(jnp.int32, (PIECE, PIECE), 0)
    col_at = lax.broadcasted_iota(jnp.int32, (PIECE, PIECE), 1)
    upper_ones = (row_at <= col_at).astype(F32)
    first_half = lax.broadcasted_iota(jnp.int32, (PIECE, LANES), 1) < LANES // 2
    heads = heads_ref[...]
    heads_twice = jnp.concatenate([heads, heads], axis=0)
    step_in = step_ref[...]
    step = jnp.maximum(step_in, 0.0) + jnp.log1p(jnp.exp(-jnp.abs(step_in)))
    cum = cum_ref[...]
    cum_t = cum.T
    same = (side_ref[:, 0:1] == seg_row_ref[0:1, :]) & (row_at <= col_at)
    bias = jnp.where(same, 0.0, -1e30)
    reach = jnp.exp2(cum) * side_ref[:, 4:5]
    tail = jnp.exp2(cum[PIECE - 1 : PIECE, :] - cum) * side_ref[:, 5:6]
    wide = spread_heads(jnp.concatenate([step, reach, tail], axis=0), heads_twice)
    b_low = bc_ref[:, 0:STATE]
    c_low = bc_ref[:, STATE : 2 * STATE]
    scores = dot_last(b_low, c_low)
    score_grad = jnp.zeros((PIECE, PIECE), F32)
    b_grad = jnp.zeros((PIECE, STATE), F32)
    c_grad = jnp.zeros((PIECE, STATE), F32)
    row_sum = jnp.zeros((PIECE, LANES), F32)
    value_sum = jnp.zeros((PIECE, LANES), F32)
    last_sum = jnp.zeros((8, LANES), F32)
    masks = [None] + [side_ref[:, 5 + k : 6 + k] for k in range(1, CONV)]
    for pair in range(channels // LANES):
        lanes = slice(pair * LANES, (pair + 1) * LANES)
        own_heads = heads[:, lanes]
        values = value_ref[:, lanes]
        dy_low = dscan_ref[:, lanes]
        dy = dy_low.astype(F32)
        wide_step = wide[0:PIECE, lanes]
        wide_reach = wide[PIECE : 2 * PIECE, lanes]
        wide_tail = wide[2 * PIECE :, lanes]
        low = (wide_step * values).astype(BF16)
        low_wide = low.astype(F32)
        leave = leaving[:, lanes]
        leave_low = leave.astype(BF16)
        enter = enter_ref[0, :, lanes]
        reached = (wide_reach * dy).astype(BF16)
        tailed = (wide_tail * low_wide).astype(BF16)
        c_grad = c_grad + dot_last(reached, enter)
        b_grad = b_grad + dot_last(tailed, leave_low)
        from_state = wide_tail * dot(b_low, leave_low)
        zero = jnp.zeros_like(low)
        dy_first = jnp.where(first_half, dy_low, zero)
        dy_second = jnp.where(first_half, zero, dy_low)
        weights = []
        for head, own in ((2 * pair, dy_first), (2 * pair + 1, dy_second)):
            gaps = (cum_t[head : head + 1, :] - cum[:, head : head + 1]) + bias
            decay = jnp.exp2(gaps)
            weights.append((scores * decay).astype(BF16))
            score_grad = score_grad + dot_last(low, own) * decay
        dx = dot(jnp.concatenate(weights, axis=1), jnp.concatenate([dy_first, dy_second], axis=0))
        dx = dx + from_state
        out = scan_ref[:, lanes] - channel_ref[5:6, lanes] * values
        row_sum = row_sum + sum_heads(dy * out - low_wide * dx, own_heads)
        value_sum = value_sum + sum_heads(values * dx, own_heads)
        kept = wide[2 * PIECE - 1 : 2 * PIECE, lanes]
        last = jnp.sum(low_wide * from_state, axis=0, keepdims=True) + kept * jnp.sum(
            enter.astype(F32) * leave, axis=0, keepdims=True
        )
        last_sum = last_sum + sum_heads(jnp.broadcast_to(last, (8, LANES)), own_heads)
        leaving[:, lanes] = kept * leave + dot_first(c_low, reached)
        dvalue = wide_step * dx + channel_ref[5:6, lanes] * dy
        dbefore = dvalue * slope_ref[:, lanes]
        later[0:PIECE, lanes] = dbefore
        inner = inner_ref[:, lanes]
        inner_grad = channel_ref[CONV - 1 : CONV, lanes] * dbefore
        channel_grad_ref[CONV - 1 : CONV, lanes] += jnp.sum(inner * dbefore, axis=0, keepdims=True)
        channel_grad_ref[CONV : CONV + 1, lanes] += jnp.sum(dbefore, axis=0, keepdims=True)
        channel_grad_ref[CONV + 1 : CONV + 2, lanes] += jnp.sum(dy * values, axis=0, keepdims=True)
        for k in range(1, CONV):
            shifted = later[k : k + PIECE, lanes] * masks[k]
            inner_grad = inner_grad + channel_ref[CONV - 1 - k : CONV - k, lanes] * shifted
            channel_grad_ref[CONV - 1 - k : CONV - k, lanes] += jnp.sum(
                inner * shifted, axis=0, keepdims=True
            )
        inner_low_ref[:, lanes] = inner_grad.astype(BF16)
    later[PIECE:, :] = later[0:8, :]
    grad_low = score_grad.astype(BF16)
    state_part_ref[:, 0:STATE] = (b_grad + dot(grad_low, c_low)).astype(BF16)
    state_part_ref[:, STATE:] = (c_grad + dot_first(grad_low, b_low)).astype(BF16)
    rate_grad = (
        jnp.dot(upper_ones, row_sum, precision=HIGH, preferred_element_type=F32) + last_sum[0:1, :]
    )
    coefficient = head_ref[1:2, :]
    step_grad = (value_sum + coefficient * rate_grad) / (1.0 + jnp.exp(-step_in))
    step_low_ref[...] = step_grad.astype(BF16)
    head_grad_ref[0:1, :] += jnp.sum(step_grad, axis=0, keepdims=True)
    head_grad_ref[1:2, :] += jnp.sum(rate_grad * step, axis=0, keepdims=True) * coefficient


def whole(shape):
    return pl.BlockSpec(shape, lambda i: (0,) * len(shape), pipeline_mode=pl.Buffered(1))


def run_forward(hidden_in, cotangent, gain, weights, tables, side, doc_row):
    rows, width = hidden_in.shape
    w_gate, w_value, w_bc, w_dt, w_out = weights
    channel_table, conv_table, head_table, heads = tables
    channels = w_gate.shape[1]
    states = w_bc.shape[1]

    def block(columns):
        return pl.BlockSpec((BLOCK, columns), lambda i: (i, 0))

    def out(columns, kind=F32):
        return jax.ShapeDtypeStruct((rows, columns), kind)

    per_block = BLOCK // PIECE
    return pl.pallas_call(
        forward_kernel,
        grid=(rows // BLOCK,),
        in_specs=[
            block(width),
            block(width),
            whole(gain.shape),
            whole(w_gate.shape),
            whole(w_value.shape),
            whole(w_bc.shape),
            whole(w_dt.shape),
            whole(w_out.shape),
            whole(channel_table.shape),
            whole(conv_table.shape),
            whole(head_table.shape),
            block(LANES),
            pl.BlockSpec((8, BLOCK), lambda i: (0, i)),
            whole(heads.shape),
        ],
        out_specs=[
            block(width),
            block(channels),
            block(channels),
            block(channels),
            block(channels),
            block(channels),
            block(channels),
            block(LANES),
            block(LANES),
            block(states),
            block(states),
            pl.BlockSpec((per_block, STATE, channels), lambda i: (i, 0, 0)),
            pl.BlockSpec((8, BLOCK), lambda i: (0, i)),
        ],
        out_shape=[
            out(width, BF16),
            out(channels),
            out(channels),
            out(channels),
            out(channels),
            out(channels),
            out(channels),
            out(LANES),
            out(LANES),
            out(states, BF16),
            out(states),
            jax.ShapeDtypeStruct((rows // PIECE, STATE, channels), BF16),
            jax.ShapeDtypeStruct((8, rows), F32),
        ],
        scratch_shapes=[
            pltpu.VMEM((BLOCK + 8, channels), F32),
            pltpu.VMEM((BLOCK + 8, states), F32),
            pltpu.VMEM((STATE, channels), F32),
        ],
        compiler_params=pltpu.CompilerParams(vmem_limit_bytes=56 << 20),
        name="forward",
    )(
        hidden_in,
        cotangent,
        gain,
        w_gate,
        w_value,
        w_bc,
        w_dt,
        w_out,
        channel_table,
        conv_table,
        head_table,
        side,
        doc_row,
        heads,
    )


def run_gate(gate_pre, scan, grad, sums, channel_table):
    rows, channels = gate_pre.shape
    block = pl.BlockSpec((BLOCK, channels), lambda i: (i, 0))
    low = jax.ShapeDtypeStruct((rows, channels), BF16)
    return pl.pallas_call(
        gate_kernel,
        grid=(rows // BLOCK,),
        in_specs=[
            block,
            block,
            block,
            pl.BlockSpec((8, BLOCK), lambda i: (0, i)),
            whole(channel_table.shape),
        ],
        out_specs=[block, block, block, whole((8, channels))],
        out_shape=[low, low, low, jax.ShapeDtypeStruct((8, channels), F32)],
        compiler_params=pltpu.CompilerParams(vmem_limit_bytes=32 << 20),
        name="gate",
    )(gate_pre, scan, grad, sums, channel_table)


def run_backward(dscan, scan, values, slope, inner, step_in, cum, bc_low, enter, tables, side, doc_row):
    rows, channels = scan.shape
    channel_table, _, head_table, heads = tables
    count = rows // PIECE
    states = bc_low.shape[1]

    def block(columns):
        return pl.BlockSpec((PIECE, columns), lambda i: (count - 1 - i, 0))

    return pl.pallas_call(
        backward_kernel,
        grid=(count,),
        in_specs=[
            block(channels),
            block(channels),
            block(channels),
            block(channels),
            block(channels),
            block(LANES),
            block(LANES),
            block(states),
            pl.BlockSpec((1, STATE, channels), lambda i: (count - 1 - i, 0, 0)),
            whole(channel_table.shape),
            whole(head_table.shape),
            block(LANES),
            pl.BlockSpec((8, PIECE), lambda i: (0, count - 1 - i)),
            whole(heads.shape),
        ],
        out_specs=[
            block(channels),
            block(LANES),
            block(states),
            whole((8, channels)),
            whole((8, LANES)),
        ],
        out_shape=[
            jax.ShapeDtypeStruct((rows, channels), BF16),
            jax.ShapeDtypeStruct((rows, LANES), BF16),
            jax.ShapeDtypeStruct((rows, states), BF16),
            jax.ShapeDtypeStruct((8, channels), F32),
            jax.ShapeDtypeStruct((8, LANES), F32),
        ],
        scratch_shapes=[
            pltpu.VMEM((PIECE + 8, channels), F32),
            pltpu.VMEM((STATE, channels), F32),
        ],
        compiler_params=pltpu.CompilerParams(vmem_limit_bytes=48 << 20),
        name="backward",
    )(
        dscan,
        scan,
        values,
        slope,
        inner,
        step_in,
        cum,
        bc_low,
        enter,
        channel_table,
        head_table,
        side,
        doc_row,
        heads,
    )


def document_tables(segments):
    seq_count, length = segments.shape
    documents = (segments + 64 * jnp.arange(seq_count, dtype=segments.dtype)[:, None]).reshape(-1)
    rows = documents.shape[0]
    padded = jnp.pad(documents, (CONV, CONV), constant_values=-1)
    columns = [documents.astype(F32)]
    for k in range(1, CONV):
        columns.append((padded[CONV - k : CONV - k + rows] == documents).astype(F32))
    pieces = documents.reshape(-1, PIECE)
    before = jnp.concatenate([jnp.full((1,), -1, documents.dtype), pieces[:-1, -1]])
    columns.append((pieces == before[:, None]).astype(F32).reshape(-1))
    columns.append((pieces == pieces[:, -1:]).astype(F32).reshape(-1))
    for k in range(1, CONV):
        columns.append((padded[CONV + k : CONV + k + rows] == documents).astype(F32))
    side = jnp.pad(jnp.stack(columns, axis=1), ((0, 0), (0, LANES - len(columns))))
    return side, jnp.broadcast_to(documents.astype(F32)[None], (8, rows))


def conv_silu(inputs, masks, weight, conv_bias):
    result = conv_bias + weight[CONV - 1] * inputs
    for k in range(1, CONV):
        shifted = jnp.pad(inputs, ((k, 0), (0, 0)))[:-k]
        result = result + weight[CONV - 1 - k] * shifted * masks[:, k : k + 1]
    return jax.nn.silu(result)


def swap(array, axis, bit):
    size = lax.axis_size(axis)
    return lax.ppermute(array, axis, [(source, source ^ bit) for source in range(size)])


def half_of(array, which):
    half = array.shape[0] // 2
    return lax.dynamic_slice_in_dim(array, which * half, half, 0)


def axis_bits(axis):
    size = lax.axis_size(axis)
    return [1 << place for place in range(size.bit_length() - 1)]


def sum_over(array, axis, order):
    place = lax.axis_index(axis)
    part = array
    for bit in order:
        mine = (place // bit) % 2
        sent = half_of(part, 1 - mine).astype(jnp.bfloat16)
        part = half_of(part, mine).astype(jnp.float32) + swap(sent, axis, bit).astype(jnp.float32)
    part = part.astype(jnp.bfloat16)
    for bit in reversed(order):
        mine = (place // bit) % 2
        other = swap(part, axis, bit)
        first = jnp.where(mine == 0, part, other)
        second = jnp.where(mine == 0, other, part)
        part = jnp.concatenate([first, second], axis=0)
    return part


def sum_rows(array):
    bits = axis_bits("dp")
    swapped = [bits[1], bits[0]] + bits[2:]
    cut = array.shape[0] * 3 // 4
    first = sum_over(array[:cut], "dp", bits)
    second = sum_over(array[cut:], "dp", swapped)
    return jnp.concatenate([first, second], axis=0).astype(jnp.float32)


def scatter_tensor(array, dim):
    part = array.astype(jnp.bfloat16)
    rank = lax.axis_index("tensor")
    bits = axis_bits("tensor")
    count = 1 << len(bits)
    shape = part.shape
    grouped = part.reshape(shape[:dim] + (2,) * len(bits) + (shape[dim] // count,) + shape[dim + 1 :])
    for place, bit in enumerate(bits):
        mine = (rank // bit) % 2
        axis_at = dim + len(bits) - 1 - place
        sent = lax.dynamic_index_in_dim(grouped, 1 - mine, axis_at, keepdims=False)
        kept = lax.dynamic_index_in_dim(grouped, mine, axis_at, keepdims=False)
        grouped = kept.astype(jnp.float32) + swap(sent.astype(jnp.bfloat16), "tensor", bit).astype(jnp.float32)
    return grouped


def sum_tensor(array):
    for bit in axis_bits("tensor"):
        array = array + swap(array, "tensor", bit)
    return array


def shards(
    hidden_in,
    pre_gain,
    w_gate,
    w_value,
    w_bc,
    w_dt,
    conv_x,
    conv_x_bias,
    conv_bc,
    conv_bc_bias,
    dt_bias,
    a_log,
    d_skip,
    gate_gain,
    w_out,
    cotangent,
    segments,
):
    row_count, width = hidden_in.shape
    channels = w_gate.shape[1]
    head_count = dt_bias.shape[0]
    head_width = channels // head_count
    ranks = lax.axis_size("tensor")
    my_rank = lax.axis_index("tensor")
    own_rows = row_count // ranks
    row_start = my_rank * own_rows
    pair_width = w_bc.shape[1] // ranks
    pair_start = my_rank * pair_width
    contract_first = (((0,), (0,)), ((), ()))
    contract_last = (((1,), (1,)), ((), ()))

    def pad_heads(array):
        return jnp.pad(array, [(0, 0)] * (array.ndim - 1) + [(0, LANES - head_count)])

    side, doc_row = document_tables(segments)
    channel_table = jnp.concatenate(
        [
            conv_x,
            conv_x_bias[None],
            jnp.repeat(d_skip, head_width)[None],
            gate_gain[None],
            jnp.zeros((1, channels), F32),
        ]
    )
    conv_table = jnp.concatenate([conv_bc, conv_bc_bias[None], jnp.zeros((3, w_bc.shape[1]), F32)])
    head_table = jnp.pad(
        jnp.stack([dt_bias, -jnp.exp(a_log)]), ((0, 6), (0, LANES - head_count))
    )
    heads = (
        lax.broadcasted_iota(jnp.int32, (LANES, channels), 1) // head_width
        == lax.broadcasted_iota(jnp.int32, (LANES, channels), 0)
    ).astype(BF16)
    tables = (channel_table, conv_table, head_table, heads)
    wide_dt = pad_heads(w_dt)
    (
        normed,
        gate_pre,
        scan,
        values,
        slope,
        inner_pre,
        gated_grad,
        step_in,
        cum,
        bc_low,
        state_pre,
        enter,
        sums,
    ) = run_forward(
        hidden_in,
        cotangent,
        jnp.broadcast_to(pre_gain[None], (8, width)),
        (w_gate, w_value, w_bc, wide_dt, w_out),
        tables,
        side,
        doc_row,
    )
    sums = sum_tensor(sums) / (channels * ranks)
    gated, gate_low, dscan, gain_rows = run_gate(gate_pre, scan, gated_grad, sums, channel_table)
    gate_gain_grad = jnp.sum(gain_rows, axis=0)
    w_out_sum = sum_rows(
        lax.dot_general(gated, cotangent, contract_first, preferred_element_type=F32)
    )
    w_gate_sum = sum_rows(
        lax.dot_general(normed, gate_low, contract_first, preferred_element_type=F32)
    )
    own_hidden = lax.dynamic_slice_in_dim(hidden_in, row_start, own_rows, 0).astype(F32)
    branch_own = scatter_tensor(jnp.dot(gated, w_out, preferred_element_type=F32), 0)
    block_out = (own_hidden + branch_own).astype(BF16)
    inner_low, step_low, state_part, channel_grads, head_grads = run_backward(
        dscan, scan, values, slope, inner_pre, step_in, cum, bc_low, enter, tables, side, doc_row
    )
    w_value_sum = sum_rows(
        lax.dot_general(normed, inner_low, contract_first, preferred_element_type=F32)
    )
    d_skip_grad = jnp.sum(channel_grads[CONV + 1].reshape(head_count, head_width), axis=-1)
    state_own = scatter_tensor(state_part, 1)
    _, state_back = jax.vjp(
        lambda inputs, weight, bias: conv_silu(inputs, side, weight, bias),
        lax.dynamic_slice_in_dim(state_pre, pair_start, pair_width, 1),
        lax.dynamic_slice_in_dim(conv_bc, pair_start, pair_width, 1),
        lax.dynamic_slice_in_dim(conv_bc_bias, pair_start, pair_width, 0),
    )
    pair_grad, pair_conv_grad, pair_bias_grad = state_back(state_own)
    pair_low = pair_grad.astype(BF16)
    pair_weight = lax.dynamic_slice_in_dim(w_bc, pair_start, pair_width, 1)
    total = lax.dot_general(gate_low, w_gate, contract_last, preferred_element_type=F32)
    total = total + lax.dot_general(
        inner_low, w_value, contract_last, preferred_element_type=F32
    )
    total = total + lax.dot_general(
        pair_low, pair_weight, contract_last, preferred_element_type=F32
    )
    total = total + lax.dot_general(step_low, wide_dt, contract_last, preferred_element_type=F32)
    normed_own = scatter_tensor(total, 0)
    hidden32 = hidden_in.astype(F32)
    inv_rms = lax.rsqrt(jnp.mean(hidden32 * hidden32, axis=-1, keepdims=True) + EPS)
    own_inv = lax.rsqrt(jnp.mean(own_hidden * own_hidden, axis=-1, keepdims=True) + EPS)
    own_cotan = lax.dynamic_slice_in_dim(cotangent, row_start, own_rows, 0).astype(F32)
    gain_scaled = normed_own * pre_gain
    own_dot = jnp.sum(gain_scaled * own_hidden, axis=-1, keepdims=True)
    hidden_grad = (
        own_cotan
        + own_inv * gain_scaled
        - own_hidden * (own_inv * own_inv * own_inv) * own_dot / width
    )
    w_bc_rows = lax.dot_general(pair_low, normed, contract_first, preferred_element_type=F32)
    w_dt_rows = lax.dot_general(step_low, normed, contract_first, preferred_element_type=F32)
    w_dt_rows = w_dt_rows[:16]
    spread = jnp.zeros((CONV + 1, w_bc.shape[1]), F32)
    spread = lax.dynamic_update_slice_in_dim(
        spread, jnp.concatenate([pair_conv_grad, pair_bias_grad[None]]), pair_start, 1
    )
    gain_part = jnp.sum(total * hidden32 * inv_rms, axis=0)
    shared = sum_tensor(jnp.concatenate([gain_part, spread.reshape(-1)]))
    small = jnp.concatenate(
        [
            channel_grads[: CONV + 1].reshape(-1),
            gate_gain_grad,
            shared,
            head_grads[0, :head_count],
            head_grads[1, :head_count],
            d_skip_grad,
        ]
    )
    small_rows = -(-small.shape[0] // width)
    dt_rows = w_dt_rows.shape[0]
    used_rows = pair_width + dt_rows + small_rows
    all_rows = -(-used_rows // 64) * 64
    packed = jnp.concatenate(
        [
            w_bc_rows,
            w_dt_rows,
            jnp.pad(small, (0, small_rows * width - small.shape[0])).reshape(small_rows, width),
            jnp.zeros((all_rows - used_rows, width), F32),
        ]
    )
    packed = sum_over(packed, "dp", axis_bits("dp")).astype(F32)
    w_bc_sum = packed[:pair_width].T
    w_dt_sum = packed[pair_width : pair_width + head_count].T
    small = packed[pair_width + dt_rows : used_rows].reshape(-1)
    pieces = []
    at = 0
    for length in (
        CONV * channels,
        channels,
        channels,
        width,
        CONV * w_bc.shape[1],
        w_bc.shape[1],
        head_count,
        head_count,
        head_count,
    ):
        pieces.append(small[at : at + length])
        at += length
    return (
        block_out,
        hidden_grad,
        pieces[3],
        w_gate_sum,
        w_value_sum,
        w_bc_sum,
        w_dt_sum,
        pieces[0].reshape(CONV, channels),
        pieces[1],
        pieces[4].reshape(CONV, -1),
        pieces[5],
        pieces[6],
        pieces[7],
        pieces[8],
        pieces[2],
        w_out_sum,
    )


def solution(mesh):
    in_specs = (
        P("dp", None),
        P(),
        P(None, "tensor"),
        P(None, "tensor"),
        P(),
        P(None, "tensor"),
        P(None, "tensor"),
        P("tensor"),
        P(),
        P(),
        P("tensor"),
        P("tensor"),
        P("tensor"),
        P("tensor"),
        P("tensor", None),
        P("dp", None),
        P("dp", None),
    )
    out_specs = (
        P(("dp", "tensor"), None),
        P(("dp", "tensor"), None),
        P(),
        P(None, "tensor"),
        P(None, "tensor"),
        P(None, "tensor"),
        P(None, "tensor"),
        P(None, "tensor"),
        P("tensor"),
        P(),
        P(),
        P("tensor"),
        P("tensor"),
        P("tensor"),
        P("tensor"),
        P("tensor", None),
    )
    return jax.shard_map(shards, mesh=mesh, in_specs=in_specs, out_specs=out_specs, check_vma=False)
```

time: 639 us -> 454 us (0.71)
  matrix products: 161 us -> 37.8 us
  other arithmetic: 111 us -> 37.9 us
  local copies, waits for them, and re-layouts: 116 us -> 47.5 us
  Pallas kernels: 0 us -> 55 us
  starting transfers between devices: 38.1 us -> 53.7 us
    dot_general x23 -> x3, matrix products: 135 us -> 17.8 us  [the longest x1 10.2 us: shards(): lax.dot_general(gate_low, w_gate, contract_last, preferred_element_type=F32)]
    pallas_call x0 -> x3, Pallas kernels: none -> 55 us  [the longest x1 26.3 us: run_forward(): pl.pallas_call(forward_kernel, grid=(rows // BLOCK,), in_specs=[block(wid...]
    reduce_sum x8 -> x4, other arithmetic: 23.3 us -> 1.81 us  [the longest x1 1.19 us: conv_silu(): result = result + weight[CONV - 1 - k] * shifted * masks[:, k:k + 1]]
    reshape x13 -> x3, local copies, waits for them, and re-layouts: 18.8 us -> 0.02 us  [the longest x1 0.01 us: shards(): jnp.pad(small, (0, small_rows * width - small.shape[0]))]
    ppermute x52, starting transfers between devices: 38.1 us -> 53.7 us  [swap(): lax.ppermute(array, axis, [(source, source ^ bit) for source in range(siz...]
    another operation x11 -> x3, other arithmetic: 17.7 us -> 2.28 us  [the longest x2 1.26 us: shards(): jnp.stack([dt_bias, -jnp.exp(a_log)])]
    mul x16 -> x1, other arithmetic: 14.4 us -> 0.47 us  [conv_silu(): result = result + weight[CONV - 1 - k] * shifted * masks[:, k:k + 1]]
    mul x9 -> x1, local copies, waits for them, and re-layouts: 11.1 us -> 0.01 us  [conv_silu(): result = conv_bias + weight[CONV - 1] * inputs]
  transfers between devices with their start and end apart: 52 -> 52, of which waited for: 34 -> 37; matrix products, arithmetic and copies ran while one was open for 16% -> 15% of each run, Pallas kernels for 0% -> 0%
where the time goes in v2:
time: 454 us; the launch traced here: 445 us
  waiting for transfers between devices  211 us (46%)
  Pallas kernels  55 us (12%)
  starting transfers between devices  53.7 us (12%)
  local copies, waits for them, and re-layouts  47.5 us (10%)
  other arithmetic  37.9 us (8%)
  matrix products  37.8 us (8%)
    ppermute x52, waiting for transfers between devices, swap(): lax.ppermute(array, axis, [(source, source ^ bit) for source in range(siz...  211 us
    ppermute x52, starting transfers between devices, swap(): lax.ppermute(array, axis, [(source, source ^ bit) for source in range(siz...  53.7 us
    pallas_call x1, Pallas kernels, run_forward(): pl.pallas_call(forward_kernel, grid=(rows // BLOCK,), in_specs=[block(wid...  26.3 us
    pallas_call x1, Pallas kernels, run_backward(): pl.pallas_call(backward_kernel, grid=(count,), in_specs=[block(channels),...  24.5 us
    convert_element_type x21, local copies, waits for them, and re-layouts, sum_over(): sent = half_of(part, 1 - mine).astype(jnp.bfloat16)  12.3 us
    dot_general x1, matrix products, shards(): lax.dot_general(gate_low, w_gate, contract_last, preferred_element_type=F32)  10.2 us
  transfers between devices with their start and end apart: 52, of which 37 were waited for; matrix products, arithmetic and copies ran while one was open for 15% of the time, Pallas kernels for 0%

profile of v2, /device:TPU:0, one launch (start us, length us, event | category | flops | bytes accessed | tf_op | source)
XLA Modules:
  0.0 445.1 jit_solution(15526129740752419862)
XLA Ops:
  15.0 26.3 %forward.1 = (bf16[1024,1536]{1,0:T(8,128)(2,1)}, f32[1024,768]{1,0:T(8,128)}, f32[1024,768]{1,0:T(8,128)}, f32[1024,768]{1,0:T(8,128)}, f32[1024,768]{1,0:T(8,1...) custom-call(bf16[1024,1536]{1,0:T(8,128)(2,1)} %hidden_ref.1, ...), custom_call_target="tpu_custom_call" | custom-call | tf_op jit(solution)/shard_map/forward/pallas_call | solution.py:380
  57.4 24.5 %backward.1 = (bf16[1024,768]{1,0:T(8,128)(2,1)S(1)}, bf16[1024,128]{1,0:T(8,128)(2,1)S(1)}, bf16[1024,256]{1,0:T(8,128)(2,1)S(1)}, f32[8,768]{1,0:T(8,128)S(1)}, f32[8,128]{1,0:T(8,128)S(1)}) custom-call(bf16[1024,768]{1,0:T(8,128)(2,1)} %copy-done.7, f32[1024,768]{1,0:T(8,128)} %get-tuple-element.39.scan_ref, f32[1024,768]{1,0:T(8,128)} %get-tuple-element.45.value_ref, ...), custom_call_target="tpu_custom_call" | custom-call | tf_op jit(solution)/shard_map/backward/pallas_call | solution.py:484
  132.9 7.3 %collective-permute-done.46 = bf16[96,1536]{1,0:T(8,128)(2,1)S(1)} collective-permute-done((bf16[96,1536]{1,0:T(8,128)(2,1)S(1)}, bf16[96,1536]{1,0:T(8,128)(2,1)S(1)}, u32[]{:S(2)}, u32[]{:S(2)}) %collective-permute-start.46) | collective-permute-done | bytes 294944 | tf_op jit(solution)/shard_map/ppermute | solution.py:569
  156.3 10.2 %fusion.1 = (f32[1536]{0:T(1024)S(1)}, bf16[1024,1536]{1,0:T(8,128)(2,1)S(1)}) fusion(bf16[1024,1536]{1,0:T(8,128)(2,1)} %hidden_ref.1, f32[1024]{0:T(1024)S(1)} %add_rsqrt_fusion, f32[1024,1536]{1,0:T(8,128)} %fusion.40, f32[1024,1536]{1,0:T(8,128)} %fusion.18, f32[1024,1536]{1,0:T(8,128)} %fusion.47, bf16[1024,768]{1,0:T(8,128)(2,1)S(1)} %copy-done.6, ...), kind=kOutput, calls=%fused_computation.3 | convolution fusion | flops 2428500480 | bytes 29108224 | tf_op jit(solution)/shard_map/dot_general | solution.py:737
  173.3 12.0 %collective-permute-done.23 = bf16[96,768]{1,0:T(8,128)(2,1)S(1)} collective-permute-done((bf16[96,768]{1,0:T(8,128)(2,1)S(1)}, bf16[96,768]{1,0:T(8,128)(2,1)S(1)}, u32[]{:S(2)}, u32[]{:S(2)}) %collective-permute-start.23) | collective-permute-done | bytes 147488 | tf_op jit(solution)/shard_map/ppermute | solution.py:569
  198.3 4.7 %collective-permute-done.48 = bf16[24,1536]{1,0:T(8,128)(2,1)S(1)} collective-permute-done((bf16[24,1536]{1,0:T(8,128)(2,1)S(1)}, bf16[24,1536]{1,0:T(8,128)(2,1)S(1)}, u32[]{:S(2)}, u32[]{:S(2)}) %collective-permute-start.48) | collective-permute-done | bytes 73760 | tf_op jit(solution)/shard_map/ppermute | solution.py:569
  209.4 5.4 %collective-permute-done.36 = bf16[48,768]{1,0:T(8,128)(2,1)S(1)} collective-permute-done((bf16[48,768]{1,0:T(8,128)(2,1)S(1)}, bf16[48,768]{1,0:T(8,128)(2,1)S(1)}, u32[]{:S(2)}, u32[]{:S(2)}) %collective-permute-start.36) | collective-permute-done | bytes 73760 | tf_op jit(solution)/shard_map/ppermute | solution.py:569
  214.8 5.8 %collective-permute-done.25 = bf16[48,768]{1,0:T(8,128)(2,1)S(1)} collective-permute-done((bf16[48,768]{1,0:T(8,128)(2,1)S(1)}, bf16[48,768]{1,0:T(8,128)(2,1)S(1)}, u32[]{:S(2)}, u32[]{:S(2)}) %collective-permute-start.25) | collective-permute-done | bytes 73760 | tf_op jit(solution)/shard_map/ppermute | solution.py:569
  220.6 6.1 %collective-permute-done.37 = bf16[48,768]{1,0:T(8,128)(2,1)S(1)} collective-permute-done((bf16[48,768]{1,0:T(8,128)(2,1)S(1)}, bf16[48,768]{1,0:T(8,128)(2,1)S(1)}, u32[]{:S(2)}, u32[]{:S(2)}) %collective-permute-start.37) | collective-permute-done | bytes 73760 | tf_op jit(solution)/shard_map/ppermute | solution.py:569
  226.7 5.2 %collective-permute-done.49 = bf16[24,1536]{1,0:T(8,128)(2,1)S(1)} collective-permute-done((bf16[24,1536]{1,0:T(8,128)(2,1)S(1)}, bf16[24,1536]{1,0:T(8,128)(2,1)S(1)}, u32[]{:S(2)}, u32[]{:S(2)}) %collective-permute-start.49) | collective-permute-done | bytes 73760 | tf_op jit(solution)/shard_map/ppermute | solution.py:569
  260.1 4.7 %collective-permute-done.12 = bf16[16,1536]{1,0:T(8,128)(2,1)S(1)} collective-permute-done((bf16[16,1536]{1,0:T(8,128)(2,1)S(1)}, bf16[16,1536]{1,0:T(8,128)(2,1)S(1)}, u32[]{:S(2)}, u32[]{:S(2)}) %collective-permute-start.12) | collective-permute-done | bytes 49184 | tf_op jit(solution)/shard_map/ppermute | solution.py:569
  265.1 4.8 %collective-permute-done.13 = bf16[16,1536]{1,0:T(8,128)(2,1)S(1)} collective-permute-done((bf16[16,1536]{1,0:T(8,128)(2,1)S(1)}, bf16[16,1536]{1,0:T(8,128)(2,1)S(1)}, u32[]{:S(2)}, u32[]{:S(2)}) %collective-permute-start.13) | collective-permute-done | bytes 49184 | tf_op jit(solution)/shard_map/ppermute | solution.py:569
  279.2 8.6 %collective-permute-done.14 = bf16[32,1536]{1,0:T(8,128)(2,1)S(1)} collective-permute-done((bf16[32,1536]{1,0:T(8,128)(2,1)S(1)}, bf16[32,1536]{1,0:T(8,128)(2,1)S(1)}, u32[]{:S(2)}, u32[]{:S(2)}) %collective-permute-start.14) | collective-permute-done | bytes 98336 | tf_op jit(solution)/shard_map/ppermute | solution.py:569
  288.2 8.3 %collective-permute-done.51 = bf16[96,1536]{1,0:T(8,128)(2,1)S(1)} collective-permute-done((bf16[96,1536]{1,0:T(8,128)(2,1)S(1)}, bf16[96,1536]{1,0:T(8,128)(2,1)S(1)}, u32[]{:S(2)}, u32[]{:S(2)}) %collective-permute-start.51) | collective-permute-done | bytes 294944 | tf_op jit(solution)/shard_map/ppermute | solution.py:569
  313.7 10.5 %collective-permute-done.29 = bf16[288,768]{1,0:T(8,128)(2,1)} collective-permute-done((bf16[288,768]{1,0:T(8,128)(2,1)}, bf16[288,768]{1,0:T(8,128)(2,1)}, u32[]{:S(2)}, u32[]{:S(2)}) %collective-permute-start.29) | collective-permute-done | bytes 442400 | tf_op jit(solution)/shard_map/ppermute | solution.py:569
  325.3 8.5 %collective-permute-done.41 = bf16[144,1536]{1,0:T(8,128)(2,1)} collective-permute-done((bf16[144,1536]{1,0:T(8,128)(2,1)}, bf16[144,1536]{1,0:T(8,128)(2,1)}, u32[]{:S(2)}, u32[]{:S(2)}) %collective-permute-start.41) | collective-permute-done | bytes 442400 | tf_op jit(solution)/shard_map/ppermute | solution.py:569
  338.1 15.0 %collective-permute-done.30 = bf16[144,768]{1,0:T(8,128)(2,1)S(1)} collective-permute-done((bf16[144,768]{1,0:T(8,128)(2,1)S(1)}, bf16[144,768]{1,0:T(8,128)(2,1)S(1)}, u32[]{:S(2)}, u32[]{:S(2)}) %collective-permute-start.30) | collective-permute-done | bytes 221216 | tf_op jit(solution)/shard_map/ppermute | solution.py:569
  353.2 9.4 %collective-permute-done.42 = bf16[72,1536]{1,0:T(8,128)(2,1)S(1)} collective-permute-done((bf16[72,1536]{1,0:T(8,128)(2,1)S(1)}, bf16[72,1536]{1,0:T(8,128)(2,1)S(1)}, u32[]{:S(2)}, u32[]{:S(2)}) %collective-permute-start.42) | collective-permute-done | bytes 221216 | tf_op jit(solution)/shard_map/ppermute | solution.py:569
  368.9 5.6 %collective-permute-done.31 = bf16[144,768]{1,0:T(8,128)(2,1)S(1)} collective-permute-done((bf16[144,768]{1,0:T(8,128)(2,1)S(1)}, bf16[144,768]{1,0:T(8,128)(2,1)S(1)}, u32[]{:S(2)}, u32[]{:S(2)}) %collective-permute-start.31) | collective-permute-done | bytes 221216 | tf_op jit(solution)/shard_map/ppermute | solution.py:569
  380.6 5.8 %collective-permute-done.20 = bf16[288,768]{1,0:T(8,128)(2,1)S(1)} collective-permute-done((bf16[288,768]{1,0:T(8,128)(2,1)S(1)}, bf16[288,768]{1,0:T(8,128)(2,1)S(1)}, u32[]{:S(2)}, u32[]{:S(2)}) %collective-permute-start.20) | collective-permute-done | bytes 442400 | tf_op jit(solution)/shard_map/ppermute | solution.py:569
  388.6 7.3 %collective-permute-done.32 = bf16[288,768]{1,0:T(8,128)(2,1)S(1)} collective-permute-done((bf16[288,768]{1,0:T(8,128)(2,1)S(1)}, bf16[288,768]{1,0:T(8,128)(2,1)S(1)}, u32[]{:S(2)}, u32[]{:S(2)}) %collective-permute-start.32) | collective-permute-done | bytes 442400 | tf_op jit(solution)/shard_map/ppermute | solution.py:569
  398.1 4.8 %collective-permute-done.44 = bf16[144,1536]{1,0:T(8,128)(2,1)S(1)} collective-permute-done((bf16[144,1536]{1,0:T(8,128)(2,1)S(1)}, bf16[144,1536]{1,0:T(8,128)(2,1)S(1)}, u32[]{:S(2)}, u32[]{:S(2)}) %collective-permute-start.44) | collective-permute-done | bytes 442400 | tf_op jit(solution)/shard_map/ppermute | solution.py:569
  409.7 18.6 %collective-permute-done.33 = bf16[576,768]{1,0:T(8,128)(2,1)S(1)} collective-permute-done((bf16[576,768]{1,0:T(8,128)(2,1)S(1)}, bf16[576,768]{1,0:T(8,128)(2,1)S(1)}, u32[]{:S(2)}, u32[]{:S(2)}) %collective-permute-start.33) | collective-permute-done | bytes 884768 | tf_op jit(solution)/shard_map/ppermute | solution.py:569
  433.8 7.7 %collective-permute-done.45 = bf16[288,1536]{1,0:T(8,128)(2,1)S(1)} collective-permute-done((bf16[288,1536]{1,0:T(8,128)(2,1)S(1)}, bf16[288,1536]{1,0:T(8,128)(2,1)S(1)}, u32[]{:S(2)}, u32[]{:S(2)}) %collective-permute-start.45) | collective-permute-done | bytes 884768 | tf_op jit(solution)/shard_map/ppermute | solution.py:569
  (374 shorter events, 215.4 us)
Async XLA Ops:
  116.5 246.2 %collective-permute-start.2 = (bf16[2,256,1536]{2,1,0:T(8,128)(2,1)}, bf16[2,256,1536]{2,1,0:T(8,128)(2,1)}, u32[]{:S(2)}, u32[]{:S(2)}) collective-permute-start(bf16[2,256,1536]{2,1,0:T(8,128)(2,1)} %dynamic-slice_bitcast_fusion.1), channel_id=1, source_target_pairs={{0,1},{1,0},{2,3},{3,2},{4,5},{5,4},{6,7},{7,6},{8,9},{9,8},{10,11... | collective-permute-start | bytes 4718600 | tf_op jit(solution)/shard_map/ppermute | solution.py:569
  118.5 24.0 %collective-permute-start.22 = (bf16[192,768]{1,0:T(8,128)(2,1)S(1)}, bf16[192,768]{1,0:T(8,128)(2,1)S(1)}, u32[]{:S(2)}, u32[]{:S(2)}) collective-permute-start(bf16[192,768]{1,0:T(8,128)(2,1)S(1)} %dynamic-slice_convert_fusion.10), channel_id=1, source_target_pairs={{0,8},{4,12},{8,0},{12,4},{16,24},{20,28},{24,16},{28,20},{1,9},{5... | collective-permute-start | bytes 884744 | tf_op jit(solution)/shard_map/ppermute | solution.py:569
  122.7 147.2 %collective-permute-start.16 = (bf16[576,768]{1,0:T(8,128)(2,1)}, bf16[576,768]{1,0:T(8,128)(2,1)}, u32[]{:S(2)}, u32[]{:S(2)}) collective-permute-start(bf16[576,768]{1,0:T(8,128)(2,1)} %dynamic-slice_convert_fusion.2), channel_id=1, source_target_pairs={{0,4},{4,0},{8,12},{12,8},{16,20},{20,16},{24,28},{28,24},{1,5},{5... | collective-permute-start | bytes 2654216 | tf_op jit(solution)/shard_map/ppermute | solution.py:569
  124.3 18.7 %collective-permute-start.34 = (bf16[192,768]{1,0:T(8,128)(2,1)S(1)}, bf16[192,768]{1,0:T(8,128)(2,1)S(1)}, u32[]{:S(2)}, u32[]{:S(2)}) collective-permute-start(bf16[192,768]{1,0:T(8,128)(2,1)S(1)} %dynamic-slice_convert_fusion.9), channel_id=1, source_target_pairs={{0,8},{4,12},{8,0},{12,4},{16,24},{20,28},{24,16},{28,20},{1,9},{5... | collective-permute-start | bytes 884744 | tf_op jit(solution)/shard_map/ppermute | solution.py:569
  140.1 136.5 %collective-permute-start.28 = (bf16[576,768]{1,0:T(8,128)(2,1)}, bf16[576,768]{1,0:T(8,128)(2,1)}, u32[]{:S(2)}, u32[]{:S(2)}) collective-permute-start(bf16[576,768]{1,0:T(8,128)(2,1)} %dynamic-slice_convert_fusion.1), channel_id=1, source_target_pairs={{0,4},{4,0},{8,12},{12,8},{16,20},{20,16},{24,28},{28,24},{1,5},{5... | collective-permute-start | bytes 2654216 | tf_op jit(solution)/shard_map/ppermute | solution.py:569
  142.5 130.0 %collective-permute-start.40 = (bf16[288,1536]{1,0:T(8,128)(2,1)}, bf16[288,1536]{1,0:T(8,128)(2,1)}, u32[]{:S(2)}, u32[]{:S(2)}) collective-permute-start(bf16[288,1536]{1,0:T(8,128)(2,1)} %dynamic-slice_convert_fusion), channel_id=1, source_target_pairs={{0,4},{4,0},{8,12},{12,8},{16,20},{20,16},{24,28},{28,24},{1,5},{5... | collective-permute-start | bytes 2654216 | tf_op jit(solution)/shard_map/ppermute | solution.py:569
  269.9 107.2 %collective-permute-start.6 = (bf16[2,256,1536]{2,1,0:T(8,128)(2,1)}, bf16[2,256,1536]{2,1,0:T(8,128)(2,1)}, u32[]{:S(2)}, u32[]{:S(2)}) collective-permute-start(bf16[2,256,1536]{2,1,0:T(8,128)(2,1)} %dynamic-slice_bitcast_fusion), channel_id=1, source_target_pairs={{0,1},{1,0},{2,3},{3,2},{4,5},{5,4},{6,7},{7,6},{8,9},{9,8},{10,11... | collective-permute-start | bytes 4718600 | tf_op jit(solution)/shard_map/ppermute | solution.py:569
  269.9 27.1 %collective-permute-start.27 = (bf16[192,768]{1,0:T(8,128)(2,1)S(1)}, bf16[192,768]{1,0:T(8,128)(2,1)S(1)}, u32[]{:S(2)}, u32[]{:S(2)}) collective-permute-start(bf16[192,768]{1,0:T(8,128)(2,1)S(1)} %pad_maximum_fusion.6), channel_id=1, source_target_pairs={{0,8},{4,12},{8,0},{12,4},{16,24},{20,28},{24,16},{28,20},{1,9},{5... | collective-permute-start | bytes 884744 | tf_op jit(solution)/shard_map/ppermute | solution.py:569
  272.4 26.3 %collective-permute-start.39 = (bf16[192,768]{1,0:T(8,128)(2,1)S(1)}, bf16[192,768]{1,0:T(8,128)(2,1)S(1)}, u32[]{:S(2)}, u32[]{:S(2)}) collective-permute-start(bf16[192,768]{1,0:T(8,128)(2,1)S(1)} %pad_maximum_fusion.7), channel_id=1, source_target_pairs={{0,8},{4,12},{8,0},{12,4},{16,24},{20,28},{24,16},{28,20},{1,9},{5... | collective-permute-start | bytes 884744 | tf_op jit(solution)/shard_map/ppermute | solution.py:569
  297.1 27.0 %collective-permute-start.29 = (bf16[288,768]{1,0:T(8,128)(2,1)}, bf16[288,768]{1,0:T(8,128)(2,1)}, u32[]{:S(2)}, u32[]{:S(2)}) collective-permute-start(bf16[288,768]{1,0:T(8,128)(2,1)} %dynamic-slice_convert_fusion.6), channel_id=1, source_target_pairs={{0,8},{4,12},{8,0},{12,4},{16,24},{20,28},{24,16},{28,20},{1,9},{5... | collective-permute-start | bytes 1327112 | tf_op jit(solution)/shard_map/ppermute | solution.py:569
  304.5 29.3 %collective-permute-start.41 = (bf16[144,1536]{1,0:T(8,128)(2,1)}, bf16[144,1536]{1,0:T(8,128)(2,1)}, u32[]{:S(2)}, u32[]{:S(2)}) collective-permute-start(bf16[144,1536]{1,0:T(8,128)(2,1)} %dynamic-slice_convert_fusion.5), channel_id=1, source_target_pairs={{0,8},{4,12},{8,0},{12,4},{16,24},{20,28},{24,16},{28,20},{1,9},{5... | collective-permute-start | bytes 1327112 | tf_op jit(solution)/shard_map/ppermute | solution.py:569
  311.6 23.4 %collective-permute-start.18 = (bf16[144,768]{1,0:T(8,128)(2,1)S(1)}, bf16[144,768]{1,0:T(8,128)(2,1)S(1)}, u32[]{:S(2)}, u32[]{:S(2)}) collective-permute-start(bf16[144,768]{1,0:T(8,128)(2,1)S(1)} %dynamic-slice_convert_fusion.14), channel_id=1, source_target_pairs={{0,16},{4,20},{8,24},{12,28},{16,0},{20,4},{24,8},{28,12},{1,17},{... | collective-permute-start | bytes 663560 | tf_op jit(solution)/shard_map/ppermute | solution.py:569
  325.3 27.8 %collective-permute-start.30 = (bf16[144,768]{1,0:T(8,128)(2,1)S(1)}, bf16[144,768]{1,0:T(8,128)(2,1)S(1)}, u32[]{:S(2)}, u32[]{:S(2)}) collective-permute-start(bf16[144,768]{1,0:T(8,128)(2,1)S(1)} %dynamic-slice_convert_fusion.13), channel_id=1, source_target_pairs={{0,16},{4,20},{8,24},{12,28},{16,0},{20,4},{24,8},{28,12},{1,17},{... | collective-permute-start | bytes 663560 | tf_op jit(solution)/shard_map/ppermute | solution.py:569
  335.0 27.6 %collective-permute-start.42 = (bf16[72,1536]{1,0:T(8,128)(2,1)S(1)}, bf16[72,1536]{1,0:T(8,128)(2,1)S(1)}, u32[]{:S(2)}, u32[]{:S(2)}) collective-permute-start(bf16[72,1536]{1,0:T(8,128)(2,1)S(1)} %dynamic-slice_convert_fusion.12), channel_id=1, source_target_pairs={{0,16},{4,20},{8,24},{12,28},{16,0},{20,4},{24,8},{28,12},{1,17},{... | collective-permute-start | bytes 663560 | tf_op jit(solution)/shard_map/ppermute | solution.py:569
  335.2 33.4 %collective-permute-start.19 = (bf16[144,768]{1,0:T(8,128)(2,1)S(1)}, bf16[144,768]{1,0:T(8,128)(2,1)S(1)}, u32[]{:S(2)}, u32[]{:S(2)}) collective-permute-start(bf16[144,768]{1,0:T(8,128)(2,1)S(1)} %add_convert_fusion.2), channel_id=1, source_target_pairs={{0,16},{4,20},{8,24},{12,28},{16,0},{20,4},{24,8},{28,12},{1,17},{... | collective-permute-start | bytes 663560 | tf_op jit(solution)/shard_map/ppermute | solution.py:569
  353.1 21.3 %collective-permute-start.31 = (bf16[144,768]{1,0:T(8,128)(2,1)S(1)}, bf16[144,768]{1,0:T(8,128)(2,1)S(1)}, u32[]{:S(2)}, u32[]{:S(2)}) collective-permute-start(bf16[144,768]{1,0:T(8,128)(2,1)S(1)} %add_convert_fusion.1), channel_id=1, source_target_pairs={{0,16},{4,20},{8,24},{12,28},{16,0},{20,4},{24,8},{28,12},{1,17},{... | collective-permute-start | bytes 663560 | tf_op jit(solution)/shard_map/ppermute | solution.py:569
  364.7 40.9 %collective-permute-start.3 = (bf16[256,1536]{1,0:T(8,128)(2,1)S(1)}, bf16[256,1536]{1,0:T(8,128)(2,1)S(1)}, u32[]{:S(2)}, u32[]{:S(2)}) collective-permute-start(bf16[256,1536]{1,0:T(8,128)(2,1)S(1)} %fusion.10), channel_id=1, source_target_pairs={{0,2},{1,3},{2,0},{3,1},{4,6},{5,7},{6,4},{7,5},{8,10},{9,11},{10,... | collective-permute-start | bytes 2359304 | tf_op jit(solution)/shard_map/ppermute | solution.py:569
  368.6 17.9 %collective-permute-start.20 = (bf16[288,768]{1,0:T(8,128)(2,1)S(1)}, bf16[288,768]{1,0:T(8,128)(2,1)S(1)}, u32[]{:S(2)}, u32[]{:S(2)}) collective-permute-start(bf16[288,768]{1,0:T(8,128)(2,1)S(1)} %pad_maximum_fusion.3), channel_id=1, source_target_pairs={{0,8},{4,12},{8,0},{12,4},{16,24},{20,28},{24,16},{28,20},{1,9},{5... | collective-permute-start | bytes 1327112 | tf_op jit(solution)/shard_map/ppermute | solution.py:569
  374.6 21.4 %collective-permute-start.32 = (bf16[288,768]{1,0:T(8,128)(2,1)S(1)}, bf16[288,768]{1,0:T(8,128)(2,1)S(1)}, u32[]{:S(2)}, u32[]{:S(2)}) collective-permute-start(bf16[288,768]{1,0:T(8,128)(2,1)S(1)} %pad_maximum_fusion.4), channel_id=1, source_target_pairs={{0,8},{4,12},{8,0},{12,4},{16,24},{20,28},{24,16},{28,20},{1,9},{5... | collective-permute-start | bytes 1327112 | tf_op jit(solution)/shard_map/ppermute | solution.py:569
  377.0 25.9 %collective-permute-start.44 = (bf16[144,1536]{1,0:T(8,128)(2,1)S(1)}, bf16[144,1536]{1,0:T(8,128)(2,1)S(1)}, u32[]{:S(2)}, u32[]{:S(2)}) collective-permute-start(bf16[144,1536]{1,0:T(8,128)(2,1)S(1)} %pad_maximum_fusion.5), channel_id=1, source_target_pairs={{0,8},{4,12},{8,0},{12,4},{16,24},{20,28},{24,16},{28,20},{1,9},{5... | collective-permute-start | bytes 1327112 | tf_op jit(solution)/shard_map/ppermute | solution.py:569
  379.1 26.0 %collective-permute-start.7 = (bf16[256,1536]{1,0:T(8,128)(2,1)S(1)}, bf16[256,1536]{1,0:T(8,128)(2,1)S(1)}, u32[]{:S(2)}, u32[]{:S(2)}) collective-permute-start(bf16[256,1536]{1,0:T(8,128)(2,1)S(1)} %fusion.11), channel_id=1, source_target_pairs={{0,2},{1,3},{2,0},{3,1},{4,6},{5,7},{6,4},{7,5},{8,10},{9,11},{10,... | collective-permute-start | bytes 2359304 | tf_op jit(solution)/shard_map/ppermute | solution.py:569
  386.7 22.6 %collective-permute-start.21 = (bf16[576,768]{1,0:T(8,128)(2,1)S(1)}, bf16[576,768]{1,0:T(8,128)(2,1)S(1)}, u32[]{:S(2)}, u32[]{:S(2)}) collective-permute-start(bf16[576,768]{1,0:T(8,128)(2,1)S(1)} %pad_maximum_fusion), channel_id=1, source_target_pairs={{0,4},{4,0},{8,12},{12,8},{16,20},{20,16},{24,28},{28,24},{1,5},{5... | collective-permute-start | bytes 2654216 | tf_op jit(solution)/shard_map/ppermute | solution.py:569
  396.2 32.1 %collective-permute-start.33 = (bf16[576,768]{1,0:T(8,128)(2,1)S(1)}, bf16[576,768]{1,0:T(8,128)(2,1)S(1)}, u32[]{:S(2)}, u32[]{:S(2)}) collective-permute-start(bf16[576,768]{1,0:T(8,128)(2,1)S(1)} %pad_maximum_fusion.1), channel_id=1, source_target_pairs={{0,4},{4,0},{8,12},{12,8},{16,20},{20,16},{24,28},{28,24},{1,5},{5... | collective-permute-start | bytes 2654216 | tf_op jit(solution)/shard_map/ppermute | solution.py:569
  403.2 38.3 %collective-permute-start.45 = (bf16[288,1536]{1,0:T(8,128)(2,1)S(1)}, bf16[288,1536]{1,0:T(8,128)(2,1)S(1)}, u32[]{:S(2)}, u32[]{:S(2)}) collective-permute-start(bf16[288,1536]{1,0:T(8,128)(2,1)S(1)} %pad_maximum_fusion.2), channel_id=1, source_target_pairs={{0,4},{4,0},{8,12},{12,8},{16,20},{20,16},{24,28},{28,24},{1,5},{5... | collective-permute-start | bytes 2654216 | tf_op jit(solution)/shard_map/ppermute | solution.py:569
  (80 other events, 750.1 us)

commit v3 on v2

v3 whole, which is shorter than its diff:
```python
import functools
import math

import jax
import jax.numpy as jnp
from jax import lax
from jax.experimental import pallas as pl
from jax.experimental.pallas import tpu as pltpu
from jax.sharding import PartitionSpec as P

STATE = 128
CONV = 4
BLOCK = 256
PIECE = 128
PACKED = 128
LANES = 128
EPS = 1e-05
HIGH = lax.Precision.HIGHEST
LOG2E = math.log2(math.e)
BF16 = jnp.bfloat16
F32 = jnp.float32


def dot(left, right):
    return jnp.dot(left, right, preferred_element_type=F32)


def dot_last(left, right):
    return lax.dot_general(left, right, (((1,), (1,)), ((), ())), preferred_element_type=F32)


def dot_first(left, right):
    return lax.dot_general(left, right, (((0,), (0,)), ((), ())), preferred_element_type=F32)


def two_terms(array):
    upper = array.astype(BF16)
    return upper, (array - upper.astype(F32)).astype(BF16)


def sigmoid(array):
    return 0.5 * jnp.tanh(0.5 * array) + 0.5


def spread_heads(array, heads_twice):
    upper, rest = two_terms(array)
    return dot(jnp.concatenate([upper, rest], axis=1), heads_twice)


def sum_heads(array, heads):
    upper, rest = two_terms(array)
    return dot_last(upper, heads) + dot_last(rest, heads)


def head_table(channels, head_count):
    head_width = channels // head_count
    channel = lax.broadcasted_iota(jnp.int32, (LANES, channels), 1)
    head = lax.broadcasted_iota(jnp.int32, (LANES, channels), 0)
    first = head * head_width
    return ((channel >= first) & (channel < first + head_width)).astype(F32).astype(BF16)


def head_rows(head_ref, heads):
    upper, rest = two_terms(head_ref[...])
    return dot(upper, heads) + dot(rest, heads)


def table_kernel(
    segment_ref,
    pre_gain_ref,
    bias_x_ref,
    gate_gain_ref,
    bias_bc_ref,
    dt_bias_ref,
    a_log_ref,
    d_skip_ref,
    token_ref,
    row_ref,
    head_ref,
):
    seq_count, length = segment_ref.shape
    place = lax.broadcasted_iota(jnp.int32, (8, length), 1)
    at_row = lax.broadcasted_iota(jnp.int32, (8, length), 0)
    for seq in range(seq_count):
        documents = jnp.broadcast_to(segment_ref[seq : seq + 1, :], (8, length)).astype(F32)
        padded = jnp.where(at_row == 0, documents, 0.0)

        def moved(by):
            other = pltpu.roll(documents, by % length, 1)
            return other, (place >= by) & (place < length + by)

        for k in range(1, CONV):
            before, inside = moved(k)
            padded = jnp.where((at_row == k) & inside & (before == documents), 1.0, padded)
        ends = []
        for piece in range(length // PIECE):
            here = slice(piece * PIECE, (piece + 1) * PIECE)
            ends.append(jnp.broadcast_to(documents[:, (piece + 1) * PIECE - 1 : (piece + 1) * PIECE], (8, PIECE)))
        starts = [jnp.full((8, PIECE), -1.0, F32)] + ends[:-1]
        padded = jnp.where((at_row == 4) & (jnp.concatenate(starts, axis=1) == documents), 1.0, padded)
        padded = jnp.where((at_row == 5) & (jnp.concatenate(ends, axis=1) == documents), 1.0, padded)
        lower = jnp.zeros((8, length), F32)
        for k in range(1, CONV):
            after, inside = moved(-k)
            hit = inside & (after == documents)
            if 5 + k < 8:
                padded = jnp.where((at_row == 5 + k) & hit, 1.0, padded)
            else:
                lower = jnp.where((at_row == 5 + k - 8) & hit, 1.0, lower)
        columns = slice(seq * length, (seq + 1) * length)
        token_ref[0:8, columns] = padded + jnp.where(at_row == 0, 64.0 * seq, 0.0)
        token_ref[8:16, columns] = lower
    row_ref[...] = jnp.zeros(row_ref.shape, F32)
    for at, ref in enumerate((pre_gain_ref, bias_x_ref, gate_gain_ref, bias_bc_ref)):
        row_ref[at : at + 1, 0 : ref.shape[0]] = ref[...].reshape(1, -1)
    head_ref[...] = jnp.zeros(head_ref.shape, F32)
    count = dt_bias_ref.shape[0]
    head_ref[0:1, 0:count] = dt_bias_ref[...].reshape(1, -1)
    head_ref[1:2, 0:count] = -jnp.exp(a_log_ref[...].reshape(1, -1))
    head_ref[2:3, 0:count] = d_skip_ref[...].reshape(1, -1)


def forward_kernel(
    hidden_ref,
    cotan_ref,
    w_gate_ref,
    w_value_ref,
    w_bc_ref,
    w_dt_ref,
    w_out_ref,
    conv_x_ref,
    conv_bc_ref,
    row_ref,
    head_ref,
    token_ref,
    normed_ref,
    mixed_ref,
    act_ref,
    turn_ref,
    grad_ref,
    scan_ref,
    value_ref,
    slope_ref,
    inner_ref,
    step_ref,
    cum_ref,
    bc_ref,
    bc_slope_ref,
    state_ref,
    enter_ref,
    sums_ref,
    tail_x,
    tail_bc,
    carried,
    wide_dt,
    gate_all,
    grad_all,
):
    block = pl.program_id(0)

    @pl.when(block == 0)
    def _():
        tail_x[0:8, :] = jnp.zeros((8, tail_x.shape[1]), F32)
        tail_bc[0:8, :] = jnp.zeros((8, tail_bc.shape[1]), F32)
        carried[...] = jnp.zeros(carried.shape, F32)
        wide_dt[...] = jnp.zeros(wide_dt.shape, BF16)
        wide_dt[0 : w_dt_ref.shape[0], :] = w_dt_ref[...]

    channels = tail_x.shape[1]
    heads = head_table(channels, w_dt_ref.shape[0])
    skips = head_rows(head_ref, heads)[2:3, :]
    side = token_ref[...].T
    hidden = hidden_ref[...].astype(F32)
    inv_rms = lax.rsqrt(jnp.mean(hidden * hidden, axis=-1, keepdims=True) + EPS)
    normed = (hidden * inv_rms * row_ref[0:1, :]).astype(BF16)
    normed_ref[...] = normed
    tail_x[8:, :] = dot(normed, w_value_ref[...])
    tail_bc[8:, :] = dot(normed, w_bc_ref[...])
    step_in = dot_last(normed, wide_dt[...]) + head_ref[0:1, :]
    step_ref[...] = step_in
    step = jnp.maximum(step_in, 0.0) + jnp.log1p(jnp.exp(-jnp.abs(step_in)))
    rate = head_ref[1:2, :] * step * LOG2E
    gate_all[...] = dot(normed, w_gate_ref[...])
    grad_all[...] = dot_last(cotan_ref[...], w_out_ref[...])
    masks = [None] + [side[:, k : k + 1] for k in range(1, CONV)]

    def conv(tail, taps_ref, bias_at, lanes):
        result = row_ref[bias_at : bias_at + 1, lanes] + taps_ref[CONV - 1 : CONV, lanes] * tail[8:, lanes]
        for k in range(1, CONV):
            shifted = tail[8 - k : 8 - k + BLOCK, lanes]
            result = result + taps_ref[CONV - 1 - k : CONV - k, lanes] * shifted * masks[k]
        return result

    for at in range(0, channels, LANES):
        lanes = slice(at, at + LANES)
        before = conv(tail_x, conv_x_ref, 1, lanes)
        half = sigmoid(before)
        value_ref[:, lanes] = (before * half).astype(BF16)
        slope_ref[:, lanes] = (half * (1.0 + before * (1.0 - half))).astype(BF16)
        inner_ref[:, lanes] = tail_x[8:, lanes].astype(BF16)
    for at in range(0, 2 * STATE, LANES):
        lanes = slice(at, at + LANES)
        before = conv(tail_bc, conv_bc_ref, 3, lanes)
        half = sigmoid(before)
        bc_ref[:, lanes] = (before * half).astype(BF16)
        bc_slope_ref[:, lanes] = (half * (1.0 + before * (1.0 - half))).astype(BF16)
        state_ref[:, lanes] = tail_bc[8:, lanes].astype(BF16)
    tail_x[0:8, :] = tail_x[BLOCK:, :]
    tail_bc[0:8, :] = tail_bc[BLOCK:, :]

    row_at = lax.broadcasted_iota(jnp.int32, (PIECE, PIECE), 0)
    col_at = lax.broadcasted_iota(jnp.int32, (PIECE, PIECE), 1)
    lower = (row_at >= col_at).astype(F32)
    first_half = lax.broadcasted_iota(jnp.int32, (PIECE, LANES), 1) < LANES // 2
    heads_twice = jnp.concatenate([heads, heads], axis=0)
    for piece in range(BLOCK // PIECE):
        rows = slice(piece * PIECE, (piece + 1) * PIECE)
        cum = jnp.dot(lower, rate[rows], precision=HIGH, preferred_element_type=F32)
        cum_ref[rows, :] = cum
        cum_t = cum.T
        same = (side[rows, 0:1] == token_ref[0:1, rows]) & (row_at >= col_at)
        bias = jnp.where(same, 0.0, -1e30)
        reach = jnp.exp2(cum) * side[rows, 4:5]
        tail = jnp.exp2(cum[PIECE - 1 : PIECE, :] - cum) * side[rows, 5:6]
        wide = spread_heads(jnp.concatenate([step[rows], reach, tail], axis=0), heads_twice)
        b_low = bc_ref[rows, 0:STATE]
        c_low = bc_ref[rows, STATE : 2 * STATE]
        scores = dot_last(c_low, b_low)
        enter = carried[...].astype(BF16)
        enter_ref[piece] = enter
        for pair in range(channels // LANES):
            lanes = slice(pair * LANES, (pair + 1) * LANES)
            values = value_ref[rows, lanes].astype(F32)
            scaled = wide[0:PIECE, lanes] * values
            low = scaled.astype(BF16)
            weights = []
            for head in (2 * pair, 2 * pair + 1):
                gaps = (cum[:, head : head + 1] - cum_t[head : head + 1, :]) + bias
                weights.append((scores * jnp.exp2(gaps)).astype(BF16))
            zero = jnp.zeros_like(low)
            both = jnp.concatenate(
                [jnp.where(first_half, low, zero), jnp.where(first_half, zero, low)], axis=0
            )
            out = dot(jnp.concatenate(weights, axis=1), both)
            out = out + dot(c_low, enter[:, lanes]) * wide[PIECE : 2 * PIECE, lanes]
            scan_ref[rows, lanes] = out + skips[:, lanes] * values
            tailed = (wide[2 * PIECE :, lanes] * scaled).astype(BF16)
            kept = wide[2 * PIECE - 1 : 2 * PIECE, lanes]
            carried[:, lanes] = kept * carried[:, lanes] + dot_first(b_low, tailed)

    ones = jnp.ones((8, LANES), BF16)
    square_part = jnp.zeros((BLOCK, LANES), F32)
    cross_part = jnp.zeros((BLOCK, LANES), F32)
    for at in range(0, channels, LANES):
        lanes = slice(at, at + LANES)
        gate = gate_all[:, lanes]
        scan = scan_ref[:, lanes]
        grad = grad_all[:, lanes]
        half = sigmoid(gate)
        act = gate * half
        mixed = scan * act
        mixed_ref[:, lanes] = mixed.astype(BF16)
        act_ref[:, lanes] = act.astype(BF16)
        turn_ref[:, lanes] = (scan * (half * (1.0 + gate * (1.0 - half)))).astype(BF16)
        grad_ref[:, lanes] = grad.astype(BF16)
        square_part = square_part + mixed * mixed
        cross_part = cross_part + mixed * (grad * row_ref[2:3, lanes])
    upper, rest = two_terms(square_part)
    squares = dot_last(ones, upper) + dot_last(ones, rest)
    upper, rest = two_terms(cross_part)
    crosses = dot_last(ones, upper) + dot_last(ones, rest)
    is_first = lax.broadcasted_iota(jnp.int32, (8, BLOCK), 0) == 0
    sums_ref[...] = jnp.where(is_first, squares, crosses)


def store_halves(total, start, rows, mine, sent_ref, kept_ref):
    half = rows // 2
    sent_ref[...] = total[pl.ds(pl.multiple_of(start + (1 - mine) * half, 8), half), :].astype(BF16)
    kept_ref[...] = total[pl.ds(pl.multiple_of(start + mine * half, 8), half), :].astype(BF16)


def gate_kernel(
    low_ref,
    mixed_ref,
    act_ref,
    turn_ref,
    grad_ref,
    sums_ref,
    row_ref,
    cotan_ref,
    gated_ref,
    gate_low_ref,
    dscan_ref,
    gain_ref,
    sent_ref,
    kept_ref,
    out_total,
):
    block = pl.program_id(0)

    @pl.when(block == 0)
    def _():
        gain_ref[...] = jnp.zeros(gain_ref.shape, F32)
        out_total[...] = jnp.zeros(out_total.shape, F32)

    row_at = lax.broadcasted_iota(jnp.int32, (8, LANES), 0)

    def column(which):
        pick = (row_at == which).astype(F32)
        return lax.dot_general(
            sums_ref[...], pick, (((0,), (0,)), ((), ())), precision=HIGH, preferred_element_type=F32
        )

    channels = mixed_ref.shape[1]
    inv_gate = lax.rsqrt(column(0) + EPS)
    pull = inv_gate * inv_gate * column(1)
    for at in range(0, channels, LANES):
        lanes = slice(at, at + LANES)
        mixed = mixed_ref[:, lanes].astype(F32)
        grad = grad_ref[:, lanes].astype(F32)
        gain = row_ref[2:3, lanes]
        normal = mixed * inv_gate
        gated_ref[:, lanes] = (normal * gain).astype(BF16)
        gain_ref[:, lanes] += jnp.sum((grad * normal).reshape(-1, 8, LANES), axis=0)
        mixed_grad = inv_gate * (grad * gain - mixed * pull)
        gate_low_ref[:, lanes] = (mixed_grad * turn_ref[:, lanes].astype(F32)).astype(BF16)
        dscan_ref[:, lanes] = (mixed_grad * act_ref[:, lanes].astype(F32)).astype(BF16)
    out_total[...] += dot_first(gated_ref[...], cotan_ref[...])

    @pl.when(block == pl.num_programs(0) - 1)
    def _():
        store_halves(out_total, 0, out_total.shape[0], low_ref[0], sent_ref, kept_ref)


def weight_kernel(low_ref, normed_ref, grad_ref, sent_ref, kept_ref, total):
    block = pl.program_id(0)
    part = dot_first(normed_ref[...], grad_ref[...])

    @pl.when(block == 0)
    def _():
        total[...] = part

    @pl.when(block > 0)
    def _():
        total[...] += part

    @pl.when(block == pl.num_programs(0) - 1)
    def _():
        store_halves(total, 0, total.shape[0], low_ref[1], sent_ref, kept_ref)


def backward_kernel(
    head_count,
    low_ref,
    dscan_ref,
    scan_ref,
    value_ref,
    slope_ref,
    inner_ref,
    step_ref,
    cum_ref,
    bc_ref,
    enter_ref,
    normed_ref,
    conv_x_ref,
    head_ref,
    token_ref,
    state_part_ref,
    inner_low_ref,
    step_low_ref,
    channel_grad_ref,
    head_grad_ref,
    step_rows_ref,
    first_sent_ref,
    first_kept_ref,
    second_sent_ref,
    second_kept_ref,
    later,
    leaving,
    value_total,
    step_total,
):
    block = pl.program_id(0)

    @pl.when(block == 0)
    def _():
        later[PIECE:, :] = jnp.zeros((8, later.shape[1]), F32)
        leaving[...] = jnp.zeros(leaving.shape, F32)
        channel_grad_ref[...] = jnp.zeros(channel_grad_ref.shape, F32)
        head_grad_ref[...] = jnp.zeros(head_grad_ref.shape, F32)
        value_total[...] = jnp.zeros(value_total.shape, F32)
        step_total[...] = jnp.zeros(step_total.shape, F32)

    channels = inner_ref.shape[1]
    row_at = lax.broadcasted_iota(jnp.int32, (PIECE, PIECE), 0)
    col_at = lax.broadcasted_iota(jnp.int32, (PIECE, PIECE), 1)
    upper_ones = (row_at <= col_at).astype(F32)
    first_half = lax.broadcasted_iota(jnp.int32, (PIECE, LANES), 1) < LANES // 2
    heads = head_table(channels, head_count)
    skips = head_rows(head_ref, heads)[2:3, :]
    side_all = token_ref[...].T
    heads_twice = jnp.concatenate([heads, heads], axis=0)
    for piece in reversed(range(BLOCK // PIECE)):
        rows = slice(piece * PIECE, (piece + 1) * PIECE)
        side = side_all[rows]
        step_in = step_ref[rows, :]
        step = jnp.maximum(step_in, 0.0) + jnp.log1p(jnp.exp(-jnp.abs(step_in)))
        cum = cum_ref[rows, :]
        cum_t = cum.T
        same = (side[:, 0:1] == token_ref[0:1, rows]) & (row_at <= col_at)
        bias = jnp.where(same, 0.0, -1e30)
        reach = jnp.exp2(cum) * side[:, 4:5]
        tail = jnp.exp2(cum[PIECE - 1 : PIECE, :] - cum) * side[:, 5:6]
        wide = spread_heads(jnp.concatenate([step, reach, tail], axis=0), heads_twice)
        b_low = bc_ref[rows, 0:STATE]
        c_low = bc_ref[rows, STATE : 2 * STATE]
        scores = dot_last(b_low, c_low)
        score_grad = jnp.zeros((PIECE, PIECE), F32)
        b_grad = jnp.zeros((PIECE, STATE), F32)
        c_grad = jnp.zeros((PIECE, STATE), F32)
        row_sum = jnp.zeros((PIECE, LANES), F32)
        value_sum = jnp.zeros((PIECE, LANES), F32)
        last_sum = jnp.zeros((8, LANES), F32)
        masks = [None] + [side[:, 5 + k : 6 + k] for k in range(1, CONV)]
        for pair in range(channels // LANES):
            lanes = slice(pair * LANES, (pair + 1) * LANES)
            own_heads = heads[:, lanes]
            values = value_ref[rows, lanes].astype(F32)
            dy_low = dscan_ref[rows, lanes]
            dy = dy_low.astype(F32)
            wide_step = wide[0:PIECE, lanes]
            wide_reach = wide[PIECE : 2 * PIECE, lanes]
            wide_tail = wide[2 * PIECE :, lanes]
            low = (wide_step * values).astype(BF16)
            low_wide = low.astype(F32)
            leave = leaving[:, lanes]
            leave_low = leave.astype(BF16)
            enter = enter_ref[piece, :, lanes]
            reached = (wide_reach * dy).astype(BF16)
            tailed = (wide_tail * low_wide).astype(BF16)
            c_grad = c_grad + dot_last(reached, enter)
            b_grad = b_grad + dot_last(tailed, leave_low)
            from_state = wide_tail * dot(b_low, leave_low)
            zero = jnp.zeros_like(low)
            dy_first = jnp.where(first_half, dy_low, zero)
            dy_second = jnp.where(first_half, zero, dy_low)
            weights = []
            for head, own in ((2 * pair, dy_first), (2 * pair + 1, dy_second)):
                gaps = (cum_t[head : head + 1, :] - cum[:, head : head + 1]) + bias
                decay = jnp.exp2(gaps)
                weights.append((scores * decay).astype(BF16))
                score_grad = score_grad + dot_last(low, own) * decay
            dx = dot(jnp.concatenate(weights, axis=1), jnp.concatenate([dy_first, dy_second], axis=0))
            dx = dx + from_state
            out = scan_ref[rows, lanes] - skips[:, lanes] * values
            row_sum = row_sum + sum_heads(dy * out - low_wide * dx, own_heads)
            value_sum = value_sum + sum_heads(values * dx, own_heads)
            kept = wide[2 * PIECE - 1 : 2 * PIECE, lanes]
            last = jnp.sum(low_wide * from_state, axis=0, keepdims=True) + kept * jnp.sum(
                enter.astype(F32) * leave, axis=0, keepdims=True
            )
            last_sum = last_sum + sum_heads(jnp.broadcast_to(last, (8, LANES)), own_heads)
            leaving[:, lanes] = kept * leave + dot_first(c_low, reached)
            dvalue = wide_step * dx + skips[:, lanes] * dy
            dbefore = dvalue * slope_ref[rows, lanes].astype(F32)
            later[0:PIECE, lanes] = dbefore
            inner = inner_ref[rows, lanes].astype(F32)
            inner_grad = conv_x_ref[CONV - 1 : CONV, lanes] * dbefore
            channel_grad_ref[CONV - 1 : CONV, lanes] += jnp.sum(inner * dbefore, axis=0, keepdims=True)
            channel_grad_ref[CONV : CONV + 1, lanes] += jnp.sum(dbefore, axis=0, keepdims=True)
            channel_grad_ref[CONV + 1 : CONV + 2, lanes] += jnp.sum(dy * values, axis=0, keepdims=True)
            for k in range(1, CONV):
                shifted = later[k : k + PIECE, lanes] * masks[k]
                inner_grad = inner_grad + conv_x_ref[CONV - 1 - k : CONV - k, lanes] * shifted
                channel_grad_ref[CONV - 1 - k : CONV - k, lanes] += jnp.sum(
                    inner * shifted, axis=0, keepdims=True
                )
            inner_low_ref[rows, lanes] = inner_grad.astype(BF16)
        later[PIECE:, :] = later[0:8, :]
        grad_low = score_grad.astype(BF16)
        state_part_ref[rows, 0:STATE] = (b_grad + dot(grad_low, c_low)).astype(BF16)
        state_part_ref[rows, STATE:] = (c_grad + dot_first(grad_low, b_low)).astype(BF16)
        rate_grad = (
            jnp.dot(upper_ones, row_sum, precision=HIGH, preferred_element_type=F32) + last_sum[0:1, :]
        )
        coefficient = head_ref[1:2, :]
        step_grad = (value_sum + coefficient * rate_grad) / (1.0 + jnp.exp(-step_in))
        step_low_ref[rows, :] = step_grad.astype(BF16)
        head_grad_ref[0:1, :] += jnp.sum(step_grad, axis=0, keepdims=True)
        head_grad_ref[1:2, :] += jnp.sum(rate_grad * step, axis=0, keepdims=True) * coefficient
    value_total[...] += dot_first(normed_ref[...], inner_low_ref[...])
    step_total[...] += dot_first(step_low_ref[...], normed_ref[...])

    @pl.when(block == pl.num_programs(0) - 1)
    def _():
        half = value_total.shape[0] // 2
        store_halves(value_total, 0, half, low_ref[0], first_sent_ref, first_kept_ref)
        store_halves(value_total, half, half, low_ref[1], second_sent_ref, second_kept_ref)
        step_rows_ref[...] = step_total[0 : step_rows_ref.shape[0], :]


def merge_kernel(
    gate_low_ref,
    inner_low_ref,
    step_low_ref,
    gated_ref,
    normed_ref,
    w_gate_ref,
    w_value_ref,
    w_dt_ref,
    w_out_ref,
    both_ref,
    gain_ref,
    wide_dt,
):
    @pl.when(pl.program_id(0) == 0)
    def _():
        gain_ref[...] = jnp.zeros(gain_ref.shape, F32)
        wide_dt[...] = jnp.zeros(wide_dt.shape, BF16)
        wide_dt[0 : w_dt_ref.shape[0], :] = w_dt_ref[...]

    width = normed_ref.shape[1]
    total = dot_last(inner_low_ref[...], w_value_ref[...]) + dot_last(gate_low_ref[...], w_gate_ref[...])
    total = total + dot(step_low_ref[...], wide_dt[...])
    both_ref[:, 0:width] = total.astype(BF16)
    gain_ref[...] += jnp.sum((total * normed_ref[...].astype(F32)).reshape(-1, 8, width), axis=0)
    both_ref[:, width:] = dot(gated_ref[...], w_out_ref[...]).astype(BF16)


def state_kernel(
    rank_ref,
    total_ref,
    slope_ref,
    state_ref,
    conv_bc_ref,
    token_ref,
    w_bc_ref,
    normed_ref,
    own_part_ref,
    rows_ref,
    conv_grad_ref,
    gain_ref,
    later,
):
    rank = rank_ref[0]
    count, columns = total_ref.shape
    side = token_ref[...].T
    later[count:, :] = jnp.zeros((8, columns), F32)
    dbefore = total_ref[...].astype(F32) * slope_ref[...].astype(F32)
    later[0:count, :] = dbefore
    state = state_ref[...].astype(F32)
    grad = conv_bc_ref[CONV - 1 : CONV, :] * dbefore
    conv_grad_ref[...] = jnp.zeros(conv_grad_ref.shape, F32)
    conv_grad_ref[CONV - 1 : CONV, :] = jnp.sum(state * dbefore, axis=0, keepdims=True)
    conv_grad_ref[CONV : CONV + 1, :] = jnp.sum(dbefore, axis=0, keepdims=True)
    for k in range(1, CONV):
        shifted = later[k : k + count, :] * side[:, 5 + k : 6 + k]
        grad = grad + conv_bc_ref[CONV - 1 - k : CONV - k, :] * shifted
        conv_grad_ref[CONV - 1 - k : CONV - k, :] = jnp.sum(state * shifted, axis=0, keepdims=True)
    later[0:count, :] = grad
    own_columns = rows_ref.shape[0]
    picked = lax.broadcasted_iota(jnp.int32, (columns, own_columns), 0) == (
        lax.broadcasted_iota(jnp.int32, (columns, own_columns), 1) + rank * own_columns
    )
    own = dot(grad.astype(BF16), picked.astype(F32).astype(BF16)).astype(BF16)
    rows_ref[...] = dot_first(own, normed_ref[...])
    own_rows = own_part_ref.shape[0]
    start = pl.multiple_of(rank * own_rows, 8)
    own_part = dot_last(later[pl.ds(start, own_rows), :].astype(BF16), w_bc_ref[...])
    own_part_ref[...] = own_part
    own_normed = normed_ref[pl.ds(pl.multiple_of(start, 16), own_rows), :].astype(F32)
    gain_ref[...] = jnp.sum((own_part * own_normed).reshape(-1, 8, own_part.shape[1]), axis=0)


def pack_kernel(
    head_count,
    low_ref,
    bc_rows_ref,
    step_rows_ref,
    channel_ref,
    gate_gain_ref,
    shared_ref,
    conv_bc_ref,
    head_ref,
    sent_ref,
    kept_ref,
    packed,
):
    channels = channel_ref.shape[1]
    packed[...] = jnp.zeros(packed.shape, F32)
    at = bc_rows_ref.shape[0]
    packed[0:at, :] = bc_rows_ref[...]
    packed[at : at + 16, :] = step_rows_ref[...]
    at += 16
    for k in range(CONV):
        packed[at + k : at + k + 1, 0:channels] = channel_ref[k : k + 1, :]
    at += CONV
    packed[at : at + 1, 0:channels] = channel_ref[CONV : CONV + 1, :]
    packed[at + 1 : at + 2, 0:channels] = jnp.sum(gate_gain_ref[...], axis=0, keepdims=True)
    packed[at + 2 : at + 3, :] = shared_ref[0:1, :]
    at += 3
    states = conv_bc_ref.shape[1]
    packed[at : at + CONV + 1, 0:states] = conv_bc_ref[0 : CONV + 1, :]
    at += CONV + 1
    skips = sum_heads(channel_ref[...], head_table(channels, head_count))
    packed[at : at + 2, 0:LANES] = head_ref[0:2, :]
    packed[at + 2 : at + 3, 0:LANES] = skips[CONV + 1 : CONV + 2, :]
    store_halves(packed, 0, packed.shape[0], low_ref[0], sent_ref, kept_ref)


def whole(shape):
    return pl.BlockSpec(shape, lambda i: (0,) * len(shape), pipeline_mode=pl.Buffered(1))


def no_cost():
    return pl.CostEstimate(flops=0, bytes_accessed=0, transcendentals=0)


def params():
    return pltpu.CompilerParams(vmem_limit_bytes=60 << 20)


def run_tables(segments, pre_gain, bias_x, gate_gain, bias_bc, dt_bias, a_log, d_skip):
    inputs = (segments, pre_gain, bias_x, gate_gain, bias_bc, dt_bias, a_log, d_skip)
    in_vmem = pl.BlockSpec(memory_space=pltpu.VMEM)
    return pl.pallas_call(
        table_kernel,
        in_specs=[in_vmem] * len(inputs),
        out_specs=[in_vmem] * 3,
        out_shape=[
            jax.ShapeDtypeStruct((16, segments.size), F32),
            jax.ShapeDtypeStruct((8, pre_gain.shape[0]), F32),
            jax.ShapeDtypeStruct((8, LANES), F32),
        ],
        compiler_params=params(),
        name="tables",
    )(*inputs)


def run_forward(hidden_in, cotangent, weights, tables, tokens):
    rows, width = hidden_in.shape
    channels = weights[0].shape[1]
    states = weights[2].shape[1]
    constants = (*weights, *tables)

    def block(columns):
        return pl.BlockSpec((BLOCK, columns), lambda i: (i, 0))

    def out(columns, kind=BF16):
        return jax.ShapeDtypeStruct((rows, columns), kind)

    return pl.pallas_call(
        forward_kernel,
        grid=(rows // BLOCK,),
        in_specs=[block(width), block(width)]
        + [whole(array.shape) for array in constants]
        + [pl.BlockSpec((tokens.shape[0], BLOCK), lambda i: (0, i))],
        out_specs=[block(width)]
        + [block(channels)] * 8
        + [block(LANES)] * 2
        + [block(states)] * 3
        + [
            pl.BlockSpec((BLOCK // PIECE, STATE, channels), lambda i: (i, 0, 0)),
            pl.BlockSpec((8, BLOCK), lambda i: (0, i)),
        ],
        out_shape=[
            out(width),
            out(channels),
            out(channels),
            out(channels),
            out(channels),
            out(channels, F32),
            out(channels),
            out(channels),
            out(channels),
            out(LANES, F32),
            out(LANES, F32),
            out(states),
            out(states),
            out(states),
            jax.ShapeDtypeStruct((rows // PIECE, STATE, channels), BF16),
            jax.ShapeDtypeStruct((8, rows), F32),
        ],
        scratch_shapes=[
            pltpu.VMEM((BLOCK + 8, channels), F32),
            pltpu.VMEM((BLOCK + 8, states), F32),
            pltpu.VMEM((STATE, channels), F32),
            pltpu.VMEM((LANES, width), BF16),
            pltpu.VMEM((BLOCK, channels), F32),
            pltpu.VMEM((BLOCK, channels), F32),
        ],
        compiler_params=params(),
        cost_estimate=no_cost(),
        name="forward",
    )(hidden_in, cotangent, *constants, tokens)


def scalar_spec():
    return pl.BlockSpec(memory_space=pltpu.SMEM)


def half_shapes(rows, columns):
    return [jax.ShapeDtypeStruct((rows // 2, columns), BF16)] * 2


def run_gate(low, forward, sums, rows_table, cotangent):
    rows, channels = forward[0].shape
    width = cotangent.shape[1]

    def block(columns):
        return pl.BlockSpec((BLOCK, columns), lambda i: (i, 0))

    shape = jax.ShapeDtypeStruct((rows, channels), BF16)
    halves = half_shapes(channels, width)
    out = pl.pallas_call(
        gate_kernel,
        grid=(rows // BLOCK,),
        in_specs=[scalar_spec()]
        + [block(channels)] * 4
        + [pl.BlockSpec((8, BLOCK), lambda i: (0, i)), whole(rows_table.shape), block(width)],
        out_specs=[block(channels)] * 3
        + [whole((8, channels))]
        + [whole(half.shape) for half in halves],
        out_shape=[shape, shape, shape, jax.ShapeDtypeStruct((8, channels), F32)] + halves,
        scratch_shapes=[pltpu.VMEM((channels, width), F32)],
        compiler_params=params(),
        cost_estimate=no_cost(),
        name="gate",
    )(low, *forward, sums, rows_table, cotangent)
    return out[:4], out[4:]


def run_weight(low, normed, grad):
    rows, width = normed.shape
    channels = grad.shape[1]
    size = 2 * BLOCK
    halves = half_shapes(width, channels)
    return pl.pallas_call(
        weight_kernel,
        grid=(rows // size,),
        in_specs=[
            scalar_spec(),
            pl.BlockSpec((size, width), lambda i: (i, 0)),
            pl.BlockSpec((size, channels), lambda i: (i, 0)),
        ],
        out_specs=[whole(half.shape) for half in halves],
        out_shape=halves,
        scratch_shapes=[pltpu.VMEM((width, channels), F32)],
        compiler_params=params(),
        cost_estimate=no_cost(),
        name="weight",
    )(low, normed, grad)


def run_backward(low, by_channel, step_in, cum, bc_low, enter, normed, conv_x, head_values, tokens, head_count):
    rows, channels = by_channel[0].shape
    width = normed.shape[1]
    count = rows // BLOCK
    states = bc_low.shape[1]

    def block(columns):
        return pl.BlockSpec((BLOCK, columns), lambda i: (count - 1 - i, 0))

    def low_rows(columns):
        return jax.ShapeDtypeStruct((rows, columns), BF16)

    halves = half_shapes(width // 2, channels) * 2
    step_rows = jax.ShapeDtypeStruct((16, width), F32)
    out = pl.pallas_call(
        functools.partial(backward_kernel, head_count),
        grid=(count,),
        in_specs=[scalar_spec()]
        + [block(channels)] * 5
        + [block(LANES), block(LANES), block(states)]
        + [pl.BlockSpec((BLOCK // PIECE, STATE, channels), lambda i: (count - 1 - i, 0, 0))]
        + [block(width), whole(conv_x.shape), whole(head_values.shape)]
        + [pl.BlockSpec((tokens.shape[0], BLOCK), lambda i: (0, count - 1 - i))],
        out_specs=[block(states), block(channels), block(LANES)]
        + [whole((8, channels)), whole((8, LANES)), whole(step_rows.shape)]
        + [whole(half.shape) for half in halves],
        out_shape=[
            low_rows(states),
            low_rows(channels),
            low_rows(LANES),
            jax.ShapeDtypeStruct((8, channels), F32),
            jax.ShapeDtypeStruct((8, LANES), F32),
            step_rows,
        ]
        + halves,
        scratch_shapes=[
            pltpu.VMEM((PIECE + 8, channels), F32),
            pltpu.VMEM((STATE, channels), F32),
            pltpu.VMEM((width, channels), F32),
            pltpu.VMEM((LANES, width), F32),
        ],
        compiler_params=params(),
        cost_estimate=no_cost(),
        name="backward",
    )(low, *by_channel, step_in, cum, bc_low, enter, normed, conv_x, head_values, tokens)
    return out[:6], out[6:]


def run_merge(gate_low, inner_low, step_low, gated, normed, weights):
    rows, width = normed.shape
    blocked = (gate_low, inner_low, step_low, gated, normed)

    def block(columns):
        return pl.BlockSpec((BLOCK, columns), lambda i: (i, 0))

    return pl.pallas_call(
        merge_kernel,
        grid=(rows // BLOCK,),
        in_specs=[block(array.shape[1]) for array in blocked] + [whole(weight.shape) for weight in weights],
        out_specs=[block(2 * width), whole((8, width))],
        out_shape=[
            jax.ShapeDtypeStruct((rows, 2 * width), BF16),
            jax.ShapeDtypeStruct((8, width), F32),
        ],
        scratch_shapes=[pltpu.VMEM((LANES, width), BF16)],
        compiler_params=params(),
        cost_estimate=no_cost(),
        name="merge",
    )(*blocked, *weights)


def run_states(rank, total, slope, state_pre, conv_bc, tokens, w_bc, normed, ranks):
    rows, columns = total.shape
    width = normed.shape[1]
    in_vmem = pl.BlockSpec(memory_space=pltpu.VMEM)
    return pl.pallas_call(
        state_kernel,
        in_specs=[scalar_spec()] + [in_vmem] * 7,
        out_specs=[in_vmem] * 4,
        out_shape=[
            jax.ShapeDtypeStruct((rows // ranks, width), F32),
            jax.ShapeDtypeStruct((columns // ranks, width), F32),
            jax.ShapeDtypeStruct((8, columns), F32),
            jax.ShapeDtypeStruct((8, width), F32),
        ],
        scratch_shapes=[pltpu.VMEM((rows + 8, columns), F32)],
        compiler_params=params(),
        cost_estimate=no_cost(),
        name="states",
    )(rank, total, slope, state_pre, conv_bc, tokens, w_bc, normed)


def run_pack(low, bc_rows, step_rows, channel_grads, gain_rows, shared, conv_bc_grads, head_grads, head_count):
    width = bc_rows.shape[1]
    in_vmem = pl.BlockSpec(memory_space=pltpu.VMEM)
    return pl.pallas_call(
        functools.partial(pack_kernel, head_count),
        in_specs=[scalar_spec()] + [in_vmem] * 7,
        out_specs=[in_vmem] * 2,
        out_shape=half_shapes(PACKED, width),
        scratch_shapes=[pltpu.VMEM((PACKED, width), F32)],
        compiler_params=params(),
        cost_estimate=no_cost(),
        name="pack",
    )(low, bc_rows, step_rows, channel_grads, gain_rows, shared, conv_bc_grads, head_grads)


def swap(array, axis, bit):
    size = lax.axis_size(axis)
    return lax.ppermute(array, axis, [(source, source ^ bit) for source in range(size)])


def axis_bits(axis):
    size = lax.axis_size(axis)
    return [1 << place for place in range(size.bit_length() - 1)]


def half_of(array, which):
    half = array.shape[0] // 2
    return lax.dynamic_slice_in_dim(array, which * half, half, 0)


def sum_tensor_low_steps(array):
    size = lax.axis_size("tensor")
    for bit in axis_bits("tensor"):
        got = yield array, "tensor", [(i, i ^ bit) for i in range(size)]
        array = (array.astype(F32) + got.astype(F32)).astype(BF16)
    return array


def sum_tensor(array):
    for bit in axis_bits("tensor"):
        array = array + swap(array, "tensor", bit)
    return array


def sum_tensor_steps(array):
    size = lax.axis_size("tensor")
    for bit in axis_bits("tensor"):
        got = yield array, "tensor", [(i, i ^ bit) for i in range(size)]
        array = array + got
    return array


def sum_steps(sent, kept, bits):
    size = lax.axis_size("dp")
    place = lax.axis_index("dp")
    mine = [(place // bit) % 2 for bit in bits]
    moves = [[(i, i ^ bit) for i in range(size)] for bit in bits]
    got = yield sent, "dp", moves[0]
    part = kept.astype(F32) + got.astype(F32)
    for which, pairs in zip(mine[1:], moves[1:]):
        got = yield half_of(part, 1 - which).astype(BF16), "dp", pairs
        part = half_of(part, which) + got.astype(F32)
    part = part.astype(BF16)
    for which, pairs in reversed(list(zip(mine[1:], moves[1:]))):
        got = yield part, "dp", pairs
        part = jnp.concatenate([jnp.where(which == 0, part, got), jnp.where(which == 0, got, part)])
    got = yield part, "dp", moves[0]
    return jnp.where(mine[0] == 0, part, got), jnp.where(mine[0] == 0, got, part)


class Order:
    def __init__(self, token):
        self.token = token
        self.waiting = {}
        self.flying = {}
        self.results = {}

    def mark(self, *arrays):
        out = lax.optimization_barrier((self.token, *arrays))
        self.token = out[0]
        return out[1] if len(arrays) == 1 else out[1:]

    def run(self, function, *arrays):
        out = function(*(self.mark(*arrays) if len(arrays) > 1 else [self.mark(*arrays)]))
        return self.mark(*out) if isinstance(out, (tuple, list)) else self.mark(out)

    def advance(self, name, steps, got):
        try:
            self.waiting[name] = (steps, steps.send(got))
        except StopIteration as end:
            self.results[name] = end.value

    def add(self, name, steps):
        self.advance(name, steps, None)

    def go(self, *names):
        for name in names:
            if name in self.waiting:
                steps, (sent, axis, moves) = self.waiting.pop(name)
                self.flying[name] = (steps, lax.ppermute(self.mark(sent), axis, moves))

    def land(self, *names):
        names = [name for name in names if name in self.flying]
        if names:
            found = [self.flying.pop(name) for name in names]
            marked = lax.optimization_barrier((self.token, *[got for _, got in found]))
            self.token = marked[0]
            for name, (steps, _), got in zip(names, found, marked[1:]):
                self.advance(name, steps, got)

    def step(self, *names):
        for name in names:
            self.land(name)
            self.go(name)

    def follow(self, *moves):
        for move in moves:
            (self.go if move[0] == "+" else self.land)(move[1:])

    def finish_all(self):
        while self.flying or self.waiting:
            self.go(*list(self.waiting))
            self.land(*list(self.flying))


MOVES = (
    ("+o", "+w", "+g", "+st"),
    ("-st", "-o", "+st", "+v", "-g", "+o", "+g", "-w", "-st"),
    ("-v", "+v", "-o", "+w", "+o", "-g", "+g"),
    ("+sh", "-v", "-sh", "+sh", "-w", "-o", "+o", "-sh"),
    ("+sm", "+v", "-g", "-sm", "+w", "-o", "+g", "+sm", "-v", "+v", "+o", "-sm", "+sm", "-w", "+w", "-v", "+v", "-sm", "-g", "+sm", "+g", "-v", "-w", "+w", "+v", "-sm", "+sm", "-w", "+w"),
    ("-sm", "+sm", "-v", "-g", "-sm", "-o", "-w"),
)


def shards(
    hidden_in,
    pre_gain,
    w_gate,
    w_value,
    w_bc,
    w_dt,
    conv_x,
    conv_x_bias,
    conv_bc,
    conv_bc_bias,
    dt_bias,
    a_log,
    d_skip,
    gate_gain,
    w_out,
    cotangent,
    segments,
):
    row_count, width = hidden_in.shape
    channels = w_gate.shape[1]
    head_count = dt_bias.shape[0]
    head_width = channels // head_count
    ranks = lax.axis_size("tensor")
    my_rank = lax.axis_index("tensor")
    own_rows = row_count // ranks
    row_start = my_rank * own_rows
    pair_width = w_bc.shape[1] // ranks
    bits = axis_bits("dp")
    crossed = [bits[1], bits[0]] + bits[2:]
    place = lax.axis_index("dp").astype(jnp.int32)
    low_bits = jnp.stack([place % 2, (place // 2) % 2])
    w_dt_rows = w_dt.T
    tokens, rows_table, head_values = run_tables(
        segments, pre_gain, conv_x_bias, gate_gain, conv_bc_bias, dt_bias, a_log, d_skip
    )
    (
        normed,
        mixed,
        act,
        turn,
        gated_grad,
        scan,
        values,
        slope,
        inner_pre,
        step_in,
        cum,
        bc_low,
        bc_slope,
        state_pre,
        enter,
        sums,
    ) = run_forward(
        hidden_in,
        cotangent,
        (w_gate, w_value, w_bc, w_dt_rows, w_out),
        (conv_x, conv_bc, rows_table, head_values),
        tokens,
    )
    sums = sum_tensor(sums) / (channels * ranks)
    (gated, gate_low, dscan, gain_rows), out_halves = run_gate(
        low_bits, (mixed, act, turn, gated_grad), sums, rows_table, cotangent
    )
    order = Order(sums[0, 0])
    order.add("o", sum_steps(*out_halves, bits))
    order.go("o")
    order.add("g", sum_steps(*order.mark(*run_weight(low_bits, normed, order.mark(gate_low))), crossed))
    order.go("g")
    (state_part, inner_low, step_low, channel_grads, head_grads, step_rows), value_halves = run_backward(
        low_bits,
        (order.mark(dscan), scan, values, slope, inner_pre),
        step_in,
        cum,
        bc_low,
        enter,
        normed,
        conv_x,
        head_values,
        tokens,
        head_count,
    )
    state_part, *value_halves = order.mark(state_part, *value_halves)
    order.land("o", "g")
    order.add("v", sum_steps(*value_halves[:2], bits))
    order.add("w", sum_steps(*value_halves[2:], crossed))
    order.add("st", sum_tensor_low_steps(state_part))
    order.follow(*MOVES[0])
    both, gain_first = order.mark(
        *run_merge(
            *order.mark(gate_low, inner_low, step_low, gated),
            normed,
            (w_gate, w_value, w_dt_rows, w_out),
        )
    )
    both_own = lax.psum_scatter(both, "tensor", scatter_dimension=0, tiled=True)
    order.follow(*MOVES[1])
    pair_part, bc_rows, conv_bc_grads, gain_second = order.mark(
        *run_states(
            jnp.reshape(my_rank.astype(jnp.int32), (1,)),
            order.mark(order.results["st"]),
            bc_slope,
            state_pre,
            conv_bc,
            tokens,
            w_bc,
            normed,
            ranks,
        )
    )
    order.follow(*MOVES[2])
    gain_part = jnp.sum(gain_first + gain_second, axis=0, keepdims=True) / rows_table[0:1]
    order.add("sh", sum_tensor_steps(order.mark(gain_part)))
    order.follow(*MOVES[3])
    packed_halves = run_pack(
        low_bits,
        bc_rows,
        step_rows,
        channel_grads,
        gain_rows,
        order.results["sh"],
        conv_bc_grads,
        head_grads,
        head_count,
    )
    order.add("sm", sum_steps(*packed_halves, bits))
    order.follow(*MOVES[4])
    own_hidden, own_cotan, both_own = order.mark(
        lax.dynamic_slice_in_dim(hidden_in, row_start, own_rows, 0),
        lax.dynamic_slice_in_dim(cotangent, row_start, own_rows, 0),
        both_own,
    )
    own_hidden = own_hidden.astype(F32)
    block_out = (own_hidden + both_own[:, width:].astype(F32)).astype(BF16)
    own_inv = lax.rsqrt(jnp.mean(own_hidden * own_hidden, axis=-1, keepdims=True) + EPS)
    gain_scaled = (both_own[:, :width].astype(F32) + pair_part) * pre_gain
    own_dot = jnp.sum(gain_scaled * own_hidden, axis=-1, keepdims=True)
    hidden_grad = (
        own_cotan.astype(F32)
        + own_inv * gain_scaled
        - own_hidden * (own_inv * own_inv * own_inv) * own_dot / width
    )
    block_out, hidden_grad = order.mark(block_out, hidden_grad)
    order.follow(*MOVES[5])
    order.finish_all()
    w_out_sum = jnp.concatenate(order.results["o"]).astype(F32)
    w_gate_sum = jnp.concatenate(order.results["g"]).astype(F32)
    w_value_sum = jnp.concatenate([*order.results["v"], *order.results["w"]]).astype(F32)
    packed = jnp.concatenate(order.results["sm"]).astype(F32)
    at = pair_width + 16
    end = at + CONV + 3
    heads_at = end + CONV + 1
    states = w_bc.shape[1]
    return (
        block_out,
        hidden_grad,
        packed[at + CONV + 2],
        w_gate_sum,
        w_value_sum,
        packed[:pair_width].T,
        packed[pair_width : pair_width + head_count].T,
        packed[at : at + CONV, :channels],
        packed[at + CONV, :channels],
        packed[end : end + CONV, :states],
        packed[end + CONV, :states],
        packed[heads_at, :head_count],
        packed[heads_at + 1, :head_count],
        packed[heads_at + 2, :head_count],
        packed[at + CONV + 1, :channels],
        w_out_sum,
    )


def solution(mesh):
    in_specs = (
        P("dp", None),
        P(),
        P(None, "tensor"),
        P(None, "tensor"),
        P(),
        P(None, "tensor"),
        P(None, "tensor"),
        P("tensor"),
        P(),
        P(),
        P("tensor"),
        P("tensor"),
        P("tensor"),
        P("tensor"),
        P("tensor", None),
        P("dp", None),
        P("dp", None),
    )
    out_specs = (
        P(("dp", "tensor"), None),
        P(("dp", "tensor"), None),
        P(),
        P(None, "tensor"),
        P(None, "tensor"),
        P(None, "tensor"),
        P(None, "tensor"),
        P(None, "tensor"),
        P("tensor"),
        P(),
        P(),
        P("tensor"),
        P("tensor"),
        P("tensor"),
        P("tensor"),
        P("tensor", None),
    )
    return jax.shard_map(shards, mesh=mesh, in_specs=in_specs, out_specs=out_specs, check_vma=False)
```

time: 454 us -> 308 us (0.68); the launches traced: 445 us -> 307 us
  waiting for transfers between devices: 211 us -> 95.6 us
  Pallas kernels: 55 us -> 101 us
  matrix products: 37.8 us -> 0 us
  local copies, waits for them, and re-layouts: 47.5 us -> 10.6 us
  between operations: 2.51 us -> 14.7 us
  starting transfers between devices: 53.7 us -> 46.7 us
    ppermute x52 -> x2, waiting for transfers between devices: 211 us -> 2.38 us  [swap(): lax.ppermute(array, axis, [(source, source ^ bit) for source in range(siz...]
    ppermute x0 -> x34, waiting for transfers between devices: none -> 93.3 us  [go(): self.flying[name] = (steps, lax.ppermute(self.mark(sent), axis, moves))]
    ppermute x52 -> x2, starting transfers between devices: 53.7 us -> 3.35 us  [swap(): lax.ppermute(array, axis, [(source, source ^ bit) for source in range(siz...]
    pallas_call x2 -> x7, Pallas kernels: 28.7 us -> 73.9 us  [the longest x1 30.9 us: run_backward(): pl.pallas_call(functools.partial(backward_kernel, head_count), grid=(coun...]
    ppermute x0 -> x34, starting transfers between devices: none -> 43.3 us  [go(): self.flying[name] = (steps, lax.ppermute(self.mark(sent), axis, moves))]
    dot_general x10 -> x0, matrix products: 37.8 us -> none  [the longest x1 10.2 us: shards(): lax.dot_general(gate_low, w_gate, contract_last, preferred_element_type=F32)]
    slice x14 -> x0, local copies, waits for them, and re-layouts: 10.7 us -> none  [the longest x3 4.28 us: sum_rows(): first = sum_over(array[:cut], 'dp', bits)]
    convert_element_type x24 -> x9, local copies, waits for them, and re-layouts: 12.5 us -> 3.23 us  [sum_steps(): got = (yield (half_of(part, 1 - which).astype(BF16), 'dp', pairs))]
  transfers between devices with their start and end apart: 52 -> 37, of which waited for: 37 -> 16; matrix products, arithmetic and copies ran while one was open for 15% -> 12% of each run, Pallas kernels for 0% -> 18%
where the time goes in v3:
time: 308 us; the launch traced here: 307 us
  Pallas kernels  101 us (33%)
  waiting for transfers between devices  95.6 us (31%)
  starting transfers between devices  46.7 us (15%)
  other arithmetic  38.7 us (13%)
  between operations  14.7 us (5%)
  local copies, waits for them, and re-layouts  10.6 us (3%)
    ppermute x34, waiting for transfers between devices, go(): self.flying[name] = (steps, lax.ppermute(self.mark(sent), axis, moves))  93.3 us
    ppermute x34, starting transfers between devices, go(): self.flying[name] = (steps, lax.ppermute(self.mark(sent), axis, moves))  43.3 us
    pallas_call x1, Pallas kernels, run_backward(): pl.pallas_call(functools.partial(backward_kernel, head_count), grid=(coun...  30.9 us
    pallas_call x1, Pallas kernels, run_forward(): pl.pallas_call(forward_kernel, grid=(rows // BLOCK,), in_specs=[block(wid...  26.7 us
    pallas_call x1, Pallas kernels, run_merge(): pl.pallas_call(merge_kernel, grid=(rows // BLOCK,), in_specs=[block(array...  14.2 us
    pallas_call x1, Pallas kernels, run_gate(): pl.pallas_call(gate_kernel, grid=(rows // BLOCK,), in_specs=[scalar_spec(...  11.4 us
    pallas_call x1, Pallas kernels, run_weight(): pl.pallas_call(weight_kernel, grid=(rows // size,), in_specs=[scalar_spec...  7.07 us
    pallas_call x1, Pallas kernels, run_states(): pl.pallas_call(state_kernel, in_specs=[scalar_spec()] + [in_vmem] * 7, ou...  6.61 us
  transfers between devices with their start and end apart: 37, of which 16 were waited for; matrix products, arithmetic and copies ran while one was open for 12% of the time, Pallas kernels for 18%

profile of v3, /device:TPU:0, one launch (start us, length us, event | category | flops | bytes accessed | tf_op | source)
XLA Modules:
  0.0 306.9 jit_solution(6640570099860238116)
XLA Ops:
  8.7 26.7 %forward.1 = (bf16[1024,1536]{1,0:T(8,128)(2,1)}, bf16[1024,768]{1,0:T(8,128)(2,1)}, bf16[1024,768]{1,0:T(8,128)(2,1)}, bf16[1024,768]{1,0:T(8,128)(2,1)}, bf16[...) custom-call(bf16[1024,1536]{1,0:T(8,128)(2,1)} %hidden_ref.1, ...), custom_call_target="tpu_custom_call" | custom-call | tf_op jit(solution)/shard_map/forward/pallas_call | solution.py:652
  37.8 2.8 collective-permute-start.1
  43.2 11.4 %gate.1 = (bf16[1024,768]{1,0:T(8,128)(2,1)}, bf16[1024,768]{1,0:T(8,128)(2,1)}, bf16[1024,768]{1,0:T(8,128)(2,1)}, f32[8,768]{1,0:T(8,128)}, bf16[384,1536]{1,0:T(8,128)(2,1)}, /*index=5*/bf16[384,1536]{1,0:T(8,128)(2,1)}) custom-call(s32[2]{0:T(128)} %pad_add_fusion.low_ref, bf16[1024,768]{1,0:T(8,128)(2,1)} %get-tuple-element.209.mixed_ref, ...), custom_call_target="tpu_custom_call" | custom-call | tf_op jit(solution)/shard_map/gate/pallas_call | solution.py:715
  54.6 7.1 %weight.1 = (bf16[768,768]{1,0:T(8,128)(2,1)}, bf16[768,768]{1,0:T(8,128)(2,1)}) custom-call(s32[2]{0:T(128)} %pad_add_fusion.low_ref, bf16[1024,1536]{1,0:T(8,128)(2,1)} %get-tuple-element.217.normed_ref, bf16[1024,768]{1,0:T(8,128)(2,1)} %get-tuple-element.258.grad_ref.gate_low_ref), custom_call_target="tpu_custom_call" | custom-call | tf_op jit(solution)/shard_map/weight/pallas_call | solution.py:738
  65.3 30.9 %backward.1 = (bf16[1024,256]{1,0:T(8,128)(2,1)}, bf16[1024,768]{1,0:T(8,128)(2,1)}, bf16[1024,128]{1,0:T(8,128)(2,1)}, f32[8,768]{1,0:T(8,128)}, f32[8,128]{1,0...) custom-call(s32[2]{0:T(128)} %pad_add_fusion.low_ref, ...), custom_call_target="tpu_custom_call" | custom-call | tf_op jit(solution)/shard_map/backward/pallas_call | solution.py:769
  102.7 14.2 %merge.1 = (bf16[1024,3072]{1,0:T(8,128)(2,1)}, f32[8,1536]{1,0:T(8,128)}) custom-call(bf16[1024,768]{1,0:T(8,128)(2,1)} %get-tuple-element.258.grad_ref.gate_low_ref, bf16[1024,768]{1,0:T(8,128)(2,1)} %get-tuple-element.259.inner_low_ref, bf16[1024,128]{1,0:T(8,128)(2,1)} %get-tuple-element.260.step_low_ref, ...), custom_call_target="tpu_custom_call" | custom-call | tf_op jit(solution)/shard_map/merge/pallas_call | solution.py:810
  125.1 7.4 %collective-permute-done.7 = bf16[384,768]{1,0:T(8,128)(2,1)S(1)} collective-permute-done((bf16[384,768]{1,0:T(8,128)(2,1)}, bf16[384,768]{1,0:T(8,128)(2,1)S(1)}, u32[]{:S(2)}, u32[]{:S(2)}) %collective-permute-start.7) | collective-permute-done | bytes 589856 | tf_op jit(solution)/shard_map/ppermute | solution.py:946
  138.9 6.6 %states.1 = (f32[256,1536]{1,0:T(8,128)}, f32[64,1536]{1,0:T(8,128)}, f32[8,256]{1,0:T(8,128)}, f32[8,1536]{1,0:T(8,128)}) custom-call(s32[1]{0:T(128)} %bitcast.4.rank_ref, bf16[1024,256]{1,0:T(8,128)(2,1)} %add_convert_fusion.total_ref, bf16[1024,256]{1,0:T(8,128)(2,1)} %get-tuple-element.290.slope_ref, bf16[1024,256]{1,0:T(8,128)(2,1)} %get-tuple-element.291.state_ref, ...), custom_call_target="tpu_custom_call" | custom-call | tf_op jit(solution)/shard_map/states/pallas_call | solution.py:830
  149.4 7.2 %collective-permute-done.10 = bf16[96,1536]{1,0:T(8,128)(2,1)} collective-permute-done((bf16[96,1536]{1,0:T(8,128)(2,1)S(1)}, bf16[96,1536]{1,0:T(8,128)(2,1)}, u32[]{:S(2)}, u32[]{:S(2)}) %collective-permute-start.10) | collective-permute-done | bytes 294944 | tf_op jit(solution)/shard_map/ppermute | solution.py:946
  157.7 4.1 %collective-permute-done.11 = bf16[192,768]{1,0:T(8,128)(2,1)} collective-permute-done((bf16[192,768]{1,0:T(8,128)(2,1)}, bf16[192,768]{1,0:T(8,128)(2,1)}, u32[]{:S(2)}, u32[]{:S(2)}) %collective-permute-start.11) | collective-permute-done | bytes 294944 | tf_op jit(solution)/shard_map/ppermute | solution.py:946
  162.9 3.4 %collective-permute-start.15 = (bf16[96,1536]{1,0:T(8,128)(2,1)S(1)}, bf16[96,1536]{1,0:T(8,128)(2,1)}, u32[]{:S(2)}, u32[]{:S(2)}) collective-permute-start(bf16[96,1536]{1,0:T(8,128)(2,1)S(1)} %add_convert_fusion.3), channel_id=1, source_target_pairs={{0,16},{4,20},{8,24},{12,28},{16,0},{20,4},{24,8},{28,12},{1,17},{... | collective-permute-start | bytes 884744 | tf_op jit(solution)/shard_map/ppermute | solution.py:946
  169.1 7.0 %collective-permute-done.12 = bf16[192,768]{1,0:T(8,128)(2,1)} collective-permute-done((bf16[192,768]{1,0:T(8,128)(2,1)}, bf16[192,768]{1,0:T(8,128)(2,1)}, u32[]{:S(2)}, u32[]{:S(2)}) %collective-permute-start.12) | collective-permute-done | bytes 294944 | tf_op jit(solution)/shard_map/ppermute | solution.py:946
  176.1 10.0 %collective-permute-done.15 = bf16[96,1536]{1,0:T(8,128)(2,1)} collective-permute-done((bf16[96,1536]{1,0:T(8,128)(2,1)S(1)}, bf16[96,1536]{1,0:T(8,128)(2,1)}, u32[]{:S(2)}, u32[]{:S(2)}) %collective-permute-start.15) | collective-permute-done | bytes 294944 | tf_op jit(solution)/shard_map/ppermute | solution.py:946
  198.5 2.9 collective-permute-start.20
  205.1 2.6 collective-permute-start.21
  210.8 2.8 collective-permute-start.24
  213.6 5.9 %collective-permute-done.23 = bf16[96,768]{1,0:T(8,128)(2,1)S(1)} collective-permute-done((bf16[96,768]{1,0:T(8,128)(2,1)S(1)}, bf16[96,768]{1,0:T(8,128)(2,1)S(1)}, u32[]{:S(2)}, u32[]{:S(2)}) %collective-permute-start.23) | collective-permute-done | bytes 147488 | tf_op jit(solution)/shard_map/ppermute | solution.py:946
  219.5 2.7 collective-permute-done.24
  222.4 2.8 collective-permute-start.30
  227.8 2.6 collective-permute-start.32
  230.4 6.8 %collective-permute-done.27 = bf16[32,1536]{1,0:T(8,128)(2,1)S(1)} collective-permute-done((bf16[32,1536]{1,0:T(8,128)(2,1)S(1)}, bf16[32,1536]{1,0:T(8,128)(2,1)S(1)}, u32[]{:S(2)}, u32[]{:S(2)}) %collective-permute-start.27) | collective-permute-done | bytes 98336 | tf_op jit(solution)/shard_map/ppermute | solution.py:946
  247.2 4.2 %collective-permute-done.33 = bf16[192,768]{1,0:T(8,128)(2,1)S(1)} collective-permute-done((bf16[192,768]{1,0:T(8,128)(2,1)S(1)}, bf16[192,768]{1,0:T(8,128)(2,1)S(1)}, u32[]{:S(2)}, u32[]{:S(2)}) %collective-permute-start.33) | collective-permute-done | bytes 294944 | tf_op jit(solution)/shard_map/ppermute | solution.py:946
  254.7 32.0 %collective-permute-done.31 = bf16[384,768]{1,0:T(8,128)(2,1)S(1)} collective-permute-done((bf16[384,768]{1,0:T(8,128)(2,1)S(1)}, bf16[384,768]{1,0:T(8,128)(2,1)S(1)}, u32[]{:S(2)}, u32[]{:S(2)}) %collective-permute-start.31) | collective-permute-done | bytes 589856 | tf_op jit(solution)/shard_map/ppermute | solution.py:946
  290.2 2.8 maximum_convert_fusion.2
  (175 shorter events, 85.1 us)
Async XLA Ops:
  7.2 288.9 %reduce-scatter.2.cloned.1.call-start = ((), (), s32[]{:S(2)}) async-start(), calls=%async_computation.1 | async-start | bytes 7864320 | tf_op jit(solution)/shard_map/reduce_scatter | solution.py:1077
  61.7 34.6 %collective-permute-start.3 = (bf16[768,768]{1,0:T(8,128)(2,1)}, bf16[768,768]{1,0:T(8,128)(2,1)S(1)}, u32[]{:S(2)}, u32[]{:S(2)}) collective-permute-start(bf16[768,768]{1,0:T(8,128)(2,1)} %get-tuple-element.242), channel_id=1, source_target_pairs={{0,8},{4,12},{8,0},{12,4},{16,24},{20,28},{24,16},{28,20},{1,9},{5... | collective-permute-start | bytes 3538952 | tf_op jit(solution)/shard_map/ppermute | solution.py:946
  63.8 32.5 %collective-permute-start.2 = (bf16[384,1536]{1,0:T(8,128)(2,1)S(1)}, bf16[384,1536]{1,0:T(8,128)(2,1)}, u32[]{:S(2)}, u32[]{:S(2)}) collective-permute-start(bf16[384,1536]{1,0:T(8,128)(2,1)S(1)} %copy-done.20), channel_id=1, source_target_pairs={{0,4},{4,0},{8,12},{12,8},{16,20},{20,16},{24,28},{28,24},{1,5},{5... | collective-permute-start | bytes 3538952 | tf_op jit(solution)/shard_map/ppermute | solution.py:946
  102.0 16.9 %collective-permute-start.4 = (bf16[1024,256]{1,0:T(8,128)(2,1)}, bf16[1024,256]{1,0:T(8,128)(2,1)}, u32[]{:S(2)}, u32[]{:S(2)}) collective-permute-start(bf16[1024,256]{1,0:T(8,128)(2,1)} %get-tuple-element.269), channel_id=1, source_target_pairs={{0,1},{1,0},{2,3},{3,2},{4,5},{5,4},{6,7},{7,6},{8,9},{9,8},{10,11... | collective-permute-start | bytes 1572872 | tf_op jit(solution)/shard_map/ppermute | solution.py:946
  102.1 18.2 %collective-permute-start.5 = (bf16[192,1536]{1,0:T(8,128)(2,1)S(1)}, bf16[192,1536]{1,0:T(8,128)(2,1)}, u32[]{:S(2)}, u32[]{:S(2)}) collective-permute-start(bf16[192,1536]{1,0:T(8,128)(2,1)S(1)} %dynamic-slice_convert_fusion.1), channel_id=1, source_target_pairs={{0,8},{4,12},{8,0},{12,4},{16,24},{20,28},{24,16},{28,20},{1,9},{5... | collective-permute-start | bytes 1769480 | tf_op jit(solution)/shard_map/ppermute | solution.py:946
  102.6 17.7 %collective-permute-start.6 = (bf16[384,768]{1,0:T(8,128)(2,1)S(1)}, bf16[384,768]{1,0:T(8,128)(2,1)}, u32[]{:S(2)}, u32[]{:S(2)}) collective-permute-start(bf16[384,768]{1,0:T(8,128)(2,1)S(1)} %dynamic-slice_convert_fusion), channel_id=1, source_target_pairs={{0,4},{4,0},{8,12},{12,8},{16,20},{20,16},{24,28},{28,24},{1,5},{5... | collective-permute-start | bytes 1769480 | tf_op jit(solution)/shard_map/ppermute | solution.py:946
  116.9 15.5 %collective-permute-start.7 = (bf16[384,768]{1,0:T(8,128)(2,1)}, bf16[384,768]{1,0:T(8,128)(2,1)S(1)}, u32[]{:S(2)}, u32[]{:S(2)}) collective-permute-start(bf16[384,768]{1,0:T(8,128)(2,1)} %get-tuple-element.283), channel_id=1, source_target_pairs={{0,8},{4,12},{8,0},{12,4},{16,24},{20,28},{24,16},{28,20},{1,9},{5... | collective-permute-start | bytes 1769480 | tf_op jit(solution)/shard_map/ppermute | solution.py:946
  120.2 17.7 %collective-permute-start.8 = (bf16[1024,256]{1,0:T(8,128)(2,1)S(1)}, bf16[1024,256]{1,0:T(8,128)(2,1)S(1)}, u32[]{:S(2)}, u32[]{:S(2)}) collective-permute-start(bf16[1024,256]{1,0:T(8,128)(2,1)S(1)} %add_convert_fusion.1), channel_id=1, source_target_pairs={{0,2},{1,3},{2,0},{3,1},{4,6},{5,7},{6,4},{7,5},{8,10},{9,11},{10,... | collective-permute-start | bytes 1572872 | tf_op jit(solution)/shard_map/ppermute | solution.py:946
  132.5 14.8 %collective-permute-start.9 = (bf16[384,768]{1,0:T(8,128)(2,1)}, bf16[384,768]{1,0:T(8,128)(2,1)}, u32[]{:S(2)}, u32[]{:S(2)}) collective-permute-start(bf16[384,768]{1,0:T(8,128)(2,1)} %get-tuple-element.304), channel_id=1, source_target_pairs={{0,4},{4,0},{8,12},{12,8},{16,20},{20,16},{24,28},{28,24},{1,5},{5... | collective-permute-start | bytes 1769480 | tf_op jit(solution)/shard_map/ppermute | solution.py:946
  134.2 22.5 %collective-permute-start.10 = (bf16[96,1536]{1,0:T(8,128)(2,1)S(1)}, bf16[96,1536]{1,0:T(8,128)(2,1)}, u32[]{:S(2)}, u32[]{:S(2)}) collective-permute-start(bf16[96,1536]{1,0:T(8,128)(2,1)S(1)} %dynamic-slice_convert_fusion.5), channel_id=1, source_target_pairs={{0,16},{4,20},{8,24},{12,28},{16,0},{20,4},{24,8},{28,12},{1,17},{... | collective-permute-start | bytes 884744 | tf_op jit(solution)/shard_map/ppermute | solution.py:946
  136.7 25.1 %collective-permute-start.11 = (bf16[192,768]{1,0:T(8,128)(2,1)}, bf16[192,768]{1,0:T(8,128)(2,1)}, u32[]{:S(2)}, u32[]{:S(2)}) collective-permute-start(bf16[192,768]{1,0:T(8,128)(2,1)} %dynamic-slice_convert_fusion.4), channel_id=1, source_target_pairs={{0,16},{4,20},{8,24},{12,28},{16,0},{20,4},{24,8},{28,12},{1,17},{... | collective-permute-start | bytes 884744 | tf_op jit(solution)/shard_map/ppermute | solution.py:946
  161.8 14.3 %collective-permute-start.12 = (bf16[192,768]{1,0:T(8,128)(2,1)}, bf16[192,768]{1,0:T(8,128)(2,1)}, u32[]{:S(2)}, u32[]{:S(2)}) collective-permute-start(bf16[192,768]{1,0:T(8,128)(2,1)} %dynamic-slice_convert_fusion.3), channel_id=1, source_target_pairs={{0,8},{4,12},{8,0},{12,4},{16,24},{20,28},{24,16},{28,20},{1,9},{5... | collective-permute-start | bytes 884744 | tf_op jit(solution)/shard_map/ppermute | solution.py:946
  162.4 13.6 %collective-permute-start.14 = (bf16[192,768]{1,0:T(8,128)(2,1)}, bf16[192,768]{1,0:T(8,128)(2,1)}, u32[]{:S(2)}, u32[]{:S(2)}) collective-permute-start(bf16[192,768]{1,0:T(8,128)(2,1)} %dynamic-slice_convert_fusion.2), channel_id=1, source_target_pairs={{0,4},{4,0},{8,12},{12,8},{16,20},{20,16},{24,28},{28,24},{1,5},{5... | collective-permute-start | bytes 884744 | tf_op jit(solution)/shard_map/ppermute | solution.py:946
  162.9 23.2 %collective-permute-start.15 = (bf16[96,1536]{1,0:T(8,128)(2,1)S(1)}, bf16[96,1536]{1,0:T(8,128)(2,1)}, u32[]{:S(2)}, u32[]{:S(2)}) collective-permute-start(bf16[96,1536]{1,0:T(8,128)(2,1)S(1)} %add_convert_fusion.3), channel_id=1, source_target_pairs={{0,16},{4,20},{8,24},{12,28},{16,0},{20,4},{24,8},{28,12},{1,17},{... | collective-permute-start | bytes 884744 | tf_op jit(solution)/shard_map/ppermute | solution.py:946
  169.0 27.3 %collective-permute-start.17 = (bf16[192,768]{1,0:T(8,128)(2,1)S(1)}, bf16[192,768]{1,0:T(8,128)(2,1)}, u32[]{:S(2)}, u32[]{:S(2)}) collective-permute-start(bf16[192,768]{1,0:T(8,128)(2,1)S(1)} %add_convert_fusion.2), channel_id=1, source_target_pairs={{0,16},{4,20},{8,24},{12,28},{16,0},{20,4},{24,8},{28,12},{1,17},{... | collective-permute-start | bytes 884744 | tf_op jit(solution)/shard_map/ppermute | solution.py:946
  189.5 49.9 %collective-permute-start.19 = (bf16[192,1536]{1,0:T(8,128)(2,1)}, bf16[192,1536]{1,0:T(8,128)(2,1)}, u32[]{:S(2)}, u32[]{:S(2)}) collective-permute-start(bf16[192,1536]{1,0:T(8,128)(2,1)} %pad_maximum_fusion.2), channel_id=1, source_target_pairs={{0,8},{4,12},{8,0},{12,4},{16,24},{20,28},{24,16},{28,20},{1,9},{5... | collective-permute-start | bytes 1769480 | tf_op jit(solution)/shard_map/ppermute | solution.py:946
  202.5 39.1 %collective-permute-start.25 = (bf16[384,768]{1,0:T(8,128)(2,1)S(1)}, bf16[384,768]{1,0:T(8,128)(2,1)S(1)}, u32[]{:S(2)}, u32[]{:S(2)}) collective-permute-start(bf16[384,768]{1,0:T(8,128)(2,1)S(1)} %pad_maximum_fusion.3), channel_id=1, source_target_pairs={{0,4},{4,0},{8,12},{12,8},{16,20},{20,16},{24,28},{28,24},{1,5},{5... | collective-permute-start | bytes 1769480 | tf_op jit(solution)/shard_map/ppermute | solution.py:946
  209.8 15.4 %collective-permute-start.22 = (bf16[96,768]{1,0:T(8,128)(2,1)S(1)}, bf16[96,768]{1,0:T(8,128)(2,1)S(1)}, u32[]{:S(2)}, u32[]{:S(2)}) collective-permute-start(bf16[96,768]{1,0:T(8,128)(2,1)S(1)} %copy-done.17), channel_id=1, source_target_pairs={{0,16},{4,20},{8,24},{12,28},{16,0},{20,4},{24,8},{28,12},{1,17},{... | collective-permute-start | bytes 442376 | tf_op jit(solution)/shard_map/ppermute | solution.py:946
  222.4 20.0 %collective-permute-start.30 = (bf16[192,768]{1,0:T(8,128)(2,1)S(1)}, bf16[192,768]{1,0:T(8,128)(2,1)S(1)}, u32[]{:S(2)}, u32[]{:S(2)}) collective-permute-start(bf16[192,768]{1,0:T(8,128)(2,1)S(1)} %pad_maximum_fusion.6), channel_id=1, source_target_pairs={{0,8},{4,12},{8,0},{12,4},{16,24},{20,28},{24,16},{28,20},{1,9},{5... | collective-permute-start | bytes 884744 | tf_op jit(solution)/shard_map/ppermute | solution.py:946
  238.0 13.4 %collective-permute-start.33 = (bf16[192,768]{1,0:T(8,128)(2,1)S(1)}, bf16[192,768]{1,0:T(8,128)(2,1)S(1)}, u32[]{:S(2)}, u32[]{:S(2)}) collective-permute-start(bf16[192,768]{1,0:T(8,128)(2,1)S(1)} %pad_maximum_fusion.7), channel_id=1, source_target_pairs={{0,4},{4,0},{8,12},{12,8},{16,20},{20,16},{24,28},{28,24},{1,5},{5... | collective-permute-start | bytes 884744 | tf_op jit(solution)/shard_map/ppermute | solution.py:946
  240.8 48.9 %collective-permute-start.35 = (bf16[384,1536]{1,0:T(8,128)(2,1)S(1)}, bf16[384,1536]{1,0:T(8,128)(2,1)S(1)}, u32[]{:S(2)}, u32[]{:S(2)}) collective-permute-start(bf16[384,1536]{1,0:T(8,128)(2,1)S(1)} %pad_maximum_fusion.1), channel_id=1, source_target_pairs={{0,4},{4,0},{8,12},{12,8},{16,20},{20,16},{24,28},{28,24},{1,5},{5... | collective-permute-start | bytes 3538952 | tf_op jit(solution)/shard_map/ppermute | solution.py:946
  241.9 51.2 %collective-permute-start.29 = (bf16[768,768]{1,0:T(8,128)(2,1)S(1)}, bf16[768,768]{1,0:T(8,128)(2,1)S(1)}, u32[]{:S(2)}, u32[]{:S(2)}) collective-permute-start(bf16[768,768]{1,0:T(8,128)(2,1)S(1)} %pad_maximum_fusion), channel_id=1, source_target_pairs={{0,8},{4,12},{8,0},{12,4},{16,24},{20,28},{24,16},{28,20},{1,9},{5... | collective-permute-start | bytes 3538952 | tf_op jit(solution)/shard_map/ppermute | solution.py:946
  242.5 44.2 %collective-permute-start.31 = (bf16[384,768]{1,0:T(8,128)(2,1)S(1)}, bf16[384,768]{1,0:T(8,128)(2,1)S(1)}, u32[]{:S(2)}, u32[]{:S(2)}) collective-permute-start(bf16[384,768]{1,0:T(8,128)(2,1)S(1)} %pad_maximum_fusion.4), channel_id=1, source_target_pairs={{0,4},{4,0},{8,12},{12,8},{16,20},{20,16},{24,28},{28,24},{1,5},{5... | collective-permute-start | bytes 1769480 | tf_op jit(solution)/shard_map/ppermute | solution.py:946
  251.6 35.4 %collective-permute-start.34 = (bf16[384,768]{1,0:T(8,128)(2,1)S(1)}, bf16[384,768]{1,0:T(8,128)(2,1)S(1)}, u32[]{:S(2)}, u32[]{:S(2)}) collective-permute-start(bf16[384,768]{1,0:T(8,128)(2,1)S(1)} %pad_maximum_fusion.5), channel_id=1, source_target_pairs={{0,8},{4,12},{8,0},{12,4},{16,24},{20,28},{24,16},{28,20},{1,9},{5... | collective-permute-start | bytes 1769480 | tf_op jit(solution)/shard_map/ppermute | solution.py:946
  (34 other events, 279.2 us)
Sparse Core Ops, SparseCore 0:
  169.1 56.8 reduce-scatter.1

commit v4 on v3

--- a/solution.py
+++ b/solution.py
@@ -12,7 +12,7 @@
 CONV = 4
 BLOCK = 256
 PIECE = 128
-PACKED = 128
+OWN_BC = 64
 LANES = 128
 EPS = 1e-05
 HIGH = lax.Precision.HIGHEST
@@ -203,8 +203,8 @@
         before = conv(tail_bc, conv_bc_ref, 3, lanes)
         half = sigmoid(before)
         bc_ref[:, lanes] = (before * half).astype(BF16)
-        bc_slope_ref[:, lanes] = (half * (1.0 + before * (1.0 - half))).astype(BF16)
-        state_ref[:, lanes] = tail_bc[8:, lanes].astype(BF16)
+        bc_slope_ref[:, lanes] = half * (1.0 + before * (1.0 - half))
+        state_ref[:, lanes] = tail_bc[8:, lanes]
     tail_x[0:8, :] = tail_x[BLOCK:, :]
     tail_bc[0:8, :] = tail_bc[BLOCK:, :]
 
@@ -273,10 +273,11 @@
     sums_ref[...] = jnp.where(is_first, squares, crosses)
 
 
-def store_halves(total, start, rows, mine, sent_ref, kept_ref):
-    half = rows // 2
-    sent_ref[...] = total[pl.ds(pl.multiple_of(start + (1 - mine) * half, 8), half), :].astype(BF16)
-    kept_ref[...] = total[pl.ds(pl.multiple_of(start + mine * half, 8), half), :].astype(BF16)
+def store_halves(total, columns, mine, sent_ref, kept_ref, at=0):
+    half = total.shape[0] // 2
+    to = slice(at, at + half)
+    for which, ref in ((1 - mine, sent_ref), (mine, kept_ref)):
+        ref[to, :] = total[pl.ds(pl.multiple_of(which * half, 8), half), columns].astype(BF16)
 
 
 def gate_kernel(
@@ -288,6 +289,7 @@
     sums_ref,
     row_ref,
     cotan_ref,
+    normed_ref,
     gated_ref,
     gate_low_ref,
     dscan_ref,
@@ -295,6 +297,7 @@
     sent_ref,
     kept_ref,
     out_total,
+    gate_total,
 ):
     block = pl.program_id(0)
 
@@ -302,6 +305,7 @@
     def _():
         gain_ref[...] = jnp.zeros(gain_ref.shape, F32)
         out_total[...] = jnp.zeros(out_total.shape, F32)
+        gate_total[...] = jnp.zeros(gate_total.shape, F32)
 
     row_at = lax.broadcasted_iota(jnp.int32, (8, LANES), 0)
 
@@ -326,13 +330,18 @@
         gate_low_ref[:, lanes] = (mixed_grad * turn_ref[:, lanes].astype(F32)).astype(BF16)
         dscan_ref[:, lanes] = (mixed_grad * act_ref[:, lanes].astype(F32)).astype(BF16)
     out_total[...] += dot_first(gated_ref[...], cotan_ref[...])
+    gate_total[...] += dot_first(normed_ref[...], gate_low_ref[...])
 
     @pl.when(block == pl.num_programs(0) - 1)
     def _():
-        store_halves(out_total, 0, out_total.shape[0], low_ref[0], sent_ref, kept_ref)
-
-
-def weight_kernel(low_ref, normed_ref, grad_ref, sent_ref, kept_ref, total):
+        rows, width = out_total.shape
+        for at in range(width // channels):
+            columns = slice(at * channels, (at + 1) * channels)
+            store_halves(out_total, columns, low_ref[0], sent_ref, kept_ref, at * rows // 2)
+        store_halves(gate_total, slice(None), low_ref[0], sent_ref, kept_ref, width // 2)
+
+
+def weight_kernel(low_ref, normed_ref, grad_ref, after_ref, sent_ref, kept_ref, total):
     block = pl.program_id(0)
     part = dot_first(normed_ref[...], grad_ref[...])
 
@@ -346,12 +355,11 @@
 
     @pl.when(block == pl.num_programs(0) - 1)
     def _():
-        store_halves(total, 0, total.shape[0], low_ref[1], sent_ref, kept_ref)
+        store_halves(total, slice(None), low_ref[0], sent_ref, kept_ref)
 
 
 def backward_kernel(
     head_count,
-    low_ref,
     dscan_ref,
     scan_ref,
     value_ref,
@@ -362,22 +370,24 @@
     bc_ref,
     enter_ref,
     normed_ref,
+    bc_slope_ref,
+    state_ref,
     conv_x_ref,
+    conv_bc_ref,
     head_ref,
     token_ref,
-    state_part_ref,
+    after_ref,
+    state_low_ref,
     inner_low_ref,
     step_low_ref,
     channel_grad_ref,
+    conv_bc_grad_ref,
     head_grad_ref,
     step_rows_ref,
-    first_sent_ref,
-    first_kept_ref,
-    second_sent_ref,
-    second_kept_ref,
+    bc_rows_ref,
     later,
+    later_bc,
     leaving,
-    value_total,
     step_total,
 ):
     block = pl.program_id(0)
@@ -385,10 +395,12 @@
     @pl.when(block == 0)
     def _():
         later[PIECE:, :] = jnp.zeros((8, later.shape[1]), F32)
+        later_bc[PIECE:, :] = jnp.zeros((8, later_bc.shape[1]), F32)
+        conv_bc_grad_ref[...] = jnp.zeros(conv_bc_grad_ref.shape, F32)
+        bc_rows_ref[...] = jnp.zeros(bc_rows_ref.shape, F32)
         leaving[...] = jnp.zeros(leaving.shape, F32)
         channel_grad_ref[...] = jnp.zeros(channel_grad_ref.shape, F32)
         head_grad_ref[...] = jnp.zeros(head_grad_ref.shape, F32)
-        value_total[...] = jnp.zeros(value_total.shape, F32)
         step_total[...] = jnp.zeros(step_total.shape, F32)
 
     channels = inner_ref.shape[1]
@@ -478,8 +490,23 @@
             inner_low_ref[rows, lanes] = inner_grad.astype(BF16)
         later[PIECE:, :] = later[0:8, :]
         grad_low = score_grad.astype(BF16)
-        state_part_ref[rows, 0:STATE] = (b_grad + dot(grad_low, c_low)).astype(BF16)
-        state_part_ref[rows, STATE:] = (c_grad + dot_first(grad_low, b_low)).astype(BF16)
+        state_parts = (b_grad + dot(grad_low, c_low), c_grad + dot_first(grad_low, b_low))
+        for at, state_part in enumerate(state_parts):
+            lanes = slice(at * STATE, (at + 1) * STATE)
+            dbefore = state_part * bc_slope_ref[rows, lanes]
+            later_bc[0:PIECE, lanes] = dbefore
+            state = state_ref[rows, lanes]
+            state_grad = conv_bc_ref[CONV - 1 : CONV, lanes] * dbefore
+            conv_bc_grad_ref[CONV - 1 : CONV, lanes] += jnp.sum(state * dbefore, axis=0, keepdims=True)
+            conv_bc_grad_ref[CONV : CONV + 1, lanes] += jnp.sum(dbefore, axis=0, keepdims=True)
+            for k in range(1, CONV):
+                shifted = later_bc[k : k + PIECE, lanes] * masks[k]
+                state_grad = state_grad + conv_bc_ref[CONV - 1 - k : CONV - k, lanes] * shifted
+                conv_bc_grad_ref[CONV - 1 - k : CONV - k, lanes] += jnp.sum(
+                    state * shifted, axis=0, keepdims=True
+                )
+            state_low_ref[rows, lanes] = state_grad.astype(BF16)
+        later_bc[PIECE:, :] = later_bc[0:8, :]
         rate_grad = (
             jnp.dot(upper_ones, row_sum, precision=HIGH, preferred_element_type=F32) + last_sum[0:1, :]
         )
@@ -488,32 +515,38 @@
         step_low_ref[rows, :] = step_grad.astype(BF16)
         head_grad_ref[0:1, :] += jnp.sum(step_grad, axis=0, keepdims=True)
         head_grad_ref[1:2, :] += jnp.sum(rate_grad * step, axis=0, keepdims=True) * coefficient
-    value_total[...] += dot_first(normed_ref[...], inner_low_ref[...])
     step_total[...] += dot_first(step_low_ref[...], normed_ref[...])
+    bc_rows_ref[...] += dot_first(state_low_ref[...], normed_ref[...])
 
     @pl.when(block == pl.num_programs(0) - 1)
     def _():
-        half = value_total.shape[0] // 2
-        store_halves(value_total, 0, half, low_ref[0], first_sent_ref, first_kept_ref)
-        store_halves(value_total, half, half, low_ref[1], second_sent_ref, second_kept_ref)
         step_rows_ref[...] = step_total[0 : step_rows_ref.shape[0], :]
 
 
 def merge_kernel(
+    core_ref,
     gate_low_ref,
     inner_low_ref,
     step_low_ref,
+    state_low_ref,
     gated_ref,
     normed_ref,
     w_gate_ref,
     w_value_ref,
     w_dt_ref,
+    w_bc_ref,
     w_out_ref,
-    both_ref,
+    row_ref,
+    after_ref,
+    sent_ref,
+    kept_ref,
     gain_ref,
     wide_dt,
 ):
-    @pl.when(pl.program_id(0) == 0)
+    block = pl.program_id(0)
+    last = pl.num_programs(0) - 1
+
+    @pl.when(block == 0)
     def _():
         gain_ref[...] = jnp.zeros(gain_ref.shape, F32)
         wide_dt[...] = jnp.zeros(wide_dt.shape, BF16)
@@ -521,91 +554,151 @@
 
     width = normed_ref.shape[1]
     total = dot_last(inner_low_ref[...], w_value_ref[...]) + dot_last(gate_low_ref[...], w_gate_ref[...])
-    total = total + dot(step_low_ref[...], wide_dt[...])
-    both_ref[:, 0:width] = total.astype(BF16)
+    total = total + dot_last(state_low_ref[...], w_bc_ref[...]) + dot(step_low_ref[...], wide_dt[...])
     gain_ref[...] += jnp.sum((total * normed_ref[...].astype(F32)).reshape(-1, 8, width), axis=0)
-    both_ref[:, width:] = dot(gated_ref[...], w_out_ref[...]).astype(BF16)
-
-
-def state_kernel(
-    rank_ref,
-    total_ref,
-    slope_ref,
-    state_ref,
-    conv_bc_ref,
-    token_ref,
-    w_bc_ref,
-    normed_ref,
-    own_part_ref,
-    rows_ref,
-    conv_grad_ref,
-    gain_ref,
-    later,
-):
-    rank = rank_ref[0]
-    count, columns = total_ref.shape
-    side = token_ref[...].T
-    later[count:, :] = jnp.zeros((8, columns), F32)
-    dbefore = total_ref[...].astype(F32) * slope_ref[...].astype(F32)
-    later[0:count, :] = dbefore
-    state = state_ref[...].astype(F32)
-    grad = conv_bc_ref[CONV - 1 : CONV, :] * dbefore
-    conv_grad_ref[...] = jnp.zeros(conv_grad_ref.shape, F32)
-    conv_grad_ref[CONV - 1 : CONV, :] = jnp.sum(state * dbefore, axis=0, keepdims=True)
-    conv_grad_ref[CONV : CONV + 1, :] = jnp.sum(dbefore, axis=0, keepdims=True)
-    for k in range(1, CONV):
-        shifted = later[k : k + count, :] * side[:, 5 + k : 6 + k]
-        grad = grad + conv_bc_ref[CONV - 1 - k : CONV - k, :] * shifted
-        conv_grad_ref[CONV - 1 - k : CONV - k, :] = jnp.sum(state * shifted, axis=0, keepdims=True)
-    later[0:count, :] = grad
-    own_columns = rows_ref.shape[0]
-    picked = lax.broadcasted_iota(jnp.int32, (columns, own_columns), 0) == (
-        lax.broadcasted_iota(jnp.int32, (columns, own_columns), 1) + rank * own_columns
-    )
-    own = dot(grad.astype(BF16), picked.astype(F32).astype(BF16)).astype(BF16)
-    rows_ref[...] = dot_first(own, normed_ref[...])
-    own_rows = own_part_ref.shape[0]
-    start = pl.multiple_of(rank * own_rows, 8)
-    own_part = dot_last(later[pl.ds(start, own_rows), :].astype(BF16), w_bc_ref[...])
-    own_part_ref[...] = own_part
-    own_normed = normed_ref[pl.ds(pl.multiple_of(start, 16), own_rows), :].astype(F32)
-    gain_ref[...] = jnp.sum((own_part * own_normed).reshape(-1, 8, own_part.shape[1]), axis=0)
+    branch = dot(gated_ref[...], w_out_ref[...]).astype(BF16)
+
+    @pl.when(2 * block < last)
+    def _():
+        sent_ref[:, 0:width] = total.astype(BF16)
+        sent_ref[:, width:] = branch
+
+    @pl.when(2 * block > last)
+    def _():
+        kept_ref[:, 0:width] = total.astype(BF16)
+        kept_ref[:, width:] = branch
+
+    @pl.when(block == last)
+    def _():
+        gain = jnp.sum(gain_ref[...], axis=0, keepdims=True) / row_ref[0:1, :]
+        gain_ref[...] = jnp.broadcast_to(gain, gain_ref.shape)
 
 
 def pack_kernel(
     head_count,
-    low_ref,
+    core_ref,
     bc_rows_ref,
     step_rows_ref,
     channel_ref,
     gate_gain_ref,
-    shared_ref,
+    gain_ref,
     conv_bc_ref,
     head_ref,
     sent_ref,
     kept_ref,
-    packed,
+    own_ref,
 ):
+    core = core_ref[0]
     channels = channel_ref.shape[1]
-    packed[...] = jnp.zeros(packed.shape, F32)
-    at = bc_rows_ref.shape[0]
-    packed[0:at, :] = bc_rows_ref[...]
-    packed[at : at + 16, :] = step_rows_ref[...]
-    at += 16
-    for k in range(CONV):
-        packed[at + k : at + k + 1, 0:channels] = channel_ref[k : k + 1, :]
-    at += CONV
-    packed[at : at + 1, 0:channels] = channel_ref[CONV : CONV + 1, :]
-    packed[at + 1 : at + 2, 0:channels] = jnp.sum(gate_gain_ref[...], axis=0, keepdims=True)
-    packed[at + 2 : at + 3, :] = shared_ref[0:1, :]
-    at += 3
+    states, width = bc_rows_ref.shape
+    folds = width // channels
+    groups = (kept_ref.shape[0] - 16) // (OWN_BC * folds)
+    for which, ref in ((1 - core, sent_ref), (core, kept_ref)):
+        for group in range(groups):
+            found = bc_rows_ref[pl.ds(pl.multiple_of((2 * group + which) * OWN_BC, 8), OWN_BC), :].astype(BF16)
+            for fold in range(folds):
+                at = (group * folds + fold) * OWN_BC
+                ref[at : at + OWN_BC, :] = found[:, fold * channels : (fold + 1) * channels]
+        shared = [gain_ref[0:1, fold * channels : (fold + 1) * channels] for fold in range(folds)]
+        conv = conv_bc_ref[0 : CONV + 1, :]
+        shared.append(jnp.concatenate([conv, jnp.zeros((CONV + 1, channels - states), F32)], axis=1))
+        shared.append(jnp.zeros((16 - folds - CONV - 1, channels), F32))
+        ref[ref.shape[0] - 16 :, :] = jnp.concatenate(shared).astype(BF16)
+    own_ref[...] = jnp.zeros(own_ref.shape, F32)
+    for fold in range(folds):
+        own_ref[16 * fold : 16 * fold + 16, :] = step_rows_ref[:, fold * channels : (fold + 1) * channels]
+    at = 16 * folds
+    own_ref[at : at + CONV + 1, :] = channel_ref[0 : CONV + 1, :]
+    own_ref[at + CONV + 1 : at + CONV + 2, :] = jnp.sum(gate_gain_ref[...], axis=0, keepdims=True)
+    skips = sum_heads(channel_ref[...], head_table(channels, head_count))
+    own_ref[at + CONV + 2 : at + CONV + 4, 0:LANES] = head_ref[0:2, :]
+    own_ref[at + CONV + 4 : at + CONV + 5, 0:LANES] = skips[CONV + 1 : CONV + 2, :]
+
+
+def unpack_kernel(
+    one_ref,
+    two_ref,
+    pre_gain_ref,
+    bc_ref,
+    dt_ref,
+    conv_x_ref,
+    bias_x_ref,
+    conv_bc_ref,
+    bias_bc_ref,
+    dt_bias_ref,
+    a_log_ref,
+    d_skip_ref,
+    gate_gain_ref,
+    total,
+):
+    total[...] = one_ref[...].astype(F32) + two_ref[...].astype(F32)
+    channels = total.shape[1]
+    own_bc, width = bc_ref.shape
+    folds = width // channels
+    for fold in range(folds):
+        bc_ref[:, fold * channels : (fold + 1) * channels] = total[fold * own_bc : (fold + 1) * own_bc, :]
+    at = folds * own_bc
+    pre_gain_ref[...] = jnp.concatenate([total[at + fold : at + fold + 1, :] for fold in range(folds)], axis=1).reshape(-1)
+    at += folds
     states = conv_bc_ref.shape[1]
-    packed[at : at + CONV + 1, 0:states] = conv_bc_ref[0 : CONV + 1, :]
-    at += CONV + 1
-    skips = sum_heads(channel_ref[...], head_table(channels, head_count))
-    packed[at : at + 2, 0:LANES] = head_ref[0:2, :]
-    packed[at + 2 : at + 3, 0:LANES] = skips[CONV + 1 : CONV + 2, :]
-    store_halves(packed, 0, packed.shape[0], low_ref[0], sent_ref, kept_ref)
+    conv_bc_ref[...] = total[at : at + CONV, 0:states]
+    bias_bc_ref[...] = total[at + CONV : at + CONV + 1, 0:states].reshape(-1)
+    at += 16 - folds
+    count = dt_ref.shape[0]
+    for fold in range(folds):
+        dt_ref[:, fold * channels : (fold + 1) * channels] = total[at + 16 * fold : at + 16 * fold + count, :]
+    at += 16 * folds
+    conv_x_ref[...] = total[at : at + CONV, :]
+    bias_x_ref[...] = total[at + CONV : at + CONV + 1, :].reshape(-1)
+    gate_gain_ref[...] = total[at + CONV + 1 : at + CONV + 2, :].reshape(-1)
+    at += CONV + 2
+    for row, ref in enumerate((dt_bias_ref, a_log_ref, d_skip_ref)):
+        ref[...] = total[at + row : at + row + 1, 0:LANES].reshape(-1)[0 : ref.shape[0]]
+
+
+def hidden_kernel(rank_ref, hidden_ref, cotan_ref, kept_ref, got_ref, row_ref, out_ref, grad_ref):
+    width = hidden_ref.shape[1]
+    hidden = hidden_ref[...].astype(F32)
+    branch = kept_ref[:, width:].astype(F32) + got_ref[:, width:].astype(F32)
+    out_ref[...] = (hidden + branch).astype(BF16)
+    inv_rms = lax.rsqrt(jnp.mean(hidden * hidden, axis=-1, keepdims=True) + EPS)
+    scaled = (kept_ref[:, 0:width].astype(F32) + got_ref[:, 0:width].astype(F32)) * row_ref[0:1, :]
+    pull = inv_rms * inv_rms * jnp.mean(scaled * hidden, axis=-1, keepdims=True)
+    grad_ref[...] = cotan_ref[...].astype(F32) + inv_rms * (scaled - hidden * pull)
+
+
+def pass_kernel(*refs):
+    pass
+
+
+def finish_kernel(which_ref, own_ref, got_ref, after_ref, out_ref):
+    which = which_ref[0]
+    out_ref[pl.ds(which, 1)] = own_ref[...].astype(F32)[None]
+    out_ref[pl.ds(1 - which, 1)] = got_ref[...].astype(F32)[None]
+
+
+def finish_pair_kernel(which_ref, own_ref, got_ref, after_ref, out_ref, gate_ref):
+    half = pl.program_id(0)
+
+    def store(ref):
+        rows, width = out_ref.shape
+        channels = gate_ref.shape[1]
+        for at in range(width // channels):
+            out_ref[:, at * channels : (at + 1) * channels] = ref[at * rows : (at + 1) * rows, :].astype(F32)
+        gate_ref[...] = ref[gate_ref.shape[0] :, :].astype(F32)
+
+    @pl.when(half == which_ref[0])
+    def _():
+        store(own_ref)
+
+    @pl.when(half != which_ref[0])
+    def _():
+        store(got_ref)
+
+
+def split_kernel(which_ref, sent_one, sent_two, kept_one, kept_two, sent_ref, kept_ref):
+    sent_ref[...] = (sent_one[...].astype(F32) + sent_two[...].astype(F32)).astype(BF16)
+    kept_ref[...] = (kept_one[...].astype(F32) + kept_two[...].astype(F32)).astype(BF16)
 
 
 def whole(shape):
@@ -676,8 +769,8 @@
             out(LANES, F32),
             out(LANES, F32),
             out(states),
-            out(states),
-            out(states),
+            out(states, F32),
+            out(states, F32),
             jax.ShapeDtypeStruct((rows // PIECE, STATE, channels), BF16),
             jax.ShapeDtypeStruct((8, rows), F32),
         ],
@@ -703,34 +796,37 @@
     return [jax.ShapeDtypeStruct((rows // 2, columns), BF16)] * 2
 
 
-def run_gate(low, forward, sums, rows_table, cotangent):
+def in_place():
+    return pl.BlockSpec(memory_space=pl.ANY)
+
+
+def run_gate(low, forward, sums, rows_table, cotangent, normed):
     rows, channels = forward[0].shape
     width = cotangent.shape[1]
+    size = 2 * BLOCK
 
     def block(columns):
-        return pl.BlockSpec((BLOCK, columns), lambda i: (i, 0))
+        return pl.BlockSpec((size, columns), lambda i: (i, 0))
 
     shape = jax.ShapeDtypeStruct((rows, channels), BF16)
-    halves = half_shapes(channels, width)
+    halves = [jax.ShapeDtypeStruct((width // 2 + width // 2, channels), BF16)] * 2
     out = pl.pallas_call(
         gate_kernel,
-        grid=(rows // BLOCK,),
+        grid=(rows // size,),
         in_specs=[scalar_spec()]
         + [block(channels)] * 4
-        + [pl.BlockSpec((8, BLOCK), lambda i: (0, i)), whole(rows_table.shape), block(width)],
-        out_specs=[block(channels)] * 3
-        + [whole((8, channels))]
-        + [whole(half.shape) for half in halves],
+        + [pl.BlockSpec((8, size), lambda i: (0, i)), whole(rows_table.shape), block(width), block(width)],
+        out_specs=[block(channels)] * 3 + [whole((8, channels))] + [whole(half.shape) for half in halves],
         out_shape=[shape, shape, shape, jax.ShapeDtypeStruct((8, channels), F32)] + halves,
-        scratch_shapes=[pltpu.VMEM((channels, width), F32)],
+        scratch_shapes=[pltpu.VMEM((channels, width), F32), pltpu.VMEM((width, channels), F32)],
         compiler_params=params(),
         cost_estimate=no_cost(),
         name="gate",
-    )(low, *forward, sums, rows_table, cotangent)
+    )(low, *forward, sums, rows_table, cotangent, normed)
     return out[:4], out[4:]
 
 
-def run_weight(low, normed, grad):
+def run_weight(low, normed, grad, after):
     rows, width = normed.shape
     channels = grad.shape[1]
     size = 2 * BLOCK
@@ -742,6 +838,7 @@
             scalar_spec(),
             pl.BlockSpec((size, width), lambda i: (i, 0)),
             pl.BlockSpec((size, channels), lambda i: (i, 0)),
+            in_place(),
         ],
         out_specs=[whole(half.shape) for half in halves],
         out_shape=halves,
@@ -749,14 +846,15 @@
         compiler_params=params(),
         cost_estimate=no_cost(),
         name="weight",
-    )(low, normed, grad)
-
-
-def run_backward(low, by_channel, step_in, cum, bc_low, enter, normed, conv_x, head_values, tokens, head_count):
+    )(low, normed, grad, after)
+
+
+def run_backward(by_channel, step_in, cum, bc_low, enter, normed, by_state, tables, after, head_count):
     rows, channels = by_channel[0].shape
     width = normed.shape[1]
     count = rows // BLOCK
     states = bc_low.shape[1]
+    conv_x, conv_bc, head_values, tokens = tables
 
     def block(columns):
         return pl.BlockSpec((BLOCK, columns), lambda i: (count - 1 - i, 0))
@@ -764,99 +862,236 @@
     def low_rows(columns):
         return jax.ShapeDtypeStruct((rows, columns), BF16)
 
-    halves = half_shapes(width // 2, channels) * 2
-    step_rows = jax.ShapeDtypeStruct((16, width), F32)
-    out = pl.pallas_call(
+    sums = [
+        jax.ShapeDtypeStruct(shape, F32)
+        for shape in ((8, channels), (8, states), (8, LANES), (16, width), (states, width))
+    ]
+    return pl.pallas_call(
         functools.partial(backward_kernel, head_count),
         grid=(count,),
-        in_specs=[scalar_spec()]
-        + [block(channels)] * 5
+        in_specs=[block(channels)] * 5
         + [block(LANES), block(LANES), block(states)]
         + [pl.BlockSpec((BLOCK // PIECE, STATE, channels), lambda i: (count - 1 - i, 0, 0))]
-        + [block(width), whole(conv_x.shape), whole(head_values.shape)]
-        + [pl.BlockSpec((tokens.shape[0], BLOCK), lambda i: (0, count - 1 - i))],
+        + [block(width), block(states), block(states)]
+        + [whole(conv_x.shape), whole(conv_bc.shape), whole(head_values.shape)]
+        + [pl.BlockSpec((tokens.shape[0], BLOCK), lambda i: (0, count - 1 - i)), in_place()],
         out_specs=[block(states), block(channels), block(LANES)]
-        + [whole((8, channels)), whole((8, LANES)), whole(step_rows.shape)]
-        + [whole(half.shape) for half in halves],
-        out_shape=[
-            low_rows(states),
-            low_rows(channels),
-            low_rows(LANES),
-            jax.ShapeDtypeStruct((8, channels), F32),
-            jax.ShapeDtypeStruct((8, LANES), F32),
-            step_rows,
-        ]
-        + halves,
+        + [whole(shape.shape) for shape in sums],
+        out_shape=[low_rows(states), low_rows(channels), low_rows(LANES)] + sums,
         scratch_shapes=[
             pltpu.VMEM((PIECE + 8, channels), F32),
+            pltpu.VMEM((PIECE + 8, states), F32),
             pltpu.VMEM((STATE, channels), F32),
-            pltpu.VMEM((width, channels), F32),
             pltpu.VMEM((LANES, width), F32),
         ],
         compiler_params=params(),
         cost_estimate=no_cost(),
         name="backward",
-    )(low, *by_channel, step_in, cum, bc_low, enter, normed, conv_x, head_values, tokens)
-    return out[:6], out[6:]
-
-
-def run_merge(gate_low, inner_low, step_low, gated, normed, weights):
+    )(*by_channel, step_in, cum, bc_low, enter, normed, *by_state, conv_x, conv_bc, head_values, tokens, after)
+
+
+def run_merge(core, blocked, weights, rows_table, after, ranks):
+    normed = blocked[-1]
     rows, width = normed.shape
-    blocked = (gate_low, inner_low, step_low, gated, normed)
+    size = rows // ranks
+    half = ranks // 2
 
     def block(columns):
-        return pl.BlockSpec((BLOCK, columns), lambda i: (i, 0))
-
+        return pl.BlockSpec(
+            (size, columns),
+            lambda i, c: (jnp.where(i < half, 2 * i + 1 - c[0], 2 * (i - half) + c[0]), 0),
+        )
+
+    def constant(shape):
+        return pl.BlockSpec(shape, lambda i, c: (0,) * len(shape), pipeline_mode=pl.Buffered(1))
+
+    out = jax.ShapeDtypeStruct((rows // 2, 2 * width), BF16)
     return pl.pallas_call(
         merge_kernel,
-        grid=(rows // BLOCK,),
-        in_specs=[block(array.shape[1]) for array in blocked] + [whole(weight.shape) for weight in weights],
-        out_specs=[block(2 * width), whole((8, width))],
-        out_shape=[
-            jax.ShapeDtypeStruct((rows, 2 * width), BF16),
-            jax.ShapeDtypeStruct((8, width), F32),
-        ],
-        scratch_shapes=[pltpu.VMEM((LANES, width), BF16)],
+        grid_spec=pltpu.PrefetchScalarGridSpec(
+            num_scalar_prefetch=1,
+            grid=(ranks,),
+            in_specs=[block(array.shape[1]) for array in blocked]
+            + [constant(array.shape) for array in (*weights, rows_table)]
+            + [in_place()],
+            out_specs=[
+                pl.BlockSpec((size, 2 * width), lambda i, c: (jnp.minimum(i, half - 1), 0)),
+                pl.BlockSpec((size, 2 * width), lambda i, c: (jnp.maximum(i - half, 0), 0)),
+                constant((8, width)),
+            ],
+            scratch_shapes=[pltpu.VMEM((LANES, width), BF16)],
+        ),
+        out_shape=[out, out, jax.ShapeDtypeStruct((8, width), F32)],
         compiler_params=params(),
         cost_estimate=no_cost(),
         name="merge",
-    )(*blocked, *weights)
-
-
-def run_states(rank, total, slope, state_pre, conv_bc, tokens, w_bc, normed, ranks):
-    rows, columns = total.shape
-    width = normed.shape[1]
+    )(core, *blocked, *weights, rows_table, after)
+
+
+def run_pack(core, bc_rows, step_rows, channel_grads, gain_rows, gain, conv_bc_grads, head_grads, head_count):
+    states, width = bc_rows.shape
+    channels = channel_grads.shape[1]
+    folds = width // channels
     in_vmem = pl.BlockSpec(memory_space=pltpu.VMEM)
-    return pl.pallas_call(
-        state_kernel,
-        in_specs=[scalar_spec()] + [in_vmem] * 7,
-        out_specs=[in_vmem] * 4,
-        out_shape=[
-            jax.ShapeDtypeStruct((rows // ranks, width), F32),
-            jax.ShapeDtypeStruct((columns // ranks, width), F32),
-            jax.ShapeDtypeStruct((8, columns), F32),
-            jax.ShapeDtypeStruct((8, width), F32),
-        ],
-        scratch_shapes=[pltpu.VMEM((rows + 8, columns), F32)],
-        compiler_params=params(),
-        cost_estimate=no_cost(),
-        name="states",
-    )(rank, total, slope, state_pre, conv_bc, tokens, w_bc, normed)
-
-
-def run_pack(low, bc_rows, step_rows, channel_grads, gain_rows, shared, conv_bc_grads, head_grads, head_count):
-    width = bc_rows.shape[1]
-    in_vmem = pl.BlockSpec(memory_space=pltpu.VMEM)
+    shared = jax.ShapeDtypeStruct((states // 2 * folds + 16, channels), BF16)
     return pl.pallas_call(
         functools.partial(pack_kernel, head_count),
         in_specs=[scalar_spec()] + [in_vmem] * 7,
-        out_specs=[in_vmem] * 2,
-        out_shape=half_shapes(PACKED, width),
-        scratch_shapes=[pltpu.VMEM((PACKED, width), F32)],
+        out_specs=[in_vmem] * 3,
+        out_shape=[shared, shared, jax.ShapeDtypeStruct((16 * folds + 16, channels), F32)],
         compiler_params=params(),
         cost_estimate=no_cost(),
         name="pack",
-    )(low, bc_rows, step_rows, channel_grads, gain_rows, shared, conv_bc_grads, head_grads)
+    )(core, bc_rows, step_rows, channel_grads, gain_rows, gain, conv_bc_grads, head_grads)
+
+
+def run_unpack(one, two, width, states, head_count):
+    rows, channels = one.shape
+    last = two.shape[0] // rows - 1
+    in_vmem = pl.BlockSpec(memory_space=pltpu.VMEM)
+    shapes = (
+        (width,),
+        (OWN_BC, width),
+        (head_count, width),
+        (CONV, channels),
+        (channels,),
+        (CONV, states),
+        (states,),
+        (head_count,),
+        (head_count,),
+        (head_count,),
+        (channels,),
+    )
+    return pl.pallas_call(
+        unpack_kernel,
+        grid=(1,),
+        in_specs=[
+            pl.BlockSpec((rows, channels), lambda i: (0, 0)),
+            pl.BlockSpec((rows, channels), lambda i: (last, 0)),
+        ],
+        out_specs=[pl.BlockSpec(shape, lambda i, rank=len(shape): (0,) * rank) for shape in shapes],
+        out_shape=[jax.ShapeDtypeStruct(shape, F32) for shape in shapes],
+        scratch_shapes=[pltpu.VMEM(one.shape, F32)],
+        compiler_params=params(),
+        cost_estimate=no_cost(),
+        name="unpack",
+    )(one, two)
+
+
+def run_hidden(rank, hidden_in, cotangent, kept, got, rows_table):
+    own_rows = kept.shape[0]
+    width = hidden_in.shape[1]
+    count = 2
+    size = own_rows // count
+
+    def own(columns):
+        return pl.BlockSpec((size, columns), lambda i, r: (r[0] * count + i, 0))
+
+    def block(columns):
+        return pl.BlockSpec((size, columns), lambda i, r: (i, 0))
+
+    return pl.pallas_call(
+        hidden_kernel,
+        grid_spec=pltpu.PrefetchScalarGridSpec(
+            num_scalar_prefetch=1,
+            grid=(count,),
+            in_specs=[
+                own(width),
+                own(width),
+                block(2 * width),
+                block(2 * width),
+                pl.BlockSpec(rows_table.shape, lambda i, r: (0, 0)),
+            ],
+            out_specs=[block(width), block(width)],
+        ),
+        out_shape=[
+            jax.ShapeDtypeStruct((own_rows, width), BF16),
+            jax.ShapeDtypeStruct((own_rows, width), F32),
+        ],
+        compiler_params=params(),
+        cost_estimate=no_cost(),
+        name="hidden",
+    )(rank, hidden_in, cotangent, kept, got, rows_table)
+
+
+def run_pass(arrays, after):
+    count = len(arrays)
+    return pl.pallas_call(
+        pass_kernel,
+        in_specs=[in_place()] * (count + 1),
+        out_specs=[in_place()] * count,
+        out_shape=[jax.ShapeDtypeStruct(array.shape, array.dtype) for array in arrays],
+        input_output_aliases={at: at for at in range(count)},
+        cost_estimate=no_cost(),
+        name="pass",
+    )(*arrays, after)
+
+
+def run_finish(which, own, got, after):
+    rows, columns = own.shape
+    size = rows // 2
+    block = pl.BlockSpec((size, columns), lambda i, w: (i, 0))
+    out = pl.pallas_call(
+        finish_kernel,
+        grid_spec=pltpu.PrefetchScalarGridSpec(
+            num_scalar_prefetch=1,
+            grid=(rows // size,),
+            in_specs=[block, block, in_place()],
+            out_specs=pl.BlockSpec((2, size, columns), lambda i, w: (0, i, 0)),
+        ),
+        out_shape=jax.ShapeDtypeStruct((2, rows, columns), F32),
+        compiler_params=params(),
+        cost_estimate=no_cost(),
+        name="finish",
+    )(jnp.reshape(which, (1,)), own, got, after)
+    return out.reshape(2 * rows, columns)
+
+
+def run_finish_pair(which, own, got, after, shape):
+    rows, channels = own.shape
+    out_rows, width = shape
+    in_vmem = pl.BlockSpec((rows, channels), lambda i, w: (0, 0), pipeline_mode=pl.Buffered(1))
+    return pl.pallas_call(
+        finish_pair_kernel,
+        grid_spec=pltpu.PrefetchScalarGridSpec(
+            num_scalar_prefetch=1,
+            grid=(2,),
+            in_specs=[in_vmem, in_vmem, in_place()],
+            out_specs=[
+                pl.BlockSpec((out_rows // 2, width), lambda i, w: (i, 0)),
+                pl.BlockSpec((width // 2, channels), lambda i, w: (i, 0)),
+            ],
+        ),
+        out_shape=[
+            jax.ShapeDtypeStruct((out_rows, width), F32),
+            jax.ShapeDtypeStruct((width, channels), F32),
+        ],
+        compiler_params=params(),
+        cost_estimate=no_cost(),
+        name="finish_pair",
+    )(jnp.reshape(which, (1,)), own, got, after)
+
+
+def run_split(one, two, which):
+    half, columns = one.shape[0] // 2, one.shape[1]
+    count = 2
+    size = half // count
+    sent = pl.BlockSpec((size, columns), lambda i, w: ((1 - w[0]) * count + i, 0))
+    kept = pl.BlockSpec((size, columns), lambda i, w: (w[0] * count + i, 0))
+    out = pl.BlockSpec((size, columns), lambda i, w: (i, 0))
+    return pl.pallas_call(
+        split_kernel,
+        grid_spec=pltpu.PrefetchScalarGridSpec(
+            num_scalar_prefetch=1,
+            grid=(count,),
+            in_specs=[sent, sent, kept, kept],
+            out_specs=[out, out],
+        ),
+        out_shape=[jax.ShapeDtypeStruct((half, columns), BF16)] * 2,
+        compiler_params=params(),
+        cost_estimate=no_cost(),
+        name="split",
+    )(jnp.reshape(which.astype(jnp.int32), (1,)), one, two, one, two)
 
 
 def swap(array, axis, bit):
@@ -872,14 +1107,6 @@
 def half_of(array, which):
     half = array.shape[0] // 2
     return lax.dynamic_slice_in_dim(array, which * half, half, 0)
-
-
-def sum_tensor_low_steps(array):
-    size = lax.axis_size("tensor")
-    for bit in axis_bits("tensor"):
-        got = yield array, "tensor", [(i, i ^ bit) for i in range(size)]
-        array = (array.astype(F32) + got.astype(F32)).astype(BF16)
-    return array
 
 
 def sum_tensor(array):
@@ -888,95 +1115,147 @@
     return array
 
 
-def sum_tensor_steps(array):
+def dp_bits(step):
+    bits = axis_bits("dp")
+    swapped = [bits[1], bits[0]] + bits[2:]
+    return bits[step], swapped[step]
+
+
+def own_bit(step):
+    first, second = dp_bits(step)
+    place = lax.axis_index("dp").astype(jnp.int32)
+    core = lax.axis_index("tensor") % 2
+    return jnp.where(core == 0, (place // first) % 2, (place // second) % 2)
+
+
+def dp_pairs(step):
+    ranks = lax.axis_size("tensor")
+    pairs = dp_bits(step)
+    return [
+        (at * ranks + rank, (at ^ pairs[rank % 2]) * ranks + rank)
+        for at in range(lax.axis_size("dp"))
+        for rank in range(ranks)
+    ]
+
+
+def in_order(which, own, got):
+    place = lax.broadcasted_iota(jnp.int32, (2, 1, 1), 0)
+    return jnp.where(place == which, own[None], got[None])
+
+
+def sum_steps(sent, kept, rider=None):
+    axes = ("dp", "tensor")
+    steps = range(1, len(axis_bits("dp")))
+    terms = [kept]
+    got = yield sent, axes, dp_pairs(0)
+
+    def total(which):
+        return sum(half_of(term, which).astype(F32) for term in terms)
+
+    for step in steps:
+        which = own_bit(step)
+        terms.append(got)
+        sent = total(1 - which).astype(BF16)
+        terms = [half_of(term, which) for term in terms]
+        got = yield sent, axes, dp_pairs(step)
+    part = sum((term.astype(F32) for term in terms), got.astype(F32)).astype(BF16)
+    extra = None
+    for step in reversed((0, *steps)):
+        if step == 1 and rider is not None:
+            extra = rider().astype(BF16)
+        rows = part.shape[0]
+        got = yield part if extra is None else jnp.concatenate([part, extra]), axes, dp_pairs(step)
+        if extra is not None:
+            extra = (extra.astype(F32) + got[rows:].astype(F32)).astype(BF16)
+        if step:
+            part = in_order(own_bit(step), part, got[:rows]).reshape(2 * rows, -1)
+    return own_bit(0), part, got, extra
+
+
+def rest_steps(rows):
+    axes = ("dp", "tensor")
+    for step in range(2, len(axis_bits("dp"))):
+        got = yield rows, axes, dp_pairs(step)
+        total = rows.astype(F32) + got.astype(F32)
+        last, rows = (rows, got), total.astype(BF16)
+    return last
+
+
+def both_steps(sent, kept):
     size = lax.axis_size("tensor")
-    for bit in axis_bits("tensor"):
-        got = yield array, "tensor", [(i, i ^ bit) for i in range(size)]
-        array = array + got
-    return array
-
-
-def sum_steps(sent, kept, bits):
-    size = lax.axis_size("dp")
-    place = lax.axis_index("dp")
-    mine = [(place // bit) % 2 for bit in bits]
-    moves = [[(i, i ^ bit) for i in range(size)] for bit in bits]
-    got = yield sent, "dp", moves[0]
-    part = kept.astype(F32) + got.astype(F32)
-    for which, pairs in zip(mine[1:], moves[1:]):
-        got = yield half_of(part, 1 - which).astype(BF16), "dp", pairs
-        part = half_of(part, which) + got.astype(F32)
-    part = part.astype(BF16)
-    for which, pairs in reversed(list(zip(mine[1:], moves[1:]))):
-        got = yield part, "dp", pairs
-        part = jnp.concatenate([jnp.where(which == 0, part, got), jnp.where(which == 0, got, part)])
-    got = yield part, "dp", moves[0]
-    return jnp.where(mine[0] == 0, part, got), jnp.where(mine[0] == 0, got, part)
+    rank = lax.axis_index("tensor")
+    got = yield sent, "tensor", [(i, i ^ 1) for i in range(size)]
+    for bit in axis_bits("tensor")[1:]:
+        sent, kept = run_split(kept, got, (rank // bit) % 2)
+        got = yield sent, "tensor", [(i, i ^ bit) for i in range(size)]
+    return kept, got
+
+
+def small_steps(sent, kept, own):
+    size = lax.axis_size("tensor")
+    rank = lax.axis_index("tensor")
+    got = yield sent, "tensor", [(i, i ^ 1) for i in range(size)]
+    total = kept.astype(F32) + got.astype(F32)
+    for bit in axis_bits("tensor")[1:]:
+        which = (rank // bit) % 2
+        shared = total[-16:].astype(BF16)
+        rows = total[:-16]
+        got = yield jnp.concatenate([half_of(rows, 1 - which).astype(BF16), shared]), "tensor", [
+            (i, i ^ bit) for i in range(size)
+        ]
+        total = jnp.concatenate([half_of(rows, which), shared.astype(F32)]) + got.astype(F32)
+    return jnp.concatenate([total, own])
 
 
 class Order:
-    def __init__(self, token):
-        self.token = token
+    def __init__(self, last):
+        self.last = last
         self.waiting = {}
         self.flying = {}
         self.results = {}
 
-    def mark(self, *arrays):
-        out = lax.optimization_barrier((self.token, *arrays))
-        self.token = out[0]
-        return out[1] if len(arrays) == 1 else out[1:]
-
-    def run(self, function, *arrays):
-        out = function(*(self.mark(*arrays) if len(arrays) > 1 else [self.mark(*arrays)]))
-        return self.mark(*out) if isinstance(out, (tuple, list)) else self.mark(out)
-
     def advance(self, name, steps, got):
         try:
-            self.waiting[name] = (steps, steps.send(got))
+            request = steps.send(got)
+            self.waiting[name] = (steps, request)
+            self.last = request[0]
         except StopIteration as end:
             self.results[name] = end.value
 
     def add(self, name, steps):
+        last = self.last
         self.advance(name, steps, None)
+        self.last = last
 
     def go(self, *names):
         for name in names:
             if name in self.waiting:
                 steps, (sent, axis, moves) = self.waiting.pop(name)
-                self.flying[name] = (steps, lax.ppermute(self.mark(sent), axis, moves))
+                self.flying[name] = (steps, lax.ppermute(sent, axis, moves))
 
     def land(self, *names):
-        names = [name for name in names if name in self.flying]
-        if names:
-            found = [self.flying.pop(name) for name in names]
-            marked = lax.optimization_barrier((self.token, *[got for _, got in found]))
-            self.token = marked[0]
-            for name, (steps, _), got in zip(names, found, marked[1:]):
-                self.advance(name, steps, got)
+        found = [(name, *self.flying.pop(name)) for name in names if name in self.flying]
+        if found:
+            passed = run_pass([got for _, _, got in found], self.last)
+            self.last = passed[0]
+            for at, ((name, steps, _), got) in enumerate(zip(found, passed)):
+                self.advance(name, steps, self.hold(got) if at else got)
+                if name in self.waiting:
+                    self.last = self.waiting[name][1][0]
+
+    def hold(self, array):
+        return run_pass([array], self.last)[0]
 
     def step(self, *names):
         for name in names:
             self.land(name)
             self.go(name)
 
-    def follow(self, *moves):
-        for move in moves:
-            (self.go if move[0] == "+" else self.land)(move[1:])
-
-    def finish_all(self):
-        while self.flying or self.waiting:
-            self.go(*list(self.waiting))
-            self.land(*list(self.flying))
-
-
-MOVES = (
-    ("+o", "+w", "+g", "+st"),
-    ("-st", "-o", "+st", "+v", "-g", "+o", "+g", "-w", "-st"),
-    ("-v", "+v", "-o", "+w", "+o", "-g", "+g"),
-    ("+sh", "-v", "-sh", "+sh", "-w", "-o", "+o", "-sh"),
-    ("+sm", "+v", "-g", "-sm", "+w", "-o", "+g", "+sm", "-v", "+v", "+o", "-sm", "+sm", "-w", "+w", "-v", "+v", "-sm", "-g", "+sm", "+g", "-v", "-w", "+w", "+v", "-sm", "+sm", "-w", "+w"),
-    ("-sm", "+sm", "-v", "-g", "-sm", "-o", "-w"),
-)
+    def result(self, name):
+        while name not in self.results:
+            self.go(name)
+            self.land(name)
+        return self.results[name]
 
 
 def shards(
@@ -1007,10 +1286,7 @@
     own_rows = row_count // ranks
     row_start = my_rank * own_rows
     pair_width = w_bc.shape[1] // ranks
-    bits = axis_bits("dp")
-    crossed = [bits[1], bits[0]] + bits[2:]
-    place = lax.axis_index("dp").astype(jnp.int32)
-    low_bits = jnp.stack([place % 2, (place // 2) % 2])
+    low = jnp.reshape(own_bit(0), (1,))
     w_dt_rows = w_dt.T
     tokens, rows_table, head_values = run_tables(
         segments, pre_gain, conv_x_bias, gate_gain, conv_bc_bias, dt_bias, a_log, d_skip
@@ -1040,114 +1316,114 @@
         tokens,
     )
     sums = sum_tensor(sums) / (channels * ranks)
-    (gated, gate_low, dscan, gain_rows), out_halves = run_gate(
-        low_bits, (mixed, act, turn, gated_grad), sums, rows_table, cotangent
+    (gated, gate_low, dscan, gain_rows), halves = run_gate(
+        low, (mixed, act, turn, gated_grad), sums, rows_table, cotangent, normed
     )
-    order = Order(sums[0, 0])
-    order.add("o", sum_steps(*out_halves, bits))
-    order.go("o")
-    order.add("g", sum_steps(*order.mark(*run_weight(low_bits, normed, order.mark(gate_low))), crossed))
-    order.go("g")
-    (state_part, inner_low, step_low, channel_grads, head_grads, step_rows), value_halves = run_backward(
-        low_bits,
-        (order.mark(dscan), scan, values, slope, inner_pre),
+    order = Order(gate_low)
+    order.add("first", sum_steps(*halves, lambda: order.result("small")))
+    order.go("first")
+    (
+        state_low,
+        inner_low,
+        step_low,
+        channel_grads,
+        conv_bc_grads,
+        head_grads,
+        step_rows,
+        bc_rows,
+    ) = run_backward(
+        (dscan, scan, values, slope, inner_pre),
         step_in,
         cum,
         bc_low,
         enter,
         normed,
-        conv_x,
-        head_values,
-        tokens,
+        (bc_slope, state_pre),
+        (conv_x, conv_bc, head_values, tokens),
+        halves[0],
         head_count,
     )
-    state_part, *value_halves = order.mark(state_part, *value_halves)
-    order.land("o", "g")
-    order.add("v", sum_steps(*value_halves[:2], bits))
-    order.add("w", sum_steps(*value_halves[2:], crossed))
-    order.add("st", sum_tensor_low_steps(state_part))
-    order.follow(*MOVES[0])
-    both, gain_first = order.mark(
-        *run_merge(
-            *order.mark(gate_low, inner_low, step_low, gated),
-            normed,
-            (w_gate, w_value, w_dt_rows, w_out),
-        )
+    order.last = inner_low
+    order.step("first")
+    sent, kept = run_weight(low, normed, inner_low, order.last)
+    order.last = kept
+    order.step("first")
+    order.add("second", sum_steps(order.hold(sent), kept))
+    order.go("second")
+    core = jnp.reshape((my_rank % 2).astype(jnp.int32), (1,))
+    both_sent, both_kept, gain = run_merge(
+        core,
+        (gate_low, inner_low, step_low, state_low, gated, normed),
+        (w_gate, w_value, w_dt_rows, w_bc, w_out),
+        rows_table,
+        order.last,
+        ranks,
     )
-    both_own = lax.psum_scatter(both, "tensor", scatter_dimension=0, tiled=True)
-    order.follow(*MOVES[1])
-    pair_part, bc_rows, conv_bc_grads, gain_second = order.mark(
-        *run_states(
-            jnp.reshape(my_rank.astype(jnp.int32), (1,)),
-            order.mark(order.results["st"]),
-            bc_slope,
-            state_pre,
-            conv_bc,
-            tokens,
-            w_bc,
-            normed,
-            ranks,
-        )
+    order.last = both_kept
+    order.land("second", "first")
+    order.go("second", "first")
+    small = run_pack(
+        core, bc_rows, step_rows, channel_grads, gain_rows, order.hold(gain), conv_bc_grads, head_grads, head_count
     )
-    order.follow(*MOVES[2])
-    gain_part = jnp.sum(gain_first + gain_second, axis=0, keepdims=True) / rows_table[0:1]
-    order.add("sh", sum_tensor_steps(order.mark(gain_part)))
-    order.follow(*MOVES[3])
-    packed_halves = run_pack(
-        low_bits,
-        bc_rows,
-        step_rows,
-        channel_grads,
-        gain_rows,
-        order.results["sh"],
-        conv_bc_grads,
-        head_grads,
-        head_count,
+    order.add("small", small_steps(*small))
+    order.go("small")
+    order.add("both", both_steps(order.hold(both_sent), both_kept))
+    order.go("both")
+    order.step("small")
+    order.land("small")
+    order.land("second", "first")
+    order.go("second", "first")
+    order.step("both")
+    order.step("second")
+    order.land("second")
+    order.land("first")
+    order.go("second", "first")
+    order.step("second")
+    which, own, got, rows = order.result("first")
+    order.add("rest", rest_steps(rows))
+    order.go("rest")
+    w_out_sum, w_gate_sum = run_finish_pair(which, own, got, order.last, w_out.shape)
+    order.last = w_out_sum
+    order.step("second")
+    kept, got = order.result("both")
+    block_out, hidden_grad = run_hidden(
+        jnp.reshape(my_rank.astype(jnp.int32), (1,)), hidden_in, cotangent, kept, got, rows_table
     )
-    order.add("sm", sum_steps(*packed_halves, bits))
-    order.follow(*MOVES[4])
-    own_hidden, own_cotan, both_own = order.mark(
-        lax.dynamic_slice_in_dim(hidden_in, row_start, own_rows, 0),
-        lax.dynamic_slice_in_dim(cotangent, row_start, own_rows, 0),
-        both_own,
-    )
-    own_hidden = own_hidden.astype(F32)
-    block_out = (own_hidden + both_own[:, width:].astype(F32)).astype(BF16)
-    own_inv = lax.rsqrt(jnp.mean(own_hidden * own_hidden, axis=-1, keepdims=True) + EPS)
-    gain_scaled = (both_own[:, :width].astype(F32) + pair_part) * pre_gain
-    own_dot = jnp.sum(gain_scaled * own_hidden, axis=-1, keepdims=True)
-    hidden_grad = (
-        own_cotan.astype(F32)
-        + own_inv * gain_scaled
-        - own_hidden * (own_inv * own_inv * own_inv) * own_dot / width
-    )
-    block_out, hidden_grad = order.mark(block_out, hidden_grad)
-    order.follow(*MOVES[5])
-    order.finish_all()
-    w_out_sum = jnp.concatenate(order.results["o"]).astype(F32)
-    w_gate_sum = jnp.concatenate(order.results["g"]).astype(F32)
-    w_value_sum = jnp.concatenate([*order.results["v"], *order.results["w"]]).astype(F32)
-    packed = jnp.concatenate(order.results["sm"]).astype(F32)
-    at = pair_width + 16
-    end = at + CONV + 3
-    heads_at = end + CONV + 1
-    states = w_bc.shape[1]
+    order.last = hidden_grad
+    one, two = order.result("rest")
+    small = run_unpack(one, two, width, w_bc.shape[1], head_count)
+    order.last = small[0]
+    which, own, got, _ = order.result("second")
+    w_value_sum = run_finish(which, own, got, order.last)
+    (
+        pre_gain_grad,
+        w_bc_rows,
+        dt_rows,
+        conv_x_grad,
+        conv_x_bias_grad,
+        conv_bc_grad,
+        conv_bc_bias_grad,
+        dt_bias_grad,
+        a_log_grad,
+        d_skip_grad,
+        gate_gain_grad,
+    ) = small
     return (
         block_out,
         hidden_grad,
-        packed[at + CONV + 2],
+        pre_gain_grad,
         w_gate_sum,
         w_value_sum,
-        packed[:pair_width].T,
-        packed[pair_width : pair_width + head_count].T,
-        packed[at : at + CONV, :channels],
-        packed[at + CONV, :channels],
-        packed[end : end + CONV, :states],
-        packed[end + CONV, :states],
-        packed[heads_at, :head_count],
-        packed[heads_at + 1, :head_count],
-        packed[heads_at + 2, :head_count],
-        packed[at + CONV + 1, :channels],
+        w_bc_rows.T,
+        dt_rows.T,
+        conv_x_grad,
+        conv_x_bias_grad,
+        conv_bc_grad,
+        conv_bc_bias_grad,
+        dt_bias_grad,
+        a_log_grad,
+        d_skip_grad,
+        gate_gain_grad,
         w_out_sum,
     )
 

time: 308 us -> 285 us (0.925)
  the two profiles are of different devices: /device:TPU:0 before, /device:TPU:8 now
where the time goes in v4:
time: 285 us; the launch traced here: 284 us
  Pallas kernels  121 us (42%)
  waiting for transfers between devices  96.4 us (34%)
  other arithmetic  28.3 us (10%)
  starting transfers between devices  19.4 us (7%)
  local copies, waits for them, and re-layouts  18.1 us (6%)
    ppermute x17, waiting for transfers between devices, go(): self.flying[name] = (steps, lax.ppermute(sent, axis, moves))  92.6 us
    pallas_call x1, Pallas kernels, run_backward(): pl.pallas_call(functools.partial(backward_kernel, head_count), grid=(coun...  30.1 us
    pallas_call x1, Pallas kernels, run_forward(): pl.pallas_call(forward_kernel, grid=(rows // BLOCK,), in_specs=[block(wid...  26.8 us
    ppermute x17, starting transfers between devices, go(): self.flying[name] = (steps, lax.ppermute(sent, axis, moves))  17.9 us
    pallas_call x1, Pallas kernels, run_merge(): pl.pallas_call(merge_kernel, grid_spec=pltpu.PrefetchScalarGridSpec(num_s...  16.7 us
    pallas_call x1, Pallas kernels, run_gate(): pl.pallas_call(gate_kernel, grid=(rows // size,), in_specs=[scalar_spec()...  16.2 us
    unnamed x52, local copies, waits for them, and re-layouts  14.4 us
    convert_element_type x4, other arithmetic, sum_steps(): sent = total(1 - which).astype(BF16)  8.65 us
  transfers between devices with their start and end apart: 19, of which 13 were waited for; matrix products, arithmetic and copies ran while one was open for 6% of the time, Pallas kernels for 25%

profile of v4, /device:TPU:8, one launch (start us, length us, event | category | flops | bytes accessed | tf_op | source)
XLA Modules:
  0.0 284.2 jit_solution(5595714825048737286)
XLA Ops:
  2.2 26.8 %forward.1 = (bf16[1024,1536]{1,0:T(8,128)(2,1)}, bf16[1024,768]{1,0:T(8,128)(2,1)}, bf16[1024,768]{1,0:T(8,128)(2,1)}, bf16[1024,768]{1,0:T(8,128)(2,1)}, bf16[...) custom-call(bf16[1024,1536]{1,0:T(8,128)(2,1)} %hidden_ref.3, ...), custom_call_target="tpu_custom_call" | custom-call | tf_op jit(solution)/shard_map/forward/pallas_call | solution.py:745
  32.7 2.4 collective-permute-done.1
  35.7 16.2 %gate.1 = (bf16[1024,768]{1,0:T(8,128)(2,1)}, bf16[1024,768]{1,0:T(8,128)(2,1)}, bf16[1024,768]{1,0:T(8,128)(2,1)}, f32[8,768]{1,0:T(8,128)}, bf16[1536,768]{1,0:T(8,128)(2,1)}, /*index=5*/bf16[1536,768]{1,0:T(8,128)(2,1)}) custom-call(s32[1]{0:T(128)} %bitcast.3.low_ref.which_ref, bf16[1024,768]{1,0:T(8,128)(2,1)} %get-tuple-element.81.mixed_ref, ...), custom_call_target="tpu_custom_call" | custom-call | tf_op jit(solution)/shard_map/gate/pallas_call | solution.py:813
  53.6 30.1 %backward.1 = (bf16[1024,256]{1,0:T(8,128)(2,1)}, bf16[1024,768]{1,0:T(8,128)(2,1)}, bf16[1024,128]{1,0:T(8,128)(2,1)}, f32[8,768]{1,0:T(8,128)}, f32[8,256]{1,0...) custom-call(bf16[1024,768]{1,0:T(8,128)(2,1)} %get-tuple-element.88.dscan_ref, ...), custom_call_target="tpu_custom_call" | custom-call | tf_op jit(solution)/shard_map/backward/pallas_call | solution.py:869
  88.0 7.0 %weight.1 = (bf16[768,768]{1,0:T(8,128)(2,1)}, bf16[768,768]{1,0:T(8,128)(2,1)}) custom-call(s32[1]{0:T(128)} %bitcast.3.low_ref.which_ref, bf16[1024,1536]{1,0:T(8,128)(2,1)} %get-tuple-element.86.normed_ref, bf16[1024,768]{1,0:T(8,128)(2,1)} %get-tuple-element.100.refs_1_.grad_ref.inner_low_ref, bf16[768,768]{1,0:T(8,128)(2,1)} %copy-done.12), custom_call_target="tpu_custom_call" | custom-call | tf_op jit(solution)/shard_map/weight/pallas_call | solution.py:834
  94.9 8.3 %collective-permute-done.3.refs_0_ = bf16[768,768]{1,0:T(8,128)(2,1)S(1)} collective-permute-done((bf16[768,768]{1,0:T(8,128)(2,1)S(1)}, bf16[768,768]{1,0:T(8,128)(2,1)S(1)}, u32[]{:S(2)}, u32[]{:S(2)}) %collective-permute-start.3) | collective-permute-done | bytes 1179680 | tf_op jit(solution)/shard_map/ppermute | solution.py:1234
  109.4 2.6 collective-permute-start.5
  112.0 16.7 %merge.1 = (bf16[512,3072]{1,0:T(8,128)(2,1)}, bf16[512,3072]{1,0:T(8,128)(2,1)}, f32[8,1536]{1,0:T(8,128)}) custom-call(s32[1]{0:T(128)} %bitcast.2.core_ref, bf16[1024,768]{1,0:T(8,128)(2,1)} %get-tuple-element.87.gate_low_ref, bf16[1024,768]{1,0:T(8,128)(2,1)} %get-tuple-element.100.refs_1_.grad_ref.inner_low_ref, ...), custom_call_target="tpu_custom_call" | custom-call | tf_op jit(solution)/shard_map/merge/pallas_call | solution.py:909
  128.7 5.8 %collective-permute-done.5.refs_1_ = bf16[384,768]{1,0:T(8,128)(2,1)S(1)} collective-permute-done((bf16[384,768]{1,0:T(8,128)(2,1)S(1)}, bf16[384,768]{1,0:T(8,128)(2,1)S(1)}, u32[]{:S(2)}, u32[]{:S(2)}) %collective-permute-start.5) | collective-permute-done | bytes 589856 | tf_op jit(solution)/shard_map/ppermute | solution.py:1234
  137.6 2.5 add_convert_fusion.1.refs_1_
  140.9 2.6 pack.1
  143.4 3.2 %collective-permute-start.8 = (bf16[384,768]{1,0:T(8,128)(2,1)}, bf16[384,768]{1,0:T(8,128)(2,1)}, u32[]{:S(2)}, u32[]{:S(2)}) collective-permute-start(bf16[384,768]{1,0:T(8,128)(2,1)} %add_convert_fusion.1.refs_1_), channel_id=1, source_target_pairs={{0,16},{1,17},{2,18},{3,19},{4,20},{5,21},{6,22},{7,23},{8,24},{9,... | collective-permute-start | bytes 1769480 | tf_op jit(solution)/shard_map/ppermute | solution.py:1234
  154.3 3.7 %collective-permute-done.10.refs_0_ = bf16[144,768]{1,0:T(8,128)(2,1)S(1)} collective-permute-done((bf16[144,768]{1,0:T(8,128)(2,1)}, bf16[144,768]{1,0:T(8,128)(2,1)S(1)}, u32[]{:S(2)}, u32[]{:S(2)}) %collective-permute-start.10) | collective-permute-done | bytes 221216 | tf_op jit(solution)/shard_map/ppermute | solution.py:1234
  159.6 12.4 %collective-permute-done.8.refs_1_ = bf16[384,768]{1,0:T(8,128)(2,1)} collective-permute-done((bf16[384,768]{1,0:T(8,128)(2,1)}, bf16[384,768]{1,0:T(8,128)(2,1)}, u32[]{:S(2)}, u32[]{:S(2)}) %collective-permute-start.8) | collective-permute-done | bytes 589856 | tf_op jit(solution)/shard_map/ppermute | solution.py:1234
  178.1 2.4 collective-permute-start.12
  182.2 4.2 %split.1 = (bf16[256,3072]{1,0:T(8,128)(2,1)}, bf16[256,3072]{1,0:T(8,128)(2,1)}) custom-call(s32[1]{0:T(128)} %bitcast.1.which_ref, bf16[512,3072]{1,0:T(8,128)(2,1)} %get-tuple-element.106.refs_2_.sent_one.kept_one, bf16[512,3072]{1,0:T(8,128)(2,1)} %pass.31.sent_two.kept_two, bf16[512,3072]{1,0:T(8,128)(2,1)} %get-tuple-element.106.refs_2_.sent_one.kept_one, ...), custom_call_target="tpu_custom_call" | custom-call | tf_op jit(solution)/shard_map/split/pallas_call | solution.py:1082
  186.4 20.5 %collective-permute-done.12.refs_0_ = bf16[192,768]{1,0:T(8,128)(2,1)S(1)} collective-permute-done((bf16[192,768]{1,0:T(8,128)(2,1)}, bf16[192,768]{1,0:T(8,128)(2,1)S(1)}, u32[]{:S(2)}, u32[]{:S(2)}) %collective-permute-start.12) | collective-permute-done | bytes 294944 | tf_op jit(solution)/shard_map/ppermute | solution.py:1234
  209.5 10.6 %collective-permute-done.13.refs_0_ = bf16[192,768]{1,0:T(8,128)(2,1)S(1)} collective-permute-done((bf16[192,768]{1,0:T(8,128)(2,1)S(1)}, bf16[192,768]{1,0:T(8,128)(2,1)S(1)}, u32[]{:S(2)}, u32[]{:S(2)}) %collective-permute-start.13) | collective-permute-done | bytes 294944 | tf_op jit(solution)/shard_map/ppermute | solution.py:1234
  231.2 14.6 %collective-permute-done.14.refs_0_ = bf16[384,768]{1,0:T(8,128)(2,1)} collective-permute-done((bf16[384,768]{1,0:T(8,128)(2,1)S(1)}, bf16[384,768]{1,0:T(8,128)(2,1)}, u32[]{:S(2)}, u32[]{:S(2)}) %collective-permute-start.14) | collective-permute-done | bytes 589856 | tf_op jit(solution)/shard_map/ppermute | solution.py:1234
  249.6 11.5 %collective-permute-done.17.refs_0_ = bf16[1728,768]{1,0:T(8,128)(2,1)S(1)} collective-permute-done((bf16[1728,768]{1,0:T(8,128)(2,1)}, bf16[1728,768]{1,0:T(8,128)(2,1)S(1)}, u32[]{:S(2)}, u32[]{:S(2)}) %collective-permute-start.17) | collective-permute-done | bytes 2654240 | tf_op jit(solution)/shard_map/ppermute | solution.py:1234
  263.8 6.4 %finish_pair.1 = (f32[768,1536]{1,0:T(8,128)}, f32[1536,768]{1,0:T(8,128)}) custom-call(s32[1]{0:T(128)} %bitcast.3.low_ref.which_ref, bf16[1536,768]{1,0:T(8,128)(2,1)} %copy-done.2, bf16[1728,768]{1,0:T(8,128)(2,1)} %pass.36.got_ref.after_ref, bf16[1728,768]{1,0:T(8,128)(2,1)} %pass.36.got_ref.after_ref), custom_call_target="tpu_custom_call" | custom-call | tf_op jit(solution)/shard_map/finish_pair/pallas_call | solution.py:1054
  270.2 3.7 %collective-permute-done.16.refs_0_ = bf16[768,768]{1,0:T(8,128)(2,1)} collective-permute-done((bf16[768,768]{1,0:T(8,128)(2,1)}, bf16[768,768]{1,0:T(8,128)(2,1)}, u32[]{:S(2)}, u32[]{:S(2)}) %collective-permute-start.16) | collective-permute-done | bytes 1179680 | tf_op jit(solution)/shard_map/ppermute | solution.py:1234
  273.9 4.0 %hidden.1 = (bf16[256,1536]{1,0:T(8,128)(2,1)}, f32[256,1536]{1,0:T(8,128)}) custom-call(s32[1]{0:T(128)} %bitcast.rank_ref, bf16[1024,1536]{1,0:T(8,128)(2,1)} %hidden_ref.3, bf16[1024,1536]{1,0:T(8,128)(2,1)} %cotan_ref.5, bf16[256,3072]{1,0:T(8,128)(2,1)} %get-tuple-element.123.kept_ref, bf16[256,3072]{1,0:T(8,128)(2,1)} %pass.38.got_ref, ...), custom_call_target="tpu_custom_call" | custom-call | tf_op jit(solution)/shard_map/hidden/pallas_call | solution.py:993
  280.6 3.6 %finish.1 = f32[2,768,768]{2,1,0:T(8,128)} custom-call(s32[1]{0:T(128)} %bitcast.3.low_ref.which_ref, bf16[768,768]{1,0:T(8,128)(2,1)} %bitcast_select_fusion.1.refs_1_.own_ref, bf16[768,768]{1,0:T(8,128)(2,1)} %pass.37.refs_1_.got_ref, f32[1536]{0:T(1024)} %get-tuple-element.64.after_ref), custom_call_target="tpu_custom_call" | custom-call | tf_op jit(solution)/shard_map/finish/pallas_call | solution.py:1034
  (133 shorter events, 61.4 us)
Async XLA Ops:
  28.9 1.5 collective-permute-start
  31.2 3.9 %collective-permute-start.1 = (f32[8,1024]{1,0:T(8,128)S(1)}, f32[8,1024]{1,0:T(8,128)S(1)}, u32[]{:S(2)}, u32[]{:S(2)}) collective-permute-start(f32[8,1024]{1,0:T(8,128)S(1)} %add.167), channel_id=1, source_target_pairs={{0,2},{1,3},{2,0},{3,1},{4,6},{5,7},{6,4},{7,5},{8,10},{9,11},{10,... | collective-permute-start | bytes 98312 | tf_op jit(solution)/shard_map/ppermute | solution.py:1099
  52.0 31.7 %collective-permute-start.2 = (bf16[1536,768]{1,0:T(8,128)(2,1)}, bf16[1536,768]{1,0:T(8,128)(2,1)S(1)}, u32[]{:S(2)}, u32[]{:S(2)}) collective-permute-start(bf16[1536,768]{1,0:T(8,128)(2,1)} %get-tuple-element.99.after_ref), channel_id=1, source_target_pairs={{0,4},{1,9},{2,6},{3,11},{4,0},{5,13},{6,2},{7,15},{8,12},{9,1},{1... | collective-permute-start | bytes 7077896 | tf_op jit(solution)/shard_map/ppermute | solution.py:1234
  87.0 16.3 %collective-permute-start.3 = (bf16[768,768]{1,0:T(8,128)(2,1)S(1)}, bf16[768,768]{1,0:T(8,128)(2,1)S(1)}, u32[]{:S(2)}, u32[]{:S(2)}) collective-permute-start(bf16[768,768]{1,0:T(8,128)(2,1)S(1)} %add_convert_fusion.after_ref), channel_id=1, source_target_pairs={{0,8},{1,5},{2,10},{3,7},{4,12},{5,1},{6,14},{7,3},{8,0},{9,13},{1... | collective-permute-start | bytes 3538952 | tf_op jit(solution)/shard_map/ppermute | solution.py:1234
  108.4 26.1 %collective-permute-start.4 = (bf16[768,768]{1,0:T(8,128)(2,1)}, bf16[768,768]{1,0:T(8,128)(2,1)}, u32[]{:S(2)}, u32[]{:S(2)}) collective-permute-start(bf16[768,768]{1,0:T(8,128)(2,1)} %pass.22), channel_id=1, source_target_pairs={{0,4},{1,9},{2,6},{3,11},{4,0},{5,13},{6,2},{7,15},{8,12},{9,1},{1... | collective-permute-start | bytes 3538952 | tf_op jit(solution)/shard_map/ppermute | solution.py:1234
  109.4 25.1 %collective-permute-start.5 = (bf16[384,768]{1,0:T(8,128)(2,1)S(1)}, bf16[384,768]{1,0:T(8,128)(2,1)S(1)}, u32[]{:S(2)}, u32[]{:S(2)}) collective-permute-start(bf16[384,768]{1,0:T(8,128)(2,1)S(1)} %copy-done.8), channel_id=1, source_target_pairs={{0,16},{1,17},{2,18},{3,19},{4,20},{5,21},{6,22},{7,23},{8,24},{9,... | collective-permute-start | bytes 1769480 | tf_op jit(solution)/shard_map/ppermute | solution.py:1234
  140.1 40.4 %collective-permute-start.6 = (bf16[512,3072]{1,0:T(8,128)(2,1)}, bf16[512,3072]{1,0:T(8,128)(2,1)S(1)}, u32[]{:S(2)}, u32[]{:S(2)}) collective-permute-start(bf16[512,3072]{1,0:T(8,128)(2,1)} %pass.25), channel_id=1, source_target_pairs={{0,1},{1,0},{2,3},{3,2},{4,5},{5,4},{6,7},{7,6},{8,9},{9,8},{10,11... | collective-permute-start | bytes 9437192 | tf_op jit(solution)/shard_map/ppermute | solution.py:1234
  143.4 3.6 %collective-permute-start.9 = (bf16[272,768]{1,0:T(8,128)(2,1)}, bf16[272,768]{1,0:T(8,128)(2,1)}, u32[]{:S(2)}, u32[]{:S(2)}) collective-permute-start(bf16[272,768]{1,0:T(8,128)(2,1)} %get-tuple-element.119), channel_id=1, source_target_pairs={{0,1},{1,0},{2,3},{3,2},{4,5},{5,4},{6,7},{7,6},{8,9},{9,8},{10,11... | collective-permute-start | bytes 1253384 | tf_op jit(solution)/shard_map/ppermute | solution.py:1234
  143.4 16.1 %collective-permute-start.7 = (bf16[384,768]{1,0:T(8,128)(2,1)}, bf16[384,768]{1,0:T(8,128)(2,1)}, u32[]{:S(2)}, u32[]{:S(2)}) collective-permute-start(bf16[384,768]{1,0:T(8,128)(2,1)} %add_convert_fusion.2.refs_1_), channel_id=1, source_target_pairs={{0,8},{1,5},{2,10},{3,7},{4,12},{5,1},{6,14},{7,3},{8,0},{9,13},{1... | collective-permute-start | bytes 1769480 | tf_op jit(solution)/shard_map/ppermute | solution.py:1234
  143.4 28.5 %collective-permute-start.8 = (bf16[384,768]{1,0:T(8,128)(2,1)}, bf16[384,768]{1,0:T(8,128)(2,1)}, u32[]{:S(2)}, u32[]{:S(2)}) collective-permute-start(bf16[384,768]{1,0:T(8,128)(2,1)} %add_convert_fusion.1.refs_1_), channel_id=1, source_target_pairs={{0,16},{1,17},{2,18},{3,19},{4,20},{5,21},{6,22},{7,23},{8,24},{9,... | collective-permute-start | bytes 1769480 | tf_op jit(solution)/shard_map/ppermute | solution.py:1234
  149.9 8.0 %collective-permute-start.10 = (bf16[144,768]{1,0:T(8,128)(2,1)}, bf16[144,768]{1,0:T(8,128)(2,1)S(1)}, u32[]{:S(2)}, u32[]{:S(2)}) collective-permute-start(bf16[144,768]{1,0:T(8,128)(2,1)} %pad_maximum_fusion.2.refs_1_), channel_id=1, source_target_pairs={{0,2},{1,3},{2,0},{3,1},{4,6},{5,7},{6,4},{7,5},{8,10},{9,11},{10,... | collective-permute-start | bytes 663560 | tf_op jit(solution)/shard_map/ppermute | solution.py:1234
  152.5 23.1 %copy-start.24 = (bf16[48,768]{1,0:T(8,128)(2,1)}, bf16[48,768]{1,0:T(8,128)(2,1)S(1)}, u32[]{:S(2)}) copy-start(bf16[48,768]{1,0:T(8,128)(2,1)S(1)} %convert.11) | copy-start | bytes 221188
  175.6 2.5 copy-start.15
  177.0 45.8 %collective-permute-start.15 = (bf16[960,768]{1,0:T(8,128)(2,1)}, bf16[960,768]{1,0:T(8,128)(2,1)}, u32[]{:S(2)}, u32[]{:S(2)}) collective-permute-start(bf16[960,768]{1,0:T(8,128)(2,1)} %pad_maximum_fusion.1.refs_1_), channel_id=1, source_target_pairs={{0,8},{1,5},{2,10},{3,7},{4,12},{5,1},{6,14},{7,3},{8,0},{9,13},{1... | collective-permute-start | bytes 4423688 | tf_op jit(solution)/shard_map/ppermute | solution.py:1234
  178.1 28.9 %collective-permute-start.12 = (bf16[192,768]{1,0:T(8,128)(2,1)}, bf16[192,768]{1,0:T(8,128)(2,1)S(1)}, u32[]{:S(2)}, u32[]{:S(2)}) collective-permute-start(bf16[192,768]{1,0:T(8,128)(2,1)} %add_convert_fusion.7.refs_1_), channel_id=1, source_target_pairs={{0,16},{1,17},{2,18},{3,19},{4,20},{5,21},{6,22},{7,23},{8,24},{9,... | collective-permute-start | bytes 884744 | tf_op jit(solution)/shard_map/ppermute | solution.py:1234
  209.2 10.9 %copy-start.13 = (bf16[192,768]{1,0:T(8,128)(2,1)}, bf16[192,768]{1,0:T(8,128)(2,1)S(1)}, u32[]{:S(2)}) copy-start(bf16[192,768]{1,0:T(8,128)(2,1)S(1)} %add_convert_fusion.6.refs_1_) | copy-start | bytes 884740
  209.2 10.9 %collective-permute-start.13 = (bf16[192,768]{1,0:T(8,128)(2,1)S(1)}, bf16[192,768]{1,0:T(8,128)(2,1)S(1)}, u32[]{:S(2)}, u32[]{:S(2)}) collective-permute-start(bf16[192,768]{1,0:T(8,128)(2,1)S(1)} %add_convert_fusion.6.refs_1_), channel_id=1, source_target_pairs={{0,16},{1,17},{2,18},{3,19},{4,20},{5,21},{6,22},{7,23},{8,24},{9,... | collective-permute-start | bytes 884744 | tf_op jit(solution)/shard_map/ppermute | solution.py:1234
  226.7 2.8 copy-start.9
  228.9 32.2 %collective-permute-start.17 = (bf16[1728,768]{1,0:T(8,128)(2,1)}, bf16[1728,768]{1,0:T(8,128)(2,1)S(1)}, u32[]{:S(2)}, u32[]{:S(2)}) collective-permute-start(bf16[1728,768]{1,0:T(8,128)(2,1)} %pad_maximum_fusion.refs_1_), channel_id=1, source_target_pairs={{0,4},{1,9},{2,6},{3,11},{4,0},{5,13},{6,2},{7,15},{8,12},{9,1},{1... | collective-permute-start | bytes 7962632 | tf_op jit(solution)/shard_map/ppermute | solution.py:1234
  229.5 16.4 %collective-permute-start.14 = (bf16[384,768]{1,0:T(8,128)(2,1)S(1)}, bf16[384,768]{1,0:T(8,128)(2,1)}, u32[]{:S(2)}, u32[]{:S(2)}) collective-permute-start(bf16[384,768]{1,0:T(8,128)(2,1)S(1)} %copy-done.9), channel_id=1, source_target_pairs={{0,8},{1,5},{2,10},{3,7},{4,12},{5,1},{6,14},{7,3},{8,0},{9,13},{1... | collective-permute-start | bytes 1769480 | tf_op jit(solution)/shard_map/ppermute | solution.py:1234
  229.5 44.4 %collective-permute-start.11 = (bf16[256,3072]{1,0:T(8,128)(2,1)}, bf16[256,3072]{1,0:T(8,128)(2,1)}, u32[]{:S(2)}, u32[]{:S(2)}) collective-permute-start(bf16[256,3072]{1,0:T(8,128)(2,1)} %get-tuple-element.124.refs_1_), channel_id=1, source_target_pairs={{0,2},{1,3},{2,0},{3,1},{4,6},{5,7},{6,4},{7,5},{8,10},{9,11},{10,... | collective-permute-start | bytes 4718600 | tf_op jit(solution)/shard_map/ppermute | solution.py:1234
  248.2 25.7 %collective-permute-start.16 = (bf16[768,768]{1,0:T(8,128)(2,1)}, bf16[768,768]{1,0:T(8,128)(2,1)}, u32[]{:S(2)}, u32[]{:S(2)}) collective-permute-start(bf16[768,768]{1,0:T(8,128)(2,1)} %bitcast_select_fusion.1.refs_1_.own_ref), channel_id=1, source_target_pairs={{0,4},{1,9},{2,6},{3,11},{4,0},{5,13},{6,2},{7,15},{8,12},{9,1},{1... | collective-permute-start | bytes 3538952 | tf_op jit(solution)/shard_map/ppermute | solution.py:1234
  263.7 6.5 %copy-start.20 = (bf16[192,768]{1,0:T(8,128)(2,1)}, bf16[192,768]{1,0:T(8,128)(2,1)S(1)}, u32[]{:S(2)}) copy-start(bf16[192,768]{1,0:T(8,128)(2,1)S(1)} %add_convert_fusion.4.one_ref) | copy-start | bytes 884740
  263.7 14.2 %collective-permute-start.18 = (bf16[192,768]{1,0:T(8,128)(2,1)S(1)}, bf16[192,768]{1,0:T(8,128)(2,1)S(1)}, u32[]{:S(2)}, u32[]{:S(2)}) collective-permute-start(bf16[192,768]{1,0:T(8,128)(2,1)S(1)} %add_convert_fusion.4.one_ref), channel_id=1, source_target_pairs={{0,16},{1,17},{2,18},{3,19},{4,20},{5,21},{6,22},{7,23},{8,24},{9,... | collective-permute-start | bytes 884744 | tf_op jit(solution)/shard_map/ppermute | solution.py:1234
  (21 other events, 27.4 us)

commit v5 on v4

--- a/solution.py
+++ b/solution.py
@@ -155,6 +155,7 @@
     wide_dt,
     gate_all,
     grad_all,
+    tailed,
 ):
     block = pl.program_id(0)
 
@@ -228,6 +229,7 @@
         scores = dot_last(c_low, b_low)
         enter = carried[...].astype(BF16)
         enter_ref[piece] = enter
+        from_state = dot(c_low, enter)
         for pair in range(channels // LANES):
             lanes = slice(pair * LANES, (pair + 1) * LANES)
             values = value_ref[rows, lanes].astype(F32)
@@ -242,11 +244,11 @@
                 [jnp.where(first_half, low, zero), jnp.where(first_half, zero, low)], axis=0
             )
             out = dot(jnp.concatenate(weights, axis=1), both)
-            out = out + dot(c_low, enter[:, lanes]) * wide[PIECE : 2 * PIECE, lanes]
+            out = out + from_state[:, lanes] * wide[PIECE : 2 * PIECE, lanes]
             scan_ref[rows, lanes] = out + skips[:, lanes] * values
-            tailed = (wide[2 * PIECE :, lanes] * scaled).astype(BF16)
-            kept = wide[2 * PIECE - 1 : 2 * PIECE, lanes]
-            carried[:, lanes] = kept * carried[:, lanes] + dot_first(b_low, tailed)
+            tailed[:, lanes] = (wide[2 * PIECE :, lanes] * scaled).astype(BF16)
+        kept = wide[2 * PIECE - 1 : 2 * PIECE, :]
+        carried[...] = kept * carried[...] + dot_first(b_low, tailed[...])
 
     ones = jnp.ones((8, LANES), BF16)
     square_part = jnp.zeros((BLOCK, LANES), F32)
@@ -280,22 +282,33 @@
         ref[to, :] = total[pl.ds(pl.multiple_of(which * half, 8), half), columns].astype(BF16)
 
 
+def gate_columns(sums_ref):
+    row_at = lax.broadcasted_iota(jnp.int32, (8, LANES), 0)
+
+    def column(which):
+        pick = (row_at == which).astype(F32)
+        return lax.dot_general(
+            sums_ref[...], pick, (((0,), (0,)), ((), ())), precision=HIGH, preferred_element_type=F32
+        )
+
+    inv_gate = lax.rsqrt(column(0) + EPS)
+    return inv_gate, inv_gate * inv_gate * column(1)
+
+
 def gate_kernel(
     low_ref,
     mixed_ref,
-    act_ref,
     turn_ref,
     grad_ref,
     sums_ref,
     row_ref,
     cotan_ref,
     normed_ref,
-    gated_ref,
     gate_low_ref,
-    dscan_ref,
     gain_ref,
     sent_ref,
     kept_ref,
+    gated,
     out_total,
     gate_total,
 ):
@@ -307,29 +320,19 @@
         out_total[...] = jnp.zeros(out_total.shape, F32)
         gate_total[...] = jnp.zeros(gate_total.shape, F32)
 
-    row_at = lax.broadcasted_iota(jnp.int32, (8, LANES), 0)
-
-    def column(which):
-        pick = (row_at == which).astype(F32)
-        return lax.dot_general(
-            sums_ref[...], pick, (((0,), (0,)), ((), ())), precision=HIGH, preferred_element_type=F32
-        )
-
     channels = mixed_ref.shape[1]
-    inv_gate = lax.rsqrt(column(0) + EPS)
-    pull = inv_gate * inv_gate * column(1)
+    inv_gate, pull = gate_columns(sums_ref)
     for at in range(0, channels, LANES):
         lanes = slice(at, at + LANES)
         mixed = mixed_ref[:, lanes].astype(F32)
         grad = grad_ref[:, lanes].astype(F32)
         gain = row_ref[2:3, lanes]
         normal = mixed * inv_gate
-        gated_ref[:, lanes] = (normal * gain).astype(BF16)
+        gated[:, lanes] = (normal * gain).astype(BF16)
         gain_ref[:, lanes] += jnp.sum((grad * normal).reshape(-1, 8, LANES), axis=0)
         mixed_grad = inv_gate * (grad * gain - mixed * pull)
         gate_low_ref[:, lanes] = (mixed_grad * turn_ref[:, lanes].astype(F32)).astype(BF16)
-        dscan_ref[:, lanes] = (mixed_grad * act_ref[:, lanes].astype(F32)).astype(BF16)
-    out_total[...] += dot_first(gated_ref[...], cotan_ref[...])
+    out_total[...] += dot_first(gated[...], cotan_ref[...])
     gate_total[...] += dot_first(normed_ref[...], gate_low_ref[...])
 
     @pl.when(block == pl.num_programs(0) - 1)
@@ -360,7 +363,11 @@
 
 def backward_kernel(
     head_count,
-    dscan_ref,
+    mixed_ref,
+    grad_ref,
+    act_ref,
+    sums_ref,
+    row_ref,
     scan_ref,
     value_ref,
     slope_ref,
@@ -389,6 +396,11 @@
     later_bc,
     leaving,
     step_total,
+    dys,
+    lows,
+    reached,
+    tailed,
+    products,
 ):
     block = pl.program_id(0)
 
@@ -411,6 +423,7 @@
     heads = head_table(channels, head_count)
     skips = head_rows(head_ref, heads)[2:3, :]
     side_all = token_ref[...].T
+    inv_gate, pull = gate_columns(sums_ref)
     heads_twice = jnp.concatenate([heads, heads], axis=0)
     for piece in reversed(range(BLOCK // PIECE)):
         rows = slice(piece * PIECE, (piece + 1) * PIECE)
@@ -428,51 +441,58 @@
         c_low = bc_ref[rows, STATE : 2 * STATE]
         scores = dot_last(b_low, c_low)
         score_grad = jnp.zeros((PIECE, PIECE), F32)
-        b_grad = jnp.zeros((PIECE, STATE), F32)
-        c_grad = jnp.zeros((PIECE, STATE), F32)
-        row_sum = jnp.zeros((PIECE, LANES), F32)
-        value_sum = jnp.zeros((PIECE, LANES), F32)
-        last_sum = jnp.zeros((8, LANES), F32)
         masks = [None] + [side[:, 5 + k : 6 + k] for k in range(1, CONV)]
+        for at in range(0, channels, LANES):
+            lanes = slice(at, at + LANES)
+            mixed = mixed_ref[rows, lanes].astype(F32)
+            grad = grad_ref[rows, lanes].astype(F32)
+            mixed_grad = inv_gate[rows] * (grad * row_ref[2:3, lanes] - mixed * pull[rows])
+            dy_low = (mixed_grad * act_ref[rows, lanes].astype(F32)).astype(BF16)
+            dys[:, lanes] = dy_low
+            dy = dy_low.astype(F32)
+            low = (wide[0:PIECE, lanes] * value_ref[rows, lanes].astype(F32)).astype(BF16)
+            lows[:, lanes] = low
+            reached[:, lanes] = (wide[PIECE : 2 * PIECE, lanes] * dy).astype(BF16)
+            tailed[:, lanes] = (wide[2 * PIECE :, lanes] * low.astype(F32)).astype(BF16)
+        leave = leaving[...]
+        leave_low = leave.astype(BF16)
+        enter_low = enter_ref[piece]
+        kept = wide[2 * PIECE - 1 : 2 * PIECE, :]
+        c_grad = dot_last(reached[...], enter_low)
+        b_grad = dot_last(tailed[...], leave_low)
+        from_states = dot(b_low, leave_low)
+        kept_sum = kept * jnp.sum(enter_low.astype(F32) * leave, axis=0, keepdims=True)
+        leaving[...] = kept * leave + dot_first(c_low, reached[...])
         for pair in range(channels // LANES):
             lanes = slice(pair * LANES, (pair + 1) * LANES)
-            own_heads = heads[:, lanes]
             values = value_ref[rows, lanes].astype(F32)
-            dy_low = dscan_ref[rows, lanes]
+            dy_low = dys[:, lanes]
             dy = dy_low.astype(F32)
             wide_step = wide[0:PIECE, lanes]
-            wide_reach = wide[PIECE : 2 * PIECE, lanes]
-            wide_tail = wide[2 * PIECE :, lanes]
-            low = (wide_step * values).astype(BF16)
+            low = lows[:, lanes]
             low_wide = low.astype(F32)
-            leave = leaving[:, lanes]
-            leave_low = leave.astype(BF16)
-            enter = enter_ref[piece, :, lanes]
-            reached = (wide_reach * dy).astype(BF16)
-            tailed = (wide_tail * low_wide).astype(BF16)
-            c_grad = c_grad + dot_last(reached, enter)
-            b_grad = b_grad + dot_last(tailed, leave_low)
-            from_state = wide_tail * dot(b_low, leave_low)
+            from_state = wide[2 * PIECE :, lanes] * from_states[:, lanes]
             zero = jnp.zeros_like(low)
-            dy_first = jnp.where(first_half, dy_low, zero)
-            dy_second = jnp.where(first_half, zero, dy_low)
+            own = jnp.concatenate(
+                [jnp.where(first_half, dy_low, zero), jnp.where(first_half, zero, dy_low)], axis=0
+            )
+            weight_grads = dot_last(low, own)
             weights = []
-            for head, own in ((2 * pair, dy_first), (2 * pair + 1, dy_second)):
+            for at, head in enumerate((2 * pair, 2 * pair + 1)):
                 gaps = (cum_t[head : head + 1, :] - cum[:, head : head + 1]) + bias
                 decay = jnp.exp2(gaps)
                 weights.append((scores * decay).astype(BF16))
-                score_grad = score_grad + dot_last(low, own) * decay
-            dx = dot(jnp.concatenate(weights, axis=1), jnp.concatenate([dy_first, dy_second], axis=0))
+                score_grad = score_grad + weight_grads[:, at * PIECE : (at + 1) * PIECE] * decay
+            dx = dot(jnp.concatenate(weights, axis=1), own)
             dx = dx + from_state
             out = scan_ref[rows, lanes] - skips[:, lanes] * values
-            row_sum = row_sum + sum_heads(dy * out - low_wide * dx, own_heads)
-            value_sum = value_sum + sum_heads(values * dx, own_heads)
-            kept = wide[2 * PIECE - 1 : 2 * PIECE, lanes]
-            last = jnp.sum(low_wide * from_state, axis=0, keepdims=True) + kept * jnp.sum(
-                enter.astype(F32) * leave, axis=0, keepdims=True
-            )
-            last_sum = last_sum + sum_heads(jnp.broadcast_to(last, (8, LANES)), own_heads)
-            leaving[:, lanes] = kept * leave + dot_first(c_low, reached)
+            last = jnp.sum(low_wide * from_state, axis=0, keepdims=True) + kept_sum[:, lanes]
+            for at, product in enumerate(
+                (dy * out - low_wide * dx, values * dx, jnp.broadcast_to(last, (16, LANES)))
+            ):
+                upper, rest = two_terms(product)
+                products[2 * at * PIECE : 2 * at * PIECE + upper.shape[0], lanes] = upper
+                products[2 * at * PIECE + upper.shape[0] : 2 * (at * PIECE + upper.shape[0]), lanes] = rest
             dvalue = wide_step * dx + skips[:, lanes] * dy
             dbefore = dvalue * slope_ref[rows, lanes].astype(F32)
             later[0:PIECE, lanes] = dbefore
@@ -488,6 +508,10 @@
                     inner * shifted, axis=0, keepdims=True
                 )
             inner_low_ref[rows, lanes] = inner_grad.astype(BF16)
+        sums = dot_last(products[...], heads)
+        row_sum = sums[0:PIECE] + sums[PIECE : 2 * PIECE]
+        value_sum = sums[2 * PIECE : 3 * PIECE] + sums[3 * PIECE : 4 * PIECE]
+        last_sum = sums[4 * PIECE : 4 * PIECE + 16] + sums[4 * PIECE + 16 : 4 * PIECE + 32]
         later[PIECE:, :] = later[0:8, :]
         grad_low = score_grad.astype(BF16)
         state_parts = (b_grad + dot(grad_low, c_low), c_grad + dot_first(grad_low, b_low))
@@ -529,8 +553,9 @@
     inner_low_ref,
     step_low_ref,
     state_low_ref,
-    gated_ref,
+    mixed_ref,
     normed_ref,
+    sums_ref,
     w_gate_ref,
     w_value_ref,
     w_dt_ref,
@@ -542,6 +567,7 @@
     kept_ref,
     gain_ref,
     wide_dt,
+    gated,
 ):
     block = pl.program_id(0)
     last = pl.num_programs(0) - 1
@@ -556,7 +582,12 @@
     total = dot_last(inner_low_ref[...], w_value_ref[...]) + dot_last(gate_low_ref[...], w_gate_ref[...])
     total = total + dot_last(state_low_ref[...], w_bc_ref[...]) + dot(step_low_ref[...], wide_dt[...])
     gain_ref[...] += jnp.sum((total * normed_ref[...].astype(F32)).reshape(-1, 8, width), axis=0)
-    branch = dot(gated_ref[...], w_out_ref[...]).astype(BF16)
+    inv_gate, _ = gate_columns(sums_ref)
+    for at in range(0, mixed_ref.shape[1], LANES):
+        lanes = slice(at, at + LANES)
+        normal = mixed_ref[:, lanes].astype(F32) * inv_gate
+        gated[:, lanes] = (normal * row_ref[2:3, lanes]).astype(BF16)
+    branch = dot(gated[...], w_out_ref[...]).astype(BF16)
 
     @pl.when(2 * block < last)
     def _():
@@ -671,34 +702,35 @@
     pass
 
 
-def finish_kernel(which_ref, own_ref, got_ref, after_ref, out_ref):
-    which = which_ref[0]
-    out_ref[pl.ds(which, 1)] = own_ref[...].astype(F32)[None]
-    out_ref[pl.ds(1 - which, 1)] = got_ref[...].astype(F32)[None]
-
-
-def finish_pair_kernel(which_ref, own_ref, got_ref, after_ref, out_ref, gate_ref):
-    half = pl.program_id(0)
-
-    def store(ref):
-        rows, width = out_ref.shape
-        channels = gate_ref.shape[1]
-        for at in range(width // channels):
-            out_ref[:, at * channels : (at + 1) * channels] = ref[at * rows : (at + 1) * rows, :].astype(F32)
-        gate_ref[...] = ref[gate_ref.shape[0] :, :].astype(F32)
-
-    @pl.when(half == which_ref[0])
-    def _():
-        store(own_ref)
-
-    @pl.when(half != which_ref[0])
-    def _():
-        store(got_ref)
+def finish_kernel(which_ref, part_ref, after_ref, out_ref):
+    out_ref[...] = part_ref[...].astype(F32)
+
+
+def finish_pair_kernel(which_ref, part_ref, after_ref, *refs):
+    out_ref, gate_ref = refs[-2:]
+    rows, width = out_ref.shape
+    channels = gate_ref.shape[1]
+    for at in range(width // channels):
+        out_ref[:, at * channels : (at + 1) * channels] = part_ref[at * rows : (at + 1) * rows, :].astype(F32)
+    gate_ref[...] = part_ref[gate_ref.shape[0] :, :].astype(F32)
+
+
+def finish_into_kernel(which_ref, part_ref, after_ref, whole_ref, out_ref):
+    finish_kernel(which_ref, part_ref, after_ref, out_ref)
 
 
 def split_kernel(which_ref, sent_one, sent_two, kept_one, kept_two, sent_ref, kept_ref):
     sent_ref[...] = (sent_one[...].astype(F32) + sent_two[...].astype(F32)).astype(BF16)
     kept_ref[...] = (kept_one[...].astype(F32) + kept_two[...].astype(F32)).astype(BF16)
+
+
+def join_kernel(which_ref, own_ref, got_ref, own_extra_ref, got_extra_ref, out_ref):
+    which = which_ref[0]
+    rows = own_ref.shape[0]
+    out_ref[pl.ds(pl.multiple_of(which * rows, 16), rows), :] = own_ref[...]
+    out_ref[pl.ds(pl.multiple_of((1 - which) * rows, 16), rows), :] = got_ref[...]
+    extra = own_extra_ref[...].astype(F32) + got_extra_ref[...].astype(F32)
+    out_ref[2 * rows :, :] = extra.astype(BF16)
 
 
 def whole(shape):
@@ -728,6 +760,10 @@
         compiler_params=params(),
         name="tables",
     )(*inputs)
+
+
+def in_place():
+    return pl.BlockSpec(memory_space=pl.ANY)
 
 
 def run_forward(hidden_in, cotangent, weights, tables, tokens):
@@ -781,6 +817,7 @@
             pltpu.VMEM((LANES, width), BF16),
             pltpu.VMEM((BLOCK, channels), F32),
             pltpu.VMEM((BLOCK, channels), F32),
+            pltpu.VMEM((PIECE, channels), BF16),
         ],
         compiler_params=params(),
         cost_estimate=no_cost(),
@@ -796,34 +833,33 @@
     return [jax.ShapeDtypeStruct((rows // 2, columns), BF16)] * 2
 
 
-def in_place():
-    return pl.BlockSpec(memory_space=pl.ANY)
-
-
 def run_gate(low, forward, sums, rows_table, cotangent, normed):
     rows, channels = forward[0].shape
     width = cotangent.shape[1]
-    size = 2 * BLOCK
 
     def block(columns):
-        return pl.BlockSpec((size, columns), lambda i: (i, 0))
-
-    shape = jax.ShapeDtypeStruct((rows, channels), BF16)
+        return pl.BlockSpec((BLOCK, columns), lambda i: (i, 0))
+
     halves = [jax.ShapeDtypeStruct((width // 2 + width // 2, channels), BF16)] * 2
     out = pl.pallas_call(
         gate_kernel,
-        grid=(rows // size,),
+        grid=(rows // BLOCK,),
         in_specs=[scalar_spec()]
-        + [block(channels)] * 4
-        + [pl.BlockSpec((8, size), lambda i: (0, i)), whole(rows_table.shape), block(width), block(width)],
-        out_specs=[block(channels)] * 3 + [whole((8, channels))] + [whole(half.shape) for half in halves],
-        out_shape=[shape, shape, shape, jax.ShapeDtypeStruct((8, channels), F32)] + halves,
-        scratch_shapes=[pltpu.VMEM((channels, width), F32), pltpu.VMEM((width, channels), F32)],
+        + [block(channels)] * 3
+        + [pl.BlockSpec((8, BLOCK), lambda i: (0, i)), whole(rows_table.shape), block(width), block(width)],
+        out_specs=[block(channels), whole((8, channels))] + [whole(half.shape) for half in halves],
+        out_shape=[jax.ShapeDtypeStruct((rows, channels), BF16), jax.ShapeDtypeStruct((8, channels), F32)]
+        + halves,
+        scratch_shapes=[
+            pltpu.VMEM((BLOCK, channels), BF16),
+            pltpu.VMEM((channels, width), F32),
+            pltpu.VMEM((width, channels), F32),
+        ],
         compiler_params=params(),
         cost_estimate=no_cost(),
         name="gate",
     )(low, *forward, sums, rows_table, cotangent, normed)
-    return out[:4], out[4:]
+    return out[:2], out[2:]
 
 
 def run_weight(low, normed, grad, after):
@@ -849,7 +885,7 @@
     )(low, normed, grad, after)
 
 
-def run_backward(by_channel, step_in, cum, bc_low, enter, normed, by_state, tables, after, head_count):
+def run_backward(gate_inputs, sums, rows_table, by_channel, step_in, cum, bc_low, enter, normed, by_state, tables, after, head_count):
     rows, channels = by_channel[0].shape
     width = normed.shape[1]
     count = rows // BLOCK
@@ -862,45 +898,53 @@
     def low_rows(columns):
         return jax.ShapeDtypeStruct((rows, columns), BF16)
 
-    sums = [
+    totals = [
         jax.ShapeDtypeStruct(shape, F32)
         for shape in ((8, channels), (8, states), (8, LANES), (16, width), (states, width))
     ]
     return pl.pallas_call(
         functools.partial(backward_kernel, head_count),
         grid=(count,),
-        in_specs=[block(channels)] * 5
+        in_specs=[block(channels)] * 3
+        + [pl.BlockSpec((8, BLOCK), lambda i: (0, count - 1 - i)), whole(rows_table.shape)]
+        + [block(channels)] * 4
         + [block(LANES), block(LANES), block(states)]
         + [pl.BlockSpec((BLOCK // PIECE, STATE, channels), lambda i: (count - 1 - i, 0, 0))]
         + [block(width), block(states), block(states)]
         + [whole(conv_x.shape), whole(conv_bc.shape), whole(head_values.shape)]
         + [pl.BlockSpec((tokens.shape[0], BLOCK), lambda i: (0, count - 1 - i)), in_place()],
         out_specs=[block(states), block(channels), block(LANES)]
-        + [whole(shape.shape) for shape in sums],
-        out_shape=[low_rows(states), low_rows(channels), low_rows(LANES)] + sums,
+        + [whole(shape.shape) for shape in totals],
+        out_shape=[low_rows(states), low_rows(channels), low_rows(LANES)] + totals,
         scratch_shapes=[
             pltpu.VMEM((PIECE + 8, channels), F32),
             pltpu.VMEM((PIECE + 8, states), F32),
             pltpu.VMEM((STATE, channels), F32),
             pltpu.VMEM((LANES, width), F32),
+            pltpu.VMEM((PIECE, channels), BF16),
+            pltpu.VMEM((PIECE, channels), BF16),
+            pltpu.VMEM((PIECE, channels), BF16),
+            pltpu.VMEM((PIECE, channels), BF16),
+            pltpu.VMEM((4 * PIECE + 32, channels), BF16),
         ],
         compiler_params=params(),
         cost_estimate=no_cost(),
         name="backward",
-    )(*by_channel, step_in, cum, bc_low, enter, normed, *by_state, conv_x, conv_bc, head_values, tokens, after)
-
-
-def run_merge(core, blocked, weights, rows_table, after, ranks):
+    )(*gate_inputs, sums, rows_table, *by_channel, step_in, cum, bc_low, enter, normed, *by_state, conv_x, conv_bc, head_values, tokens, after)
+
+
+def run_merge(core, blocked, sums, weights, rows_table, after, ranks):
     normed = blocked[-1]
     rows, width = normed.shape
+    channels = weights[0].shape[1]
     size = rows // ranks
     half = ranks // 2
 
+    def rank_at(i, c):
+        return jnp.where(i < half, 2 * i + 1 - c[0], 2 * (i - half) + c[0])
+
     def block(columns):
-        return pl.BlockSpec(
-            (size, columns),
-            lambda i, c: (jnp.where(i < half, 2 * i + 1 - c[0], 2 * (i - half) + c[0]), 0),
-        )
+        return pl.BlockSpec((size, columns), lambda i, c: (rank_at(i, c), 0))
 
     def constant(shape):
         return pl.BlockSpec(shape, lambda i, c: (0,) * len(shape), pipeline_mode=pl.Buffered(1))
@@ -912,6 +956,7 @@
             num_scalar_prefetch=1,
             grid=(ranks,),
             in_specs=[block(array.shape[1]) for array in blocked]
+            + [pl.BlockSpec((8, size), lambda i, c: (0, rank_at(i, c)))]
             + [constant(array.shape) for array in (*weights, rows_table)]
             + [in_place()],
             out_specs=[
@@ -919,13 +964,13 @@
                 pl.BlockSpec((size, 2 * width), lambda i, c: (jnp.maximum(i - half, 0), 0)),
                 constant((8, width)),
             ],
-            scratch_shapes=[pltpu.VMEM((LANES, width), BF16)],
+            scratch_shapes=[pltpu.VMEM((LANES, width), BF16), pltpu.VMEM((size, channels), BF16)],
         ),
         out_shape=[out, out, jax.ShapeDtypeStruct((8, width), F32)],
         compiler_params=params(),
         cost_estimate=no_cost(),
         name="merge",
-    )(core, *blocked, *weights, rows_table, after)
+    )(core, *blocked, sums, *weights, rows_table, after)
 
 
 def run_pack(core, bc_rows, step_rows, channel_grads, gain_rows, gain, conv_bc_grads, head_grads, head_count):
@@ -1027,49 +1072,48 @@
     )(*arrays, after)
 
 
-def run_finish(which, own, got, after):
-    rows, columns = own.shape
-    size = rows // 2
-    block = pl.BlockSpec((size, columns), lambda i, w: (i, 0))
-    out = pl.pallas_call(
-        finish_kernel,
+def run_finish(which, part, after, rows, into=None):
+    columns = part.shape[1]
+    count = 2
+    size = rows // count
+    inputs = [part, after] + ([] if into is None else [into])
+    return pl.pallas_call(
+        finish_kernel if into is None else finish_into_kernel,
         grid_spec=pltpu.PrefetchScalarGridSpec(
             num_scalar_prefetch=1,
-            grid=(rows // size,),
-            in_specs=[block, block, in_place()],
-            out_specs=pl.BlockSpec((2, size, columns), lambda i, w: (0, i, 0)),
+            grid=(count,),
+            in_specs=[pl.BlockSpec((size, columns), lambda i, w: (i, 0))] + [in_place()] * (len(inputs) - 1),
+            out_specs=pl.BlockSpec((size, columns), lambda i, w: (w[0] * count + i, 0)),
         ),
-        out_shape=jax.ShapeDtypeStruct((2, rows, columns), F32),
+        out_shape=jax.ShapeDtypeStruct((2 * rows, columns), F32),
+        input_output_aliases={} if into is None else {3: 0},
         compiler_params=params(),
         cost_estimate=no_cost(),
         name="finish",
-    )(jnp.reshape(which, (1,)), own, got, after)
-    return out.reshape(2 * rows, columns)
-
-
-def run_finish_pair(which, own, got, after, shape):
-    rows, channels = own.shape
-    out_rows, width = shape
-    in_vmem = pl.BlockSpec((rows, channels), lambda i, w: (0, 0), pipeline_mode=pl.Buffered(1))
+    )(jnp.reshape(which, (1,)), *inputs)
+
+
+def run_finish_pair(which, part, after, out_shape, gate_shape, into=()):
+    out_rows, out_columns = out_shape
+    gate_rows, gate_columns = gate_shape
     return pl.pallas_call(
         finish_pair_kernel,
         grid_spec=pltpu.PrefetchScalarGridSpec(
             num_scalar_prefetch=1,
-            grid=(2,),
-            in_specs=[in_vmem, in_vmem, in_place()],
+            grid=(1,),
+            in_specs=[pl.BlockSpec((gate_rows, gate_columns), lambda i, w: (0, 0))]
+            + [in_place()] * (1 + len(into)),
             out_specs=[
-                pl.BlockSpec((out_rows // 2, width), lambda i, w: (i, 0)),
-                pl.BlockSpec((width // 2, channels), lambda i, w: (i, 0)),
+                pl.BlockSpec((out_rows // 2, out_columns), lambda i, w: (w[0], 0)),
+                pl.BlockSpec((gate_rows // 2, gate_columns), lambda i, w: (w[0], 0)),
             ],
         ),
-        out_shape=[
-            jax.ShapeDtypeStruct((out_rows, width), F32),
-            jax.ShapeDtypeStruct((width, channels), F32),
-        ],
+        out_shape=[jax.ShapeDtypeStruct(out_shape, F32), jax.ShapeDtypeStruct(gate_shape, F32)],
+        input_output_aliases={3 + at: at for at in range(len(into))},
         compiler_params=params(),
         cost_estimate=no_cost(),
         name="finish_pair",
-    )(jnp.reshape(which, (1,)), own, got, after)
+    )(jnp.reshape(which, (1,)), part, after, *into)
 
 
 def run_split(one, two, which):
@@ -1094,6 +1138,27 @@
     )(jnp.reshape(which.astype(jnp.int32), (1,)), one, two, one, two)
 
 
+def run_join(which, own, got, extra_rows):
+    rows = own.shape[0] - extra_rows
+    columns = own.shape[1]
+    matrix = pl.BlockSpec((rows, columns), lambda i, w: (0, 0))
+    extra = pl.BlockSpec((extra_rows, columns), lambda i, w: (rows // extra_rows, 0))
+    shape = (2 * rows + extra_rows, columns)
+    return pl.pallas_call(
+        join_kernel,
+        grid_spec=pltpu.PrefetchScalarGridSpec(
+            num_scalar_prefetch=1,
+            grid=(1,),
+            in_specs=[matrix, matrix, extra, extra],
+            out_specs=pl.BlockSpec(shape, lambda i, w: (0, 0)),
+        ),
+        out_shape=jax.ShapeDtypeStruct(shape, BF16),
+        compiler_params=params(),
+        cost_estimate=no_cost(),
+        name="join",
+    )(jnp.reshape(which, (1,)), own, got, own, got)
+
+
 def swap(array, axis, bit):
     size = lax.axis_size(axis)
     return lax.ppermute(array, axis, [(source, source ^ bit) for source in range(size)])
@@ -1143,7 +1208,7 @@
     return jnp.where(place == which, own[None], got[None])
 
 
-def sum_steps(sent, kept, rider=None):
+def sum_steps(sent, kept, rider=None, own=None):
     axes = ("dp", "tensor")
     steps = range(1, len(axis_bits("dp")))
     terms = [kept]
@@ -1159,16 +1224,21 @@
         terms = [half_of(term, which) for term in terms]
         got = yield sent, axes, dp_pairs(step)
     part = sum((term.astype(F32) for term in terms), got.astype(F32)).astype(BF16)
-    extra = None
+    extra = 0
     for step in reversed((0, *steps)):
         if step == 1 and rider is not None:
-            extra = rider().astype(BF16)
-        rows = part.shape[0]
-        got = yield part if extra is None else jnp.concatenate([part, extra]), axes, dp_pairs(step)
-        if extra is not None:
-            extra = (extra.astype(F32) + got[rows:].astype(F32)).astype(BF16)
-        if step:
-            part = in_order(own_bit(step), part, got[:rows]).reshape(2 * rows, -1)
+            rows = rider().astype(BF16)
+            extra = rows.shape[0]
+            part = jnp.concatenate([part, rows])
+        if step == 0 and own is not None:
+            own.append(part)
+        got = yield part, axes, dp_pairs(step)
+        if step and extra:
+            part = run_join(own_bit(step), part, got, extra)
+        elif step:
+            part = in_order(own_bit(step), part, got).reshape(2 * part.shape[0], -1)
+    if extra:
+        extra = (part[-extra:].astype(F32) + got[-extra:].astype(F32)).astype(BF16)
     return own_bit(0), part, got, extra
 
 
@@ -1212,6 +1282,7 @@
         self.last = last
         self.waiting = {}
         self.flying = {}
+        self.arrived = {}
         self.results = {}
 
     def advance(self, name, steps, got):
@@ -1233,15 +1304,25 @@
                 steps, (sent, axis, moves) = self.waiting.pop(name)
                 self.flying[name] = (steps, lax.ppermute(sent, axis, moves))
 
-    def land(self, *names):
+    def arrive(self, *names):
         found = [(name, *self.flying.pop(name)) for name in names if name in self.flying]
         if found:
             passed = run_pass([got for _, _, got in found], self.last)
             self.last = passed[0]
-            for at, ((name, steps, _), got) in enumerate(zip(found, passed)):
-                self.advance(name, steps, self.hold(got) if at else got)
+            for (name, steps, _), got in zip(found, passed):
+                self.arrived[name] = (steps, got)
+
+    def take(self, *names):
+        for name in names:
+            if name in self.arrived:
+                steps, got = self.arrived.pop(name)
+                self.advance(name, steps, got if got is self.last else self.hold(got))
                 if name in self.waiting:
                     self.last = self.waiting[name][1][0]
+
+    def land(self, *names):
+        self.arrive(*names)
+        self.take(*names)
 
     def hold(self, array):
         return run_pass([array], self.last)[0]
@@ -1250,6 +1331,11 @@
         for name in names:
             self.land(name)
             self.go(name)
+
+    def until(self, name, found):
+        while not found:
+            self.step(name)
+        return found[0]
 
     def result(self, name):
         while name not in self.results:
@@ -1316,11 +1402,12 @@
         tokens,
     )
     sums = sum_tensor(sums) / (channels * ranks)
-    (gated, gate_low, dscan, gain_rows), halves = run_gate(
-        low, (mixed, act, turn, gated_grad), sums, rows_table, cotangent, normed
+    (gate_low, gain_rows), halves = run_gate(
+        low, (mixed, turn, gated_grad), sums, rows_table, cotangent, normed
     )
     order = Order(gate_low)
-    order.add("first", sum_steps(*halves, lambda: order.result("small")))
+    first_own, second_own = [], []
+    order.add("first", sum_steps(*halves, lambda: order.result("small"), first_own))
     order.go("first")
     (
         state_low,
@@ -1332,7 +1419,10 @@
         step_rows,
         bc_rows,
     ) = run_backward(
-        (dscan, scan, values, slope, inner_pre),
+        (mixed, gated_grad, act),
+        sums,
+        rows_table,
+        (scan, values, slope, inner_pre),
         step_in,
         cum,
         bc_low,
@@ -1348,12 +1438,13 @@
     sent, kept = run_weight(low, normed, inner_low, order.last)
     order.last = kept
     order.step("first")
-    order.add("second", sum_steps(order.hold(sent), kept))
+    order.add("second", sum_steps(order.hold(sent), kept, None, second_own))
     order.go("second")
     core = jnp.reshape((my_rank % 2).astype(jnp.int32), (1,))
     both_sent, both_kept, gain = run_merge(
         core,
-        (gate_low, inner_low, step_low, state_low, gated, normed),
+        (gate_low, inner_low, step_low, state_low, mixed, normed),
+        sums,
         (w_gate, w_value, w_dt_rows, w_bc, w_out),
         rows_table,
         order.last,
@@ -1373,18 +1464,25 @@
     order.land("small")
     order.land("second", "first")
     order.go("second", "first")
+    order.step("second")
     order.step("both")
-    order.step("second")
     order.land("second")
     order.land("first")
     order.go("second", "first")
     order.step("second")
-    which, own, got, rows = order.result("first")
+    which = own_bit(0)
+    sums_first = run_finish_pair(which, order.until("first", first_own), order.last, w_out.shape, w_gate.shape)
+    order.last = sums_first[0]
+    own = order.until("second", second_own)
+    w_value_sum = run_finish(which, own, order.last, own.shape[0])
+    order.last = w_value_sum
+    _, _, got, rows = order.result("first")
     order.add("rest", rest_steps(rows))
     order.go("rest")
-    w_out_sum, w_gate_sum = run_finish_pair(which, own, got, order.last, w_out.shape)
+    w_out_sum, w_gate_sum = run_finish_pair(
+        1 - which, got, order.last, w_out.shape, w_gate.shape, sums_first
+    )
     order.last = w_out_sum
-    order.step("second")
     kept, got = order.result("both")
     block_out, hidden_grad = run_hidden(
         jnp.reshape(my_rank.astype(jnp.int32), (1,)), hidden_in, cotangent, kept, got, rows_table
@@ -1393,8 +1491,8 @@
     one, two = order.result("rest")
     small = run_unpack(one, two, width, w_bc.shape[1], head_count)
     order.last = small[0]
-    which, own, got, _ = order.result("second")
-    w_value_sum = run_finish(which, own, got, order.last)
+    _, own, got, _ = order.result("second")
+    w_value_sum = run_finish(1 - which, got, order.last, own.shape[0], w_value_sum)
     (
         pre_gain_grad,
         w_bc_rows,

time: 285 us -> 273 us (0.958)
  the two profiles are of different devices: /device:TPU:8 before, /device:TPU:0 now
where the time goes in v5:
time: 273 us; the launch traced here: 272 us
  Pallas kernels  121 us (44%)
  waiting for transfers between devices  69.1 us (25%)
  starting transfers between devices  42.1 us (15%)
  other arithmetic  24.9 us (9%)
  local copies, waits for them, and re-layouts  13.3 us (5%)
    ppermute x17, waiting for transfers between devices, go(): self.flying[name] = (steps, lax.ppermute(sent, axis, moves))  66.1 us
    ppermute x17, starting transfers between devices, go(): self.flying[name] = (steps, lax.ppermute(sent, axis, moves))  38.8 us
    pallas_call x1, Pallas kernels, run_forward(): pl.pallas_call(forward_kernel, grid=(rows // BLOCK,), in_specs=[block(wid...  25.8 us
    pallas_call x1, Pallas kernels, run_backward(): pl.pallas_call(functools.partial(backward_kernel, head_count), grid=(coun...  25.4 us
    pallas_call x1, Pallas kernels, run_merge(): pl.pallas_call(merge_kernel, grid_spec=pltpu.PrefetchScalarGridSpec(num_s...  18 us
    pallas_call x1, Pallas kernels, run_gate(): pl.pallas_call(gate_kernel, grid=(rows // BLOCK,), in_specs=[scalar_spec(...  14.4 us
    unnamed x38, local copies, waits for them, and re-layouts  11.1 us
    convert_element_type x4, other arithmetic, sum_steps(): sent = total(1 - which).astype(BF16)  8.67 us
  transfers between devices with their start and end apart: 19, of which 11 were waited for; matrix products, arithmetic and copies ran while one was open for 6% of the time, Pallas kernels for 26%

profile of v5, /device:TPU:0, one launch (start us, length us, event | category | flops | bytes accessed | tf_op | source)
XLA Modules:
  0.0 271.7 jit_solution(3411430863475165188)
XLA Ops:
  2.2 25.8 %forward.1 = (bf16[1024,1536]{1,0:T(8,128)(2,1)}, bf16[1024,768]{1,0:T(8,128)(2,1)}, bf16[1024,768]{1,0:T(8,128)(2,1)}, bf16[1024,768]{1,0:T(8,128)(2,1)}, bf16[...) custom-call(bf16[1024,1536]{1,0:T(8,128)(2,1)} %hidden_ref.3, ...), custom_call_target="tpu_custom_call" | custom-call | tf_op jit(solution)/shard_map/forward/pallas_call | solution.py:781
  30.3 2.8 %collective-permute-start.1 = (f32[8,1024]{1,0:T(8,128)S(1)}, f32[8,1024]{1,0:T(8,128)S(1)}, u32[]{:S(2)}, u32[]{:S(2)}) collective-permute-start(f32[8,1024]{1,0:T(8,128)S(1)} %add.161), channel_id=1, source_target_pairs={{0,2},{1,3},{2,0},{3,1},{4,6},{5,7},{6,4},{7,5},{8,10},{9,11},{10,... | collective-permute-start | bytes 98312 | tf_op jit(solution)/shard_map/ppermute | solution.py:1164
  35.6 14.4 %gate.1 = (bf16[1024,768]{1,0:T(8,128)(2,1)}, f32[8,768]{1,0:T(8,128)}, bf16[1536,768]{1,0:T(8,128)(2,1)}, bf16[1536,768]{1,0:T(8,128)(2,1)}) custom-call(s32[1]{0:T(128)} %bitcast.3.low_ref.which_ref, bf16[1024,768]{1,0:T(8,128)(2,1)} %get-tuple-element.81.mixed_ref, bf16[1024,768]{1,0:T(8,128)(2,1)} %get-tuple-element.82.turn_ref, ...), custom_call_target="tpu_custom_call" | custom-call | tf_op jit(solution)/shard_map/gate/pallas_call | solution.py:844
  52.2 25.4 %backward.1 = (bf16[1024,256]{1,0:T(8,128)(2,1)}, bf16[1024,768]{1,0:T(8,128)(2,1)}, bf16[1024,128]{1,0:T(8,128)(2,1)}, f32[8,768]{1,0:T(8,128)}, f32[8,256]{1,0...) custom-call(bf16[1024,768]{1,0:T(8,128)(2,1)} %get-tuple-element.81.mixed_ref, ...), custom_call_target="tpu_custom_call" | custom-call | tf_op jit(solution)/shard_map/backward/pallas_call | solution.py:905
  84.7 7.0 %weight.1 = (bf16[768,768]{1,0:T(8,128)(2,1)}, bf16[768,768]{1,0:T(8,128)(2,1)}) custom-call(s32[1]{0:T(128)} %bitcast.3.low_ref.which_ref, bf16[1024,1536]{1,0:T(8,128)(2,1)} %get-tuple-element.85.normed_ref, bf16[1024,768]{1,0:T(8,128)(2,1)} %get-tuple-element.99.refs_1_.grad_ref.inner_low_ref, bf16[768,768]{1,0:T(8,128)(2,1)} %copy-done.9), custom_call_target="tpu_custom_call" | custom-call | tf_op jit(solution)/shard_map/weight/pallas_call | solution.py:870
  91.6 7.2 %collective-permute-done.3.refs_0_ = bf16[768,768]{1,0:T(8,128)(2,1)S(1)} collective-permute-done((bf16[768,768]{1,0:T(8,128)(2,1)S(1)}, bf16[768,768]{1,0:T(8,128)(2,1)S(1)}, u32[]{:S(2)}, u32[]{:S(2)}) %collective-permute-start.3) | collective-permute-done | bytes 1179680 | tf_op jit(solution)/shard_map/ppermute | solution.py:1305
  106.0 2.6 collective-permute-start.5
  108.5 18.0 %merge.1 = (bf16[512,3072]{1,0:T(8,128)(2,1)}, bf16[512,3072]{1,0:T(8,128)(2,1)}, f32[8,1536]{1,0:T(8,128)}) custom-call(s32[1]{0:T(128)} %bitcast.2.core_ref, bf16[1024,768]{1,0:T(8,128)(2,1)} %get-tuple-element.86.gate_low_ref, bf16[1024,768]{1,0:T(8,128)(2,1)} %get-tuple-element.99.refs_1_.grad_ref.inner_low_ref, ...), custom_call_target="tpu_custom_call" | custom-call | tf_op jit(solution)/shard_map/merge/pallas_call | solution.py:953
  132.1 2.6 pack.1
  137.3 3.1 %collective-permute-start.8 = (bf16[384,768]{1,0:T(8,128)(2,1)}, bf16[384,768]{1,0:T(8,128)(2,1)}, u32[]{:S(2)}, u32[]{:S(2)}) collective-permute-start(bf16[384,768]{1,0:T(8,128)(2,1)} %add_convert_fusion.1.refs_1_), channel_id=1, source_target_pairs={{0,16},{1,17},{2,18},{3,19},{4,20},{5,21},{6,22},{7,23},{8,24},{9,... | collective-permute-start | bytes 1769480 | tf_op jit(solution)/shard_map/ppermute | solution.py:1305
  140.5 4.0 %collective-permute-start.7 = (bf16[384,768]{1,0:T(8,128)(2,1)}, bf16[384,768]{1,0:T(8,128)(2,1)}, u32[]{:S(2)}, u32[]{:S(2)}) collective-permute-start(bf16[384,768]{1,0:T(8,128)(2,1)} %add_convert_fusion.2.refs_1_), channel_id=1, source_target_pairs={{0,8},{1,5},{2,10},{3,7},{4,12},{5,1},{6,14},{7,3},{8,0},{9,13},{1... | collective-permute-start | bytes 1769480 | tf_op jit(solution)/shard_map/ppermute | solution.py:1305
  154.2 13.2 %collective-permute-done.8.refs_1_ = bf16[384,768]{1,0:T(8,128)(2,1)} collective-permute-done((bf16[384,768]{1,0:T(8,128)(2,1)}, bf16[384,768]{1,0:T(8,128)(2,1)}, u32[]{:S(2)}, u32[]{:S(2)}) %collective-permute-start.8) | collective-permute-done | bytes 589856 | tf_op jit(solution)/shard_map/ppermute | solution.py:1305
  172.9 3.4 %collective-permute-start.11 = (bf16[192,768]{1,0:T(8,128)(2,1)}, bf16[192,768]{1,0:T(8,128)(2,1)S(1)}, u32[]{:S(2)}, u32[]{:S(2)}) collective-permute-start(bf16[192,768]{1,0:T(8,128)(2,1)} %add_convert_fusion.6.refs_1_), channel_id=1, source_target_pairs={{0,16},{1,17},{2,18},{3,19},{4,20},{5,21},{6,22},{7,23},{8,24},{9,... | collective-permute-start | bytes 884744 | tf_op jit(solution)/shard_map/ppermute | solution.py:1305
  176.3 23.0 %collective-permute-done.11.refs_0_ = bf16[192,768]{1,0:T(8,128)(2,1)S(1)} collective-permute-done((bf16[192,768]{1,0:T(8,128)(2,1)}, bf16[192,768]{1,0:T(8,128)(2,1)S(1)}, u32[]{:S(2)}, u32[]{:S(2)}) %collective-permute-start.11) | collective-permute-done | bytes 294944 | tf_op jit(solution)/shard_map/ppermute | solution.py:1305
  201.5 3.3 %collective-permute-start.14 = (bf16[192,768]{1,0:T(8,128)(2,1)S(1)}, bf16[192,768]{1,0:T(8,128)(2,1)}, u32[]{:S(2)}, u32[]{:S(2)}) collective-permute-start(bf16[192,768]{1,0:T(8,128)(2,1)S(1)} %add_convert_fusion.5.refs_1_), channel_id=1, source_target_pairs={{0,16},{1,17},{2,18},{3,19},{4,20},{5,21},{6,22},{7,23},{8,24},{9,... | collective-permute-start | bytes 884744 | tf_op jit(solution)/shard_map/ppermute | solution.py:1305
  206.7 4.2 %split.1 = (bf16[256,3072]{1,0:T(8,128)(2,1)}, bf16[256,3072]{1,0:T(8,128)(2,1)}) custom-call(s32[1]{0:T(128)} %bitcast.1.which_ref, bf16[512,3072]{1,0:T(8,128)(2,1)} %get-tuple-element.104.refs_2_.sent_one.kept_one, bf16[512,3072]{1,0:T(8,128)(2,1)} %pass.32.sent_two.kept_two, bf16[512,3072]{1,0:T(8,128)(2,1)} %get-tuple-element.104.refs_2_.sent_one.kept_one, ...), custom_call_target="tpu_custom_call" | custom-call | tf_op jit(solution)/shard_map/split/pallas_call | solution.py:1126
  214.2 3.5 %join.1.refs_1_.part_ref = bf16[1728,768]{1,0:T(8,128)(2,1)} custom-call(s32[1]{0:T(128)} %bitcast.8.which_ref, bf16[960,768]{1,0:T(8,128)(2,1)} %pad_maximum_fusion.refs_1_.own_ref.own_extra_ref, bf16[960,768]{1,0:T(8,128)(2,1)} %pass.34.got_ref.got_extra_ref, bf16[960,768]{1,0:T(8,128)(2,1)} %pad_maximum_fusion.refs_1_.own_ref.own_extra_ref, ...), custom_call_target="tpu_custom_call" | custom-call | tf_op jit(solution)/shard_map/join/pallas_call | solution.py:1147
  218.3 4.8 %collective-permute-start.16 = (bf16[384,768]{1,0:T(8,128)(2,1)S(1)}, bf16[384,768]{1,0:T(8,128)(2,1)}, u32[]{:S(2)}, u32[]{:S(2)}) collective-permute-start(bf16[384,768]{1,0:T(8,128)(2,1)S(1)} %copy-done.6), channel_id=1, source_target_pairs={{0,8},{1,5},{2,10},{3,7},{4,12},{5,1},{6,14},{7,3},{8,0},{9,13},{1... | collective-permute-start | bytes 1769480 | tf_op jit(solution)/shard_map/ppermute | solution.py:1305
  224.7 12.8 %collective-permute-done.16.refs_0_ = bf16[384,768]{1,0:T(8,128)(2,1)} collective-permute-done((bf16[384,768]{1,0:T(8,128)(2,1)S(1)}, bf16[384,768]{1,0:T(8,128)(2,1)}, u32[]{:S(2)}, u32[]{:S(2)}) %collective-permute-start.16) | collective-permute-done | bytes 589856 | tf_op jit(solution)/shard_map/ppermute | solution.py:1305
  240.7 4.0 %finish_pair.2 = (f32[768,1536]{1,0:T(8,128)}, f32[1536,768]{1,0:T(8,128)}) custom-call(s32[1]{0:T(128)} %bitcast.3.low_ref.which_ref, bf16[1728,768]{1,0:T(8,128)(2,1)} %join.1.refs_1_.part_ref, bf16[768,768]{1,0:T(8,128)(2,1)} %bitcast_select_fusion.after_ref.part_ref), custom_call_target="tpu_custom_call" | custom-call | tf_op jit(solution)/shard_map/finish_pair/pallas_call | solution.py:1099
  247.2 2.8 %collective-permute-done.15.refs_0_ = bf16[1728,768]{1,0:T(8,128)(2,1)S(1)} collective-permute-done((bf16[1728,768]{1,0:T(8,128)(2,1)}, bf16[1728,768]{1,0:T(8,128)(2,1)S(1)}, u32[]{:S(2)}, u32[]{:S(2)}) %collective-permute-start.15) | collective-permute-done | bytes 2654240 | tf_op jit(solution)/shard_map/ppermute | solution.py:1305
  252.6 3.6 %collective-permute-start.17 = (bf16[192,768]{1,0:T(8,128)(2,1)S(1)}, bf16[192,768]{1,0:T(8,128)(2,1)S(1)}, u32[]{:S(2)}, u32[]{:S(2)}) collective-permute-start(bf16[192,768]{1,0:T(8,128)(2,1)S(1)} %add_convert_fusion.4.one_ref), channel_id=1, source_target_pairs={{0,16},{1,17},{2,18},{3,19},{4,20},{5,21},{6,22},{7,23},{8,24},{9,... | collective-permute-start | bytes 884744 | tf_op jit(solution)/shard_map/ppermute | solution.py:1305
  256.2 4.0 %finish_pair.3 = (f32[768,1536]{1,0:T(8,128)}, f32[1536,768]{1,0:T(8,128)}) custom-call(s32[1]{0:T(128)} %bitcast.7.which_ref, bf16[1728,768]{1,0:T(8,128)(2,1)} %pass.36.part_ref.after_ref, bf16[1728,768]{1,0:T(8,128)(2,1)} %pass.36.part_ref.after_ref, ...), custom_call_target="tpu_custom_call", output_to_operand_aliasing={{0}: (3, {}), {1}: (4, {})} | custom-call | tf_op jit(solution)/shard_map/finish_pair/pallas_call | solution.py:1099
  260.2 4.0 %hidden.1 = (bf16[256,1536]{1,0:T(8,128)(2,1)}, f32[256,1536]{1,0:T(8,128)}) custom-call(s32[1]{0:T(128)} %bitcast.rank_ref, bf16[1024,1536]{1,0:T(8,128)(2,1)} %hidden_ref.3, bf16[1024,1536]{1,0:T(8,128)(2,1)} %cotan_ref.5, bf16[256,3072]{1,0:T(8,128)(2,1)} %get-tuple-element.121.kept_ref, bf16[256,3072]{1,0:T(8,128)(2,1)} %pass.37.got_ref, ...), custom_call_target="tpu_custom_call" | custom-call | tf_op jit(solution)/shard_map/hidden/pallas_call | solution.py:1038
  (116 shorter events, 71.4 us)
Async XLA Ops:
  28.0 1.6 collective-permute-start
  30.3 4.7 %collective-permute-start.1 = (f32[8,1024]{1,0:T(8,128)S(1)}, f32[8,1024]{1,0:T(8,128)S(1)}, u32[]{:S(2)}, u32[]{:S(2)}) collective-permute-start(f32[8,1024]{1,0:T(8,128)S(1)} %add.161), channel_id=1, source_target_pairs={{0,2},{1,3},{2,0},{3,1},{4,6},{5,7},{6,4},{7,5},{8,10},{9,11},{10,... | collective-permute-start | bytes 98312 | tf_op jit(solution)/shard_map/ppermute | solution.py:1164
  50.0 29.2 %collective-permute-start.2 = (bf16[1536,768]{1,0:T(8,128)(2,1)}, bf16[1536,768]{1,0:T(8,128)(2,1)S(1)}, u32[]{:S(2)}, u32[]{:S(2)}) collective-permute-start(bf16[1536,768]{1,0:T(8,128)(2,1)} %get-tuple-element.98.after_ref), channel_id=1, source_target_pairs={{0,4},{1,9},{2,6},{3,11},{4,0},{5,13},{6,2},{7,15},{8,12},{9,1},{1... | collective-permute-start | bytes 7077896 | tf_op jit(solution)/shard_map/ppermute | solution.py:1305
  82.5 2.2 copy-start.9
  82.5 16.3 %collective-permute-start.3 = (bf16[768,768]{1,0:T(8,128)(2,1)S(1)}, bf16[768,768]{1,0:T(8,128)(2,1)S(1)}, u32[]{:S(2)}, u32[]{:S(2)}) collective-permute-start(bf16[768,768]{1,0:T(8,128)(2,1)S(1)} %add_convert_fusion.after_ref), channel_id=1, source_target_pairs={{0,8},{1,5},{2,10},{3,7},{4,12},{5,1},{6,14},{7,3},{8,0},{9,13},{1... | collective-permute-start | bytes 3538952 | tf_op jit(solution)/shard_map/ppermute | solution.py:1305
  104.0 22.6 %collective-permute-start.4 = (bf16[768,768]{1,0:T(8,128)(2,1)}, bf16[768,768]{1,0:T(8,128)(2,1)}, u32[]{:S(2)}, u32[]{:S(2)}) collective-permute-start(bf16[768,768]{1,0:T(8,128)(2,1)} %pass.22), channel_id=1, source_target_pairs={{0,4},{1,9},{2,6},{3,11},{4,0},{5,13},{6,2},{7,15},{8,12},{9,1},{1... | collective-permute-start | bytes 3538952 | tf_op jit(solution)/shard_map/ppermute | solution.py:1305
  106.0 20.6 %collective-permute-start.5 = (bf16[384,768]{1,0:T(8,128)(2,1)S(1)}, bf16[384,768]{1,0:T(8,128)(2,1)S(1)}, u32[]{:S(2)}, u32[]{:S(2)}) collective-permute-start(bf16[384,768]{1,0:T(8,128)(2,1)S(1)} %copy-done.5), channel_id=1, source_target_pairs={{0,16},{1,17},{2,18},{3,19},{4,20},{5,21},{6,22},{7,23},{8,24},{9,... | collective-permute-start | bytes 1769480 | tf_op jit(solution)/shard_map/ppermute | solution.py:1305
  127.3 2.3 copy-start.8
  134.7 9.8 %collective-permute-start.9 = (bf16[272,768]{1,0:T(8,128)(2,1)}, bf16[272,768]{1,0:T(8,128)(2,1)}, u32[]{:S(2)}, u32[]{:S(2)}) collective-permute-start(bf16[272,768]{1,0:T(8,128)(2,1)} %get-tuple-element.117), channel_id=1, source_target_pairs={{0,1},{1,0},{2,3},{3,2},{4,5},{5,4},{6,7},{7,6},{8,9},{9,8},{10,11... | collective-permute-start | bytes 1253384 | tf_op jit(solution)/shard_map/ppermute | solution.py:1305
  137.3 67.7 %collective-permute-start.6 = (bf16[512,3072]{1,0:T(8,128)(2,1)}, bf16[512,3072]{1,0:T(8,128)(2,1)S(1)}, u32[]{:S(2)}, u32[]{:S(2)}) collective-permute-start(bf16[512,3072]{1,0:T(8,128)(2,1)} %pass.25), channel_id=1, source_target_pairs={{0,1},{1,0},{2,3},{3,2},{4,5},{5,4},{6,7},{7,6},{8,9},{9,8},{10,11... | collective-permute-start | bytes 9437192 | tf_op jit(solution)/shard_map/ppermute | solution.py:1305
  137.3 30.1 %collective-permute-start.8 = (bf16[384,768]{1,0:T(8,128)(2,1)}, bf16[384,768]{1,0:T(8,128)(2,1)}, u32[]{:S(2)}, u32[]{:S(2)}) collective-permute-start(bf16[384,768]{1,0:T(8,128)(2,1)} %add_convert_fusion.1.refs_1_), channel_id=1, source_target_pairs={{0,16},{1,17},{2,18},{3,19},{4,20},{5,21},{6,22},{7,23},{8,24},{9,... | collective-permute-start | bytes 1769480 | tf_op jit(solution)/shard_map/ppermute | solution.py:1305
  140.5 26.9 %collective-permute-start.7 = (bf16[384,768]{1,0:T(8,128)(2,1)}, bf16[384,768]{1,0:T(8,128)(2,1)}, u32[]{:S(2)}, u32[]{:S(2)}) collective-permute-start(bf16[384,768]{1,0:T(8,128)(2,1)} %add_convert_fusion.2.refs_1_), channel_id=1, source_target_pairs={{0,8},{1,5},{2,10},{3,7},{4,12},{5,1},{6,14},{7,3},{8,0},{9,13},{1... | collective-permute-start | bytes 1769480 | tf_op jit(solution)/shard_map/ppermute | solution.py:1305
  147.4 6.1 %collective-permute-start.10 = (bf16[144,768]{1,0:T(8,128)(2,1)}, bf16[144,768]{1,0:T(8,128)(2,1)S(1)}, u32[]{:S(2)}, u32[]{:S(2)}) collective-permute-start(bf16[144,768]{1,0:T(8,128)(2,1)} %pad_maximum_fusion.1.refs_1_), channel_id=1, source_target_pairs={{0,2},{1,3},{2,0},{3,1},{4,6},{5,7},{6,4},{7,5},{8,10},{9,11},{10,... | collective-permute-start | bytes 663560 | tf_op jit(solution)/shard_map/ppermute | solution.py:1305
  172.2 42.0 %collective-permute-start.13 = (bf16[960,768]{1,0:T(8,128)(2,1)}, bf16[960,768]{1,0:T(8,128)(2,1)}, u32[]{:S(2)}, u32[]{:S(2)}) collective-permute-start(bf16[960,768]{1,0:T(8,128)(2,1)} %pad_maximum_fusion.refs_1_.own_ref.own_extra_ref), channel_id=1, source_target_pairs={{0,8},{1,5},{2,10},{3,7},{4,12},{5,1},{6,14},{7,3},{8,0},{9,13},{1... | collective-permute-start | bytes 4423688 | tf_op jit(solution)/shard_map/ppermute | solution.py:1305
  172.9 26.4 %collective-permute-start.11 = (bf16[192,768]{1,0:T(8,128)(2,1)}, bf16[192,768]{1,0:T(8,128)(2,1)S(1)}, u32[]{:S(2)}, u32[]{:S(2)}) collective-permute-start(bf16[192,768]{1,0:T(8,128)(2,1)} %add_convert_fusion.6.refs_1_), channel_id=1, source_target_pairs={{0,16},{1,17},{2,18},{3,19},{4,20},{5,21},{6,22},{7,23},{8,24},{9,... | collective-permute-start | bytes 884744 | tf_op jit(solution)/shard_map/ppermute | solution.py:1305
  201.5 3.5 %copy-start.10 = (bf16[192,768]{1,0:T(8,128)(2,1)}, bf16[192,768]{1,0:T(8,128)(2,1)S(1)}, u32[]{:S(2)}) copy-start(bf16[192,768]{1,0:T(8,128)(2,1)S(1)} %add_convert_fusion.5.refs_1_) | copy-start | bytes 884740
  201.5 10.8 %collective-permute-start.14 = (bf16[192,768]{1,0:T(8,128)(2,1)S(1)}, bf16[192,768]{1,0:T(8,128)(2,1)}, u32[]{:S(2)}, u32[]{:S(2)}) collective-permute-start(bf16[192,768]{1,0:T(8,128)(2,1)S(1)} %add_convert_fusion.5.refs_1_), channel_id=1, source_target_pairs={{0,16},{1,17},{2,18},{3,19},{4,20},{5,21},{6,22},{7,23},{8,24},{9,... | collective-permute-start | bytes 884744 | tf_op jit(solution)/shard_map/ppermute | solution.py:1305
  214.2 4.1 %copy-start.6 = (bf16[384,768]{1,0:T(8,128)(2,1)S(1)}, bf16[384,768]{1,0:T(8,128)(2,1)}, u32[]{:S(2)}) copy-start(bf16[384,768]{1,0:T(8,128)(2,1)} %bitcast_select_fusion.2.refs_1_) | copy-start | bytes 1769476
  217.8 32.2 %collective-permute-start.15 = (bf16[1728,768]{1,0:T(8,128)(2,1)}, bf16[1728,768]{1,0:T(8,128)(2,1)S(1)}, u32[]{:S(2)}, u32[]{:S(2)}) collective-permute-start(bf16[1728,768]{1,0:T(8,128)(2,1)} %join.1.refs_1_.part_ref), channel_id=1, source_target_pairs={{0,4},{1,9},{2,6},{3,11},{4,0},{5,13},{6,2},{7,15},{8,12},{9,1},{1... | collective-permute-start | bytes 7962632 | tf_op jit(solution)/shard_map/ppermute | solution.py:1305
  218.3 19.2 %collective-permute-start.16 = (bf16[384,768]{1,0:T(8,128)(2,1)S(1)}, bf16[384,768]{1,0:T(8,128)(2,1)}, u32[]{:S(2)}, u32[]{:S(2)}) collective-permute-start(bf16[384,768]{1,0:T(8,128)(2,1)S(1)} %copy-done.6), channel_id=1, source_target_pairs={{0,8},{1,5},{2,10},{3,7},{4,12},{5,1},{6,14},{7,3},{8,0},{9,13},{1... | collective-permute-start | bytes 1769480 | tf_op jit(solution)/shard_map/ppermute | solution.py:1305
  223.1 37.1 %collective-permute-start.12 = (bf16[256,3072]{1,0:T(8,128)(2,1)}, bf16[256,3072]{1,0:T(8,128)(2,1)}, u32[]{:S(2)}, u32[]{:S(2)}) collective-permute-start(bf16[256,3072]{1,0:T(8,128)(2,1)} %get-tuple-element.122.refs_1_), channel_id=1, source_target_pairs={{0,2},{1,3},{2,0},{3,1},{4,6},{5,7},{6,4},{7,5},{8,10},{9,11},{10,... | collective-permute-start | bytes 4718600 | tf_op jit(solution)/shard_map/ppermute | solution.py:1305
  239.7 29.4 %collective-permute-start.18 = (bf16[768,768]{1,0:T(8,128)(2,1)}, bf16[768,768]{1,0:T(8,128)(2,1)}, u32[]{:S(2)}, u32[]{:S(2)}) collective-permute-start(bf16[768,768]{1,0:T(8,128)(2,1)} %bitcast_select_fusion.after_ref.part_ref), channel_id=1, source_target_pairs={{0,4},{1,9},{2,6},{3,11},{4,0},{5,13},{6,2},{7,15},{8,12},{9,1},{1... | collective-permute-start | bytes 3538952 | tf_op jit(solution)/shard_map/ppermute | solution.py:1305
  252.6 7.6 %copy-start.16 = (bf16[192,768]{1,0:T(8,128)(2,1)}, bf16[192,768]{1,0:T(8,128)(2,1)S(1)}, u32[]{:S(2)}) copy-start(bf16[192,768]{1,0:T(8,128)(2,1)S(1)} %add_convert_fusion.4.one_ref) | copy-start | bytes 884740
  252.6 13.9 %collective-permute-start.17 = (bf16[192,768]{1,0:T(8,128)(2,1)S(1)}, bf16[192,768]{1,0:T(8,128)(2,1)S(1)}, u32[]{:S(2)}, u32[]{:S(2)}) collective-permute-start(bf16[192,768]{1,0:T(8,128)(2,1)S(1)} %add_convert_fusion.4.one_ref), channel_id=1, source_target_pairs={{0,16},{1,17},{2,18},{3,19},{4,20},{5,21},{6,22},{7,23},{8,24},{9,... | collective-permute-start | bytes 884744 | tf_op jit(solution)/shard_map/ppermute | solution.py:1305
  (14 other events, 17.5 us)

commit v6 on v5

--- a/solution.py
+++ b/solution.py
@@ -13,6 +13,7 @@
 BLOCK = 256
 PIECE = 128
 OWN_BC = 64
+SHARED_AT = 128
 LANES = 128
 EPS = 1e-05
 HIGH = lax.Precision.HIGHEST
@@ -36,6 +37,14 @@
 def two_terms(array):
     upper = array.astype(BF16)
     return upper, (array - upper.astype(F32)).astype(BF16)
+
+
+def sum_rows(ones, array):
+    first = array.astype(BF16)
+    second, third = two_terms(array - first.astype(F32))
+    sums = dot(ones.astype(BF16), jnp.concatenate([first, second, third], axis=1))
+    columns = array.shape[1]
+    return sums[:, 0:columns] + sums[:, columns : 2 * columns] + sums[:, 2 * columns :]
 
 
 def sigmoid(array):
@@ -211,19 +220,27 @@
 
     row_at = lax.broadcasted_iota(jnp.int32, (PIECE, PIECE), 0)
     col_at = lax.broadcasted_iota(jnp.int32, (PIECE, PIECE), 1)
-    lower = (row_at >= col_at).astype(F32)
     first_half = lax.broadcasted_iota(jnp.int32, (PIECE, LANES), 1) < LANES // 2
     heads_twice = jnp.concatenate([heads, heads], axis=0)
+    block_row = lax.broadcasted_iota(jnp.int32, (BLOCK, BLOCK), 0)
+    block_col = lax.broadcasted_iota(jnp.int32, (BLOCK, BLOCK), 1)
+    lower = (block_row >= block_col) & (block_row // PIECE == block_col // PIECE)
+    cums = sum_rows(lower.astype(F32), rate)
+    cum_ref[...] = cums
+    cums_t = cums.T
+    lasts = [
+        jnp.broadcast_to(cums[at + PIECE - 1 : at + PIECE, :], (PIECE, LANES)) for at in range(0, BLOCK, PIECE)
+    ]
+    reach = jnp.exp2(cums) * side[:, 4:5]
+    tail = jnp.exp2(jnp.concatenate(lasts) - cums) * side[:, 5:6]
+    wides = spread_heads(jnp.concatenate([step, reach, tail], axis=0), heads_twice)
     for piece in range(BLOCK // PIECE):
         rows = slice(piece * PIECE, (piece + 1) * PIECE)
-        cum = jnp.dot(lower, rate[rows], precision=HIGH, preferred_element_type=F32)
-        cum_ref[rows, :] = cum
-        cum_t = cum.T
+        cum = cums[rows]
+        cum_t = cums_t[:, rows]
         same = (side[rows, 0:1] == token_ref[0:1, rows]) & (row_at >= col_at)
         bias = jnp.where(same, 0.0, -1e30)
-        reach = jnp.exp2(cum) * side[rows, 4:5]
-        tail = jnp.exp2(cum[PIECE - 1 : PIECE, :] - cum) * side[rows, 5:6]
-        wide = spread_heads(jnp.concatenate([step[rows], reach, tail], axis=0), heads_twice)
+        wide = jnp.concatenate([wides[at + piece * PIECE : at + (piece + 1) * PIECE] for at in range(0, 3 * BLOCK, BLOCK)])
         b_low = bc_ref[rows, 0:STATE]
         c_low = bc_ref[rows, STATE : 2 * STATE]
         scores = dot_last(c_low, b_low)
@@ -727,10 +744,27 @@
 def join_kernel(which_ref, own_ref, got_ref, own_extra_ref, got_extra_ref, out_ref):
     which = which_ref[0]
     rows = own_ref.shape[0]
+    extra_rows = own_extra_ref.shape[0]
     out_ref[pl.ds(pl.multiple_of(which * rows, 16), rows), :] = own_ref[...]
     out_ref[pl.ds(pl.multiple_of((1 - which) * rows, 16), rows), :] = got_ref[...]
     extra = own_extra_ref[...].astype(F32) + got_extra_ref[...].astype(F32)
-    out_ref[2 * rows :, :] = extra.astype(BF16)
+    at = 2 * rows
+    out_ref[at : at + extra_rows, :] = extra.astype(BF16)
+    shared = slice(SHARED_AT, SHARED_AT + 16)
+    out_ref[at + SHARED_AT : at + SHARED_AT + 16, :] = own_extra_ref[shared, :]
+    out_ref[at + extra_rows : at + extra_rows + 16, :] = got_extra_ref[shared, :]
+    out_ref[at + extra_rows + 16 :, :] = jnp.zeros((48, out_ref.shape[1]), BF16)
+
+
+def rider_kernel(core_ref, own_ref, got_ref, out_ref):
+    rows = out_ref.shape[0]
+    out_ref[...] = (own_ref[0:rows, :].astype(F32) + got_ref[0:rows, :].astype(F32)).astype(BF16)
+    shared, second = slice(SHARED_AT, SHARED_AT + 16), slice(rows, rows + 16)
+    own, near = own_ref[shared, :].astype(F32), own_ref[second, :].astype(F32)
+    other, far = got_ref[shared, :].astype(F32), got_ref[second, :].astype(F32)
+    is_first = core_ref[0] == 0
+    total = (own + jnp.where(is_first, other, near)) + (jnp.where(is_first, near, other) + far)
+    out_ref[shared, :] = total.astype(BF16)
 
 
 def whole(shape):
@@ -1143,7 +1177,7 @@
     columns = own.shape[1]
     matrix = pl.BlockSpec((rows, columns), lambda i, w: (0, 0))
     extra = pl.BlockSpec((extra_rows, columns), lambda i, w: (rows // extra_rows, 0))
-    shape = (2 * rows + extra_rows, columns)
+    shape = (2 * rows + extra_rows + 64, columns)
     return pl.pallas_call(
         join_kernel,
         grid_spec=pltpu.PrefetchScalarGridSpec(
@@ -1157,6 +1191,22 @@
         cost_estimate=no_cost(),
         name="join",
     )(jnp.reshape(which, (1,)), own, got, own, got)
+
+
+def run_rider(core, own, got, rows):
+    columns = own.shape[1]
+    held = rows + 64
+    last = pl.BlockSpec((held, columns), lambda i: (own.shape[0] // held - 1, 0))
+    return pl.pallas_call(
+        rider_kernel,
+        grid=(1,),
+        in_specs=[scalar_spec(), last, last],
+        out_specs=pl.BlockSpec((rows, columns), lambda i: (0, 0)),
+        out_shape=jax.ShapeDtypeStruct((rows, columns), BF16),
+        compiler_params=params(),
+        cost_estimate=no_cost(),
+        name="rider",
+    )(core, own, got)
 
 
 def swap(array, axis, bit):
@@ -1238,7 +1288,8 @@
         elif step:
             part = in_order(own_bit(step), part, got).reshape(2 * part.shape[0], -1)
     if extra:
-        extra = (part[-extra:].astype(F32) + got[-extra:].astype(F32)).astype(BF16)
+        core = (lax.axis_index("tensor") % 2).astype(jnp.int32)
+        extra = run_rider(jnp.reshape(core, (1,)), part, got, extra)
     return own_bit(0), part, got, extra
 
 
@@ -1268,7 +1319,7 @@
     total = kept.astype(F32) + got.astype(F32)
     for bit in axis_bits("tensor")[1:]:
         which = (rank // bit) % 2
-        shared = total[-16:].astype(BF16)
+        shared = lax.reduce_precision(total[-16:], 8, 7).astype(BF16)
         rows = total[:-16]
         got = yield jnp.concatenate([half_of(rows, 1 - which).astype(BF16), shared]), "tensor", [
             (i, i ^ bit) for i in range(size)

time: 273 us -> 273 us (level)
    unnamed x38 -> x36, local copies, waits for them, and re-layouts: 11.1 us -> 11.1 us
  transfers between devices with their start and end apart: 19 -> 19, of which waited for: 11 -> 11; matrix products, arithmetic and copies ran while one was open for 6% -> 6% of each run, Pallas kernels for 26% -> 27%
where the time goes in v6:
time: 273 us; the launch traced here: 272 us
  Pallas kernels  123 us (45%)
  waiting for transfers between devices  69.4 us (25%)
  starting transfers between devices  42.1 us (15%)
  other arithmetic  23.8 us (9%)
  local copies, waits for them, and re-layouts  13.3 us (5%)
    ppermute x17, waiting for transfers between devices, go(): self.flying[name] = (steps, lax.ppermute(sent, axis, moves))  66.5 us
    ppermute x17, starting transfers between devices, go(): self.flying[name] = (steps, lax.ppermute(sent, axis, moves))  38.7 us
    pallas_call x1, Pallas kernels, run_backward(): pl.pallas_call(functools.partial(backward_kernel, head_count), grid=(coun...  25.4 us
    pallas_call x1, Pallas kernels, run_forward(): pl.pallas_call(forward_kernel, grid=(rows // BLOCK,), in_specs=[block(wid...  25.1 us
    pallas_call x1, Pallas kernels, run_merge(): pl.pallas_call(merge_kernel, grid_spec=pltpu.PrefetchScalarGridSpec(num_s...  18 us
    pallas_call x1, Pallas kernels, run_gate(): pl.pallas_call(gate_kernel, grid=(rows // BLOCK,), in_specs=[scalar_spec(...  14.4 us
    unnamed x36, local copies, waits for them, and re-layouts  11.1 us
    convert_element_type x4, other arithmetic, sum_steps(): sent = total(1 - which).astype(BF16)  8.67 us
  transfers between devices with their start and end apart: 19, of which 11 were waited for; matrix products, arithmetic and copies ran while one was open for 6% of the time, Pallas kernels for 27%

profile of v6, /device:TPU:0, one launch (start us, length us, event | category | flops | bytes accessed | tf_op | source)
XLA Modules:
  0.0 272.1 jit_solution(10070751122992415439)
XLA Ops:
  2.2 25.1 %forward.1 = (bf16[1024,1536]{1,0:T(8,128)(2,1)}, bf16[1024,768]{1,0:T(8,128)(2,1)}, bf16[1024,768]{1,0:T(8,128)(2,1)}, bf16[1024,768]{1,0:T(8,128)(2,1)}, bf16[...) custom-call(bf16[1024,1536]{1,0:T(8,128)(2,1)} %hidden_ref.3, ...), custom_call_target="tpu_custom_call" | custom-call | tf_op jit(solution)/shard_map/forward/pallas_call | solution.py:815
  29.6 2.8 %collective-permute-start.1 = (f32[8,1024]{1,0:T(8,128)S(1)}, f32[8,1024]{1,0:T(8,128)S(1)}, u32[]{:S(2)}, u32[]{:S(2)}) collective-permute-start(f32[8,1024]{1,0:T(8,128)S(1)} %add.159), channel_id=1, source_target_pairs={{0,2},{1,3},{2,0},{3,1},{4,6},{5,7},{6,4},{7,5},{8,10},{9,11},{10,... | collective-permute-start | bytes 98312 | tf_op jit(solution)/shard_map/ppermute | solution.py:1214
  35.0 14.4 %gate.1 = (bf16[1024,768]{1,0:T(8,128)(2,1)}, f32[8,768]{1,0:T(8,128)}, bf16[1536,768]{1,0:T(8,128)(2,1)}, bf16[1536,768]{1,0:T(8,128)(2,1)}) custom-call(s32[1]{0:T(128)} %bitcast.3.low_ref.which_ref, bf16[1024,768]{1,0:T(8,128)(2,1)} %get-tuple-element.81.mixed_ref, bf16[1024,768]{1,0:T(8,128)(2,1)} %get-tuple-element.82.turn_ref, ...), custom_call_target="tpu_custom_call" | custom-call | tf_op jit(solution)/shard_map/gate/pallas_call | solution.py:878
  51.5 25.4 %backward.1 = (bf16[1024,256]{1,0:T(8,128)(2,1)}, bf16[1024,768]{1,0:T(8,128)(2,1)}, bf16[1024,128]{1,0:T(8,128)(2,1)}, f32[8,768]{1,0:T(8,128)}, f32[8,256]{1,0...) custom-call(bf16[1024,768]{1,0:T(8,128)(2,1)} %get-tuple-element.81.mixed_ref, ...), custom_call_target="tpu_custom_call" | custom-call | tf_op jit(solution)/shard_map/backward/pallas_call | solution.py:939
  84.0 7.0 %weight.1 = (bf16[768,768]{1,0:T(8,128)(2,1)}, bf16[768,768]{1,0:T(8,128)(2,1)}) custom-call(s32[1]{0:T(128)} %bitcast.3.low_ref.which_ref, bf16[1024,1536]{1,0:T(8,128)(2,1)} %get-tuple-element.85.normed_ref, bf16[1024,768]{1,0:T(8,128)(2,1)} %get-tuple-element.99.refs_1_.grad_ref.inner_low_ref, bf16[768,768]{1,0:T(8,128)(2,1)} %copy-done.9), custom_call_target="tpu_custom_call" | custom-call | tf_op jit(solution)/shard_map/weight/pallas_call | solution.py:904
  91.0 7.2 %collective-permute-done.3.refs_0_ = bf16[768,768]{1,0:T(8,128)(2,1)S(1)} collective-permute-done((bf16[768,768]{1,0:T(8,128)(2,1)S(1)}, bf16[768,768]{1,0:T(8,128)(2,1)S(1)}, u32[]{:S(2)}, u32[]{:S(2)}) %collective-permute-start.3) | collective-permute-done | bytes 1179680 | tf_op jit(solution)/shard_map/ppermute | solution.py:1356
  105.3 2.6 collective-permute-start.5
  107.9 18.0 %merge.1 = (bf16[512,3072]{1,0:T(8,128)(2,1)}, bf16[512,3072]{1,0:T(8,128)(2,1)}, f32[8,1536]{1,0:T(8,128)}) custom-call(s32[1]{0:T(128)} %bitcast.2.core_ref, bf16[1024,768]{1,0:T(8,128)(2,1)} %get-tuple-element.86.gate_low_ref, bf16[1024,768]{1,0:T(8,128)(2,1)} %get-tuple-element.99.refs_1_.grad_ref.inner_low_ref, ...), custom_call_target="tpu_custom_call" | custom-call | tf_op jit(solution)/shard_map/merge/pallas_call | solution.py:987
  131.5 2.6 pack.1
  136.7 3.1 %collective-permute-start.8 = (bf16[384,768]{1,0:T(8,128)(2,1)}, bf16[384,768]{1,0:T(8,128)(2,1)}, u32[]{:S(2)}, u32[]{:S(2)}) collective-permute-start(bf16[384,768]{1,0:T(8,128)(2,1)} %add_convert_fusion.1.refs_1_), channel_id=1, source_target_pairs={{0,16},{1,17},{2,18},{3,19},{4,20},{5,21},{6,22},{7,23},{8,24},{9,... | collective-permute-start | bytes 1769480 | tf_op jit(solution)/shard_map/ppermute | solution.py:1356
  139.8 4.0 %collective-permute-start.7 = (bf16[384,768]{1,0:T(8,128)(2,1)}, bf16[384,768]{1,0:T(8,128)(2,1)}, u32[]{:S(2)}, u32[]{:S(2)}) collective-permute-start(bf16[384,768]{1,0:T(8,128)(2,1)} %add_convert_fusion.2.refs_1_), channel_id=1, source_target_pairs={{0,8},{1,5},{2,10},{3,7},{4,12},{5,1},{6,14},{7,3},{8,0},{9,13},{1... | collective-permute-start | bytes 1769480 | tf_op jit(solution)/shard_map/ppermute | solution.py:1356
  153.5 13.2 %collective-permute-done.8.refs_1_ = bf16[384,768]{1,0:T(8,128)(2,1)} collective-permute-done((bf16[384,768]{1,0:T(8,128)(2,1)}, bf16[384,768]{1,0:T(8,128)(2,1)}, u32[]{:S(2)}, u32[]{:S(2)}) %collective-permute-start.8) | collective-permute-done | bytes 589856 | tf_op jit(solution)/shard_map/ppermute | solution.py:1356
  172.3 3.4 %collective-permute-start.11 = (bf16[192,768]{1,0:T(8,128)(2,1)}, bf16[192,768]{1,0:T(8,128)(2,1)S(1)}, u32[]{:S(2)}, u32[]{:S(2)}) collective-permute-start(bf16[192,768]{1,0:T(8,128)(2,1)} %add_convert_fusion.5.refs_1_), channel_id=1, source_target_pairs={{0,16},{1,17},{2,18},{3,19},{4,20},{5,21},{6,22},{7,23},{8,24},{9,... | collective-permute-start | bytes 884744 | tf_op jit(solution)/shard_map/ppermute | solution.py:1356
  175.7 23.0 %collective-permute-done.11.refs_0_ = bf16[192,768]{1,0:T(8,128)(2,1)S(1)} collective-permute-done((bf16[192,768]{1,0:T(8,128)(2,1)}, bf16[192,768]{1,0:T(8,128)(2,1)S(1)}, u32[]{:S(2)}, u32[]{:S(2)}) %collective-permute-start.11) | collective-permute-done | bytes 294944 | tf_op jit(solution)/shard_map/ppermute | solution.py:1356
  200.9 3.3 %collective-permute-start.14 = (bf16[192,768]{1,0:T(8,128)(2,1)S(1)}, bf16[192,768]{1,0:T(8,128)(2,1)}, u32[]{:S(2)}, u32[]{:S(2)}) collective-permute-start(bf16[192,768]{1,0:T(8,128)(2,1)S(1)} %add_convert_fusion.4.refs_1_), channel_id=1, source_target_pairs={{0,16},{1,17},{2,18},{3,19},{4,20},{5,21},{6,22},{7,23},{8,24},{9,... | collective-permute-start | bytes 884744 | tf_op jit(solution)/shard_map/ppermute | solution.py:1356
  206.0 4.2 %split.1 = (bf16[256,3072]{1,0:T(8,128)(2,1)}, bf16[256,3072]{1,0:T(8,128)(2,1)}) custom-call(s32[1]{0:T(128)} %bitcast.1.which_ref, bf16[512,3072]{1,0:T(8,128)(2,1)} %get-tuple-element.104.refs_2_.sent_one.kept_one, bf16[512,3072]{1,0:T(8,128)(2,1)} %pass.32.sent_two.kept_two, bf16[512,3072]{1,0:T(8,128)(2,1)} %get-tuple-element.104.refs_2_.sent_one.kept_one, ...), custom_call_target="tpu_custom_call" | custom-call | tf_op jit(solution)/shard_map/split/pallas_call | solution.py:1160
  213.6 3.6 %join.1.refs_1_.part_ref.own_ref = bf16[1792,768]{1,0:T(8,128)(2,1)} custom-call(s32[1]{0:T(128)} %bitcast.8.which_ref, bf16[960,768]{1,0:T(8,128)(2,1)} %pad_maximum_fusion.refs_1_.own_ref.own_extra_ref, bf16[960,768]{1,0:T(8,128)(2,1)} %pass.34.got_ref.got_extra_ref, bf16[960,768]{1,0:T(8,128)(2,1)} %pad_maximum_fusion.refs_1_.own_ref.own_extra_ref, ...), custom_call_target="tpu_custom_call" | custom-call | tf_op jit(solution)/shard_map/join/pallas_call | solution.py:1181
  217.7 4.8 %collective-permute-start.16 = (bf16[384,768]{1,0:T(8,128)(2,1)S(1)}, bf16[384,768]{1,0:T(8,128)(2,1)}, u32[]{:S(2)}, u32[]{:S(2)}) collective-permute-start(bf16[384,768]{1,0:T(8,128)(2,1)S(1)} %copy-done.6), channel_id=1, source_target_pairs={{0,8},{1,5},{2,10},{3,7},{4,12},{5,1},{6,14},{7,3},{8,0},{9,13},{1... | collective-permute-start | bytes 1769480 | tf_op jit(solution)/shard_map/ppermute | solution.py:1356
  224.1 12.8 %collective-permute-done.16.refs_0_ = bf16[384,768]{1,0:T(8,128)(2,1)} collective-permute-done((bf16[384,768]{1,0:T(8,128)(2,1)S(1)}, bf16[384,768]{1,0:T(8,128)(2,1)}, u32[]{:S(2)}, u32[]{:S(2)}) %collective-permute-start.16) | collective-permute-done | bytes 589856 | tf_op jit(solution)/shard_map/ppermute | solution.py:1356
  240.0 4.0 %finish_pair.2 = (f32[768,1536]{1,0:T(8,128)}, f32[1536,768]{1,0:T(8,128)}) custom-call(s32[1]{0:T(128)} %bitcast.3.low_ref.which_ref, bf16[1792,768]{1,0:T(8,128)(2,1)} %join.1.refs_1_.part_ref.own_ref, bf16[768,768]{1,0:T(8,128)(2,1)} %bitcast_select_fusion.after_ref.part_ref), custom_call_target="tpu_custom_call" | custom-call | tf_op jit(solution)/shard_map/finish_pair/pallas_call | solution.py:1133
  246.5 3.9 %collective-permute-done.15.refs_0_ = bf16[1792,768]{1,0:T(8,128)(2,1)S(1)} collective-permute-done((bf16[1792,768]{1,0:T(8,128)(2,1)}, bf16[1792,768]{1,0:T(8,128)(2,1)S(1)}, u32[]{:S(2)}, u32[]{:S(2)}) %collective-permute-start.15) | collective-permute-done | bytes 2752544 | tf_op jit(solution)/shard_map/ppermute | solution.py:1356
  253.8 3.5 %collective-permute-start.17 = (bf16[192,768]{1,0:T(8,128)(2,1)}, bf16[192,768]{1,0:T(8,128)(2,1)S(1)}, u32[]{:S(2)}, u32[]{:S(2)}) collective-permute-start(bf16[192,768]{1,0:T(8,128)(2,1)} %rider.1.one_ref), channel_id=1, source_target_pairs={{0,16},{1,17},{2,18},{3,19},{4,20},{5,21},{6,22},{7,23},{8,24},{9,... | collective-permute-start | bytes 884744 | tf_op jit(solution)/shard_map/ppermute | solution.py:1356
  257.3 4.0 %finish_pair.3 = (f32[768,1536]{1,0:T(8,128)}, f32[1536,768]{1,0:T(8,128)}) custom-call(s32[1]{0:T(128)} %bitcast.7.which_ref, bf16[1792,768]{1,0:T(8,128)(2,1)} %pass.36.part_ref.after_ref.got_ref, bf16[1792,768]{1,0:T(8,128)(2,1)} %pass.36.part_ref.after_ref.got_ref, ...), custom_call_target="tpu_custom_call", output_to_operand_aliasing={{0}: (3, {}), {1}: (4, {})} | custom-call | tf_op jit(solution)/shard_map/finish_pair/pallas_call | solution.py:1133
  261.3 4.0 %hidden.1 = (bf16[256,1536]{1,0:T(8,128)(2,1)}, f32[256,1536]{1,0:T(8,128)}) custom-call(s32[1]{0:T(128)} %bitcast.rank_ref, bf16[1024,1536]{1,0:T(8,128)(2,1)} %hidden_ref.3, bf16[1024,1536]{1,0:T(8,128)(2,1)} %cotan_ref.5, bf16[256,3072]{1,0:T(8,128)(2,1)} %get-tuple-element.121.kept_ref, bf16[256,3072]{1,0:T(8,128)(2,1)} %pass.37.got_ref, ...), custom_call_target="tpu_custom_call" | custom-call | tf_op jit(solution)/shard_map/hidden/pallas_call | solution.py:1072
  (114 shorter events, 71.4 us)
Async XLA Ops:
  27.3 1.6 collective-permute-start
  29.6 4.7 %collective-permute-start.1 = (f32[8,1024]{1,0:T(8,128)S(1)}, f32[8,1024]{1,0:T(8,128)S(1)}, u32[]{:S(2)}, u32[]{:S(2)}) collective-permute-start(f32[8,1024]{1,0:T(8,128)S(1)} %add.159), channel_id=1, source_target_pairs={{0,2},{1,3},{2,0},{3,1},{4,6},{5,7},{6,4},{7,5},{8,10},{9,11},{10,... | collective-permute-start | bytes 98312 | tf_op jit(solution)/shard_map/ppermute | solution.py:1214
  49.4 29.2 %collective-permute-start.2 = (bf16[1536,768]{1,0:T(8,128)(2,1)}, bf16[1536,768]{1,0:T(8,128)(2,1)S(1)}, u32[]{:S(2)}, u32[]{:S(2)}) collective-permute-start(bf16[1536,768]{1,0:T(8,128)(2,1)} %get-tuple-element.98.after_ref), channel_id=1, source_target_pairs={{0,4},{1,9},{2,6},{3,11},{4,0},{5,13},{6,2},{7,15},{8,12},{9,1},{1... | collective-permute-start | bytes 7077896 | tf_op jit(solution)/shard_map/ppermute | solution.py:1356
  81.8 2.2 copy-start.9
  81.9 16.3 %collective-permute-start.3 = (bf16[768,768]{1,0:T(8,128)(2,1)S(1)}, bf16[768,768]{1,0:T(8,128)(2,1)S(1)}, u32[]{:S(2)}, u32[]{:S(2)}) collective-permute-start(bf16[768,768]{1,0:T(8,128)(2,1)S(1)} %add_convert_fusion.after_ref), channel_id=1, source_target_pairs={{0,8},{1,5},{2,10},{3,7},{4,12},{5,1},{6,14},{7,3},{8,0},{9,13},{1... | collective-permute-start | bytes 3538952 | tf_op jit(solution)/shard_map/ppermute | solution.py:1356
  103.3 2.0 copy-start.5
  103.3 22.6 %collective-permute-start.4 = (bf16[768,768]{1,0:T(8,128)(2,1)}, bf16[768,768]{1,0:T(8,128)(2,1)}, u32[]{:S(2)}, u32[]{:S(2)}) collective-permute-start(bf16[768,768]{1,0:T(8,128)(2,1)} %pass.22), channel_id=1, source_target_pairs={{0,4},{1,9},{2,6},{3,11},{4,0},{5,13},{6,2},{7,15},{8,12},{9,1},{1... | collective-permute-start | bytes 3538952 | tf_op jit(solution)/shard_map/ppermute | solution.py:1356
  105.3 20.6 %collective-permute-start.5 = (bf16[384,768]{1,0:T(8,128)(2,1)S(1)}, bf16[384,768]{1,0:T(8,128)(2,1)S(1)}, u32[]{:S(2)}, u32[]{:S(2)}) collective-permute-start(bf16[384,768]{1,0:T(8,128)(2,1)S(1)} %copy-done.5), channel_id=1, source_target_pairs={{0,16},{1,17},{2,18},{3,19},{4,20},{5,21},{6,22},{7,23},{8,24},{9,... | collective-permute-start | bytes 1769480 | tf_op jit(solution)/shard_map/ppermute | solution.py:1356
  126.7 2.3 copy-start.8
  134.1 9.8 %collective-permute-start.9 = (bf16[272,768]{1,0:T(8,128)(2,1)}, bf16[272,768]{1,0:T(8,128)(2,1)}, u32[]{:S(2)}, u32[]{:S(2)}) collective-permute-start(bf16[272,768]{1,0:T(8,128)(2,1)} %get-tuple-element.117), channel_id=1, source_target_pairs={{0,1},{1,0},{2,3},{3,2},{4,5},{5,4},{6,7},{7,6},{8,9},{9,8},{10,11... | collective-permute-start | bytes 1253384 | tf_op jit(solution)/shard_map/ppermute | solution.py:1356
  136.6 67.7 %collective-permute-start.6 = (bf16[512,3072]{1,0:T(8,128)(2,1)}, bf16[512,3072]{1,0:T(8,128)(2,1)S(1)}, u32[]{:S(2)}, u32[]{:S(2)}) collective-permute-start(bf16[512,3072]{1,0:T(8,128)(2,1)} %pass.25), channel_id=1, source_target_pairs={{0,1},{1,0},{2,3},{3,2},{4,5},{5,4},{6,7},{7,6},{8,9},{9,8},{10,11... | collective-permute-start | bytes 9437192 | tf_op jit(solution)/shard_map/ppermute | solution.py:1356
  136.7 30.1 %collective-permute-start.8 = (bf16[384,768]{1,0:T(8,128)(2,1)}, bf16[384,768]{1,0:T(8,128)(2,1)}, u32[]{:S(2)}, u32[]{:S(2)}) collective-permute-start(bf16[384,768]{1,0:T(8,128)(2,1)} %add_convert_fusion.1.refs_1_), channel_id=1, source_target_pairs={{0,16},{1,17},{2,18},{3,19},{4,20},{5,21},{6,22},{7,23},{8,24},{9,... | collective-permute-start | bytes 1769480 | tf_op jit(solution)/shard_map/ppermute | solution.py:1356
  139.8 26.9 %collective-permute-start.7 = (bf16[384,768]{1,0:T(8,128)(2,1)}, bf16[384,768]{1,0:T(8,128)(2,1)}, u32[]{:S(2)}, u32[]{:S(2)}) collective-permute-start(bf16[384,768]{1,0:T(8,128)(2,1)} %add_convert_fusion.2.refs_1_), channel_id=1, source_target_pairs={{0,8},{1,5},{2,10},{3,7},{4,12},{5,1},{6,14},{7,3},{8,0},{9,13},{1... | collective-permute-start | bytes 1769480 | tf_op jit(solution)/shard_map/ppermute | solution.py:1356
  146.7 6.1 %collective-permute-start.10 = (bf16[144,768]{1,0:T(8,128)(2,1)}, bf16[144,768]{1,0:T(8,128)(2,1)S(1)}, u32[]{:S(2)}, u32[]{:S(2)}) collective-permute-start(bf16[144,768]{1,0:T(8,128)(2,1)} %pad_maximum_fusion.1.refs_1_), channel_id=1, source_target_pairs={{0,2},{1,3},{2,0},{3,1},{4,6},{5,7},{6,4},{7,5},{8,10},{9,11},{10,... | collective-permute-start | bytes 663560 | tf_op jit(solution)/shard_map/ppermute | solution.py:1356
  171.6 42.0 %collective-permute-start.13 = (bf16[960,768]{1,0:T(8,128)(2,1)}, bf16[960,768]{1,0:T(8,128)(2,1)}, u32[]{:S(2)}, u32[]{:S(2)}) collective-permute-start(bf16[960,768]{1,0:T(8,128)(2,1)} %pad_maximum_fusion.refs_1_.own_ref.own_extra_ref), channel_id=1, source_target_pairs={{0,8},{1,5},{2,10},{3,7},{4,12},{5,1},{6,14},{7,3},{8,0},{9,13},{1... | collective-permute-start | bytes 4423688 | tf_op jit(solution)/shard_map/ppermute | solution.py:1356
  172.3 26.4 %collective-permute-start.11 = (bf16[192,768]{1,0:T(8,128)(2,1)}, bf16[192,768]{1,0:T(8,128)(2,1)S(1)}, u32[]{:S(2)}, u32[]{:S(2)}) collective-permute-start(bf16[192,768]{1,0:T(8,128)(2,1)} %add_convert_fusion.5.refs_1_), channel_id=1, source_target_pairs={{0,16},{1,17},{2,18},{3,19},{4,20},{5,21},{6,22},{7,23},{8,24},{9,... | collective-permute-start | bytes 884744 | tf_op jit(solution)/shard_map/ppermute | solution.py:1356
  200.8 3.5 %copy-start.10 = (bf16[192,768]{1,0:T(8,128)(2,1)}, bf16[192,768]{1,0:T(8,128)(2,1)S(1)}, u32[]{:S(2)}) copy-start(bf16[192,768]{1,0:T(8,128)(2,1)S(1)} %add_convert_fusion.4.refs_1_) | copy-start | bytes 884740
  200.9 10.8 %collective-permute-start.14 = (bf16[192,768]{1,0:T(8,128)(2,1)S(1)}, bf16[192,768]{1,0:T(8,128)(2,1)}, u32[]{:S(2)}, u32[]{:S(2)}) collective-permute-start(bf16[192,768]{1,0:T(8,128)(2,1)S(1)} %add_convert_fusion.4.refs_1_), channel_id=1, source_target_pairs={{0,16},{1,17},{2,18},{3,19},{4,20},{5,21},{6,22},{7,23},{8,24},{9,... | collective-permute-start | bytes 884744 | tf_op jit(solution)/shard_map/ppermute | solution.py:1356
  213.6 4.1 %copy-start.6 = (bf16[384,768]{1,0:T(8,128)(2,1)S(1)}, bf16[384,768]{1,0:T(8,128)(2,1)}, u32[]{:S(2)}) copy-start(bf16[384,768]{1,0:T(8,128)(2,1)} %bitcast_select_fusion.2.refs_1_) | copy-start | bytes 1769476
  217.1 33.3 %collective-permute-start.15 = (bf16[1792,768]{1,0:T(8,128)(2,1)}, bf16[1792,768]{1,0:T(8,128)(2,1)S(1)}, u32[]{:S(2)}, u32[]{:S(2)}) collective-permute-start(bf16[1792,768]{1,0:T(8,128)(2,1)} %join.1.refs_1_.part_ref.own_ref), channel_id=1, source_target_pairs={{0,4},{1,9},{2,6},{3,11},{4,0},{5,13},{6,2},{7,15},{8,12},{9,1},{1... | collective-permute-start | bytes 8257544 | tf_op jit(solution)/shard_map/ppermute | solution.py:1356
  217.7 19.2 %collective-permute-start.16 = (bf16[384,768]{1,0:T(8,128)(2,1)S(1)}, bf16[384,768]{1,0:T(8,128)(2,1)}, u32[]{:S(2)}, u32[]{:S(2)}) collective-permute-start(bf16[384,768]{1,0:T(8,128)(2,1)S(1)} %copy-done.6), channel_id=1, source_target_pairs={{0,8},{1,5},{2,10},{3,7},{4,12},{5,1},{6,14},{7,3},{8,0},{9,13},{1... | collective-permute-start | bytes 1769480 | tf_op jit(solution)/shard_map/ppermute | solution.py:1356
  222.5 38.9 %collective-permute-start.12 = (bf16[256,3072]{1,0:T(8,128)(2,1)}, bf16[256,3072]{1,0:T(8,128)(2,1)}, u32[]{:S(2)}, u32[]{:S(2)}) collective-permute-start(bf16[256,3072]{1,0:T(8,128)(2,1)} %get-tuple-element.122.refs_1_), channel_id=1, source_target_pairs={{0,2},{1,3},{2,0},{3,1},{4,6},{5,7},{6,4},{7,5},{8,10},{9,11},{10,... | collective-permute-start | bytes 4718600 | tf_op jit(solution)/shard_map/ppermute | solution.py:1356
  239.1 30.5 %collective-permute-start.18 = (bf16[768,768]{1,0:T(8,128)(2,1)}, bf16[768,768]{1,0:T(8,128)(2,1)}, u32[]{:S(2)}, u32[]{:S(2)}) collective-permute-start(bf16[768,768]{1,0:T(8,128)(2,1)} %bitcast_select_fusion.after_ref.part_ref), channel_id=1, source_target_pairs={{0,4},{1,9},{2,6},{3,11},{4,0},{5,13},{6,2},{7,15},{8,12},{9,1},{1... | collective-permute-start | bytes 3538952 | tf_op jit(solution)/shard_map/ppermute | solution.py:1356
  253.8 13.1 %collective-permute-start.17 = (bf16[192,768]{1,0:T(8,128)(2,1)}, bf16[192,768]{1,0:T(8,128)(2,1)S(1)}, u32[]{:S(2)}, u32[]{:S(2)}) collective-permute-start(bf16[192,768]{1,0:T(8,128)(2,1)} %rider.1.one_ref), channel_id=1, source_target_pairs={{0,16},{1,17},{2,18},{3,19},{4,20},{5,21},{6,22},{7,23},{8,24},{9,... | collective-permute-start | bytes 884744 | tf_op jit(solution)/shard_map/ppermute | solution.py:1356
  (13 other events, 15.5 us)

commit v7 on v6

--- a/solution.py
+++ b/solution.py
@@ -579,9 +579,14 @@
     w_bc_ref,
     w_out_ref,
     row_ref,
+    conv_bc_ref,
     after_ref,
+    _,
+    __,
     sent_ref,
     kept_ref,
+    first_shared_ref,
+    second_shared_ref,
     gain_ref,
     wide_dt,
     gated,
@@ -619,7 +624,15 @@
     @pl.when(block == last)
     def _():
         gain = jnp.sum(gain_ref[...], axis=0, keepdims=True) / row_ref[0:1, :]
-        gain_ref[...] = jnp.broadcast_to(gain, gain_ref.shape)
+        channels = first_shared_ref.shape[1]
+        states = conv_bc_ref.shape[1]
+        rows = [gain[:, at : at + channels] for at in range(0, width, channels)]
+        conv = conv_bc_ref[0 : CONV + 1, :]
+        rows.append(jnp.concatenate([conv, jnp.zeros((CONV + 1, channels - states), F32)], axis=1))
+        rows.append(jnp.zeros((16 - width // channels - CONV - 1, channels), F32))
+        shared = jnp.concatenate(rows).astype(BF16)
+        first_shared_ref[...] = shared
+        second_shared_ref[...] = shared
 
 
 def pack_kernel(
@@ -629,8 +642,6 @@
     step_rows_ref,
     channel_ref,
     gate_gain_ref,
-    gain_ref,
-    conv_bc_ref,
     head_ref,
     sent_ref,
     kept_ref,
@@ -638,7 +649,7 @@
 ):
     core = core_ref[0]
     channels = channel_ref.shape[1]
-    states, width = bc_rows_ref.shape
+    width = bc_rows_ref.shape[1]
     folds = width // channels
     groups = (kept_ref.shape[0] - 16) // (OWN_BC * folds)
     for which, ref in ((1 - core, sent_ref), (core, kept_ref)):
@@ -647,11 +658,6 @@
             for fold in range(folds):
                 at = (group * folds + fold) * OWN_BC
                 ref[at : at + OWN_BC, :] = found[:, fold * channels : (fold + 1) * channels]
-        shared = [gain_ref[0:1, fold * channels : (fold + 1) * channels] for fold in range(folds)]
-        conv = conv_bc_ref[0 : CONV + 1, :]
-        shared.append(jnp.concatenate([conv, jnp.zeros((CONV + 1, channels - states), F32)], axis=1))
-        shared.append(jnp.zeros((16 - folds - CONV - 1, channels), F32))
-        ref[ref.shape[0] - 16 :, :] = jnp.concatenate(shared).astype(BF16)
     own_ref[...] = jnp.zeros(own_ref.shape, F32)
     for fold in range(folds):
         own_ref[16 * fold : 16 * fold + 16, :] = step_rows_ref[:, fold * channels : (fold + 1) * channels]
@@ -967,7 +973,7 @@
     )(*gate_inputs, sums, rows_table, *by_channel, step_in, cum, bc_low, enter, normed, *by_state, conv_x, conv_bc, head_values, tokens, after)
 
 
-def run_merge(core, blocked, sums, weights, rows_table, after, ranks):
+def run_merge(core, blocked, sums, weights, rows_table, conv_bc_grads, after, packed, ranks):
     normed = blocked[-1]
     rows, width = normed.shape
     channels = weights[0].shape[1]
@@ -984,6 +990,9 @@
         return pl.BlockSpec(shape, lambda i, c: (0,) * len(shape), pipeline_mode=pl.Buffered(1))
 
     out = jax.ShapeDtypeStruct((rows // 2, 2 * width), BF16)
+    last = packed[0].shape[0] // 16 - 1
+    shared = pl.BlockSpec((16, channels), lambda i, c: (last, 0))
+    first = 5 + len(blocked) + len(weights)
     return pl.pallas_call(
         merge_kernel,
         grid_spec=pltpu.PrefetchScalarGridSpec(
@@ -991,23 +1000,29 @@
             grid=(ranks,),
             in_specs=[block(array.shape[1]) for array in blocked]
             + [pl.BlockSpec((8, size), lambda i, c: (0, rank_at(i, c)))]
-            + [constant(array.shape) for array in (*weights, rows_table)]
-            + [in_place()],
+            + [constant(array.shape) for array in (*weights, rows_table, conv_bc_grads)]
+            + [in_place()] * 3,
             out_specs=[
                 pl.BlockSpec((size, 2 * width), lambda i, c: (jnp.minimum(i, half - 1), 0)),
                 pl.BlockSpec((size, 2 * width), lambda i, c: (jnp.maximum(i - half, 0), 0)),
-                constant((8, width)),
+                shared,
+                shared,
             ],
-            scratch_shapes=[pltpu.VMEM((LANES, width), BF16), pltpu.VMEM((size, channels), BF16)],
+            scratch_shapes=[
+                pltpu.VMEM((8, width), F32),
+                pltpu.VMEM((LANES, width), BF16),
+                pltpu.VMEM((size, channels), BF16),
+            ],
         ),
-        out_shape=[out, out, jax.ShapeDtypeStruct((8, width), F32)],
+        out_shape=[out, out] + [jax.ShapeDtypeStruct(array.shape, BF16) for array in packed],
+        input_output_aliases={first: 2, first + 1: 3},
         compiler_params=params(),
         cost_estimate=no_cost(),
         name="merge",
-    )(core, *blocked, sums, *weights, rows_table, after)
-
-
-def run_pack(core, bc_rows, step_rows, channel_grads, gain_rows, gain, conv_bc_grads, head_grads, head_count):
+    )(core, *blocked, sums, *weights, rows_table, conv_bc_grads, after, *packed)
+
+
+def run_pack(core, bc_rows, step_rows, channel_grads, gain_rows, head_grads, head_count):
     states, width = bc_rows.shape
     channels = channel_grads.shape[1]
     folds = width // channels
@@ -1015,13 +1030,13 @@
     shared = jax.ShapeDtypeStruct((states // 2 * folds + 16, channels), BF16)
     return pl.pallas_call(
         functools.partial(pack_kernel, head_count),
-        in_specs=[scalar_spec()] + [in_vmem] * 7,
+        in_specs=[scalar_spec()] + [in_vmem] * 5,
         out_specs=[in_vmem] * 3,
         out_shape=[shared, shared, jax.ShapeDtypeStruct((16 * folds + 16, channels), F32)],
         compiler_params=params(),
         cost_estimate=no_cost(),
         name="pack",
-    )(core, bc_rows, step_rows, channel_grads, gain_rows, gain, conv_bc_grads, head_grads)
+    )(core, bc_rows, step_rows, channel_grads, gain_rows, head_grads)
 
 
 def run_unpack(one, two, width, states, head_count):
@@ -1492,22 +1507,24 @@
     order.add("second", sum_steps(order.hold(sent), kept, None, second_own))
     order.go("second")
     core = jnp.reshape((my_rank % 2).astype(jnp.int32), (1,))
-    both_sent, both_kept, gain = run_merge(
+    small_sent, small_kept, small_own = run_pack(
+        core, bc_rows, step_rows, channel_grads, gain_rows, head_grads, head_count
+    )
+    both_sent, both_kept, small_sent, small_kept = run_merge(
         core,
         (gate_low, inner_low, step_low, state_low, mixed, normed),
         sums,
         (w_gate, w_value, w_dt_rows, w_bc, w_out),
         rows_table,
+        conv_bc_grads,
         order.last,
+        (small_sent, small_kept),
         ranks,
     )
     order.last = both_kept
     order.land("second", "first")
     order.go("second", "first")
-    small = run_pack(
-        core, bc_rows, step_rows, channel_grads, gain_rows, order.hold(gain), conv_bc_grads, head_grads, head_count
-    )
-    order.add("small", small_steps(*small))
+    order.add("small", small_steps(order.hold(small_sent), small_kept, small_own))
     order.go("small")
     order.add("both", both_steps(order.hold(both_sent), both_kept))
     order.go("both")

time: 273 us -> 270 us (0.989)
  transfers between devices with their start and end apart: 19 -> 19, of which waited for: 11 -> 11; matrix products, arithmetic and copies ran while one was open for 6% -> 6% of each run, Pallas kernels for 27% -> 28%
where the time goes in v7:
time: 270 us
  Pallas kernels  123 us (46%)
  waiting for transfers between devices  69.5 us (26%)
  starting transfers between devices  39.4 us (15%)
  other arithmetic  23.8 us (9%)
  local copies, waits for them, and re-layouts  13.3 us (5%)
    ppermute x17, waiting for transfers between devices, go(): self.flying[name] = (steps, lax.ppermute(sent, axis, moves))  66.5 us
    ppermute x17, starting transfers between devices, go(): self.flying[name] = (steps, lax.ppermute(sent, axis, moves))  36 us
    pallas_call x1, Pallas kernels, run_backward(): pl.pallas_call(functools.partial(backward_kernel, head_count), grid=(coun...  25.4 us
    pallas_call x1, Pallas kernels, run_forward(): pl.pallas_call(forward_kernel, grid=(rows // BLOCK,), in_specs=[block(wid...  25.1 us
    pallas_call x1, Pallas kernels, run_merge(): pl.pallas_call(merge_kernel, grid_spec=pltpu.PrefetchScalarGridSpec(num_s...  18 us
    pallas_call x1, Pallas kernels, run_gate(): pl.pallas_call(gate_kernel, grid=(rows // BLOCK,), in_specs=[scalar_spec(...  14.4 us
    unnamed x36, local copies, waits for them, and re-layouts  11.1 us
    convert_element_type x4, other arithmetic, sum_steps(): sent = total(1 - which).astype(BF16)  8.67 us
  transfers between devices with their start and end apart: 19, of which 11 were waited for; matrix products, arithmetic and copies ran while one was open for 6% of the time, Pallas kernels for 28%

profile of v7, /device:TPU:0, one launch (start us, length us, event | category | flops | bytes accessed | tf_op | source)
XLA Modules:
  0.0 269.6 jit_solution(6856567414299876353)
XLA Ops:
  2.2 25.1 %forward.1 = (bf16[1024,1536]{1,0:T(8,128)(2,1)}, bf16[1024,768]{1,0:T(8,128)(2,1)}, bf16[1024,768]{1,0:T(8,128)(2,1)}, bf16[1024,768]{1,0:T(8,128)(2,1)}, bf16[...) custom-call(bf16[1024,1536]{1,0:T(8,128)(2,1)} %hidden_ref.3, ...), custom_call_target="tpu_custom_call" | custom-call | tf_op jit(solution)/shard_map/forward/pallas_call | solution.py:821
  29.6 2.8 %collective-permute-start.1 = (f32[8,1024]{1,0:T(8,128)S(1)}, f32[8,1024]{1,0:T(8,128)S(1)}, u32[]{:S(2)}, u32[]{:S(2)}) collective-permute-start(f32[8,1024]{1,0:T(8,128)S(1)} %add.159), channel_id=1, source_target_pairs={{0,2},{1,3},{2,0},{3,1},{4,6},{5,7},{6,4},{7,5},{8,10},{9,11},{10,... | collective-permute-start | bytes 98312 | tf_op jit(solution)/shard_map/ppermute | solution.py:1229
  35.0 14.4 %gate.1 = (bf16[1024,768]{1,0:T(8,128)(2,1)}, f32[8,768]{1,0:T(8,128)}, bf16[1536,768]{1,0:T(8,128)(2,1)}, bf16[1536,768]{1,0:T(8,128)(2,1)}) custom-call(s32[1]{0:T(128)} %bitcast.3.low_ref.which_ref, bf16[1024,768]{1,0:T(8,128)(2,1)} %get-tuple-element.82.mixed_ref, bf16[1024,768]{1,0:T(8,128)(2,1)} %get-tuple-element.83.turn_ref, ...), custom_call_target="tpu_custom_call" | custom-call | tf_op jit(solution)/shard_map/gate/pallas_call | solution.py:884
  51.5 25.4 %backward.1 = (bf16[1024,256]{1,0:T(8,128)(2,1)}, bf16[1024,768]{1,0:T(8,128)(2,1)}, bf16[1024,128]{1,0:T(8,128)(2,1)}, f32[8,768]{1,0:T(8,128)}, f32[8,256]{1,0...) custom-call(bf16[1024,768]{1,0:T(8,128)(2,1)} %get-tuple-element.82.mixed_ref, ...), custom_call_target="tpu_custom_call" | custom-call | tf_op jit(solution)/shard_map/backward/pallas_call | solution.py:945
  84.0 7.0 %weight.1 = (bf16[768,768]{1,0:T(8,128)(2,1)}, bf16[768,768]{1,0:T(8,128)(2,1)}) custom-call(s32[1]{0:T(128)} %bitcast.3.low_ref.which_ref, bf16[1024,1536]{1,0:T(8,128)(2,1)} %get-tuple-element.86.normed_ref, bf16[1024,768]{1,0:T(8,128)(2,1)} %get-tuple-element.100.refs_1_.grad_ref.inner_low_ref, bf16[768,768]{1,0:T(8,128)(2,1)} %copy-done.9), custom_call_target="tpu_custom_call" | custom-call | tf_op jit(solution)/shard_map/weight/pallas_call | solution.py:910
  91.0 7.2 %collective-permute-done.3.refs_0_ = bf16[768,768]{1,0:T(8,128)(2,1)S(1)} collective-permute-done((bf16[768,768]{1,0:T(8,128)(2,1)S(1)}, bf16[768,768]{1,0:T(8,128)(2,1)S(1)}, u32[]{:S(2)}, u32[]{:S(2)}) %collective-permute-start.3) | collective-permute-done | bytes 1179680 | tf_op jit(solution)/shard_map/ppermute | solution.py:1371
  105.3 2.6 collective-permute-start.5
  107.9 2.6 pack.1
  110.5 18.0 %merge.1 = (bf16[512,3072]{1,0:T(8,128)(2,1)}, bf16[512,3072]{1,0:T(8,128)(2,1)}, bf16[272,768]{1,0:T(8,128)(2,1)}, bf16[272,768]{1,0:T(8,128)(2,1)}) custom-call(s32[1]{0:T(128)} %bitcast.2.core_ref, bf16[1024,768]{1,0:T(8,128)(2,1)} %get-tuple-element.87.gate_low_ref, ...), custom_call_target="tpu_custom_call", output_to_operand_aliasing={{2}: (16, {}), {3}: (17, {})} | custom-call | tf_op jit(solution)/shard_map/merge/pallas_call | solution.py:996
  137.2 4.1 %collective-permute-start.7 = (bf16[384,768]{1,0:T(8,128)(2,1)}, bf16[384,768]{1,0:T(8,128)(2,1)}, u32[]{:S(2)}, u32[]{:S(2)}) collective-permute-start(bf16[384,768]{1,0:T(8,128)(2,1)} %add_convert_fusion.2.refs_1_), channel_id=1, source_target_pairs={{0,8},{1,5},{2,10},{3,7},{4,12},{5,1},{6,14},{7,3},{8,0},{9,13},{1... | collective-permute-start | bytes 1769480 | tf_op jit(solution)/shard_map/ppermute | solution.py:1371
  150.9 13.2 %collective-permute-done.8.refs_1_ = bf16[384,768]{1,0:T(8,128)(2,1)} collective-permute-done((bf16[384,768]{1,0:T(8,128)(2,1)}, bf16[384,768]{1,0:T(8,128)(2,1)}, u32[]{:S(2)}, u32[]{:S(2)}) %collective-permute-start.8) | collective-permute-done | bytes 589856 | tf_op jit(solution)/shard_map/ppermute | solution.py:1371
  169.7 3.4 %collective-permute-start.11 = (bf16[192,768]{1,0:T(8,128)(2,1)}, bf16[192,768]{1,0:T(8,128)(2,1)S(1)}, u32[]{:S(2)}, u32[]{:S(2)}) collective-permute-start(bf16[192,768]{1,0:T(8,128)(2,1)} %add_convert_fusion.5.refs_1_), channel_id=1, source_target_pairs={{0,16},{1,17},{2,18},{3,19},{4,20},{5,21},{6,22},{7,23},{8,24},{9,... | collective-permute-start | bytes 884744 | tf_op jit(solution)/shard_map/ppermute | solution.py:1371
  173.1 23.0 %collective-permute-done.11.refs_0_ = bf16[192,768]{1,0:T(8,128)(2,1)S(1)} collective-permute-done((bf16[192,768]{1,0:T(8,128)(2,1)}, bf16[192,768]{1,0:T(8,128)(2,1)S(1)}, u32[]{:S(2)}, u32[]{:S(2)}) %collective-permute-start.11) | collective-permute-done | bytes 294944 | tf_op jit(solution)/shard_map/ppermute | solution.py:1371
  198.3 3.3 %collective-permute-start.14 = (bf16[192,768]{1,0:T(8,128)(2,1)S(1)}, bf16[192,768]{1,0:T(8,128)(2,1)}, u32[]{:S(2)}, u32[]{:S(2)}) collective-permute-start(bf16[192,768]{1,0:T(8,128)(2,1)S(1)} %add_convert_fusion.4.refs_1_), channel_id=1, source_target_pairs={{0,16},{1,17},{2,18},{3,19},{4,20},{5,21},{6,22},{7,23},{8,24},{9,... | collective-permute-start | bytes 884744 | tf_op jit(solution)/shard_map/ppermute | solution.py:1371
  203.5 4.2 %split.1 = (bf16[256,3072]{1,0:T(8,128)(2,1)}, bf16[256,3072]{1,0:T(8,128)(2,1)}) custom-call(s32[1]{0:T(128)} %bitcast.1.which_ref, bf16[512,3072]{1,0:T(8,128)(2,1)} %get-tuple-element.113.refs_2_.sent_one.kept_one, bf16[512,3072]{1,0:T(8,128)(2,1)} %pass.32.sent_two.kept_two, bf16[512,3072]{1,0:T(8,128)(2,1)} %get-tuple-element.113.refs_2_.sent_one.kept_one, ...), custom_call_target="tpu_custom_call" | custom-call | tf_op jit(solution)/shard_map/split/pallas_call | solution.py:1175
  211.0 3.6 %join.1.refs_1_.part_ref.own_ref = bf16[1792,768]{1,0:T(8,128)(2,1)} custom-call(s32[1]{0:T(128)} %bitcast.8.which_ref, bf16[960,768]{1,0:T(8,128)(2,1)} %pad_maximum_fusion.refs_1_.own_ref.own_extra_ref, bf16[960,768]{1,0:T(8,128)(2,1)} %pass.34.got_ref.got_extra_ref, bf16[960,768]{1,0:T(8,128)(2,1)} %pad_maximum_fusion.refs_1_.own_ref.own_extra_ref, ...), custom_call_target="tpu_custom_call" | custom-call | tf_op jit(solution)/shard_map/join/pallas_call | solution.py:1196
  214.9 5.0 %collective-permute-start.16 = (bf16[384,768]{1,0:T(8,128)(2,1)S(1)}, bf16[384,768]{1,0:T(8,128)(2,1)}, u32[]{:S(2)}, u32[]{:S(2)}) collective-permute-start(bf16[384,768]{1,0:T(8,128)(2,1)S(1)} %copy-done.6), channel_id=1, source_target_pairs={{0,8},{1,5},{2,10},{3,7},{4,12},{5,1},{6,14},{7,3},{8,0},{9,13},{1... | collective-permute-start | bytes 1769480 | tf_op jit(solution)/shard_map/ppermute | solution.py:1371
  221.5 12.8 %collective-permute-done.16.refs_0_ = bf16[384,768]{1,0:T(8,128)(2,1)} collective-permute-done((bf16[384,768]{1,0:T(8,128)(2,1)S(1)}, bf16[384,768]{1,0:T(8,128)(2,1)}, u32[]{:S(2)}, u32[]{:S(2)}) %collective-permute-start.16) | collective-permute-done | bytes 589856 | tf_op jit(solution)/shard_map/ppermute | solution.py:1371
  237.4 4.0 %finish_pair.2 = (f32[768,1536]{1,0:T(8,128)}, f32[1536,768]{1,0:T(8,128)}) custom-call(s32[1]{0:T(128)} %bitcast.3.low_ref.which_ref, bf16[1792,768]{1,0:T(8,128)(2,1)} %join.1.refs_1_.part_ref.own_ref, bf16[768,768]{1,0:T(8,128)(2,1)} %bitcast_select_fusion.after_ref.part_ref), custom_call_target="tpu_custom_call" | custom-call | tf_op jit(solution)/shard_map/finish_pair/pallas_call | solution.py:1148
  244.0 3.9 %collective-permute-done.15.refs_0_ = bf16[1792,768]{1,0:T(8,128)(2,1)S(1)} collective-permute-done((bf16[1792,768]{1,0:T(8,128)(2,1)}, bf16[1792,768]{1,0:T(8,128)(2,1)S(1)}, u32[]{:S(2)}, u32[]{:S(2)}) %collective-permute-start.15) | collective-permute-done | bytes 2752544 | tf_op jit(solution)/shard_map/ppermute | solution.py:1371
  251.3 3.5 %collective-permute-start.17 = (bf16[192,768]{1,0:T(8,128)(2,1)}, bf16[192,768]{1,0:T(8,128)(2,1)S(1)}, u32[]{:S(2)}, u32[]{:S(2)}) collective-permute-start(bf16[192,768]{1,0:T(8,128)(2,1)} %rider.1.one_ref), channel_id=1, source_target_pairs={{0,16},{1,17},{2,18},{3,19},{4,20},{5,21},{6,22},{7,23},{8,24},{9,... | collective-permute-start | bytes 884744 | tf_op jit(solution)/shard_map/ppermute | solution.py:1371
  254.8 4.0 %finish_pair.3 = (f32[768,1536]{1,0:T(8,128)}, f32[1536,768]{1,0:T(8,128)}) custom-call(s32[1]{0:T(128)} %bitcast.7.which_ref, bf16[1792,768]{1,0:T(8,128)(2,1)} %pass.36.part_ref.after_ref.got_ref, bf16[1792,768]{1,0:T(8,128)(2,1)} %pass.36.part_ref.after_ref.got_ref, ...), custom_call_target="tpu_custom_call", output_to_operand_aliasing={{0}: (3, {}), {1}: (4, {})} | custom-call | tf_op jit(solution)/shard_map/finish_pair/pallas_call | solution.py:1148
  258.8 4.0 %hidden.1 = (bf16[256,1536]{1,0:T(8,128)(2,1)}, f32[256,1536]{1,0:T(8,128)}) custom-call(s32[1]{0:T(128)} %bitcast.rank_ref, bf16[1024,1536]{1,0:T(8,128)(2,1)} %hidden_ref.3, bf16[1024,1536]{1,0:T(8,128)(2,1)} %cotan_ref.5, bf16[256,3072]{1,0:T(8,128)(2,1)} %get-tuple-element.123.kept_ref, bf16[256,3072]{1,0:T(8,128)(2,1)} %pass.37.got_ref, ...), custom_call_target="tpu_custom_call" | custom-call | tf_op jit(solution)/shard_map/hidden/pallas_call | solution.py:1087
  267.0 2.6 finish.3
  (114 shorter events, 69.1 us)
Async XLA Ops:
  27.3 1.6 collective-permute-start
  29.6 4.7 %collective-permute-start.1 = (f32[8,1024]{1,0:T(8,128)S(1)}, f32[8,1024]{1,0:T(8,128)S(1)}, u32[]{:S(2)}, u32[]{:S(2)}) collective-permute-start(f32[8,1024]{1,0:T(8,128)S(1)} %add.159), channel_id=1, source_target_pairs={{0,2},{1,3},{2,0},{3,1},{4,6},{5,7},{6,4},{7,5},{8,10},{9,11},{10,... | collective-permute-start | bytes 98312 | tf_op jit(solution)/shard_map/ppermute | solution.py:1229
  49.4 29.2 %collective-permute-start.2 = (bf16[1536,768]{1,0:T(8,128)(2,1)}, bf16[1536,768]{1,0:T(8,128)(2,1)S(1)}, u32[]{:S(2)}, u32[]{:S(2)}) collective-permute-start(bf16[1536,768]{1,0:T(8,128)(2,1)} %get-tuple-element.99.after_ref), channel_id=1, source_target_pairs={{0,4},{1,9},{2,6},{3,11},{4,0},{5,13},{6,2},{7,15},{8,12},{9,1},{1... | collective-permute-start | bytes 7077896 | tf_op jit(solution)/shard_map/ppermute | solution.py:1371
  81.8 2.2 copy-start.9
  81.9 16.3 %collective-permute-start.3 = (bf16[768,768]{1,0:T(8,128)(2,1)S(1)}, bf16[768,768]{1,0:T(8,128)(2,1)S(1)}, u32[]{:S(2)}, u32[]{:S(2)}) collective-permute-start(bf16[768,768]{1,0:T(8,128)(2,1)S(1)} %add_convert_fusion.after_ref), channel_id=1, source_target_pairs={{0,8},{1,5},{2,10},{3,7},{4,12},{5,1},{6,14},{7,3},{8,0},{9,13},{1... | collective-permute-start | bytes 3538952 | tf_op jit(solution)/shard_map/ppermute | solution.py:1371
  103.3 2.0 copy-start.5
  103.3 25.2 %collective-permute-start.4 = (bf16[768,768]{1,0:T(8,128)(2,1)}, bf16[768,768]{1,0:T(8,128)(2,1)}, u32[]{:S(2)}, u32[]{:S(2)}) collective-permute-start(bf16[768,768]{1,0:T(8,128)(2,1)} %pass.22), channel_id=1, source_target_pairs={{0,4},{1,9},{2,6},{3,11},{4,0},{5,13},{6,2},{7,15},{8,12},{9,1},{1... | collective-permute-start | bytes 3538952 | tf_op jit(solution)/shard_map/ppermute | solution.py:1371
  105.3 23.2 %collective-permute-start.5 = (bf16[384,768]{1,0:T(8,128)(2,1)S(1)}, bf16[384,768]{1,0:T(8,128)(2,1)S(1)}, u32[]{:S(2)}, u32[]{:S(2)}) collective-permute-start(bf16[384,768]{1,0:T(8,128)(2,1)S(1)} %copy-done.5), channel_id=1, source_target_pairs={{0,16},{1,17},{2,18},{3,19},{4,20},{5,21},{6,22},{7,23},{8,24},{9,... | collective-permute-start | bytes 1769480 | tf_op jit(solution)/shard_map/ppermute | solution.py:1371
  129.3 2.3 copy-start.8
  134.1 7.1 %collective-permute-start.9 = (bf16[272,768]{1,0:T(8,128)(2,1)}, bf16[272,768]{1,0:T(8,128)(2,1)}, u32[]{:S(2)}, u32[]{:S(2)}) collective-permute-start(bf16[272,768]{1,0:T(8,128)(2,1)} %pass.26), channel_id=1, source_target_pairs={{0,1},{1,0},{2,3},{3,2},{4,5},{5,4},{6,7},{7,6},{8,9},{9,8},{10,11... | collective-permute-start | bytes 1253384 | tf_op jit(solution)/shard_map/ppermute | solution.py:1371
  134.1 67.7 %collective-permute-start.6 = (bf16[512,3072]{1,0:T(8,128)(2,1)}, bf16[512,3072]{1,0:T(8,128)(2,1)S(1)}, u32[]{:S(2)}, u32[]{:S(2)}) collective-permute-start(bf16[512,3072]{1,0:T(8,128)(2,1)} %pass.25), channel_id=1, source_target_pairs={{0,1},{1,0},{2,3},{3,2},{4,5},{5,4},{6,7},{7,6},{8,9},{9,8},{10,11... | collective-permute-start | bytes 9437192 | tf_op jit(solution)/shard_map/ppermute | solution.py:1371
  134.7 29.5 %collective-permute-start.8 = (bf16[384,768]{1,0:T(8,128)(2,1)}, bf16[384,768]{1,0:T(8,128)(2,1)}, u32[]{:S(2)}, u32[]{:S(2)}) collective-permute-start(bf16[384,768]{1,0:T(8,128)(2,1)} %add_convert_fusion.1.refs_1_), channel_id=1, source_target_pairs={{0,16},{1,17},{2,18},{3,19},{4,20},{5,21},{6,22},{7,23},{8,24},{9,... | collective-permute-start | bytes 1769480 | tf_op jit(solution)/shard_map/ppermute | solution.py:1371
  137.2 27.0 %collective-permute-start.7 = (bf16[384,768]{1,0:T(8,128)(2,1)}, bf16[384,768]{1,0:T(8,128)(2,1)}, u32[]{:S(2)}, u32[]{:S(2)}) collective-permute-start(bf16[384,768]{1,0:T(8,128)(2,1)} %add_convert_fusion.2.refs_1_), channel_id=1, source_target_pairs={{0,8},{1,5},{2,10},{3,7},{4,12},{5,1},{6,14},{7,3},{8,0},{9,13},{1... | collective-permute-start | bytes 1769480 | tf_op jit(solution)/shard_map/ppermute | solution.py:1371
  144.1 6.1 %collective-permute-start.10 = (bf16[144,768]{1,0:T(8,128)(2,1)}, bf16[144,768]{1,0:T(8,128)(2,1)S(1)}, u32[]{:S(2)}, u32[]{:S(2)}) collective-permute-start(bf16[144,768]{1,0:T(8,128)(2,1)} %pad_maximum_fusion.1.refs_1_), channel_id=1, source_target_pairs={{0,2},{1,3},{2,0},{3,1},{4,6},{5,7},{6,4},{7,5},{8,10},{9,11},{10,... | collective-permute-start | bytes 663560 | tf_op jit(solution)/shard_map/ppermute | solution.py:1371
  169.0 42.1 %collective-permute-start.13 = (bf16[960,768]{1,0:T(8,128)(2,1)}, bf16[960,768]{1,0:T(8,128)(2,1)}, u32[]{:S(2)}, u32[]{:S(2)}) collective-permute-start(bf16[960,768]{1,0:T(8,128)(2,1)} %pad_maximum_fusion.refs_1_.own_ref.own_extra_ref), channel_id=1, source_target_pairs={{0,8},{1,5},{2,10},{3,7},{4,12},{5,1},{6,14},{7,3},{8,0},{9,13},{1... | collective-permute-start | bytes 4423688 | tf_op jit(solution)/shard_map/ppermute | solution.py:1371
  169.7 26.4 %collective-permute-start.11 = (bf16[192,768]{1,0:T(8,128)(2,1)}, bf16[192,768]{1,0:T(8,128)(2,1)S(1)}, u32[]{:S(2)}, u32[]{:S(2)}) collective-permute-start(bf16[192,768]{1,0:T(8,128)(2,1)} %add_convert_fusion.5.refs_1_), channel_id=1, source_target_pairs={{0,16},{1,17},{2,18},{3,19},{4,20},{5,21},{6,22},{7,23},{8,24},{9,... | collective-permute-start | bytes 884744 | tf_op jit(solution)/shard_map/ppermute | solution.py:1371
  198.3 3.5 %copy-start.10 = (bf16[192,768]{1,0:T(8,128)(2,1)}, bf16[192,768]{1,0:T(8,128)(2,1)S(1)}, u32[]{:S(2)}) copy-start(bf16[192,768]{1,0:T(8,128)(2,1)S(1)} %add_convert_fusion.4.refs_1_) | copy-start | bytes 884740
  198.3 10.8 %collective-permute-start.14 = (bf16[192,768]{1,0:T(8,128)(2,1)S(1)}, bf16[192,768]{1,0:T(8,128)(2,1)}, u32[]{:S(2)}, u32[]{:S(2)}) collective-permute-start(bf16[192,768]{1,0:T(8,128)(2,1)S(1)} %add_convert_fusion.4.refs_1_), channel_id=1, source_target_pairs={{0,16},{1,17},{2,18},{3,19},{4,20},{5,21},{6,22},{7,23},{8,24},{9,... | collective-permute-start | bytes 884744 | tf_op jit(solution)/shard_map/ppermute | solution.py:1371
  211.0 3.8 %copy-start.6 = (bf16[384,768]{1,0:T(8,128)(2,1)S(1)}, bf16[384,768]{1,0:T(8,128)(2,1)}, u32[]{:S(2)}) copy-start(bf16[384,768]{1,0:T(8,128)(2,1)} %bitcast_select_fusion.2.refs_1_) | copy-start | bytes 1769476
  214.6 33.3 %collective-permute-start.15 = (bf16[1792,768]{1,0:T(8,128)(2,1)}, bf16[1792,768]{1,0:T(8,128)(2,1)S(1)}, u32[]{:S(2)}, u32[]{:S(2)}) collective-permute-start(bf16[1792,768]{1,0:T(8,128)(2,1)} %join.1.refs_1_.part_ref.own_ref), channel_id=1, source_target_pairs={{0,4},{1,9},{2,6},{3,11},{4,0},{5,13},{6,2},{7,15},{8,12},{9,1},{1... | collective-permute-start | bytes 8257544 | tf_op jit(solution)/shard_map/ppermute | solution.py:1371
  214.9 19.3 %collective-permute-start.16 = (bf16[384,768]{1,0:T(8,128)(2,1)S(1)}, bf16[384,768]{1,0:T(8,128)(2,1)}, u32[]{:S(2)}, u32[]{:S(2)}) collective-permute-start(bf16[384,768]{1,0:T(8,128)(2,1)S(1)} %copy-done.6), channel_id=1, source_target_pairs={{0,8},{1,5},{2,10},{3,7},{4,12},{5,1},{6,14},{7,3},{8,0},{9,13},{1... | collective-permute-start | bytes 1769480 | tf_op jit(solution)/shard_map/ppermute | solution.py:1371
  219.9 38.9 %collective-permute-start.12 = (bf16[256,3072]{1,0:T(8,128)(2,1)}, bf16[256,3072]{1,0:T(8,128)(2,1)}, u32[]{:S(2)}, u32[]{:S(2)}) collective-permute-start(bf16[256,3072]{1,0:T(8,128)(2,1)} %get-tuple-element.124.refs_1_), channel_id=1, source_target_pairs={{0,2},{1,3},{2,0},{3,1},{4,6},{5,7},{6,4},{7,5},{8,10},{9,11},{10,... | collective-permute-start | bytes 4718600 | tf_op jit(solution)/shard_map/ppermute | solution.py:1371
  236.5 30.5 %collective-permute-start.18 = (bf16[768,768]{1,0:T(8,128)(2,1)}, bf16[768,768]{1,0:T(8,128)(2,1)}, u32[]{:S(2)}, u32[]{:S(2)}) collective-permute-start(bf16[768,768]{1,0:T(8,128)(2,1)} %bitcast_select_fusion.after_ref.part_ref), channel_id=1, source_target_pairs={{0,4},{1,9},{2,6},{3,11},{4,0},{5,13},{6,2},{7,15},{8,12},{9,1},{1... | collective-permute-start | bytes 3538952 | tf_op jit(solution)/shard_map/ppermute | solution.py:1371
  251.3 13.1 %collective-permute-start.17 = (bf16[192,768]{1,0:T(8,128)(2,1)}, bf16[192,768]{1,0:T(8,128)(2,1)S(1)}, u32[]{:S(2)}, u32[]{:S(2)}) collective-permute-start(bf16[192,768]{1,0:T(8,128)(2,1)} %rider.1.one_ref), channel_id=1, source_target_pairs={{0,16},{1,17},{2,18},{3,19},{4,20},{5,21},{6,22},{7,23},{8,24},{9,... | collective-permute-start | bytes 884744 | tf_op jit(solution)/shard_map/ppermute | solution.py:1371
  (13 other events, 15.5 us)

commit v8 on v7

--- a/solution.py
+++ b/solution.py
@@ -750,27 +750,25 @@
 def join_kernel(which_ref, own_ref, got_ref, own_extra_ref, got_extra_ref, out_ref):
     which = which_ref[0]
     rows = own_ref.shape[0]
-    extra_rows = own_extra_ref.shape[0]
     out_ref[pl.ds(pl.multiple_of(which * rows, 16), rows), :] = own_ref[...]
     out_ref[pl.ds(pl.multiple_of((1 - which) * rows, 16), rows), :] = got_ref[...]
     extra = own_extra_ref[...].astype(F32) + got_extra_ref[...].astype(F32)
     at = 2 * rows
-    out_ref[at : at + extra_rows, :] = extra.astype(BF16)
+    out_ref[at:, :] = extra.astype(BF16)
     shared = slice(SHARED_AT, SHARED_AT + 16)
-    out_ref[at + SHARED_AT : at + SHARED_AT + 16, :] = own_extra_ref[shared, :]
-    out_ref[at + extra_rows : at + extra_rows + 16, :] = got_extra_ref[shared, :]
-    out_ref[at + extra_rows + 16 :, :] = jnp.zeros((48, out_ref.shape[1]), BF16)
+    own_rows, got_rows = own_extra_ref[shared, :].astype(F32), got_extra_ref[shared, :].astype(F32)
+    both_rows = jnp.concatenate([own_rows[0:8], got_rows[0:8]])
+    out_ref[at + SHARED_AT : at + SHARED_AT + 16, :] = both_rows.astype(BF16)
 
 
 def rider_kernel(core_ref, own_ref, got_ref, out_ref):
-    rows = out_ref.shape[0]
-    out_ref[...] = (own_ref[0:rows, :].astype(F32) + got_ref[0:rows, :].astype(F32)).astype(BF16)
-    shared, second = slice(SHARED_AT, SHARED_AT + 16), slice(rows, rows + 16)
-    own, near = own_ref[shared, :].astype(F32), own_ref[second, :].astype(F32)
-    other, far = got_ref[shared, :].astype(F32), got_ref[second, :].astype(F32)
+    out_ref[...] = (own_ref[...].astype(F32) + got_ref[...].astype(F32)).astype(BF16)
+    shared = slice(SHARED_AT, SHARED_AT + 16)
+    own, got = own_ref[shared, :].astype(F32), got_ref[shared, :].astype(F32)
     is_first = core_ref[0] == 0
-    total = (own + jnp.where(is_first, other, near)) + (jnp.where(is_first, near, other) + far)
-    out_ref[shared, :] = total.astype(BF16)
+    first = own[0:8] + jnp.where(is_first, got[0:8], own[8:16])
+    second = jnp.where(is_first, own[8:16], got[0:8]) + got[8:16]
+    out_ref[shared, :] = jnp.concatenate([first + second, jnp.zeros_like(first)]).astype(BF16)
 
 
 def whole(shape):
@@ -1192,7 +1190,7 @@
     columns = own.shape[1]
     matrix = pl.BlockSpec((rows, columns), lambda i, w: (0, 0))
     extra = pl.BlockSpec((extra_rows, columns), lambda i, w: (rows // extra_rows, 0))
-    shape = (2 * rows + extra_rows + 64, columns)
+    shape = (2 * rows + extra_rows, columns)
     return pl.pallas_call(
         join_kernel,
         grid_spec=pltpu.PrefetchScalarGridSpec(
@@ -1210,8 +1208,7 @@
 
 def run_rider(core, own, got, rows):
     columns = own.shape[1]
-    held = rows + 64
-    last = pl.BlockSpec((held, columns), lambda i: (own.shape[0] // held - 1, 0))
+    last = pl.BlockSpec((rows, columns), lambda i: (own.shape[0] // rows - 1, 0))
     return pl.pallas_call(
         rider_kernel,
         grid=(1,),

time: 270 us -> 269 us (level)
  no operation moved by 1% of the time
where the time goes in v8:
time: 269 us; the launch traced here: 268 us
  Pallas kernels  123 us (46%)
  waiting for transfers between devices  68.6 us (26%)
  starting transfers between devices  39.4 us (15%)
  other arithmetic  23.8 us (9%)
  local copies, waits for them, and re-layouts  13.3 us (5%)
    ppermute x17, waiting for transfers between devices, go(): self.flying[name] = (steps, lax.ppermute(sent, axis, moves))  65.6 us
    ppermute x17, starting transfers between devices, go(): self.flying[name] = (steps, lax.ppermute(sent, axis, moves))  36 us
    pallas_call x1, Pallas kernels, run_backward(): pl.pallas_call(functools.partial(backward_kernel, head_count), grid=(coun...  25.4 us
    pallas_call x1, Pallas kernels, run_forward(): pl.pallas_call(forward_kernel, grid=(rows // BLOCK,), in_specs=[block(wid...  25.1 us
    pallas_call x1, Pallas kernels, run_merge(): pl.pallas_call(merge_kernel, grid_spec=pltpu.PrefetchScalarGridSpec(num_s...  18 us
    pallas_call x1, Pallas kernels, run_gate(): pl.pallas_call(gate_kernel, grid=(rows // BLOCK,), in_specs=[scalar_spec(...  14.4 us
    unnamed x36, local copies, waits for them, and re-layouts  11.1 us
    convert_element_type x4, other arithmetic, sum_steps(): sent = total(1 - which).astype(BF16)  8.67 us
  transfers between devices with their start and end apart: 19, of which 11 were waited for; matrix products, arithmetic and copies ran while one was open for 6% of the time, Pallas kernels for 28%

profile of v8, /device:TPU:0, one launch (start us, length us, event | category | flops | bytes accessed | tf_op | source)
XLA Modules:
  0.0 268.5 jit_solution(9721237095850772051)
XLA Ops:
  2.2 25.1 %forward.1 = (bf16[1024,1536]{1,0:T(8,128)(2,1)}, bf16[1024,768]{1,0:T(8,128)(2,1)}, bf16[1024,768]{1,0:T(8,128)(2,1)}, bf16[1024,768]{1,0:T(8,128)(2,1)}, bf16[...) custom-call(bf16[1024,1536]{1,0:T(8,128)(2,1)} %hidden_ref.3, ...), custom_call_target="tpu_custom_call" | custom-call | tf_op jit(solution)/shard_map/forward/pallas_call | solution.py:819
  29.6 2.8 %collective-permute-start.1 = (f32[8,1024]{1,0:T(8,128)S(1)}, f32[8,1024]{1,0:T(8,128)S(1)}, u32[]{:S(2)}, u32[]{:S(2)}) collective-permute-start(f32[8,1024]{1,0:T(8,128)S(1)} %add.159), channel_id=1, source_target_pairs={{0,2},{1,3},{2,0},{3,1},{4,6},{5,7},{6,4},{7,5},{8,10},{9,11},{10,... | collective-permute-start | bytes 98312 | tf_op jit(solution)/shard_map/ppermute | solution.py:1226
  35.0 14.4 %gate.1 = (bf16[1024,768]{1,0:T(8,128)(2,1)}, f32[8,768]{1,0:T(8,128)}, bf16[1536,768]{1,0:T(8,128)(2,1)}, bf16[1536,768]{1,0:T(8,128)(2,1)}) custom-call(s32[1]{0:T(128)} %bitcast.3.low_ref.which_ref, bf16[1024,768]{1,0:T(8,128)(2,1)} %get-tuple-element.82.mixed_ref, bf16[1024,768]{1,0:T(8,128)(2,1)} %get-tuple-element.83.turn_ref, ...), custom_call_target="tpu_custom_call" | custom-call | tf_op jit(solution)/shard_map/gate/pallas_call | solution.py:882
  51.5 25.4 %backward.1 = (bf16[1024,256]{1,0:T(8,128)(2,1)}, bf16[1024,768]{1,0:T(8,128)(2,1)}, bf16[1024,128]{1,0:T(8,128)(2,1)}, f32[8,768]{1,0:T(8,128)}, f32[8,256]{1,0...) custom-call(bf16[1024,768]{1,0:T(8,128)(2,1)} %get-tuple-element.82.mixed_ref, ...), custom_call_target="tpu_custom_call" | custom-call | tf_op jit(solution)/shard_map/backward/pallas_call | solution.py:943
  84.0 6.9 %weight.1 = (bf16[768,768]{1,0:T(8,128)(2,1)}, bf16[768,768]{1,0:T(8,128)(2,1)}) custom-call(s32[1]{0:T(128)} %bitcast.3.low_ref.which_ref, bf16[1024,1536]{1,0:T(8,128)(2,1)} %get-tuple-element.86.normed_ref, bf16[1024,768]{1,0:T(8,128)(2,1)} %get-tuple-element.100.refs_1_.grad_ref.inner_low_ref, bf16[768,768]{1,0:T(8,128)(2,1)} %copy-done.9), custom_call_target="tpu_custom_call" | custom-call | tf_op jit(solution)/shard_map/weight/pallas_call | solution.py:908
  90.9 7.3 %collective-permute-done.3.refs_0_ = bf16[768,768]{1,0:T(8,128)(2,1)S(1)} collective-permute-done((bf16[768,768]{1,0:T(8,128)(2,1)S(1)}, bf16[768,768]{1,0:T(8,128)(2,1)S(1)}, u32[]{:S(2)}, u32[]{:S(2)}) %collective-permute-start.3) | collective-permute-done | bytes 1179680 | tf_op jit(solution)/shard_map/ppermute | solution.py:1368
  105.3 2.6 collective-permute-start.5
  107.9 2.6 pack.1
  110.5 18.0 %merge.1 = (bf16[512,3072]{1,0:T(8,128)(2,1)}, bf16[512,3072]{1,0:T(8,128)(2,1)}, bf16[272,768]{1,0:T(8,128)(2,1)}, bf16[272,768]{1,0:T(8,128)(2,1)}) custom-call(s32[1]{0:T(128)} %bitcast.2.core_ref, bf16[1024,768]{1,0:T(8,128)(2,1)} %get-tuple-element.87.gate_low_ref, ...), custom_call_target="tpu_custom_call", output_to_operand_aliasing={{2}: (16, {}), {3}: (17, {})} | custom-call | tf_op jit(solution)/shard_map/merge/pallas_call | solution.py:994
  137.2 4.1 %collective-permute-start.7 = (bf16[384,768]{1,0:T(8,128)(2,1)}, bf16[384,768]{1,0:T(8,128)(2,1)}, u32[]{:S(2)}, u32[]{:S(2)}) collective-permute-start(bf16[384,768]{1,0:T(8,128)(2,1)} %add_convert_fusion.2.refs_1_), channel_id=1, source_target_pairs={{0,8},{1,5},{2,10},{3,7},{4,12},{5,1},{6,14},{7,3},{8,0},{9,13},{1... | collective-permute-start | bytes 1769480 | tf_op jit(solution)/shard_map/ppermute | solution.py:1368
  150.9 13.2 %collective-permute-done.8.refs_1_ = bf16[384,768]{1,0:T(8,128)(2,1)} collective-permute-done((bf16[384,768]{1,0:T(8,128)(2,1)}, bf16[384,768]{1,0:T(8,128)(2,1)}, u32[]{:S(2)}, u32[]{:S(2)}) %collective-permute-start.8) | collective-permute-done | bytes 589856 | tf_op jit(solution)/shard_map/ppermute | solution.py:1368
  169.7 3.4 %collective-permute-start.11 = (bf16[192,768]{1,0:T(8,128)(2,1)}, bf16[192,768]{1,0:T(8,128)(2,1)S(1)}, u32[]{:S(2)}, u32[]{:S(2)}) collective-permute-start(bf16[192,768]{1,0:T(8,128)(2,1)} %add_convert_fusion.5.refs_1_), channel_id=1, source_target_pairs={{0,16},{1,17},{2,18},{3,19},{4,20},{5,21},{6,22},{7,23},{8,24},{9,... | collective-permute-start | bytes 884744 | tf_op jit(solution)/shard_map/ppermute | solution.py:1368
  173.1 23.0 %collective-permute-done.11.refs_0_ = bf16[192,768]{1,0:T(8,128)(2,1)S(1)} collective-permute-done((bf16[192,768]{1,0:T(8,128)(2,1)}, bf16[192,768]{1,0:T(8,128)(2,1)S(1)}, u32[]{:S(2)}, u32[]{:S(2)}) %collective-permute-start.11) | collective-permute-done | bytes 294944 | tf_op jit(solution)/shard_map/ppermute | solution.py:1368
  198.3 3.3 %collective-permute-start.14 = (bf16[192,768]{1,0:T(8,128)(2,1)S(1)}, bf16[192,768]{1,0:T(8,128)(2,1)}, u32[]{:S(2)}, u32[]{:S(2)}) collective-permute-start(bf16[192,768]{1,0:T(8,128)(2,1)S(1)} %add_convert_fusion.4.refs_1_), channel_id=1, source_target_pairs={{0,16},{1,17},{2,18},{3,19},{4,20},{5,21},{6,22},{7,23},{8,24},{9,... | collective-permute-start | bytes 884744 | tf_op jit(solution)/shard_map/ppermute | solution.py:1368
  203.5 4.2 %split.1 = (bf16[256,3072]{1,0:T(8,128)(2,1)}, bf16[256,3072]{1,0:T(8,128)(2,1)}) custom-call(s32[1]{0:T(128)} %bitcast.1.which_ref, bf16[512,3072]{1,0:T(8,128)(2,1)} %get-tuple-element.113.refs_2_.sent_one.kept_one, bf16[512,3072]{1,0:T(8,128)(2,1)} %pass.32.sent_two.kept_two, bf16[512,3072]{1,0:T(8,128)(2,1)} %get-tuple-element.113.refs_2_.sent_one.kept_one, ...), custom_call_target="tpu_custom_call" | custom-call | tf_op jit(solution)/shard_map/split/pallas_call | solution.py:1173
  211.0 3.5 %join.1.refs_1_.part_ref.own_ref = bf16[1728,768]{1,0:T(8,128)(2,1)} custom-call(s32[1]{0:T(128)} %bitcast.8.which_ref, bf16[960,768]{1,0:T(8,128)(2,1)} %pad_maximum_fusion.refs_1_.own_ref.own_extra_ref, bf16[960,768]{1,0:T(8,128)(2,1)} %pass.34.got_ref.got_extra_ref, bf16[960,768]{1,0:T(8,128)(2,1)} %pad_maximum_fusion.refs_1_.own_ref.own_extra_ref, ...), custom_call_target="tpu_custom_call" | custom-call | tf_op jit(solution)/shard_map/join/pallas_call | solution.py:1194
  214.9 5.0 %collective-permute-start.16 = (bf16[384,768]{1,0:T(8,128)(2,1)S(1)}, bf16[384,768]{1,0:T(8,128)(2,1)}, u32[]{:S(2)}, u32[]{:S(2)}) collective-permute-start(bf16[384,768]{1,0:T(8,128)(2,1)S(1)} %copy-done.6), channel_id=1, source_target_pairs={{0,8},{1,5},{2,10},{3,7},{4,12},{5,1},{6,14},{7,3},{8,0},{9,13},{1... | collective-permute-start | bytes 1769480 | tf_op jit(solution)/shard_map/ppermute | solution.py:1368
  221.5 12.8 %collective-permute-done.16.refs_0_ = bf16[384,768]{1,0:T(8,128)(2,1)} collective-permute-done((bf16[384,768]{1,0:T(8,128)(2,1)S(1)}, bf16[384,768]{1,0:T(8,128)(2,1)}, u32[]{:S(2)}, u32[]{:S(2)}) %collective-permute-start.16) | collective-permute-done | bytes 589856 | tf_op jit(solution)/shard_map/ppermute | solution.py:1368
  237.4 4.0 %finish_pair.2 = (f32[768,1536]{1,0:T(8,128)}, f32[1536,768]{1,0:T(8,128)}) custom-call(s32[1]{0:T(128)} %bitcast.3.low_ref.which_ref, bf16[1728,768]{1,0:T(8,128)(2,1)} %join.1.refs_1_.part_ref.own_ref, bf16[768,768]{1,0:T(8,128)(2,1)} %bitcast_select_fusion.after_ref.part_ref), custom_call_target="tpu_custom_call" | custom-call | tf_op jit(solution)/shard_map/finish_pair/pallas_call | solution.py:1146
  244.0 2.8 %collective-permute-done.15.refs_0_ = bf16[1728,768]{1,0:T(8,128)(2,1)S(1)} collective-permute-done((bf16[1728,768]{1,0:T(8,128)(2,1)}, bf16[1728,768]{1,0:T(8,128)(2,1)S(1)}, u32[]{:S(2)}, u32[]{:S(2)}) %collective-permute-start.15) | collective-permute-done | bytes 2654240 | tf_op jit(solution)/shard_map/ppermute | solution.py:1368
  250.1 3.5 %collective-permute-start.17 = (bf16[192,768]{1,0:T(8,128)(2,1)}, bf16[192,768]{1,0:T(8,128)(2,1)S(1)}, u32[]{:S(2)}, u32[]{:S(2)}) collective-permute-start(bf16[192,768]{1,0:T(8,128)(2,1)} %rider.1.one_ref), channel_id=1, source_target_pairs={{0,16},{1,17},{2,18},{3,19},{4,20},{5,21},{6,22},{7,23},{8,24},{9,... | collective-permute-start | bytes 884744 | tf_op jit(solution)/shard_map/ppermute | solution.py:1368
  253.6 4.0 %finish_pair.3 = (f32[768,1536]{1,0:T(8,128)}, f32[1536,768]{1,0:T(8,128)}) custom-call(s32[1]{0:T(128)} %bitcast.7.which_ref, bf16[1728,768]{1,0:T(8,128)(2,1)} %pass.36.part_ref.after_ref.got_ref, bf16[1728,768]{1,0:T(8,128)(2,1)} %pass.36.part_ref.after_ref.got_ref, ...), custom_call_target="tpu_custom_call", output_to_operand_aliasing={{0}: (3, {}), {1}: (4, {})} | custom-call | tf_op jit(solution)/shard_map/finish_pair/pallas_call | solution.py:1146
  257.6 4.0 %hidden.1 = (bf16[256,1536]{1,0:T(8,128)(2,1)}, f32[256,1536]{1,0:T(8,128)}) custom-call(s32[1]{0:T(128)} %bitcast.rank_ref, bf16[1024,1536]{1,0:T(8,128)(2,1)} %hidden_ref.3, bf16[1024,1536]{1,0:T(8,128)(2,1)} %cotan_ref.5, bf16[256,3072]{1,0:T(8,128)(2,1)} %get-tuple-element.123.kept_ref, bf16[256,3072]{1,0:T(8,128)(2,1)} %pass.37.got_ref, ...), custom_call_target="tpu_custom_call" | custom-call | tf_op jit(solution)/shard_map/hidden/pallas_call | solution.py:1085
  265.9 2.6 finish.3
  (114 shorter events, 69.1 us)
Async XLA Ops:
  27.3 1.6 collective-permute-start
  29.6 4.7 %collective-permute-start.1 = (f32[8,1024]{1,0:T(8,128)S(1)}, f32[8,1024]{1,0:T(8,128)S(1)}, u32[]{:S(2)}, u32[]{:S(2)}) collective-permute-start(f32[8,1024]{1,0:T(8,128)S(1)} %add.159), channel_id=1, source_target_pairs={{0,2},{1,3},{2,0},{3,1},{4,6},{5,7},{6,4},{7,5},{8,10},{9,11},{10,... | collective-permute-start | bytes 98312 | tf_op jit(solution)/shard_map/ppermute | solution.py:1226
  49.4 29.2 %collective-permute-start.2 = (bf16[1536,768]{1,0:T(8,128)(2,1)}, bf16[1536,768]{1,0:T(8,128)(2,1)S(1)}, u32[]{:S(2)}, u32[]{:S(2)}) collective-permute-start(bf16[1536,768]{1,0:T(8,128)(2,1)} %get-tuple-element.99.after_ref), channel_id=1, source_target_pairs={{0,4},{1,9},{2,6},{3,11},{4,0},{5,13},{6,2},{7,15},{8,12},{9,1},{1... | collective-permute-start | bytes 7077896 | tf_op jit(solution)/shard_map/ppermute | solution.py:1368
  81.8 2.2 copy-start.9
  81.9 16.3 %collective-permute-start.3 = (bf16[768,768]{1,0:T(8,128)(2,1)S(1)}, bf16[768,768]{1,0:T(8,128)(2,1)S(1)}, u32[]{:S(2)}, u32[]{:S(2)}) collective-permute-start(bf16[768,768]{1,0:T(8,128)(2,1)S(1)} %add_convert_fusion.after_ref), channel_id=1, source_target_pairs={{0,8},{1,5},{2,10},{3,7},{4,12},{5,1},{6,14},{7,3},{8,0},{9,13},{1... | collective-permute-start | bytes 3538952 | tf_op jit(solution)/shard_map/ppermute | solution.py:1368
  103.3 2.0 copy-start.5
  103.3 25.2 %collective-permute-start.4 = (bf16[768,768]{1,0:T(8,128)(2,1)}, bf16[768,768]{1,0:T(8,128)(2,1)}, u32[]{:S(2)}, u32[]{:S(2)}) collective-permute-start(bf16[768,768]{1,0:T(8,128)(2,1)} %pass.22), channel_id=1, source_target_pairs={{0,4},{1,9},{2,6},{3,11},{4,0},{5,13},{6,2},{7,15},{8,12},{9,1},{1... | collective-permute-start | bytes 3538952 | tf_op jit(solution)/shard_map/ppermute | solution.py:1368
  105.3 23.2 %collective-permute-start.5 = (bf16[384,768]{1,0:T(8,128)(2,1)S(1)}, bf16[384,768]{1,0:T(8,128)(2,1)S(1)}, u32[]{:S(2)}, u32[]{:S(2)}) collective-permute-start(bf16[384,768]{1,0:T(8,128)(2,1)S(1)} %copy-done.5), channel_id=1, source_target_pairs={{0,16},{1,17},{2,18},{3,19},{4,20},{5,21},{6,22},{7,23},{8,24},{9,... | collective-permute-start | bytes 1769480 | tf_op jit(solution)/shard_map/ppermute | solution.py:1368
  129.4 2.3 copy-start.8
  134.2 7.1 %collective-permute-start.9 = (bf16[272,768]{1,0:T(8,128)(2,1)}, bf16[272,768]{1,0:T(8,128)(2,1)}, u32[]{:S(2)}, u32[]{:S(2)}) collective-permute-start(bf16[272,768]{1,0:T(8,128)(2,1)} %pass.26), channel_id=1, source_target_pairs={{0,1},{1,0},{2,3},{3,2},{4,5},{5,4},{6,7},{7,6},{8,9},{9,8},{10,11... | collective-permute-start | bytes 1253384 | tf_op jit(solution)/shard_map/ppermute | solution.py:1368
  134.2 67.6 %collective-permute-start.6 = (bf16[512,3072]{1,0:T(8,128)(2,1)}, bf16[512,3072]{1,0:T(8,128)(2,1)S(1)}, u32[]{:S(2)}, u32[]{:S(2)}) collective-permute-start(bf16[512,3072]{1,0:T(8,128)(2,1)} %pass.25), channel_id=1, source_target_pairs={{0,1},{1,0},{2,3},{3,2},{4,5},{5,4},{6,7},{7,6},{8,9},{9,8},{10,11... | collective-permute-start | bytes 9437192 | tf_op jit(solution)/shard_map/ppermute | solution.py:1368
  134.7 29.5 %collective-permute-start.8 = (bf16[384,768]{1,0:T(8,128)(2,1)}, bf16[384,768]{1,0:T(8,128)(2,1)}, u32[]{:S(2)}, u32[]{:S(2)}) collective-permute-start(bf16[384,768]{1,0:T(8,128)(2,1)} %add_convert_fusion.1.refs_1_), channel_id=1, source_target_pairs={{0,16},{1,17},{2,18},{3,19},{4,20},{5,21},{6,22},{7,23},{8,24},{9,... | collective-permute-start | bytes 1769480 | tf_op jit(solution)/shard_map/ppermute | solution.py:1368
  137.2 27.0 %collective-permute-start.7 = (bf16[384,768]{1,0:T(8,128)(2,1)}, bf16[384,768]{1,0:T(8,128)(2,1)}, u32[]{:S(2)}, u32[]{:S(2)}) collective-permute-start(bf16[384,768]{1,0:T(8,128)(2,1)} %add_convert_fusion.2.refs_1_), channel_id=1, source_target_pairs={{0,8},{1,5},{2,10},{3,7},{4,12},{5,1},{6,14},{7,3},{8,0},{9,13},{1... | collective-permute-start | bytes 1769480 | tf_op jit(solution)/shard_map/ppermute | solution.py:1368
  144.1 6.1 %collective-permute-start.10 = (bf16[144,768]{1,0:T(8,128)(2,1)}, bf16[144,768]{1,0:T(8,128)(2,1)S(1)}, u32[]{:S(2)}, u32[]{:S(2)}) collective-permute-start(bf16[144,768]{1,0:T(8,128)(2,1)} %pad_maximum_fusion.1.refs_1_), channel_id=1, source_target_pairs={{0,2},{1,3},{2,0},{3,1},{4,6},{5,7},{6,4},{7,5},{8,10},{9,11},{10,... | collective-permute-start | bytes 663560 | tf_op jit(solution)/shard_map/ppermute | solution.py:1368
  169.0 42.1 %collective-permute-start.13 = (bf16[960,768]{1,0:T(8,128)(2,1)}, bf16[960,768]{1,0:T(8,128)(2,1)}, u32[]{:S(2)}, u32[]{:S(2)}) collective-permute-start(bf16[960,768]{1,0:T(8,128)(2,1)} %pad_maximum_fusion.refs_1_.own_ref.own_extra_ref), channel_id=1, source_target_pairs={{0,8},{1,5},{2,10},{3,7},{4,12},{5,1},{6,14},{7,3},{8,0},{9,13},{1... | collective-permute-start | bytes 4423688 | tf_op jit(solution)/shard_map/ppermute | solution.py:1368
  169.7 26.4 %collective-permute-start.11 = (bf16[192,768]{1,0:T(8,128)(2,1)}, bf16[192,768]{1,0:T(8,128)(2,1)S(1)}, u32[]{:S(2)}, u32[]{:S(2)}) collective-permute-start(bf16[192,768]{1,0:T(8,128)(2,1)} %add_convert_fusion.5.refs_1_), channel_id=1, source_target_pairs={{0,16},{1,17},{2,18},{3,19},{4,20},{5,21},{6,22},{7,23},{8,24},{9,... | collective-permute-start | bytes 884744 | tf_op jit(solution)/shard_map/ppermute | solution.py:1368
  198.3 3.5 %copy-start.10 = (bf16[192,768]{1,0:T(8,128)(2,1)}, bf16[192,768]{1,0:T(8,128)(2,1)S(1)}, u32[]{:S(2)}) copy-start(bf16[192,768]{1,0:T(8,128)(2,1)S(1)} %add_convert_fusion.4.refs_1_) | copy-start | bytes 884740
  198.3 10.8 %collective-permute-start.14 = (bf16[192,768]{1,0:T(8,128)(2,1)S(1)}, bf16[192,768]{1,0:T(8,128)(2,1)}, u32[]{:S(2)}, u32[]{:S(2)}) collective-permute-start(bf16[192,768]{1,0:T(8,128)(2,1)S(1)} %add_convert_fusion.4.refs_1_), channel_id=1, source_target_pairs={{0,16},{1,17},{2,18},{3,19},{4,20},{5,21},{6,22},{7,23},{8,24},{9,... | collective-permute-start | bytes 884744 | tf_op jit(solution)/shard_map/ppermute | solution.py:1368
  211.0 3.8 %copy-start.6 = (bf16[384,768]{1,0:T(8,128)(2,1)S(1)}, bf16[384,768]{1,0:T(8,128)(2,1)}, u32[]{:S(2)}) copy-start(bf16[384,768]{1,0:T(8,128)(2,1)} %bitcast_select_fusion.2.refs_1_) | copy-start | bytes 1769476
  214.6 32.2 %collective-permute-start.15 = (bf16[1728,768]{1,0:T(8,128)(2,1)}, bf16[1728,768]{1,0:T(8,128)(2,1)S(1)}, u32[]{:S(2)}, u32[]{:S(2)}) collective-permute-start(bf16[1728,768]{1,0:T(8,128)(2,1)} %join.1.refs_1_.part_ref.own_ref), channel_id=1, source_target_pairs={{0,4},{1,9},{2,6},{3,11},{4,0},{5,13},{6,2},{7,15},{8,12},{9,1},{1... | collective-permute-start | bytes 7962632 | tf_op jit(solution)/shard_map/ppermute | solution.py:1368
  214.9 19.3 %collective-permute-start.16 = (bf16[384,768]{1,0:T(8,128)(2,1)S(1)}, bf16[384,768]{1,0:T(8,128)(2,1)}, u32[]{:S(2)}, u32[]{:S(2)}) collective-permute-start(bf16[384,768]{1,0:T(8,128)(2,1)S(1)} %copy-done.6), channel_id=1, source_target_pairs={{0,8},{1,5},{2,10},{3,7},{4,12},{5,1},{6,14},{7,3},{8,0},{9,13},{1... | collective-permute-start | bytes 1769480 | tf_op jit(solution)/shard_map/ppermute | solution.py:1368
  219.9 37.8 %collective-permute-start.12 = (bf16[256,3072]{1,0:T(8,128)(2,1)}, bf16[256,3072]{1,0:T(8,128)(2,1)}, u32[]{:S(2)}, u32[]{:S(2)}) collective-permute-start(bf16[256,3072]{1,0:T(8,128)(2,1)} %get-tuple-element.124.refs_1_), channel_id=1, source_target_pairs={{0,2},{1,3},{2,0},{3,1},{4,6},{5,7},{6,4},{7,5},{8,10},{9,11},{10,... | collective-permute-start | bytes 4718600 | tf_op jit(solution)/shard_map/ppermute | solution.py:1368
  236.5 29.4 %collective-permute-start.18 = (bf16[768,768]{1,0:T(8,128)(2,1)}, bf16[768,768]{1,0:T(8,128)(2,1)}, u32[]{:S(2)}, u32[]{:S(2)}) collective-permute-start(bf16[768,768]{1,0:T(8,128)(2,1)} %bitcast_select_fusion.after_ref.part_ref), channel_id=1, source_target_pairs={{0,4},{1,9},{2,6},{3,11},{4,0},{5,13},{6,2},{7,15},{8,12},{9,1},{1... | collective-permute-start | bytes 3538952 | tf_op jit(solution)/shard_map/ppermute | solution.py:1368
  250.1 13.1 %collective-permute-start.17 = (bf16[192,768]{1,0:T(8,128)(2,1)}, bf16[192,768]{1,0:T(8,128)(2,1)S(1)}, u32[]{:S(2)}, u32[]{:S(2)}) collective-permute-start(bf16[192,768]{1,0:T(8,128)(2,1)} %rider.1.one_ref), channel_id=1, source_target_pairs={{0,16},{1,17},{2,18},{3,19},{4,20},{5,21},{6,22},{7,23},{8,24},{9,... | collective-permute-start | bytes 884744 | tf_op jit(solution)/shard_map/ppermute | solution.py:1368
  (13 other events, 15.5 us)

commit v9 on v8

--- a/solution.py
+++ b/solution.py
@@ -1553,11 +1553,11 @@
         jnp.reshape(my_rank.astype(jnp.int32), (1,)), hidden_in, cotangent, kept, got, rows_table
     )
     order.last = hidden_grad
+    _, own, got, _ = order.result("second")
+    w_value_sum = run_finish(1 - which, got, order.last, own.shape[0], w_value_sum)
+    order.last = w_value_sum
     one, two = order.result("rest")
     small = run_unpack(one, two, width, w_bc.shape[1], head_count)
-    order.last = small[0]
-    _, own, got, _ = order.result("second")
-    w_value_sum = run_finish(1 - which, got, order.last, own.shape[0], w_value_sum)
     (
         pre_gain_grad,
         w_bc_rows,

time: 269 us -> 268 us (level)
  transfers between devices with their start and end apart: 19 -> 19, of which waited for: 11 -> 10; matrix products, arithmetic and copies ran while one was open for 6% -> 6% of each run, Pallas kernels for 28% -> 29%
where the time goes in v9:
time: 268 us; the launch traced here: 267 us
  Pallas kernels  123 us (46%)
  waiting for transfers between devices  66.9 us (25%)
  starting transfers between devices  39.4 us (15%)
  other arithmetic  23.8 us (9%)
  local copies, waits for them, and re-layouts  13.3 us (5%)
    ppermute x17, waiting for transfers between devices, go(): self.flying[name] = (steps, lax.ppermute(sent, axis, moves))  64 us
    ppermute x17, starting transfers between devices, go(): self.flying[name] = (steps, lax.ppermute(sent, axis, moves))  36 us
    pallas_call x1, Pallas kernels, run_backward(): pl.pallas_call(functools.partial(backward_kernel, head_count), grid=(coun...  25.4 us
    pallas_call x1, Pallas kernels, run_forward(): pl.pallas_call(forward_kernel, grid=(rows // BLOCK,), in_specs=[block(wid...  25.1 us
    pallas_call x1, Pallas kernels, run_merge(): pl.pallas_call(merge_kernel, grid_spec=pltpu.PrefetchScalarGridSpec(num_s...  18 us
    pallas_call x1, Pallas kernels, run_gate(): pl.pallas_call(gate_kernel, grid=(rows // BLOCK,), in_specs=[scalar_spec(...  14.4 us
    unnamed x36, local copies, waits for them, and re-layouts  11.1 us
    convert_element_type x4, other arithmetic, sum_steps(): sent = total(1 - which).astype(BF16)  8.67 us
  transfers between devices with their start and end apart: 19, of which 10 were waited for; matrix products, arithmetic and copies ran while one was open for 6% of the time, Pallas kernels for 29%

profile of v9, /device:TPU:0, one launch (start us, length us, event | category | flops | bytes accessed | tf_op | source)
XLA Modules:
  0.0 267.0 jit_solution(14599500018676129276)
XLA Ops:
  2.2 25.1 %forward.1 = (bf16[1024,1536]{1,0:T(8,128)(2,1)}, bf16[1024,768]{1,0:T(8,128)(2,1)}, bf16[1024,768]{1,0:T(8,128)(2,1)}, bf16[1024,768]{1,0:T(8,128)(2,1)}, bf16[...) custom-call(bf16[1024,1536]{1,0:T(8,128)(2,1)} %hidden_ref.3, ...), custom_call_target="tpu_custom_call" | custom-call | tf_op jit(solution)/shard_map/forward/pallas_call | solution.py:819
  29.6 2.8 %collective-permute-start.1 = (f32[8,1024]{1,0:T(8,128)S(1)}, f32[8,1024]{1,0:T(8,128)S(1)}, u32[]{:S(2)}, u32[]{:S(2)}) collective-permute-start(f32[8,1024]{1,0:T(8,128)S(1)} %add.159), channel_id=1, source_target_pairs={{0,2},{1,3},{2,0},{3,1},{4,6},{5,7},{6,4},{7,5},{8,10},{9,11},{10,... | collective-permute-start | bytes 98312 | tf_op jit(solution)/shard_map/ppermute | solution.py:1226
  35.0 14.4 %gate.1 = (bf16[1024,768]{1,0:T(8,128)(2,1)}, f32[8,768]{1,0:T(8,128)}, bf16[1536,768]{1,0:T(8,128)(2,1)}, bf16[1536,768]{1,0:T(8,128)(2,1)}) custom-call(s32[1]{0:T(128)} %bitcast.3.low_ref.which_ref, bf16[1024,768]{1,0:T(8,128)(2,1)} %get-tuple-element.82.mixed_ref, bf16[1024,768]{1,0:T(8,128)(2,1)} %get-tuple-element.83.turn_ref, ...), custom_call_target="tpu_custom_call" | custom-call | tf_op jit(solution)/shard_map/gate/pallas_call | solution.py:882
  51.5 25.4 %backward.1 = (bf16[1024,256]{1,0:T(8,128)(2,1)}, bf16[1024,768]{1,0:T(8,128)(2,1)}, bf16[1024,128]{1,0:T(8,128)(2,1)}, f32[8,768]{1,0:T(8,128)}, f32[8,256]{1,0...) custom-call(bf16[1024,768]{1,0:T(8,128)(2,1)} %get-tuple-element.82.mixed_ref, ...), custom_call_target="tpu_custom_call" | custom-call | tf_op jit(solution)/shard_map/backward/pallas_call | solution.py:943
  84.0 6.9 %weight.1 = (bf16[768,768]{1,0:T(8,128)(2,1)}, bf16[768,768]{1,0:T(8,128)(2,1)}) custom-call(s32[1]{0:T(128)} %bitcast.3.low_ref.which_ref, bf16[1024,1536]{1,0:T(8,128)(2,1)} %get-tuple-element.86.normed_ref, bf16[1024,768]{1,0:T(8,128)(2,1)} %get-tuple-element.100.refs_1_.grad_ref.inner_low_ref, bf16[768,768]{1,0:T(8,128)(2,1)} %copy-done.9), custom_call_target="tpu_custom_call" | custom-call | tf_op jit(solution)/shard_map/weight/pallas_call | solution.py:908
  90.9 7.3 %collective-permute-done.3.refs_0_ = bf16[768,768]{1,0:T(8,128)(2,1)S(1)} collective-permute-done((bf16[768,768]{1,0:T(8,128)(2,1)S(1)}, bf16[768,768]{1,0:T(8,128)(2,1)S(1)}, u32[]{:S(2)}, u32[]{:S(2)}) %collective-permute-start.3) | collective-permute-done | bytes 1179680 | tf_op jit(solution)/shard_map/ppermute | solution.py:1368
  105.3 2.6 collective-permute-start.5
  107.9 2.6 pack.1
  110.5 18.0 %merge.1 = (bf16[512,3072]{1,0:T(8,128)(2,1)}, bf16[512,3072]{1,0:T(8,128)(2,1)}, bf16[272,768]{1,0:T(8,128)(2,1)}, bf16[272,768]{1,0:T(8,128)(2,1)}) custom-call(s32[1]{0:T(128)} %bitcast.2.core_ref, bf16[1024,768]{1,0:T(8,128)(2,1)} %get-tuple-element.87.gate_low_ref, ...), custom_call_target="tpu_custom_call", output_to_operand_aliasing={{2}: (16, {}), {3}: (17, {})} | custom-call | tf_op jit(solution)/shard_map/merge/pallas_call | solution.py:994
  137.2 4.1 %collective-permute-start.7 = (bf16[384,768]{1,0:T(8,128)(2,1)}, bf16[384,768]{1,0:T(8,128)(2,1)}, u32[]{:S(2)}, u32[]{:S(2)}) collective-permute-start(bf16[384,768]{1,0:T(8,128)(2,1)} %add_convert_fusion.2.refs_1_), channel_id=1, source_target_pairs={{0,8},{1,5},{2,10},{3,7},{4,12},{5,1},{6,14},{7,3},{8,0},{9,13},{1... | collective-permute-start | bytes 1769480 | tf_op jit(solution)/shard_map/ppermute | solution.py:1368
  150.9 13.2 %collective-permute-done.8.refs_1_ = bf16[384,768]{1,0:T(8,128)(2,1)} collective-permute-done((bf16[384,768]{1,0:T(8,128)(2,1)}, bf16[384,768]{1,0:T(8,128)(2,1)}, u32[]{:S(2)}, u32[]{:S(2)}) %collective-permute-start.8) | collective-permute-done | bytes 589856 | tf_op jit(solution)/shard_map/ppermute | solution.py:1368
  169.7 3.4 %collective-permute-start.11 = (bf16[192,768]{1,0:T(8,128)(2,1)}, bf16[192,768]{1,0:T(8,128)(2,1)S(1)}, u32[]{:S(2)}, u32[]{:S(2)}) collective-permute-start(bf16[192,768]{1,0:T(8,128)(2,1)} %add_convert_fusion.5.refs_1_), channel_id=1, source_target_pairs={{0,16},{1,17},{2,18},{3,19},{4,20},{5,21},{6,22},{7,23},{8,24},{9,... | collective-permute-start | bytes 884744 | tf_op jit(solution)/shard_map/ppermute | solution.py:1368
  173.1 23.0 %collective-permute-done.11.refs_0_ = bf16[192,768]{1,0:T(8,128)(2,1)S(1)} collective-permute-done((bf16[192,768]{1,0:T(8,128)(2,1)}, bf16[192,768]{1,0:T(8,128)(2,1)S(1)}, u32[]{:S(2)}, u32[]{:S(2)}) %collective-permute-start.11) | collective-permute-done | bytes 294944 | tf_op jit(solution)/shard_map/ppermute | solution.py:1368
  198.3 3.3 %collective-permute-start.14 = (bf16[192,768]{1,0:T(8,128)(2,1)S(1)}, bf16[192,768]{1,0:T(8,128)(2,1)}, u32[]{:S(2)}, u32[]{:S(2)}) collective-permute-start(bf16[192,768]{1,0:T(8,128)(2,1)S(1)} %add_convert_fusion.4.refs_1_), channel_id=1, source_target_pairs={{0,16},{1,17},{2,18},{3,19},{4,20},{5,21},{6,22},{7,23},{8,24},{9,... | collective-permute-start | bytes 884744 | tf_op jit(solution)/shard_map/ppermute | solution.py:1368
  203.5 4.2 %split.1 = (bf16[256,3072]{1,0:T(8,128)(2,1)}, bf16[256,3072]{1,0:T(8,128)(2,1)}) custom-call(s32[1]{0:T(128)} %bitcast.1.which_ref, bf16[512,3072]{1,0:T(8,128)(2,1)} %get-tuple-element.113.refs_2_.sent_one.kept_one, bf16[512,3072]{1,0:T(8,128)(2,1)} %pass.32.sent_two.kept_two, bf16[512,3072]{1,0:T(8,128)(2,1)} %get-tuple-element.113.refs_2_.sent_one.kept_one, ...), custom_call_target="tpu_custom_call" | custom-call | tf_op jit(solution)/shard_map/split/pallas_call | solution.py:1173
  211.0 3.5 %join.1.refs_1_.part_ref.own_ref = bf16[1728,768]{1,0:T(8,128)(2,1)} custom-call(s32[1]{0:T(128)} %bitcast.8.which_ref, bf16[960,768]{1,0:T(8,128)(2,1)} %pad_maximum_fusion.refs_1_.own_ref.own_extra_ref, bf16[960,768]{1,0:T(8,128)(2,1)} %pass.34.got_ref.got_extra_ref, bf16[960,768]{1,0:T(8,128)(2,1)} %pad_maximum_fusion.refs_1_.own_ref.own_extra_ref, ...), custom_call_target="tpu_custom_call" | custom-call | tf_op jit(solution)/shard_map/join/pallas_call | solution.py:1194
  214.9 5.0 %collective-permute-start.16 = (bf16[384,768]{1,0:T(8,128)(2,1)S(1)}, bf16[384,768]{1,0:T(8,128)(2,1)}, u32[]{:S(2)}, u32[]{:S(2)}) collective-permute-start(bf16[384,768]{1,0:T(8,128)(2,1)S(1)} %copy-done.6), channel_id=1, source_target_pairs={{0,8},{1,5},{2,10},{3,7},{4,12},{5,1},{6,14},{7,3},{8,0},{9,13},{1... | collective-permute-start | bytes 1769480 | tf_op jit(solution)/shard_map/ppermute | solution.py:1368
  221.5 12.8 %collective-permute-done.16.refs_0_ = bf16[384,768]{1,0:T(8,128)(2,1)} collective-permute-done((bf16[384,768]{1,0:T(8,128)(2,1)S(1)}, bf16[384,768]{1,0:T(8,128)(2,1)}, u32[]{:S(2)}, u32[]{:S(2)}) %collective-permute-start.16) | collective-permute-done | bytes 589856 | tf_op jit(solution)/shard_map/ppermute | solution.py:1368
  237.4 4.0 %finish_pair.2 = (f32[768,1536]{1,0:T(8,128)}, f32[1536,768]{1,0:T(8,128)}) custom-call(s32[1]{0:T(128)} %bitcast.3.low_ref.which_ref, bf16[1728,768]{1,0:T(8,128)(2,1)} %join.1.refs_1_.part_ref.own_ref, bf16[768,768]{1,0:T(8,128)(2,1)} %bitcast_select_fusion.after_ref.part_ref), custom_call_target="tpu_custom_call" | custom-call | tf_op jit(solution)/shard_map/finish_pair/pallas_call | solution.py:1146
  244.0 2.8 %collective-permute-done.15.refs_0_ = bf16[1728,768]{1,0:T(8,128)(2,1)S(1)} collective-permute-done((bf16[1728,768]{1,0:T(8,128)(2,1)}, bf16[1728,768]{1,0:T(8,128)(2,1)S(1)}, u32[]{:S(2)}, u32[]{:S(2)}) %collective-permute-start.15) | collective-permute-done | bytes 2654240 | tf_op jit(solution)/shard_map/ppermute | solution.py:1368
  250.1 3.5 %collective-permute-start.17 = (bf16[192,768]{1,0:T(8,128)(2,1)}, bf16[192,768]{1,0:T(8,128)(2,1)S(1)}, u32[]{:S(2)}, u32[]{:S(2)}) collective-permute-start(bf16[192,768]{1,0:T(8,128)(2,1)} %rider.1.one_ref), channel_id=1, source_target_pairs={{0,16},{1,17},{2,18},{3,19},{4,20},{5,21},{6,22},{7,23},{8,24},{9,... | collective-permute-start | bytes 884744 | tf_op jit(solution)/shard_map/ppermute | solution.py:1368
  253.6 4.0 %finish_pair.3 = (f32[768,1536]{1,0:T(8,128)}, f32[1536,768]{1,0:T(8,128)}) custom-call(s32[1]{0:T(128)} %bitcast.7.which_ref, bf16[1728,768]{1,0:T(8,128)(2,1)} %pass.36.part_ref.after_ref.got_ref, bf16[1728,768]{1,0:T(8,128)(2,1)} %pass.36.part_ref.after_ref.got_ref, ...), custom_call_target="tpu_custom_call", output_to_operand_aliasing={{0}: (3, {}), {1}: (4, {})} | custom-call | tf_op jit(solution)/shard_map/finish_pair/pallas_call | solution.py:1146
  257.6 4.0 %hidden.1 = (bf16[256,1536]{1,0:T(8,128)(2,1)}, f32[256,1536]{1,0:T(8,128)}) custom-call(s32[1]{0:T(128)} %bitcast.rank_ref, bf16[1024,1536]{1,0:T(8,128)(2,1)} %hidden_ref.3, bf16[1024,1536]{1,0:T(8,128)(2,1)} %cotan_ref.5, bf16[256,3072]{1,0:T(8,128)(2,1)} %get-tuple-element.123.kept_ref, bf16[256,3072]{1,0:T(8,128)(2,1)} %pass.37.got_ref, ...), custom_call_target="tpu_custom_call" | custom-call | tf_op jit(solution)/shard_map/hidden/pallas_call | solution.py:1085
  261.6 2.6 finish.3.refs_1_
  (114 shorter events, 67.5 us)
Async XLA Ops:
  27.3 1.6 collective-permute-start
  29.6 4.7 %collective-permute-start.1 = (f32[8,1024]{1,0:T(8,128)S(1)}, f32[8,1024]{1,0:T(8,128)S(1)}, u32[]{:S(2)}, u32[]{:S(2)}) collective-permute-start(f32[8,1024]{1,0:T(8,128)S(1)} %add.159), channel_id=1, source_target_pairs={{0,2},{1,3},{2,0},{3,1},{4,6},{5,7},{6,4},{7,5},{8,10},{9,11},{10,... | collective-permute-start | bytes 98312 | tf_op jit(solution)/shard_map/ppermute | solution.py:1226
  49.4 29.2 %collective-permute-start.2 = (bf16[1536,768]{1,0:T(8,128)(2,1)}, bf16[1536,768]{1,0:T(8,128)(2,1)S(1)}, u32[]{:S(2)}, u32[]{:S(2)}) collective-permute-start(bf16[1536,768]{1,0:T(8,128)(2,1)} %get-tuple-element.99.after_ref), channel_id=1, source_target_pairs={{0,4},{1,9},{2,6},{3,11},{4,0},{5,13},{6,2},{7,15},{8,12},{9,1},{1... | collective-permute-start | bytes 7077896 | tf_op jit(solution)/shard_map/ppermute | solution.py:1368
  81.8 2.2 copy-start.9
  81.9 16.3 %collective-permute-start.3 = (bf16[768,768]{1,0:T(8,128)(2,1)S(1)}, bf16[768,768]{1,0:T(8,128)(2,1)S(1)}, u32[]{:S(2)}, u32[]{:S(2)}) collective-permute-start(bf16[768,768]{1,0:T(8,128)(2,1)S(1)} %add_convert_fusion.after_ref), channel_id=1, source_target_pairs={{0,8},{1,5},{2,10},{3,7},{4,12},{5,1},{6,14},{7,3},{8,0},{9,13},{1... | collective-permute-start | bytes 3538952 | tf_op jit(solution)/shard_map/ppermute | solution.py:1368
  103.3 2.0 copy-start.5
  103.3 25.2 %collective-permute-start.4 = (bf16[768,768]{1,0:T(8,128)(2,1)}, bf16[768,768]{1,0:T(8,128)(2,1)}, u32[]{:S(2)}, u32[]{:S(2)}) collective-permute-start(bf16[768,768]{1,0:T(8,128)(2,1)} %pass.22), channel_id=1, source_target_pairs={{0,4},{1,9},{2,6},{3,11},{4,0},{5,13},{6,2},{7,15},{8,12},{9,1},{1... | collective-permute-start | bytes 3538952 | tf_op jit(solution)/shard_map/ppermute | solution.py:1368
  105.3 23.2 %collective-permute-start.5 = (bf16[384,768]{1,0:T(8,128)(2,1)S(1)}, bf16[384,768]{1,0:T(8,128)(2,1)S(1)}, u32[]{:S(2)}, u32[]{:S(2)}) collective-permute-start(bf16[384,768]{1,0:T(8,128)(2,1)S(1)} %copy-done.5), channel_id=1, source_target_pairs={{0,16},{1,17},{2,18},{3,19},{4,20},{5,21},{6,22},{7,23},{8,24},{9,... | collective-permute-start | bytes 1769480 | tf_op jit(solution)/shard_map/ppermute | solution.py:1368
  129.4 2.3 copy-start.8
  134.2 7.1 %collective-permute-start.9 = (bf16[272,768]{1,0:T(8,128)(2,1)}, bf16[272,768]{1,0:T(8,128)(2,1)}, u32[]{:S(2)}, u32[]{:S(2)}) collective-permute-start(bf16[272,768]{1,0:T(8,128)(2,1)} %pass.26), channel_id=1, source_target_pairs={{0,1},{1,0},{2,3},{3,2},{4,5},{5,4},{6,7},{7,6},{8,9},{9,8},{10,11... | collective-permute-start | bytes 1253384 | tf_op jit(solution)/shard_map/ppermute | solution.py:1368
  134.2 67.6 %collective-permute-start.6 = (bf16[512,3072]{1,0:T(8,128)(2,1)}, bf16[512,3072]{1,0:T(8,128)(2,1)S(1)}, u32[]{:S(2)}, u32[]{:S(2)}) collective-permute-start(bf16[512,3072]{1,0:T(8,128)(2,1)} %pass.25), channel_id=1, source_target_pairs={{0,1},{1,0},{2,3},{3,2},{4,5},{5,4},{6,7},{7,6},{8,9},{9,8},{10,11... | collective-permute-start | bytes 9437192 | tf_op jit(solution)/shard_map/ppermute | solution.py:1368
  134.7 29.5 %collective-permute-start.8 = (bf16[384,768]{1,0:T(8,128)(2,1)}, bf16[384,768]{1,0:T(8,128)(2,1)}, u32[]{:S(2)}, u32[]{:S(2)}) collective-permute-start(bf16[384,768]{1,0:T(8,128)(2,1)} %add_convert_fusion.1.refs_1_), channel_id=1, source_target_pairs={{0,16},{1,17},{2,18},{3,19},{4,20},{5,21},{6,22},{7,23},{8,24},{9,... | collective-permute-start | bytes 1769480 | tf_op jit(solution)/shard_map/ppermute | solution.py:1368
  137.2 27.0 %collective-permute-start.7 = (bf16[384,768]{1,0:T(8,128)(2,1)}, bf16[384,768]{1,0:T(8,128)(2,1)}, u32[]{:S(2)}, u32[]{:S(2)}) collective-permute-start(bf16[384,768]{1,0:T(8,128)(2,1)} %add_convert_fusion.2.refs_1_), channel_id=1, source_target_pairs={{0,8},{1,5},{2,10},{3,7},{4,12},{5,1},{6,14},{7,3},{8,0},{9,13},{1... | collective-permute-start | bytes 1769480 | tf_op jit(solution)/shard_map/ppermute | solution.py:1368
  144.1 6.1 %collective-permute-start.10 = (bf16[144,768]{1,0:T(8,128)(2,1)}, bf16[144,768]{1,0:T(8,128)(2,1)S(1)}, u32[]{:S(2)}, u32[]{:S(2)}) collective-permute-start(bf16[144,768]{1,0:T(8,128)(2,1)} %pad_maximum_fusion.1.refs_1_), channel_id=1, source_target_pairs={{0,2},{1,3},{2,0},{3,1},{4,6},{5,7},{6,4},{7,5},{8,10},{9,11},{10,... | collective-permute-start | bytes 663560 | tf_op jit(solution)/shard_map/ppermute | solution.py:1368
  169.0 42.1 %collective-permute-start.13 = (bf16[960,768]{1,0:T(8,128)(2,1)}, bf16[960,768]{1,0:T(8,128)(2,1)}, u32[]{:S(2)}, u32[]{:S(2)}) collective-permute-start(bf16[960,768]{1,0:T(8,128)(2,1)} %pad_maximum_fusion.refs_1_.own_ref.own_extra_ref), channel_id=1, source_target_pairs={{0,8},{1,5},{2,10},{3,7},{4,12},{5,1},{6,14},{7,3},{8,0},{9,13},{1... | collective-permute-start | bytes 4423688 | tf_op jit(solution)/shard_map/ppermute | solution.py:1368
  169.7 26.4 %collective-permute-start.11 = (bf16[192,768]{1,0:T(8,128)(2,1)}, bf16[192,768]{1,0:T(8,128)(2,1)S(1)}, u32[]{:S(2)}, u32[]{:S(2)}) collective-permute-start(bf16[192,768]{1,0:T(8,128)(2,1)} %add_convert_fusion.5.refs_1_), channel_id=1, source_target_pairs={{0,16},{1,17},{2,18},{3,19},{4,20},{5,21},{6,22},{7,23},{8,24},{9,... | collective-permute-start | bytes 884744 | tf_op jit(solution)/shard_map/ppermute | solution.py:1368
  198.3 3.5 %copy-start.10 = (bf16[192,768]{1,0:T(8,128)(2,1)}, bf16[192,768]{1,0:T(8,128)(2,1)S(1)}, u32[]{:S(2)}) copy-start(bf16[192,768]{1,0:T(8,128)(2,1)S(1)} %add_convert_fusion.4.refs_1_) | copy-start | bytes 884740
  198.3 10.8 %collective-permute-start.14 = (bf16[192,768]{1,0:T(8,128)(2,1)S(1)}, bf16[192,768]{1,0:T(8,128)(2,1)}, u32[]{:S(2)}, u32[]{:S(2)}) collective-permute-start(bf16[192,768]{1,0:T(8,128)(2,1)S(1)} %add_convert_fusion.4.refs_1_), channel_id=1, source_target_pairs={{0,16},{1,17},{2,18},{3,19},{4,20},{5,21},{6,22},{7,23},{8,24},{9,... | collective-permute-start | bytes 884744 | tf_op jit(solution)/shard_map/ppermute | solution.py:1368
  211.0 3.8 %copy-start.6 = (bf16[384,768]{1,0:T(8,128)(2,1)S(1)}, bf16[384,768]{1,0:T(8,128)(2,1)}, u32[]{:S(2)}) copy-start(bf16[384,768]{1,0:T(8,128)(2,1)} %bitcast_select_fusion.2.refs_1_) | copy-start | bytes 1769476
  214.6 32.2 %collective-permute-start.15 = (bf16[1728,768]{1,0:T(8,128)(2,1)}, bf16[1728,768]{1,0:T(8,128)(2,1)S(1)}, u32[]{:S(2)}, u32[]{:S(2)}) collective-permute-start(bf16[1728,768]{1,0:T(8,128)(2,1)} %join.1.refs_1_.part_ref.own_ref), channel_id=1, source_target_pairs={{0,4},{1,9},{2,6},{3,11},{4,0},{5,13},{6,2},{7,15},{8,12},{9,1},{1... | collective-permute-start | bytes 7962632 | tf_op jit(solution)/shard_map/ppermute | solution.py:1368
  214.9 19.3 %collective-permute-start.16 = (bf16[384,768]{1,0:T(8,128)(2,1)S(1)}, bf16[384,768]{1,0:T(8,128)(2,1)}, u32[]{:S(2)}, u32[]{:S(2)}) collective-permute-start(bf16[384,768]{1,0:T(8,128)(2,1)S(1)} %copy-done.6), channel_id=1, source_target_pairs={{0,8},{1,5},{2,10},{3,7},{4,12},{5,1},{6,14},{7,3},{8,0},{9,13},{1... | collective-permute-start | bytes 1769480 | tf_op jit(solution)/shard_map/ppermute | solution.py:1368
  219.9 37.8 %collective-permute-start.12 = (bf16[256,3072]{1,0:T(8,128)(2,1)}, bf16[256,3072]{1,0:T(8,128)(2,1)}, u32[]{:S(2)}, u32[]{:S(2)}) collective-permute-start(bf16[256,3072]{1,0:T(8,128)(2,1)} %get-tuple-element.124.refs_1_), channel_id=1, source_target_pairs={{0,2},{1,3},{2,0},{3,1},{4,6},{5,7},{6,4},{7,5},{8,10},{9,11},{10,... | collective-permute-start | bytes 4718600 | tf_op jit(solution)/shard_map/ppermute | solution.py:1368
  236.5 25.2 %collective-permute-start.18 = (bf16[768,768]{1,0:T(8,128)(2,1)}, bf16[768,768]{1,0:T(8,128)(2,1)}, u32[]{:S(2)}, u32[]{:S(2)}) collective-permute-start(bf16[768,768]{1,0:T(8,128)(2,1)} %bitcast_select_fusion.after_ref.part_ref), channel_id=1, source_target_pairs={{0,4},{1,9},{2,6},{3,11},{4,0},{5,13},{6,2},{7,15},{8,12},{9,1},{1... | collective-permute-start | bytes 3538952 | tf_op jit(solution)/shard_map/ppermute | solution.py:1368
  250.1 14.1 %collective-permute-start.17 = (bf16[192,768]{1,0:T(8,128)(2,1)}, bf16[192,768]{1,0:T(8,128)(2,1)S(1)}, u32[]{:S(2)}, u32[]{:S(2)}) collective-permute-start(bf16[192,768]{1,0:T(8,128)(2,1)} %rider.1.one_ref), channel_id=1, source_target_pairs={{0,16},{1,17},{2,18},{3,19},{4,20},{5,21},{6,22},{7,23},{8,24},{9,... | collective-permute-start | bytes 884744 | tf_op jit(solution)/shard_map/ppermute | solution.py:1368
  (13 other events, 15.5 us)
